TPU v7x, 32 devices: a whole 2x2x4 slice. The times are simulated.
32 devices in a mesh: gy: 4 (over y, x), gx: 8 (over z, core).
Axes of the slice: x: 2, y: 2, z: 4, core: 2. Of those that a mesh axis runs over, the one named last changes fastest.
Arguments:
- direction: float32 [4, 32, 16, 512], P(None, 'gx', 'gy'), may hold values from -6 to 6
- solution: float32 [4, 32, 16, 512], P(None, 'gx', 'gy'), may hold values from -6 to 6
- residual: float32 [4, 32, 16, 512], P(None, 'gx', 'gy'), may hold values from -6 to 6
- north_coef: float32 [16, 512], P('gy'), may hold values from 0.12 to 0.25
- east_coef: float32 [16, 512], P('gy'), may hold values from 0.12 to 0.25
- ocean: int32 [16, 512], P('gy'), may hold values 0 or 1
- vert_coef: float32 [32, 16, 512], P(None, 'gy', 'gx'), may hold values from 0.1 to 10
- obs_owner: int32 [4, 8, 512, 1], P('gy', 'gx'), may hold values from 0 to 31; in each aligned block of 512 rows (0 to 511, 512 to 1023, ..., all dimensions but the last counted through in order) at most 32 rows name the same one
- obs_row: int32 [4, 8, 512], P('gy', 'gx'), may hold values from 0 to 2
- obs_col: int32 [4, 8, 512], P('gy', 'gx'), may hold values from 0 to 62
- obs_frac: float32 [4, 8, 2, 512], P('gy', 'gx'), may hold values from 0 to 1
- error_inverse: float32 [4, 8, 128, 128], P('gy', 'gx'), may hold values from -3 to 6, as said below
Outputs:
- solution_next: float32 [4, 32, 16, 512], P(None, 'gx', 'gy')
- residual_next: float32 [4, 32, 16, 512], P(None, 'gx', 'gy')
- direction_next: float32 [4, 32, 16, 512], P(None, 'gx', 'gy')
Inputs may be any that keep to these rules, and one draw needn't show every extreme that they name: `obs_owner`: the observations of one device name each owner at most 32 times, and in every draw some device names some owner exactly 32 times. `error_inverse`: symmetric positive definite for every owner.
All inputs are finite; a program needn't handle non-finite values. No bound on the sum of `ocean` on one device may be relied on, other than what follows from the above.
Results may differ from a plain program's by a relative error of at most 0.000078.
Values sent between devices are 32-bit elements; how exact they have to be, the bound alone decides.
No kernel may reach another device: no remote copies, remote signals or barrier semaphores. Data moves between devices by JAX's collectives and lax.ppermute only.
A program may use at most 128 MiB of HBM per device.

v0:
```python
import jax
import jax.numpy as jnp
from jax import lax
from jax.sharding import PartitionSpec as P

NSTEP = 4


def padded(cells, sides, width):
    for axis, dim in sides:
        count = lax.axis_size(axis)
        ends = count - 1
        head = lax.slice_in_dim(cells, 0, width, axis=dim)
        tail = lax.slice_in_dim(cells, cells.shape[dim] - width, cells.shape[dim], axis=dim)
        cells = jnp.concatenate(
            [
                lax.ppermute(tail, axis, [(i, (i + 1) % count) for i in range(ends)]),
                cells,
                lax.ppermute(head, axis, [((i + 1) % count, i) for i in range(ends)]),
            ],
            axis=dim,
        )
    return cells


def lateral_faces(north_ext, east_ext, ocean_ext):
    ocean_next = jnp.concatenate([ocean_ext[1:], jnp.zeros_like(ocean_ext[:1])], axis=0)
    north_face = north_ext * ocean_ext * ocean_next
    east_face = east_ext * ocean_ext * jnp.roll(ocean_ext, -1, axis=1)
    return (north_face, east_face, ocean_ext)


def diffuse_once(values_grid, north_face, east_face, ocean_ext):
    north_flux = north_face[:-1] * (values_grid[:, :, 1:, :] - values_grid[:, :, :-1, :])
    east_flux = east_face * (jnp.roll(values_grid, -1, axis=3) - values_grid)
    lateral = east_flux - jnp.roll(east_flux, 1, axis=3)
    return (
        ocean_ext[1:-1] * values_grid[:, :, 1:-1, :]
        + north_flux[:, :, 1:, :]
        - north_flux[:, :, :-1, :]
        + lateral[:, :, 1:-1, :]
    )


def lateral_pass(values_tile, faces):
    north_face, east_face, ocean_ext = faces
    grown = padded(values_tile, (("gy", 2),), NSTEP)
    total_rows = grown.shape[2]
    for step_index in range(NSTEP):
        upper = total_rows - step_index
        grown = diffuse_once(
            grown,
            north_face[step_index:upper],
            east_face[step_index:upper],
            ocean_ext[step_index:upper],
        )
    return grown


def vertical_factors(vert_coef):
    inverse_rows = []
    upper_ratio = []
    for layer_index in range(vert_coef.shape[0]):
        diagonal = 1.0 + vert_coef[layer_index]
        if layer_index > 0:
            diagonal = (
                diagonal + vert_coef[layer_index - 1] + vert_coef[layer_index - 1] * upper_ratio[-1]
            )
        inverse = 1.0 / diagonal
        inverse_rows.append(inverse)
        upper_ratio.append(-vert_coef[layer_index] * inverse)
    return (inverse_rows, upper_ratio)


def vertical_solve(values_col, vert_coef, factors):
    inverse_rows, upper_ratio = factors
    layers = values_col.shape[1]
    forward = []
    for layer_index in range(layers):
        source = values_col[:, layer_index]
        if layer_index > 0:
            source = source + vert_coef[layer_index - 1] * forward[-1]
        forward.append(source * inverse_rows[layer_index])
    result = [forward[-1]]
    for layer_index in range(layers - 2, -1, -1):
        result.append(forward[layer_index] - upper_ratio[layer_index] * result[-1])
    return jnp.stack(result[::-1], axis=1)


def observe_weigh_spread(columns, obs_owner, obs_row, obs_col, obs_frac, error_inverse):
    var_count, lev_count, lat_rows, lon_cols = columns.shape
    kv_width = var_count * lev_count
    rows_y = lax.axis_size("gy")
    cols_x = lax.axis_size("gx")
    device_count = rows_y * cols_x
    obs_count = obs_row.shape[-1]
    capacity = 2 * obs_count // device_count
    flat = columns.reshape(kv_width, lat_rows * lon_cols)
    cell = obs_row.reshape(-1) * lon_cols + obs_col.reshape(-1)
    corners = (cell, cell + 1, cell + lon_cols, cell + lon_cols + 1)
    lat_frac = obs_frac[0, 0, 0]
    lon_frac = obs_frac[0, 0, 1]
    weights = (
        (1.0 - lat_frac) * (1.0 - lon_frac),
        (1.0 - lat_frac) * lon_frac,
        lat_frac * (1.0 - lon_frac),
        lat_frac * lon_frac,
    )
    profile = weights[0] * jnp.take(flat, corners[0], axis=1)
    for corner_index in range(1, 4):
        profile = profile + weights[corner_index] * jnp.take(flat, corners[corner_index], axis=1)
    owners = obs_owner.reshape(-1)
    onehot = (owners[:, None] == jnp.arange(device_count, dtype=jnp.int32)[None, :]).astype(
        jnp.int32
    )
    running = jnp.cumsum(onehot, axis=0)
    rank_in = jnp.sum(running * onehot, axis=1) - 1
    slot = owners * capacity + rank_in
    outgoing = jnp.zeros((device_count * capacity, kv_width), jnp.float32).at[slot].set(profile.T)
    outgoing = outgoing.reshape(rows_y, cols_x, capacity, kv_width)
    matrix = error_inverse.reshape(kv_width, kv_width)
    arrived = lax.all_to_all(
        lax.all_to_all(outgoing, "gy", split_axis=0, concat_axis=0, tiled=True),
        "gx",
        split_axis=1,
        concat_axis=1,
        tiled=True,
    )
    weighted = jnp.dot(
        arrived.reshape(-1, kv_width),
        matrix,
        precision=lax.Precision.HIGHEST,
        preferred_element_type=jnp.float32,
    ).reshape(rows_y, cols_x, capacity, kv_width)
    returned = lax.all_to_all(
        lax.all_to_all(weighted, "gy", split_axis=0, concat_axis=0, tiled=True),
        "gx",
        split_axis=1,
        concat_axis=1,
        tiled=True,
    )
    back = returned.reshape(device_count * capacity, kv_width)[slot].T
    spread = jnp.zeros((kv_width, lat_rows * lon_cols), jnp.float32)
    for corner_index in range(4):
        spread = spread.at[:, corners[corner_index]].add(weights[corner_index] * back)
    return spread.reshape(var_count, lev_count, lat_rows, lon_cols)


def per_device(
    direction,
    solution,
    residual,
    north_coef,
    east_coef,
    ocean,
    vert_coef,
    obs_owner,
    obs_row,
    obs_col,
    obs_frac,
    error_inverse,
):
    stacked = jnp.stack([north_coef, east_coef, ocean.astype(jnp.float32)])
    reach = NSTEP
    grown_coef = padded(stacked, (("gy", 1),), reach)
    faces = lateral_faces(grown_coef[0], grown_coef[1], grown_coef[2])
    factors = vertical_factors(vert_coef)
    smoothed = lateral_pass(direction, faces)
    columns = lax.all_to_all(smoothed, "gx", split_axis=3, concat_axis=1, tiled=True)
    columns = vertical_solve(columns, vert_coef, factors)
    spread = observe_weigh_spread(columns, obs_owner, obs_row, obs_col, obs_frac, error_inverse)
    spread = vertical_solve(spread, vert_coef, factors)
    tiles = lax.all_to_all(spread, "gx", split_axis=1, concat_axis=3, tiled=True)
    image = direction + lateral_pass(tiles, faces)
    norm_now, curvature = lax.psum(
        (jnp.sum(residual * residual), jnp.sum(direction * image)), ("gy", "gx")
    )
    alpha = norm_now / curvature
    residual_next = residual - alpha * image
    norm_next = lax.psum(jnp.sum(residual_next * residual_next), ("gy", "gx"))
    solution_next = solution + alpha * direction
    direction_next = residual_next + norm_next / norm_now * direction
    return (solution_next, residual_next, direction_next)


def solution(mesh):
    return jax.shard_map(
        per_device,
        mesh=mesh,
        in_specs=(
            P(None, "gx", "gy", None),
            P(None, "gx", "gy", None),
            P(None, "gx", "gy", None),
            P("gy", None),
            P("gy", None),
            P("gy", None),
            P(None, "gy", "gx"),
            P("gy", "gx", None, None),
            P("gy", "gx", None),
            P("gy", "gx", None),
            P("gy", "gx", None, None),
            P("gy", "gx", None, None),
        ),
        out_specs=(P(None, "gx", "gy", None), P(None, "gx", "gy", None), P(None, "gx", "gy", None)),
        check_vma=False,
    )
```

profile of v0, /device:TPU:0, one launch (start us, length us, event | category | flops | bytes accessed | tf_op | source)
XLA Modules:
  0.0 276.7 jit_solution(15101729497796541389)
XLA Ops:
  0.7 0.8 fusion.155
  1.4 0.7 pad_maximum_fusion.11
  2.1 4.8 %collective-permute-start = (f32[3,4,512]{2,1,0:T(4,128)S(1)}, f32[3,4,512]{2,1,0:T(4,128)S(1)}, u32[]{:S(2)}, u32[]{:S(2)}) collective-permute-start(f32[3,4,512]{2,1,0:T(4,128)S(1)} %pad_maximum_fusion.11), channel_id=1, source_target_pairs={{0,8},{8,16},{16,24},{1,9},{9,17},{17,25},{2,10},{10,18},{18,26},{... | collective-permute-start | bytes 73736 | tf_op jit(solution)/shard_map/ppermute | solution.py:17
  7.0 1.3 collective-permute-start.1
  8.3 4.6 %collective-permute-start.2 = (f32[4,4,4,512]{3,2,1,0:T(4,128)}, f32[4,4,4,512]{3,2,1,0:T(4,128)S(1)}, u32[]{:S(2)}, u32[]{:S(2)}) collective-permute-start(f32[4,4,4,512]{3,2,1,0:T(4,128)} %param.14), channel_id=1, source_target_pairs={{0,8},{8,16},{16,24},{1,9},{9,17},{17,25},{2,10},{10,18},{18,26},{... | collective-permute-start | bytes 393224 | tf_op jit(solution)/shard_map/ppermute | solution.py:17
  12.8 1.3 collective-permute-start.3
  14.9 0.7 fusion.102
  15.6 0.7 fusion.103
  16.3 0.7 fusion.104
  17.0 0.7 fusion.105
  17.7 0.7 fusion.106
  18.4 0.7 fusion.107
  19.1 0.7 fusion.108
  19.8 0.7 fusion.109
  20.6 0.7 fusion.110
  21.3 0.7 fusion.111
  22.0 0.7 fusion.112
  22.7 0.7 fusion.113
  23.4 0.7 fusion.114
  24.1 0.7 fusion.115
  24.8 0.7 fusion.116
  25.5 0.7 fusion.117
  26.3 0.7 fusion.118
  27.0 0.7 fusion.119
  27.7 0.7 fusion.120
  28.4 0.7 fusion.121
  29.1 0.7 fusion.122
  29.8 0.7 fusion.123
  30.5 0.7 fusion.124
  31.2 0.7 fusion.125
  35.5 0.9 fusion.131
  36.4 0.8 fusion.156
  37.8 1.2 reduce-window.6
  39.2 0.8 fusion.62
  40.8 0.7 pad_maximum_fusion.10
  41.8 1.0 pad_maximum_fusion.2
  45.7 3.3 %copy.147 = f32[4,4,4,512]{2,1,0,3:T(4,128)} copy(f32[4,4,4,512]{3,2,1,0:T(4,128)S(1)} %fusion.47) | data formatting | bytes 262144 | tf_op jit(solution)/shard_map/add | solution.py:38
  49.1 7.1 %reshape.403 = f32[8,1,4096]{2,1,0:T(1,128)} reshape(f32[512,4,4,4]{3,2,1,0:T(4,128)} %bitcast.337) | data formatting | bytes 262144
  56.1 4.9 %all-to-all-start = ((f32[8,1,4096]{2,1,0:T(1,128)}), f32[8,1,4096]{2,1,0:T(1,128)S(1)}, u32[]{:S(2)}, u32[]{:S(2)}) async-start(f32[8,1,4096]{2,1,0:T(1,128)} %reshape.403), calls=%async_computation | async-start | bytes 262144 | tf_op jit(solution)/shard_map/all_to_all | solution.py:169
  61.1 6.7 %all-to-all-done = f32[8,1,4096]{2,1,0:T(1,128)S(1)} async-done(((f32[8,1,4096]{2,1,0:T(1,128)}), f32[8,1,4096]{2,1,0:T(1,128)S(1)}, u32[]{:S(2)}, u32[]{:S(2)}) %all-to-all-start) | async-done | bytes 131104 | tf_op jit(solution)/shard_map/all_to_all | solution.py:169
  68.3 1.0 reduce.2
  69.3 7.4 %reshape.404 = f32[512,4,4,4]{3,2,1,0:T(4,128)} reshape(f32[8,4096]{1,0:T(8,128)S(1)} %reduce.2) | data formatting | bytes 262144
  76.7 3.7 %copy.148 = f32[4,4,4,8,64]{4,1,3,2,0:T(4,128)S(1)} copy(f32[4,4,4,8,64]{2,1,0,4,3:T(4,128)} %bitcast.338) | data formatting | bytes 262144 | tf_op jit(solution)/shard_map/all_to_all | solution.py:169
  82.2 6.4 %scatter_custom_fusion = f32[1024,128]{1,0:T(8,128)S(1)} fusion(s32[512]{0:T(512)S(1)} %bitcast.504, f32[]{:T(128)} %constant.8.clone.1, f32[]{:T(128)} %constant.15.clone.4, f32[512]{0:T(512)S(1)} %get-tuple-element.240, f32[512]{0:T(512)S(1)} %get-tuple-element.239, f32[512]{0:T(512)S(1)} %get-tuple-element.241, f32[512]{0:T(512)S(1)} %get-tuple-element.238, ...), kind=kCustom, calls=%fused_computation.82 | custom fusion | flops 720896 | bytes 1075208 | tf_op jit(solution)/shard_map/scatter | solution.py:119
  88.6 13.8 %all_to_all.56 = f32[4,8,32,128]{3,2,1,0:T(8,128)S(1)} all-to-all(f32[4,8,32,128]{3,2,1,0:T(8,128)S(1)} %bitcast.346), channel_id=1, replica_groups=mesh['gy'=4,'gx'=8] {'gy'}, dimensions={0} | all-to-all | bytes 1048576 | tf_op jit(solution)/shard_map/all_to_all | solution.py:123
  102.4 18.0 %all_to_all.57 = f32[4,8,32,128]{3,2,0,1:T(8,128)S(1)} all-to-all(f32[4,8,32,128]{3,2,0,1:T(8,128)S(1)} %copy.154), channel_id=1, replica_groups=mesh['gy'=4,'gx'=8] {'gx'}, dimensions={1} | all-to-all | bytes 1048576 | tf_op jit(solution)/shard_map/all_to_all | solution.py:122
  121.0 10.8 %all_to_all.58 = f32[4,8,32,128]{3,2,1,0:T(8,128)S(1)} all-to-all(f32[4,8,32,128]{3,2,1,0:T(8,128)S(1)} %fusion.10), channel_id=1, replica_groups=mesh['gy'=4,'gx'=8] {'gy'}, dimensions={0} | all-to-all | bytes 1048576 | tf_op jit(solution)/shard_map/all_to_all | solution.py:136
  131.8 0.8 copy.156
  132.6 3.5 %all-to-all-start.4 = ((f32[4,8,32,128]{3,2,0,1:T(8,128)}), f32[4,8,32,128]{3,2,0,1:T(8,128)S(1)}, u32[]{:S(2)}, u32[]{:S(2)}) async-start(f32[4,8,32,128]{3,2,0,1:T(8,128)} %copy.156), calls=%async_computation.4 | async-start | bytes 1048576 | tf_op jit(solution)/shard_map/all_to_all | solution.py:135
  136.2 15.2 %all-to-all-done.4 = f32[4,8,32,128]{3,2,0,1:T(8,128)S(1)} async-done(((f32[4,8,32,128]{3,2,0,1:T(8,128)}), f32[4,8,32,128]{3,2,0,1:T(8,128)S(1)}, u32[]{:S(2)}, u32[]{:S(2)}) %all-to-all-start.4) | async-done | bytes 524320 | tf_op jit(solution)/shard_map/all_to_all | solution.py:135
  151.5 1.0 gather_fusion
  152.5 2.4 scatter_custom_fusion.1
  154.9 3.5 %scatter_custom_fusion.2 = f32[128,256]{0,1:T(8,128)S(1)} fusion(f32[128,256]{0,1:T(8,128)S(1)} %scatter_custom_fusion.1, s32[512]{0:T(512)S(1)} %bitcast.511, f32[512,128]{1,0:T(8,128)S(1)} %gather_fusion, f32[512]{0:T(512)S(1)} %get-tuple-element.241), kind=kCustom, calls=%fused_computation.99 | custom fusion | flops 131072 | bytes 395264 | tf_op jit(solution)/shard_map/scatter-add | solution.py:145
  158.4 3.5 %scatter_custom_fusion.3 = f32[128,256]{0,1:T(8,128)S(1)} fusion(f32[128,256]{0,1:T(8,128)S(1)} %scatter_custom_fusion.2, s32[512]{0:T(512)S(1)} %bitcast.510, f32[512,128]{1,0:T(8,128)S(1)} %gather_fusion, f32[512]{0:T(512)S(1)} %get-tuple-element.239), kind=kCustom, calls=%fused_computation.97 | custom fusion | flops 131072 | bytes 395264 | tf_op jit(solution)/shard_map/scatter-add | solution.py:145
  161.9 3.8 %scatter_custom_fusion.4 = f32[128,256]{0,1:T(8,128)S(1)} fusion(f32[128,256]{0,1:T(8,128)S(1)} %scatter_custom_fusion.3, s32[512]{0:T(512)S(1)} %bitcast.509, f32[512,128]{1,0:T(8,128)S(1)} %gather_fusion, f32[512]{0:T(512)S(1)} %get-tuple-element.240), kind=kCustom, calls=%fused_computation.95 | custom fusion | flops 131072 | bytes 395264 | tf_op jit(solution)/shard_map/scatter-add | solution.py:145
  167.8 9.2 %all_to_all.59 = f32[8,1,4096]{2,1,0:T(1,128)S(1)} all-to-all(f32[8,1,4096]{2,1,0:T(1,128)S(1)} %reshape.405), channel_id=1, replica_groups=mesh['gy'=4,'gx'=8] {'gx'}, dimensions={0} | all-to-all | bytes 262144 | tf_op jit(solution)/shard_map/all_to_all | solution.py:173
  177.0 1.0 reduce.3
  178.4 2.8 %collective-permute-start.4 = (f32[4,4,4,512]{3,2,1,0:T(4,128)S(1)}, f32[4,4,4,512]{3,2,1,0:T(4,128)S(1)}, u32[]{:S(2)}, u32[]{:S(2)}) collective-permute-start(f32[4,4,4,512]{3,2,1,0:T(4,128)S(1)} %all_to_all.49), channel_id=1, source_target_pairs={{0,8},{8,16},{16,24},{1,9},{9,17},{17,25},{2,10},{10,18},{18,26},{... | collective-permute-start | bytes 393224 | tf_op jit(solution)/shard_map/ppermute | solution.py:17
  181.2 1.3 collective-permute-start.5
  183.7 4.7 %collective-permute-done.5 = f32[4,4,4,512]{3,2,1,0:T(4,128)S(1)} collective-permute-done((f32[4,4,4,512]{3,2,1,0:T(4,128)S(1)}, f32[4,4,4,512]{3,2,1,0:T(4,128)S(1)}, u32[]{:S(2)}, u32[]{:S(2)}) %collective-permute-start.5) | collective-permute-done | bytes 131104 | tf_op jit(solution)/shard_map/ppermute | solution.py:19
  191.3 0.8 multiply_reduce_fusion.1
  192.1 39.0 %all-reduce.1 = (f32[]{:T(128)}, f32[]{:T(128)}) all-reduce(f32[]{:T(128)} %multiply_reduce_fusion.2, f32[]{:T(128)} %get-tuple-element.8), channel_id=1, replica_groups=mesh['gy'=4,'gx'=8] {'gy','gx'}, use_global_device_ids=true, to_apply=%region_1.2 | all-reduce | flops 2 | bytes 16 | tf_op jit(solution)/shard_map/psum | solution.py:175
  233.0 41.6 %psum.23 = f32[]{:T(128)} all-reduce(f32[]{:T(128)} %get-tuple-element.6), channel_id=1, replica_groups=mesh['gy'=4,'gx'=8] {'gy','gx'}, use_global_device_ids=true, to_apply=%region_13.15 | all-reduce | flops 1 | bytes 8 | tf_op jit(solution)/shard_map/psum | solution.py:180
  276.0 0.7 multiply_add_fusion
  (124 shorter events, 19.0 us)
Async XLA Ops:
  0.6 119.8 %copy-start = (f32[1,1,128,128]{3,2,1,0:T(8,128)S(1)}, f32[1,1,128,128]{3,2,1,0:T(8,128)}, u32[]{:S(2)}) copy-start(f32[1,1,128,128]{3,2,1,0:T(8,128)} %param.25) | copy-start | bytes 196612
  0.6 42.4 %copy-start.1 = (f32[4,4,4,512]{3,2,1,0:T(4,128)S(1)}, f32[4,4,4,512]{3,2,1,0:T(4,128)}, u32[]{:S(2)}) copy-start(f32[4,4,4,512]{3,2,1,0:T(4,128)} %param.14) | copy-start | bytes 393220
  2.1 38.6 %collective-permute-start = (f32[3,4,512]{2,1,0:T(4,128)S(1)}, f32[3,4,512]{2,1,0:T(4,128)S(1)}, u32[]{:S(2)}, u32[]{:S(2)}) collective-permute-start(f32[3,4,512]{2,1,0:T(4,128)S(1)} %pad_maximum_fusion.11), channel_id=1, source_target_pairs={{0,8},{8,16},{16,24},{1,9},{9,17},{17,25},{2,10},{10,18},{18,26},{... | collective-permute-start | bytes 73736 | tf_op jit(solution)/shard_map/ppermute | solution.py:17
  7.0 33.8 %collective-permute-start.1 = (f32[3,4,512]{2,1,0:T(4,128)S(1)}, f32[3,4,512]{2,1,0:T(4,128)S(1)}, u32[]{:S(2)}, u32[]{:S(2)}) collective-permute-start(f32[3,4,512]{2,1,0:T(4,128)S(1)} %pad_maximum_fusion.11), channel_id=1, source_target_pairs={{8,0},{16,8},{24,16},{9,1},{17,9},{25,17},{10,2},{18,10},{26,18},{... | collective-permute-start | bytes 73736 | tf_op jit(solution)/shard_map/ppermute | solution.py:19
  8.3 33.5 %collective-permute-start.2 = (f32[4,4,4,512]{3,2,1,0:T(4,128)}, f32[4,4,4,512]{3,2,1,0:T(4,128)S(1)}, u32[]{:S(2)}, u32[]{:S(2)}) collective-permute-start(f32[4,4,4,512]{3,2,1,0:T(4,128)} %param.14), channel_id=1, source_target_pairs={{0,8},{8,16},{16,24},{1,9},{9,17},{17,25},{2,10},{10,18},{18,26},{... | collective-permute-start | bytes 393224 | tf_op jit(solution)/shard_map/ppermute | solution.py:17
  12.8 29.0 %collective-permute-start.3 = (f32[4,4,4,512]{3,2,1,0:T(4,128)}, f32[4,4,4,512]{3,2,1,0:T(4,128)S(1)}, u32[]{:S(2)}, u32[]{:S(2)}) collective-permute-start(f32[4,4,4,512]{3,2,1,0:T(4,128)} %param.14), channel_id=1, source_target_pairs={{8,0},{16,8},{24,16},{9,1},{17,9},{25,17},{10,2},{18,10},{26,18},{... | collective-permute-start | bytes 393224 | tf_op jit(solution)/shard_map/ppermute | solution.py:19
  45.7 15.3 %copy-start.2 = (f32[32,4,64]{2,1,0:T(4,128)S(1)}, f32[32,4,64]{2,1,0:T(4,128)}, u32[]{:S(2)}) copy-start(f32[32,4,64]{2,1,0:T(4,128)} %param.20) | copy-start | bytes 98308
  56.1 11.7 %all-to-all-start = ((f32[8,1,4096]{2,1,0:T(1,128)}), f32[8,1,4096]{2,1,0:T(1,128)S(1)}, u32[]{:S(2)}, u32[]{:S(2)}) async-start(f32[8,1,4096]{2,1,0:T(1,128)} %reshape.403), calls=%async_computation | async-start | bytes 262144 | tf_op jit(solution)/shard_map/all_to_all | solution.py:169
  132.6 18.8 %all-to-all-start.4 = ((f32[4,8,32,128]{3,2,0,1:T(8,128)}), f32[4,8,32,128]{3,2,0,1:T(8,128)S(1)}, u32[]{:S(2)}, u32[]{:S(2)}) async-start(f32[4,8,32,128]{3,2,0,1:T(8,128)} %copy.156), calls=%async_computation.4 | async-start | bytes 1048576 | tf_op jit(solution)/shard_map/all_to_all | solution.py:135
  152.5 30.0 %copy-start.4 = (f32[4,4,4,512]{3,2,1,0:T(4,128)S(1)}, f32[4,4,4,512]{3,2,1,0:T(4,128)}, u32[]{:S(2)}) copy-start(f32[4,4,4,512]{3,2,1,0:T(4,128)} %param.16) | copy-start | bytes 393220
  178.4 5.3 %collective-permute-start.4 = (f32[4,4,4,512]{3,2,1,0:T(4,128)S(1)}, f32[4,4,4,512]{3,2,1,0:T(4,128)S(1)}, u32[]{:S(2)}, u32[]{:S(2)}) collective-permute-start(f32[4,4,4,512]{3,2,1,0:T(4,128)S(1)} %all_to_all.49), channel_id=1, source_target_pairs={{0,8},{8,16},{16,24},{1,9},{9,17},{17,25},{2,10},{10,18},{18,26},{... | collective-permute-start | bytes 393224 | tf_op jit(solution)/shard_map/ppermute | solution.py:17
  181.2 7.2 %collective-permute-start.5 = (f32[4,4,4,512]{3,2,1,0:T(4,128)S(1)}, f32[4,4,4,512]{3,2,1,0:T(4,128)S(1)}, u32[]{:S(2)}, u32[]{:S(2)}) collective-permute-start(f32[4,4,4,512]{3,2,1,0:T(4,128)S(1)} %all_to_all.49), channel_id=1, source_target_pairs={{8,0},{16,8},{24,16},{9,1},{17,9},{25,17},{10,2},{18,10},{26,18},{... | collective-permute-start | bytes 393224 | tf_op jit(solution)/shard_map/ppermute | solution.py:19
  190.3 85.6 %copy-start.5 = (f32[4,4,4,512]{3,2,1,0:T(4,128)S(1)}, f32[4,4,4,512]{3,2,1,0:T(4,128)}, u32[]{:S(2)}) copy-start(f32[4,4,4,512]{3,2,1,0:T(4,128)} %param.15) | copy-start | bytes 393220
  233.0 43.7 %copy-start.3 = (f32[4,4,4,512]{3,2,1,0:T(4,128)}, f32[4,4,4,512]{3,2,1,0:T(4,128)S(1)}, u32[]{:S(2)}) copy-start(f32[4,4,4,512]{3,2,1,0:T(4,128)S(1)} %get-tuple-element.7) | copy-start | bytes 393220
where the time goes:
time: 279 us; the launch traced here: 277 us
  blocking collectives  132 us (47%)
  other arithmetic  58.4 us (21%)
  local copies, waits for them, and re-layouts  29.7 us (11%)
  waiting for transfers between devices  27.2 us (10%)
  starting transfers between devices  24.5 us (9%)
  between operations  4.09 us (1%)
    psum x1, blocking collectives, per_device(): norm_next = lax.psum(jnp.sum(residual_next * residual_next), ('gy', 'gx'))  41.6 us
    psum x1, blocking collectives, per_device(): lax.psum((jnp.sum(residual * residual), jnp.sum(direction * image)), ('gy...  39 us
    mul x30, other arithmetic, vertical_solve(): result.append(forward[layer_index] - upper_ratio[layer_index] * result[-1])  21.5 us
    all_to_all x1, blocking collectives, observe_weigh_spread(): lax.all_to_all(lax.all_to_all(outgoing, 'gy', split_axis=0, concat_axis=0...  18 us
    all_to_all x1, waiting for transfers between devices, observe_weigh_spread(): lax.all_to_all(lax.all_to_all(weighted, 'gy', split_axis=0, concat_axis=0...  15.2 us
    unnamed x16, local copies, waits for them, and re-layouts  14.9 us
    all_to_all x1, blocking collectives, observe_weigh_spread(): lax.all_to_all(outgoing, 'gy', split_axis=0, concat_axis=0, tiled=True)  13.8 us
    scatter-add x4, other arithmetic, observe_weigh_spread(): spread.at[:, corners[corner_index]].add(weights[corner_index] * back)  13.2 us
  transfers between devices with their start and end apart: 8, of which 4 were waited for; matrix products, arithmetic and copies ran while one was open for 10% of the time, Pallas kernels for 0%

commit v1 on v0

--- a/solution.py
+++ b/solution.py
@@ -1,9 +1,455 @@
+import functools
+import math
+
 import jax
 import jax.numpy as jnp
 from jax import lax
+from jax.experimental import pallas as pl
+from jax.experimental.pallas import tpu as pltpu
 from jax.sharding import PartitionSpec as P
 
 NSTEP = 4
+LANES = 128
+HIGHEST = lax.Precision.HIGHEST
+
+
+def to_native(tile):
+    kv, rows, lons = tile.shape[0] * tile.shape[1], tile.shape[2], tile.shape[3]
+    return tile.reshape(kv, rows, lons // LANES, LANES).swapaxes(1, 2).reshape(-1, LANES)
+
+
+def from_native(flat, shape):
+    kv, rows, lons = shape[0] * shape[1], shape[2], shape[3]
+    return flat.reshape(kv, lons // LANES, rows, LANES).swapaxes(1, 2).reshape(shape)
+
+
+def native_rows(ref, base, row, rows, tiles, half):
+    parts = [
+        ref[pl.ds(base + (half * 8 * tiles + tile) * rows + row, 8, stride=tiles * rows), :]
+        for tile in range(tiles)
+    ]
+    return jnp.concatenate(parts, axis=1)
+
+
+def lane_low(shape):
+    return lax.broadcasted_iota(jnp.int32, shape, 1) < LANES // 2
+
+
+def lateral_rows(rows, coef, reach):
+    for step in range(reach):
+        after = []
+        for i in range(1, len(rows) - 1):
+            at = step + i
+            u = rows[i]
+            width = u.shape[1]
+            after.append(
+                coef[0, at : at + 1, :] * u
+                + coef[1, at : at + 1, :] * rows[i + 1]
+                + coef[2, at : at + 1, :] * rows[i - 1]
+                + coef[3, at : at + 1, :] * pltpu.roll(u, width - 1, 1)
+                + coef[4, at : at + 1, :] * pltpu.roll(u, 1, 1)
+            )
+        rows = after
+    return rows
+
+
+def first_lateral_kernel(kv, rows, tiles, own_ref, low_ref, high_ref, packed_ref, coef_ref, ext_ref):
+    lons = tiles * LANES
+    cells = kv * tiles * rows
+    ext_ref[...] = jnp.zeros_like(ext_ref)
+    for kind in range(3):
+        for block, ref in enumerate((low_ref, own_ref, high_ref)):
+            for tile in range(tiles):
+                start = cells + (kind * tiles + tile) * rows
+                ext_ref[kind, block * rows : (block + 1) * rows, tile * LANES : (tile + 1) * LANES] = ref[
+                    start : start + rows, :
+                ]
+    total = ext_ref.shape[1]
+    north, east, ocean = ext_ref[0], ext_ref[1], ext_ref[2]
+    north_face = north * ocean * pltpu.roll(ocean, total - 1, 0)
+    east_face = east * ocean * pltpu.roll(ocean, lons - 1, 1)
+    south_face = pltpu.roll(north_face, 1, 0)
+    west_face = pltpu.roll(east_face, 1, 1)
+    coef_ref[0] = ocean - north_face - south_face - east_face - west_face
+    coef_ref[1] = north_face
+    coef_ref[2] = south_face
+    coef_ref[3] = east_face
+    coef_ref[4] = west_face
+    low = lane_low((8, LANES))
+    for half in range(kv // 8):
+        grown = [
+            native_rows(ref, 0, row, rows, tiles, half)
+            for ref in (low_ref, own_ref, high_ref)
+            for row in range(rows)
+        ]
+        done = lateral_rows(grown, coef_ref, rows)
+        for pair in range(rows // 2):
+            for tile in range(tiles):
+                first = done[2 * pair][:, tile * LANES : (tile + 1) * LANES]
+                second = done[2 * pair + 1][:, tile * LANES : (tile + 1) * LANES]
+                at = pair * kv + half * 8
+                packed_ref[2 * tile, at : at + 8, :] = jnp.where(
+                    low, first, pltpu.roll(second, LANES // 2, 1)
+                )
+                packed_ref[2 * tile + 1, at : at + 8, :] = jnp.where(
+                    low, pltpu.roll(first, LANES // 2, 1), second
+                )
+
+
+def second_lateral_kernel(
+    kv, rows, tiles, own_ref, low_ref, high_ref, coef_ref, direction_ref, residual_ref, image_ref, sums_ref
+):
+    low = lane_low((8, LANES))
+    totals = [jnp.zeros((8, tiles * LANES), jnp.float32) for _ in range(4)]
+    for half in range(kv // 8):
+        grown = []
+        for ref in (low_ref, own_ref, high_ref):
+            for pair in range(rows // 2):
+                firsts, seconds = [], []
+                at = pair * kv + half * 8
+                for tile in range(tiles):
+                    even = ref[2 * tile, at : at + 8, :]
+                    odd = ref[2 * tile + 1, at : at + 8, :]
+                    firsts.append(jnp.where(low, even, pltpu.roll(odd, LANES // 2, 1)))
+                    seconds.append(jnp.where(low, pltpu.roll(even, LANES // 2, 1), odd))
+                grown.append(jnp.concatenate(firsts, axis=1))
+                grown.append(jnp.concatenate(seconds, axis=1))
+        done = lateral_rows(grown, coef_ref, rows)
+        for row in range(rows):
+            direction = native_rows(direction_ref, 0, row, rows, tiles, half)
+            residual = native_rows(residual_ref, 0, row, rows, tiles, half)
+            image = direction + done[row]
+            for tile in range(tiles):
+                image_ref[pl.ds((half * 8 * tiles + tile) * rows + row, 8, stride=tiles * rows), :] = image[
+                    :, tile * LANES : (tile + 1) * LANES
+                ]
+            totals[0] = totals[0] + residual * residual
+            totals[1] = totals[1] + direction * image
+            totals[2] = totals[2] + residual * image
+            totals[3] = totals[3] + image * image
+    lane = lax.broadcasted_iota(jnp.int32, (1, LANES), 1)
+    line = jnp.zeros((1, LANES), jnp.float32)
+    for at, total in enumerate(totals):
+        line = jnp.where(lane == at, jnp.sum(total), line)
+    for device in range(sums_ref.shape[0]):
+        sums_ref[device] = line
+
+
+def update_kernel(sums_ref, direction_ref, solution_ref, residual_ref, image_ref, sol_ref, res_ref, dir_ref):
+    line = jnp.sum(sums_ref[...], axis=0)
+    lane = lax.broadcasted_iota(jnp.int32, line.shape, 1)
+
+    def pick(at):
+        return jnp.sum(jnp.where(lane == at, line, 0.0), axis=1, keepdims=True)
+
+    norm_now, curvature, cross, square = pick(0), pick(1), pick(2), pick(3)
+    alpha = norm_now / curvature
+    norm_next = norm_now - 2.0 * alpha * cross + alpha * alpha * square
+    beta = norm_next / norm_now
+    direction = direction_ref[...]
+    residual_next = residual_ref[...] - alpha * image_ref[...]
+    sol_ref[...] = solution_ref[...] + alpha * direction
+    res_ref[...] = residual_next
+    dir_ref[...] = residual_next + beta * direction
+
+
+def prepare_kernel(
+    strides, capacity, lon_cols, me_ref, vert_ref, owner_ref, row_ref, col_ref, frac_ref, factor_ref, interp_ref
+):
+    layers = vert_ref.shape[0]
+    top = lax.broadcasted_iota(jnp.int32, (8, LANES), 0) < 4
+    coef = [
+        jnp.where(top, vert_ref[layer, 0:1, :], vert_ref[layer, 1:2, :]) for layer in range(layers)
+    ]
+    ratio = None
+    for layer in range(layers):
+        diagonal = 1.0 + coef[layer]
+        if layer > 0:
+            diagonal = diagonal + coef[layer - 1] - coef[layer - 1] * ratio
+        inverse = 1.0 / diagonal
+        ratio = coef[layer] * inverse
+        factor_ref[0, layer] = inverse
+        factor_ref[1, layer] = coef[layer - 1] * inverse if layer > 0 else jnp.zeros_like(inverse)
+        factor_ref[2, layer] = ratio
+    count = owner_ref.shape[1]
+    devices = 1 << len(strides)
+    slots = devices * capacity
+    apart = jnp.bitwise_xor(owner_ref[...], me_ref[0])
+    place = jnp.zeros_like(apart)
+    for bit, stride in enumerate(strides):
+        place = place + jnp.where(jnp.bitwise_and(apart, stride) != 0, 1 << bit, 0)
+    named = jnp.where(
+        lax.broadcasted_iota(jnp.int32, (devices, count), 0) == place, 1.0, 0.0
+    )
+    before = jnp.where(
+        lax.broadcasted_iota(jnp.int32, (count, count), 0)
+        <= lax.broadcasted_iota(jnp.int32, (count, count), 1),
+        1.0,
+        0.0,
+    )
+    running = jnp.dot(named, before, preferred_element_type=jnp.float32)
+    rank = jnp.sum(named * running, axis=0, keepdims=True) - 1.0
+    slot = place * capacity + rank.astype(jnp.int32)
+    chosen = jnp.where(
+        lax.broadcasted_iota(jnp.int32, (slots, count), 0) == slot, 1.0, 0.0
+    )
+    lat_frac = frac_ref[0:1, :]
+    lon_frac = frac_ref[1:2, :]
+    cell = (row_ref[...] * lon_cols + col_ref[...]).astype(jnp.float32)
+    values = jnp.concatenate(
+        [
+            (1.0 - lat_frac) * (1.0 - lon_frac),
+            (1.0 - lat_frac) * lon_frac,
+            lat_frac * (1.0 - lon_frac),
+            lat_frac * lon_frac,
+            cell,
+            jnp.zeros((3, count), jnp.float32),
+        ],
+        axis=0,
+    )
+    placed = lax.dot_general(
+        values, chosen, (((1,), (1,)), ((), ())), precision=HIGHEST, preferred_element_type=jnp.float32
+    )
+    first = jnp.round(placed[4:5, :]).astype(jnp.int32)
+    index = lax.broadcasted_iota(jnp.int32, interp_ref.shape, 0)
+    away = index - first
+    interp_ref[...] = jnp.where(
+        away == 0,
+        placed[0:1, :],
+        jnp.where(
+            away == 1,
+            placed[1:2, :],
+            jnp.where(away == lon_cols, placed[2:3, :], jnp.where(away == lon_cols + 1, placed[3:4, :], 0.0)),
+        ),
+    )
+
+
+def solve_columns(read, write, factor_ref, layers):
+    forward = []
+    for layer in range(layers):
+        value = read(layer) * factor_ref[0, layer]
+        if layer > 0:
+            value = value + factor_ref[1, layer] * forward[-1]
+        forward.append(value)
+    value = forward[-1]
+    write(layers - 1, value)
+    for layer in range(layers - 2, -1, -1):
+        value = forward[layer] + factor_ref[2, layer] * value
+        write(layer, value)
+
+
+def observe_kernel(
+    layers, held, capacity, packed_ref, factor_ref, interp_ref, near_ref, far_ref, out_ref, column_ref
+):
+    kv = near_ref.shape[1]
+    block = 8 * held
+
+    def packed_at(layer):
+        return pl.ds((layer // held) * block + layer % held, 8, stride=held)
+
+    def column_at(layer):
+        return pl.ds(layer, 8, stride=layers)
+
+    def read_packed(layer):
+        return packed_ref[packed_at(layer), :]
+
+    def write_column(layer, value):
+        column_ref[column_at(layer), :] = value
+
+    solve_columns(read_packed, write_column, factor_ref, layers)
+    columns = jnp.concatenate([column_ref[0:kv, :], column_ref[kv : 2 * kv, :]], axis=1)
+    interp = interp_ref[...]
+    profile = jnp.dot(columns, interp, precision=HIGHEST, preferred_element_type=jnp.float32)
+    owners = LANES // capacity
+    mine = lax.broadcasted_iota(jnp.int32, (kv, LANES), 1) // capacity
+    near = near_ref.shape[0]
+    parts = []
+    for tile in range(profile.shape[1] // LANES):
+        values = profile[:, tile * LANES : (tile + 1) * LANES]
+        first = tile * owners
+        ref, at = (near_ref, first) if first < near else (far_ref, first - near)
+        matrices = ref[at : at + owners].reshape(owners * kv, kv)
+        product = jnp.dot(matrices, values, precision=HIGHEST, preferred_element_type=jnp.float32)
+        kept = product[0:kv]
+        for owner in range(1, owners):
+            kept = jnp.where(mine == owner, product[owner * kv : (owner + 1) * kv], kept)
+        parts.append(kept)
+    weighted = jnp.concatenate(parts, axis=1)
+    spread = lax.dot_general(
+        weighted, interp, (((1,), (1,)), ((), ())), precision=HIGHEST, preferred_element_type=jnp.float32
+    )
+    column_ref[0:kv, :] = spread[:, :LANES]
+    column_ref[kv : 2 * kv, :] = spread[:, LANES:]
+
+    def read_column(layer):
+        return column_ref[column_at(layer), :]
+
+    def write_packed(layer, value):
+        out_ref[packed_at(layer), :] = value
+
+    solve_columns(read_column, write_packed, factor_ref, layers)
+
+
+def vmem(count):
+    return [pl.BlockSpec(memory_space=pltpu.VMEM)] * count
+
+
+def call(kernel, out_shape, inputs, scratch=(), smem_first=False, flops=1_000_000):
+    specs = vmem(len(inputs))
+    if smem_first:
+        specs[0] = pl.BlockSpec(memory_space=pltpu.SMEM)
+    many = isinstance(out_shape, (list, tuple))
+    moved = sum(math.prod(x.shape) * 4 for x in inputs)
+    return pl.pallas_call(
+        kernel,
+        out_shape=out_shape,
+        in_specs=specs,
+        out_specs=tuple(vmem(len(out_shape))) if many else vmem(1)[0],
+        scratch_shapes=list(scratch),
+        compiler_params=pltpu.CompilerParams(vmem_limit_bytes=32 * 1024 * 1024),
+        cost_estimate=pl.CostEstimate(flops=flops, bytes_accessed=moved, transcendentals=0),
+    )(*inputs)
+
+
+def f32(*shape):
+    return jax.ShapeDtypeStruct(shape, jnp.float32)
+
+
+def from_neighbours(block):
+    count = lax.axis_size("gy")
+    low = lax.ppermute(block, "gy", [(i, i + 1) for i in range(count - 1)])
+    high = lax.ppermute(block, "gy", [(i + 1, i) for i in range(count - 1)])
+    return low, high
+
+
+def gather_order(rows_y, cols_x):
+    order = []
+    stride = cols_x // 2
+    while stride > 1:
+        order.append(("gx", stride))
+        stride //= 2
+    stride = rows_y // 2
+    while stride >= 1:
+        order.append(("gy", stride))
+        stride //= 2
+    if cols_x > 1:
+        order.append(("gx", 1))
+    numbers = [stride * (cols_x if axis == "gy" else 1) for axis, stride in order]
+    return order, numbers
+
+
+def per_device_gathered(
+    direction,
+    solution,
+    residual,
+    north_coef,
+    east_coef,
+    ocean,
+    vert_coef,
+    obs_owner,
+    obs_row,
+    obs_col,
+    obs_frac,
+    error_inverse,
+):
+    var_count, held, rows, lons = direction.shape
+    kv = var_count * held
+    tiles = lons // LANES
+    layers, _, lon_cols = vert_coef.shape
+    rows_y, cols_x = lax.axis_size("gy"), lax.axis_size("gx")
+    device_count = rows_y * cols_x
+    obs_count = obs_row.shape[-1]
+    capacity = 2 * obs_count // device_count
+    wide = error_inverse.shape[-1]
+    cells = rows * lon_cols
+    order, numbers = gather_order(rows_y, cols_x)
+
+    direction_n = to_native(direction)
+    residual_n = to_native(residual)
+    solution_n = to_native(solution)
+    lateral = jnp.stack([north_coef, east_coef, ocean.astype(jnp.float32)])[:, None]
+    own = jnp.concatenate([direction_n, to_native(lateral)], axis=0)
+    low, high = from_neighbours(own)
+
+    blocks = error_inverse.reshape(1, wide, wide)
+    other = None
+    for axis, stride in order:
+        if other is not None:
+            blocks = jnp.concatenate([blocks, other], axis=0)
+        other = lax.ppermute(blocks, axis, [(i, i ^ stride) for i in range(lax.axis_size(axis))])
+
+    me = (lax.axis_index("gy") * cols_x + lax.axis_index("gx")).astype(jnp.int32).reshape(1)
+    factors, interp = call(
+        functools.partial(prepare_kernel, tuple(numbers), capacity, lon_cols),
+        (f32(3, layers, 8, LANES), f32(cells, device_count * capacity)),
+        (
+            me,
+            vert_coef.reshape(layers, cells // LANES, LANES),
+            obs_owner.reshape(1, obs_count),
+            obs_row.reshape(1, obs_count),
+            obs_col.reshape(1, obs_count),
+            obs_frac.reshape(2, obs_count),
+        ),
+        smem_first=True,
+        flops=20_000_000,
+    )
+
+    extended = 3 * rows + (-3 * rows) % 8
+    packed, coef = call(
+        functools.partial(first_lateral_kernel, kv, rows, tiles),
+        (f32(cols_x, 2 * kv, LANES), f32(5, extended, lons)),
+        (own, low, high),
+        scratch=(pltpu.VMEM((3, extended, lons), jnp.float32),),
+        flops=4_000_000,
+    )
+    columns = lax.all_to_all(packed, "gx", split_axis=0, concat_axis=0, tiled=True)
+    spread = call(
+        functools.partial(observe_kernel, layers, held, capacity),
+        f32(cols_x * 2 * kv, LANES),
+        (columns.reshape(cols_x * 2 * kv, LANES), factors, interp, blocks, other),
+        scratch=(pltpu.VMEM((2 * wide, LANES), jnp.float32),),
+        flops=1_000_000_000,
+    )
+    tile = lax.all_to_all(
+        spread.reshape(cols_x, 2 * kv, LANES), "gx", split_axis=0, concat_axis=0, tiled=True
+    )
+    low, high = from_neighbours(tile)
+    image, sums = call(
+        functools.partial(second_lateral_kernel, kv, rows, tiles),
+        (f32(*direction_n.shape), f32(device_count, 1, LANES)),
+        (tile, low, high, coef, direction_n, residual_n),
+        flops=4_000_000,
+    )
+    sums = lax.all_to_all(sums, ("gy", "gx"), split_axis=0, concat_axis=0, tiled=True)
+    after = call(
+        update_kernel,
+        (f32(*direction_n.shape),) * 3,
+        (sums, direction_n, solution_n, residual_n, image),
+    )
+    return tuple(from_native(x, direction.shape) for x in after)
+
+
+def gathers(mesh, shapes):
+    rows_y, cols_x = mesh.shape["gy"], mesh.shape["gx"]
+    devices = rows_y * cols_x
+    direction, vert_coef, obs_row, error_inverse = shapes
+    var_count, layers, lat_rows, lons = direction
+    rows, held = lat_rows // rows_y, layers // cols_x
+    obs_count, wide = obs_row[-1], error_inverse[-1]
+    capacity = 2 * obs_count // devices
+    return (
+        devices & (devices - 1) == 0
+        and devices > 1
+        and rows == NSTEP == 4
+        and var_count == 4
+        and (var_count * held) % 8 == 0
+        and lons // cols_x * 2 == LANES
+        and wide == LANES
+        and capacity > 0
+        and LANES % capacity == 0
+        and devices // 2 % (LANES // capacity) == 0
+        and devices * wide * wide * 4 <= 8 * 1024 * 1024
+    )
 
 
 def padded(cells, sides, width):
@@ -184,23 +630,27 @@
 
 
 def solution(mesh):
-    return jax.shard_map(
-        per_device,
-        mesh=mesh,
-        in_specs=(
-            P(None, "gx", "gy", None),
-            P(None, "gx", "gy", None),
-            P(None, "gx", "gy", None),
-            P("gy", None),
-            P("gy", None),
-            P("gy", None),
-            P(None, "gy", "gx"),
-            P("gy", "gx", None, None),
-            P("gy", "gx", None),
-            P("gy", "gx", None),
-            P("gy", "gx", None, None),
-            P("gy", "gx", None, None),
-        ),
-        out_specs=(P(None, "gx", "gy", None), P(None, "gx", "gy", None), P(None, "gx", "gy", None)),
-        check_vma=False,
-    )
+    in_specs = (
+        P(None, "gx", "gy", None),
+        P(None, "gx", "gy", None),
+        P(None, "gx", "gy", None),
+        P("gy", None),
+        P("gy", None),
+        P("gy", None),
+        P(None, "gy", "gx"),
+        P("gy", "gx", None, None),
+        P("gy", "gx", None),
+        P("gy", "gx", None),
+        P("gy", "gx", None, None),
+        P("gy", "gx", None, None),
+    )
+    out_specs = (P(None, "gx", "gy", None),) * 3
+
+    def step(*arrays):
+        shapes = [arrays[at].shape for at in (0, 6, 8, 11)]
+        local = per_device_gathered if gathers(mesh, shapes) else per_device
+        return jax.shard_map(
+            local, mesh=mesh, in_specs=in_specs, out_specs=out_specs, check_vma=False
+        )(*arrays)
+
+    return step

time: 279 us -> 96.4 us (0.35)
  blocking collectives: 132 us -> 23.3 us
  other arithmetic: 58.4 us -> 0.93 us
  local copies, waits for them, and re-layouts: 29.7 us -> 4.05 us
  Pallas kernels: 0 us -> 9.73 us
  starting transfers between devices: 24.5 us -> 27.8 us
  between operations: 4.09 us -> 0.85 us
    psum x2 -> x0, blocking collectives: 80.6 us -> none  [the longest x1 41.6 us: per_device(): norm_next = lax.psum(jnp.sum(residual_next * residual_next), ('gy', 'gx'))]
    all_to_all x4 -> x2, blocking collectives: 51.7 us -> 23.3 us  [the longest x1 13.9 us: per_device_gathered(): lax.all_to_all(sums, ('gy', 'gx'), split_axis=0, concat_axis=0, tiled=True)]
    mul x51 -> x0, other arithmetic: 23.8 us -> none  [the longest x30 21.5 us: vertical_solve(): result.append(forward[layer_index] - upper_ratio[layer_index] * result[-1])]
    ppermute x6 -> x9, waiting for transfers between devices: 5.22 us -> 26.4 us  [the longest x5 21 us: per_device_gathered(): lax.ppermute(blocks, axis, [(i, i ^ stride) for i in range(lax.axis_size(...]
    all_to_all x2 -> x1, waiting for transfers between devices: 22 us -> 2.79 us  [per_device_gathered(): lax.all_to_all(packed, 'gx', split_axis=0, concat_axis=0, tiled=True)]
    scatter-add x4 -> x0, other arithmetic: 13.2 us -> none  [observe_weigh_spread(): spread.at[:, corners[corner_index]].add(weights[corner_index] * back)]
    unnamed x16 -> x36, local copies, waits for them, and re-layouts: 14.9 us -> 3.92 us
    pallas_call x0 -> x5, Pallas kernels: none -> 9.73 us  [call(): pl.pallas_call(kernel, out_shape=out_shape, in_specs=specs, out_specs=tup...]
  transfers between devices with their start and end apart: 8 -> 10, of which waited for: 4 -> 9; matrix products, arithmetic and copies ran while one was open for 10% -> 0% of each run, Pallas kernels for 0% -> 4%
where the time goes in v1:
time: 96.4 us; the launch traced here: 95.9 us
  waiting for transfers between devices  29.2 us (30%)
  starting transfers between devices  27.8 us (29%)
  blocking collectives  23.3 us (24%)
  Pallas kernels  9.73 us (10%)
  local copies, waits for them, and re-layouts  4.05 us (4%)
    ppermute x5, waiting for transfers between devices, per_device_gathered(): lax.ppermute(blocks, axis, [(i, i ^ stride) for i in range(lax.axis_size(...  21 us
    all_to_all x1, blocking collectives, per_device_gathered(): lax.all_to_all(sums, ('gy', 'gx'), split_axis=0, concat_axis=0, tiled=True)  13.9 us
    pallas_call x5, Pallas kernels, call(): pl.pallas_call(kernel, out_shape=out_shape, in_specs=specs, out_specs=tup...  9.73 us
    ppermute x2, starting transfers between devices, from_neighbours(): low = lax.ppermute(block, 'gy', [(i, i + 1) for i in range(count - 1)])  9.58 us
    all_to_all x1, blocking collectives, per_device_gathered(): lax.all_to_all(spread.reshape(cols_x, 2 * kv, LANES), 'gx', split_axis=0,...  9.4 us
    ppermute x5, starting transfers between devices, per_device_gathered(): lax.ppermute(blocks, axis, [(i, i ^ stride) for i in range(lax.axis_size(...  8.46 us
    all_to_all x1, starting transfers between devices, per_device_gathered(): lax.all_to_all(packed, 'gx', split_axis=0, concat_axis=0, tiled=True)  7.19 us
    unnamed x36, local copies, waits for them, and re-layouts  3.92 us
  transfers between devices with their start and end apart: 10, of which 9 were waited for; matrix products, arithmetic and copies ran while one was open for 0% of the time, Pallas kernels for 4%

profile of v1, /device:TPU:0, one launch (start us, length us, event | category | flops | bytes accessed | tf_op | source)
XLA Modules:
  0.0 95.9 jit_solution(1416460602449861090)
XLA Ops:
  0.6 0.0 copy-start.11
  0.6 4.1 %collective-permute-start.2 = (f32[1,128,128]{2,1,0:T(8,128)}, f32[1,128,128]{2,1,0:T(8,128)S(1)}, u32[]{:S(2)}, u32[]{:S(2)}) collective-permute-start(f32[1,128,128]{2,1,0:T(8,128)} %bitcast.58), channel_id=1, source_target_pairs={{0,4},{1,5},{2,6},{3,7},{4,0},{5,1},{6,2},{7,3},{8,12},{9,13},{10,... | collective-permute-start | bytes 196616 | tf_op jit(solution)/shard_map/ppermute | solution.py:379
  4.7 3.9 %collective-permute-done.2 = f32[1,128,128]{2,1,0:T(8,128)S(1)} collective-permute-done((f32[1,128,128]{2,1,0:T(8,128)}, f32[1,128,128]{2,1,0:T(8,128)S(1)}, u32[]{:S(2)}, u32[]{:S(2)}) %collective-permute-start.2) | collective-permute-done | bytes 65568 | tf_op jit(solution)/shard_map/ppermute | solution.py:379
  8.6 0.9 pad_maximum_fusion.3
  9.5 0.7 collective-permute-start.3
  10.2 4.3 %collective-permute-done.3 = f32[2,128,128]{2,1,0:T(8,128)S(1)} collective-permute-done((f32[2,128,128]{2,1,0:T(8,128)S(1)}, f32[2,128,128]{2,1,0:T(8,128)S(1)}, u32[]{:S(2)}, u32[]{:S(2)}) %collective-permute-start.3) | collective-permute-done | bytes 131104 | tf_op jit(solution)/shard_map/ppermute | solution.py:379
  14.5 0.0 copy-done.11
  14.5 1.8 %collective-permute-start.4 = (f32[4,128,128]{2,1,0:T(8,128)S(1)}, f32[4,128,128]{2,1,0:T(8,128)S(1)}, u32[]{:S(2)}, u32[]{:S(2)}) collective-permute-start(f32[4,128,128]{2,1,0:T(8,128)S(1)} %pad_maximum_fusion.1), channel_id=1, source_target_pairs={{0,16},{8,24},{16,0},{24,8},{1,17},{9,25},{17,1},{25,9},{2,18},{10... | collective-permute-start | bytes 786440 | tf_op jit(solution)/shard_map/ppermute | solution.py:379
  16.3 4.6 %collective-permute-done.4 = f32[4,128,128]{2,1,0:T(8,128)S(1)} collective-permute-done((f32[4,128,128]{2,1,0:T(8,128)S(1)}, f32[4,128,128]{2,1,0:T(8,128)S(1)}, u32[]{:S(2)}, u32[]{:S(2)}) %collective-permute-start.4) | collective-permute-done | bytes 262176 | tf_op jit(solution)/shard_map/ppermute | solution.py:379
  21.0 1.8 %collective-permute-start.5 = (f32[8,128,128]{2,1,0:T(8,128)S(1)}, f32[8,128,128]{2,1,0:T(8,128)S(1)}, u32[]{:S(2)}, u32[]{:S(2)}) collective-permute-start(f32[8,128,128]{2,1,0:T(8,128)S(1)} %pad_maximum_fusion), channel_id=1, source_target_pairs={{0,8},{8,0},{16,24},{24,16},{1,9},{9,1},{17,25},{25,17},{2,10},{10... | collective-permute-start | bytes 1572872 | tf_op jit(solution)/shard_map/ppermute | solution.py:379
  22.8 0.0 copy-start.13
  22.8 8.2 %collective-permute-done.5 = f32[8,128,128]{2,1,0:T(8,128)S(1)} collective-permute-done((f32[8,128,128]{2,1,0:T(8,128)S(1)}, f32[8,128,128]{2,1,0:T(8,128)S(1)}, u32[]{:S(2)}, u32[]{:S(2)}) %collective-permute-start.5) | collective-permute-done | bytes 524320 | tf_op jit(solution)/shard_map/ppermute | solution.py:379
  31.0 0.0 copy-start
  31.1 0.0 copy-start.14
  31.1 0.0 copy-start.15
  31.1 0.1 collective-permute-start.6
  31.2 0.0 copy-done.13
  31.2 0.6 copy-done.14
  31.8 0.0 copy-done.15
  31.8 0.1 copy-done
  32.0 1.3 %collective-permute-start.1 = (f32[304,128]{1,0:T(8,128)S(1)}, f32[304,128]{1,0:T(8,128)S(1)}, u32[]{:S(2)}, u32[]{:S(2)}) collective-permute-start(f32[304,128]{1,0:T(8,128)S(1)} %pad_maximum_fusion.2.own_ref), channel_id=1, source_target_pairs={{8,0},{16,8},{24,16},{9,1},{17,9},{25,17},{10,2},{18,10},{26,18},{... | collective-permute-start | bytes 466952 | tf_op jit(solution)/shard_map/ppermute | solution.py:321
  33.3 4.6 %collective-permute-start = (f32[304,128]{1,0:T(8,128)S(1)}, f32[304,128]{1,0:T(8,128)S(1)}, u32[]{:S(2)}, u32[]{:S(2)}) collective-permute-start(f32[304,128]{1,0:T(8,128)S(1)} %pad_maximum_fusion.2.own_ref), channel_id=1, source_target_pairs={{0,8},{8,16},{16,24},{1,9},{9,17},{17,25},{2,10},{10,18},{18,26},{... | collective-permute-start | bytes 466952 | tf_op jit(solution)/shard_map/ppermute | solution.py:320
  37.8 1.7 %collective-permute-done.1.high_ref = f32[304,128]{1,0:T(8,128)S(1)} collective-permute-done((f32[304,128]{1,0:T(8,128)S(1)}, f32[304,128]{1,0:T(8,128)S(1)}, u32[]{:S(2)}, u32[]{:S(2)}) %collective-permute-start.1) | collective-permute-done | bytes 155680 | tf_op jit(solution)/shard_map/ppermute | solution.py:321
  39.6 1.2 %collective-permute-done.low_ref = f32[304,128]{1,0:T(8,128)S(1)} collective-permute-done((f32[304,128]{1,0:T(8,128)S(1)}, f32[304,128]{1,0:T(8,128)S(1)}, u32[]{:S(2)}, u32[]{:S(2)}) %collective-permute-start) | collective-permute-done | bytes 155680 | tf_op jit(solution)/shard_map/ppermute | solution.py:320
  40.8 1.6 %shard_map.139 = (f32[8,32,128]{2,1,0:T(8,128)}, f32[5,16,512]{2,1,0:T(8,128)S(1)}) custom-call(f32[304,128]{1,0:T(8,128)S(1)} %pad_maximum_fusion.2.own_ref, f32[304,128]{1,0:T(8,128)S(1)} %collective-permute-done.low_ref, f32[304,128]{1,0:T(8,128)S(1)} %collective-permute-done.1.high_ref), custom_call_target="tpu_custom_call" | custom-call | flops 4000000 | bytes 466944 | tf_op jit(solution)/shard_map/pallas_call | solution.py:303
  42.3 0.0 copy-start.4
  42.3 0.7 copy-done.4
  43.0 0.0 copy-start.12
  43.0 7.2 %all-to-all-start = ((f32[8,32,128]{2,1,0:T(8,128)}), f32[8,32,128]{2,1,0:T(8,128)S(1)}, u32[]{:S(2)}, u32[]{:S(2)}) async-start(f32[8,32,128]{2,1,0:T(8,128)} %get-tuple-element.12), calls=%async_computation | async-start | bytes 262144 | tf_op jit(solution)/shard_map/all_to_all | solution.py:405
  50.2 0.0 copy-done.12
  50.2 0.0 copy-start.9
  50.2 0.0 copy-start.10
  50.2 0.1 reshape.83.vert_ref
  50.3 0.0 copy-start.7
  50.4 0.0 copy-start.8
  50.4 0.5 copy-done.9
  50.9 0.0 copy-done.10
  50.9 0.1 copy-done.7
  51.0 0.0 copy-done.8
  51.0 2.4 %shard_map.140 = (f32[3,32,8,128]{3,2,1,0:T(8,128)S(1)}, f32[256,1024]{1,0:T(8,128)S(1)}) custom-call(s32[1]{0:T(128)} %bitcast.9.me_ref, f32[32,2,128]{2,1,0:T(2,128)S(1)} %reshape.83.vert_ref, s32[1,512]{1,0:T(1,128)S(1)} %bitcast.55, s32[1,512]{1,0:T(1,128)S(1)} %bitcast.56, s32[1,512]{1,0:T(1,128)S(1)} %bitcast.57, f32[2,512]{1,0:T(2,128)S(1)} %bitcast.54), custom_call_target="tpu_custom_call" | custom-call | flops 20000000 | bytes 43012 | tf_op jit(solution)/shard_map/pallas_call | solution.py:303
  53.4 0.0 copy-start.2
  53.4 0.8 copy-done.2
  54.2 2.8 %all-to-all-done = f32[8,32,128]{2,1,0:T(8,128)S(1)} async-done(((f32[8,32,128]{2,1,0:T(8,128)}), f32[8,32,128]{2,1,0:T(8,128)S(1)}, u32[]{:S(2)}, u32[]{:S(2)}) %all-to-all-start) | async-done | bytes 131104 | tf_op jit(solution)/shard_map/all_to_all | solution.py:405
  57.0 0.0 collective-permute-done.6.far_ref
  57.0 0.0 copy-start.3
  57.0 1.0 %copy-done.3 = f32[3,32,8,128]{3,2,1,0:T(8,128)S(1)} copy-done((f32[3,32,8,128]{3,2,1,0:T(8,128)S(1)}, f32[3,32,8,128]{3,2,1,0:T(8,128)}, u32[]{:S(2)}) %copy-start.3) | copy-done | bytes 393240
  58.0 0.0 copy-start.5
  58.0 4.0 %shard_map.141 = f32[256,128]{1,0:T(8,128)S(1)} custom-call(f32[256,128]{1,0:T(8,128)S(1)} %bitcast.51, f32[3,32,8,128]{3,2,1,0:T(8,128)S(1)} %copy-done.3, f32[256,1024]{1,0:T(8,128)S(1)} %get-tuple-element.14.interp_ref, f32[16,128,128]{2,1,0:T(8,128)S(1)} %constant_dynamic-update-slice_fusion.near_ref, f32[16,128,128]{2,1,0:T(8,128)S(1)} %collective-permute-done.6.far_ref), custom_call_target="tpu_custom_call" | custom-call | flops 1000000000 | bytes 3670016 | tf_op jit(solution)/shard_map/pallas_call | solution.py:303
  61.9 0.0 copy-start.1
  62.0 9.4 %all_to_all.15.own_ref = f32[8,32,128]{2,1,0:T(8,128)S(1)} all-to-all(f32[8,32,128]{2,1,0:T(8,128)S(1)} %bitcast.52), channel_id=1, replica_groups=mesh['gy'=4,'gx'=8] {'gx'}, dimensions={0} | all-to-all | bytes 262144 | tf_op jit(solution)/shard_map/all_to_all | solution.py:413
  71.4 1.3 %collective-permute-start.8 = (f32[8,32,128]{2,1,0:T(8,128)S(1)}, f32[8,32,128]{2,1,0:T(8,128)S(1)}, u32[]{:S(2)}, u32[]{:S(2)}) collective-permute-start(f32[8,32,128]{2,1,0:T(8,128)S(1)} %all_to_all.15.own_ref), channel_id=1, source_target_pairs={{8,0},{16,8},{24,16},{9,1},{17,9},{25,17},{10,2},{18,10},{26,18},{... | collective-permute-start | bytes 393224 | tf_op jit(solution)/shard_map/ppermute | solution.py:321
  72.6 5.0 %collective-permute-start.7 = (f32[8,32,128]{2,1,0:T(8,128)S(1)}, f32[8,32,128]{2,1,0:T(8,128)S(1)}, u32[]{:S(2)}, u32[]{:S(2)}) collective-permute-start(f32[8,32,128]{2,1,0:T(8,128)S(1)} %all_to_all.15.own_ref), channel_id=1, source_target_pairs={{0,8},{8,16},{16,24},{1,9},{9,17},{17,25},{2,10},{10,18},{18,26},{... | collective-permute-start | bytes 393224 | tf_op jit(solution)/shard_map/ppermute | solution.py:320
  77.7 1.2 %collective-permute-done.8.high_ref = f32[8,32,128]{2,1,0:T(8,128)S(1)} collective-permute-done((f32[8,32,128]{2,1,0:T(8,128)S(1)}, f32[8,32,128]{2,1,0:T(8,128)S(1)}, u32[]{:S(2)}, u32[]{:S(2)}) %collective-permute-start.8) | collective-permute-done | bytes 131104 | tf_op jit(solution)/shard_map/ppermute | solution.py:321
  78.9 1.2 %collective-permute-done.7.low_ref = f32[8,32,128]{2,1,0:T(8,128)S(1)} collective-permute-done((f32[8,32,128]{2,1,0:T(8,128)S(1)}, f32[8,32,128]{2,1,0:T(8,128)S(1)}, u32[]{:S(2)}, u32[]{:S(2)}) %collective-permute-start.7) | collective-permute-done | bytes 131104 | tf_op jit(solution)/shard_map/ppermute | solution.py:320
  80.2 0.0 copy-done.5
  80.2 0.0 copy-done.1
  80.2 0.0 copy-start.6
  80.2 0.9 shard_map.142
  81.1 13.9 %all_to_all.16.sums_ref = f32[32,1,128]{2,1,0:T(1,128)S(1)} all-to-all(f32[32,1,128]{2,1,0:T(1,128)S(1)} %get-tuple-element.16), channel_id=1, replica_groups=mesh['gy'=4,'gx'=8] {'gy','gx'}, dimensions={0} | all-to-all | bytes 32768 | tf_op jit(solution)/shard_map/all_to_all | solution.py:423
  95.0 0.0 copy-done.6
  95.0 0.9 shard_map.143
  (10 shorter events, 0.2 us)
Async XLA Ops:
  0.6 13.9 %copy-start.11 = (f32[1,1,128,128]{3,2,1,0:T(8,128)S(1)}, f32[1,1,128,128]{3,2,1,0:T(8,128)}, u32[]{:S(2)}) copy-start(f32[1,1,128,128]{3,2,1,0:T(8,128)} %param.23) | copy-start | bytes 196612
  0.6 8.0 %collective-permute-start.2 = (f32[1,128,128]{2,1,0:T(8,128)}, f32[1,128,128]{2,1,0:T(8,128)S(1)}, u32[]{:S(2)}, u32[]{:S(2)}) collective-permute-start(f32[1,128,128]{2,1,0:T(8,128)} %bitcast.58), channel_id=1, source_target_pairs={{0,4},{1,5},{2,6},{3,7},{4,0},{5,1},{6,2},{7,3},{8,12},{9,13},{10,... | collective-permute-start | bytes 196616 | tf_op jit(solution)/shard_map/ppermute | solution.py:379
  9.5 5.0 %collective-permute-start.3 = (f32[2,128,128]{2,1,0:T(8,128)S(1)}, f32[2,128,128]{2,1,0:T(8,128)S(1)}, u32[]{:S(2)}, u32[]{:S(2)}) collective-permute-start(f32[2,128,128]{2,1,0:T(8,128)S(1)} %pad_maximum_fusion.3), channel_id=1, source_target_pairs={{0,2},{1,3},{2,0},{3,1},{4,6},{5,7},{6,4},{7,5},{8,10},{9,11},{10,... | collective-permute-start | bytes 393224 | tf_op jit(solution)/shard_map/ppermute | solution.py:379
  14.5 6.4 %collective-permute-start.4 = (f32[4,128,128]{2,1,0:T(8,128)S(1)}, f32[4,128,128]{2,1,0:T(8,128)S(1)}, u32[]{:S(2)}, u32[]{:S(2)}) collective-permute-start(f32[4,128,128]{2,1,0:T(8,128)S(1)} %pad_maximum_fusion.1), channel_id=1, source_target_pairs={{0,16},{8,24},{16,0},{24,8},{1,17},{9,25},{17,1},{25,9},{2,18},{10... | collective-permute-start | bytes 786440 | tf_op jit(solution)/shard_map/ppermute | solution.py:379
  21.0 10.1 %collective-permute-start.5 = (f32[8,128,128]{2,1,0:T(8,128)S(1)}, f32[8,128,128]{2,1,0:T(8,128)S(1)}, u32[]{:S(2)}, u32[]{:S(2)}) collective-permute-start(f32[8,128,128]{2,1,0:T(8,128)S(1)} %pad_maximum_fusion), channel_id=1, source_target_pairs={{0,8},{8,0},{16,24},{24,16},{1,9},{9,1},{17,25},{25,17},{2,10},{10... | collective-permute-start | bytes 1572872 | tf_op jit(solution)/shard_map/ppermute | solution.py:379
  22.8 8.4 %copy-start.13 = (s32[4,512]{1,0:T(4,128)S(1)}, s32[4,512]{1,0:T(4,128)}, u32[]{:S(2)}) copy-start(s32[4,512]{1,0:T(4,128)} %param.17) | copy-start | bytes 24580
  31.0 0.9 copy-start
  31.1 0.7 copy-start.14
  31.1 0.7 copy-start.15
  31.1 25.9 %collective-permute-start.6 = (f32[16,128,128]{2,1,0:T(8,128)S(1)}, f32[16,128,128]{2,1,0:T(8,128)S(1)}, u32[]{:S(2)}, u32[]{:S(2)}) collective-permute-start(f32[16,128,128]{2,1,0:T(8,128)S(1)} %constant_dynamic-update-slice_fusion.near_ref), channel_id=1, source_target_pairs={{0,1},{1,0},{2,3},{3,2},{4,5},{5,4},{6,7},{7,6},{8,9},{9,8},{10,11... | collective-permute-start | bytes 3145736 | tf_op jit(solution)/shard_map/ppermute | solution.py:379
  32.0 7.6 %collective-permute-start.1 = (f32[304,128]{1,0:T(8,128)S(1)}, f32[304,128]{1,0:T(8,128)S(1)}, u32[]{:S(2)}, u32[]{:S(2)}) collective-permute-start(f32[304,128]{1,0:T(8,128)S(1)} %pad_maximum_fusion.2.own_ref), channel_id=1, source_target_pairs={{8,0},{16,8},{24,16},{9,1},{17,9},{25,17},{10,2},{18,10},{26,18},{... | collective-permute-start | bytes 466952 | tf_op jit(solution)/shard_map/ppermute | solution.py:321
  33.3 7.5 %collective-permute-start = (f32[304,128]{1,0:T(8,128)S(1)}, f32[304,128]{1,0:T(8,128)S(1)}, u32[]{:S(2)}, u32[]{:S(2)}) collective-permute-start(f32[304,128]{1,0:T(8,128)S(1)} %pad_maximum_fusion.2.own_ref), channel_id=1, source_target_pairs={{0,8},{8,16},{16,24},{1,9},{9,17},{17,25},{2,10},{10,18},{18,26},{... | collective-permute-start | bytes 466952 | tf_op jit(solution)/shard_map/ppermute | solution.py:320
  42.3 0.7 copy-start.4
  43.0 7.2 %copy-start.12 = (f32[32,4,64]{2,1,0:T(4,128)S(1)}, f32[32,4,64]{2,1,0:T(4,128)}, u32[]{:S(2)}) copy-start(f32[32,4,64]{2,1,0:T(4,128)} %param.18) | copy-start | bytes 98308
  43.0 14.0 %all-to-all-start = ((f32[8,32,128]{2,1,0:T(8,128)}), f32[8,32,128]{2,1,0:T(8,128)S(1)}, u32[]{:S(2)}, u32[]{:S(2)}) async-start(f32[8,32,128]{2,1,0:T(8,128)} %get-tuple-element.12), calls=%async_computation | async-start | bytes 262144 | tf_op jit(solution)/shard_map/all_to_all | solution.py:405
  50.2 0.7 copy-start.9
  50.2 0.7 copy-start.10
  50.3 0.7 copy-start.7
  50.4 0.7 copy-start.8
  53.4 0.8 copy-start.2
  57.0 1.0 %copy-start.3 = (f32[3,32,8,128]{3,2,1,0:T(8,128)S(1)}, f32[3,32,8,128]{3,2,1,0:T(8,128)}, u32[]{:S(2)}) copy-start(f32[3,32,8,128]{3,2,1,0:T(8,128)} %copy-done.2) | copy-start | bytes 1179652
  58.0 22.2 %copy-start.5 = (f32[5,16,512]{2,1,0:T(8,128)S(1)}, f32[5,16,512]{2,1,0:T(8,128)}, u32[]{:S(2)}) copy-start(f32[5,16,512]{2,1,0:T(8,128)} %copy-done.4) | copy-start | bytes 491524
  61.9 18.2 %copy-start.1 = (f32[4,4,4,512]{3,2,1,0:T(4,128)S(1)}, f32[4,4,4,512]{3,2,1,0:T(4,128)}, u32[]{:S(2)}) copy-start(f32[4,4,4,512]{3,2,1,0:T(4,128)} %param.14) | copy-start | bytes 393220
  71.4 7.6 %collective-permute-start.8 = (f32[8,32,128]{2,1,0:T(8,128)S(1)}, f32[8,32,128]{2,1,0:T(8,128)S(1)}, u32[]{:S(2)}, u32[]{:S(2)}) collective-permute-start(f32[8,32,128]{2,1,0:T(8,128)S(1)} %all_to_all.15.own_ref), channel_id=1, source_target_pairs={{8,0},{16,8},{24,16},{9,1},{17,9},{25,17},{10,2},{18,10},{26,18},{... | collective-permute-start | bytes 393224 | tf_op jit(solution)/shard_map/ppermute | solution.py:321
  72.6 7.5 %collective-permute-start.7 = (f32[8,32,128]{2,1,0:T(8,128)S(1)}, f32[8,32,128]{2,1,0:T(8,128)S(1)}, u32[]{:S(2)}, u32[]{:S(2)}) collective-permute-start(f32[8,32,128]{2,1,0:T(8,128)S(1)} %all_to_all.15.own_ref), channel_id=1, source_target_pairs={{0,8},{8,16},{16,24},{1,9},{9,17},{17,25},{2,10},{10,18},{18,26},{... | collective-permute-start | bytes 393224 | tf_op jit(solution)/shard_map/ppermute | solution.py:320
  80.2 14.8 %copy-start.6 = (f32[4,4,4,512]{3,2,1,0:T(4,128)S(1)}, f32[4,4,4,512]{3,2,1,0:T(4,128)}, u32[]{:S(2)}) copy-start(f32[4,4,4,512]{3,2,1,0:T(4,128)} %param.13) | copy-start | bytes 393220

commit v2 on v1

--- a/solution.py
+++ b/solution.py
@@ -53,9 +53,35 @@
     return rows
 
 
-def first_lateral_kernel(kv, rows, tiles, own_ref, low_ref, high_ref, packed_ref, coef_ref, ext_ref):
+def sort_halo(flags_ref, pair_ref, cross_ref, low_ref, high_ref):
+    odd = flags_ref[1] == 1
+
+    @pl.when(odd)
+    def _():
+        low_ref[...] = pair_ref[...]
+        high_ref[...] = cross_ref[...]
+
+    @pl.when(jnp.logical_not(odd))
+    def _():
+        low_ref[...] = cross_ref[...]
+        high_ref[...] = pair_ref[...]
+
+    @pl.when(flags_ref[2] == 1)
+    def _():
+        low_ref[...] = jnp.zeros_like(low_ref)
+
+    @pl.when(flags_ref[3] == 1)
+    def _():
+        high_ref[...] = jnp.zeros_like(high_ref)
+
+
+def first_lateral_kernel(kv, rows, tiles, count, flags_ref, own_ref, pair_ref, cross_ref, *refs):
+    blocks, (packed_ref, coef_ref, held_ref, ext_ref, low_ref, high_ref) = refs[:count], refs[count:]
     lons = tiles * LANES
     cells = kv * tiles * rows
+    for at, block in enumerate(blocks):
+        held_ref[at] = block[0]
+    sort_halo(flags_ref, pair_ref, cross_ref, low_ref, high_ref)
     ext_ref[...] = jnp.zeros_like(ext_ref)
     for kind in range(3):
         for block, ref in enumerate((low_ref, own_ref, high_ref)):
@@ -97,8 +123,22 @@
 
 
 def second_lateral_kernel(
-    kv, rows, tiles, own_ref, low_ref, high_ref, coef_ref, direction_ref, residual_ref, image_ref, sums_ref
+    kv,
+    rows,
+    tiles,
+    flags_ref,
+    own_ref,
+    pair_ref,
+    cross_ref,
+    coef_ref,
+    direction_ref,
+    residual_ref,
+    image_ref,
+    sums_ref,
+    low_ref,
+    high_ref,
 ):
+    sort_halo(flags_ref, pair_ref, cross_ref, low_ref, high_ref)
     low = lane_low((8, LANES))
     totals = [jnp.zeros((8, tiles * LANES), jnp.float32) for _ in range(4)]
     for half in range(kv // 8):
@@ -154,7 +194,7 @@
 
 
 def prepare_kernel(
-    strides, capacity, lon_cols, me_ref, vert_ref, owner_ref, row_ref, col_ref, frac_ref, factor_ref, interp_ref
+    devices, capacity, lon_cols, flags_ref, vert_ref, owner_ref, row_ref, col_ref, frac_ref, factor_ref, interp_ref
 ):
     layers = vert_ref.shape[0]
     top = lax.broadcasted_iota(jnp.int32, (8, LANES), 0) < 4
@@ -172,12 +212,9 @@
         factor_ref[1, layer] = coef[layer - 1] * inverse if layer > 0 else jnp.zeros_like(inverse)
         factor_ref[2, layer] = ratio
     count = owner_ref.shape[1]
-    devices = 1 << len(strides)
     slots = devices * capacity
-    apart = jnp.bitwise_xor(owner_ref[...], me_ref[0])
-    place = jnp.zeros_like(apart)
-    for bit, stride in enumerate(strides):
-        place = place + jnp.where(jnp.bitwise_and(apart, stride) != 0, 1 << bit, 0)
+    apart = jnp.bitwise_xor(owner_ref[...], flags_ref[0])
+    place = jnp.bitwise_and(apart, 1) * (devices // 2) + jnp.right_shift(apart, 1)
     named = jnp.where(
         lax.broadcasted_iota(jnp.int32, (devices, count), 0) == place, 1.0, 0.0
     )
@@ -294,19 +331,18 @@
     return [pl.BlockSpec(memory_space=pltpu.VMEM)] * count
 
 
-def call(kernel, out_shape, inputs, scratch=(), smem_first=False, flops=1_000_000):
+def call(kernel, out_shape, inputs, scratch=(), smem_first=False, flops=1_000_000, mib=8):
     specs = vmem(len(inputs))
     if smem_first:
         specs[0] = pl.BlockSpec(memory_space=pltpu.SMEM)
-    many = isinstance(out_shape, (list, tuple))
     moved = sum(math.prod(x.shape) * 4 for x in inputs)
     return pl.pallas_call(
         kernel,
         out_shape=out_shape,
         in_specs=specs,
-        out_specs=tuple(vmem(len(out_shape))) if many else vmem(1)[0],
+        out_specs=tuple(vmem(len(out_shape))) if isinstance(out_shape, tuple) else vmem(1)[0],
         scratch_shapes=list(scratch),
-        compiler_params=pltpu.CompilerParams(vmem_limit_bytes=32 * 1024 * 1024),
+        compiler_params=pltpu.CompilerParams(vmem_limit_bytes=mib * 1024 * 1024),
         cost_estimate=pl.CostEstimate(flops=flops, bytes_accessed=moved, transcendentals=0),
     )(*inputs)
 
@@ -317,25 +353,13 @@
 
 def from_neighbours(block):
     count = lax.axis_size("gy")
-    low = lax.ppermute(block, "gy", [(i, i + 1) for i in range(count - 1)])
-    high = lax.ppermute(block, "gy", [(i + 1, i) for i in range(count - 1)])
-    return low, high
-
-
-def gather_order(rows_y, cols_x):
-    order = []
-    stride = cols_x // 2
-    while stride > 1:
-        order.append(("gx", stride))
-        stride //= 2
-    stride = rows_y // 2
-    while stride >= 1:
-        order.append(("gy", stride))
-        stride //= 2
-    if cols_x > 1:
-        order.append(("gx", 1))
-    numbers = [stride * (cols_x if axis == "gy" else 1) for axis, stride in order]
-    return order, numbers
+    pair = lax.ppermute(block, "gy", [(i, i ^ 1) for i in range(count)])
+    cross = lax.ppermute(block, "gy", [(i, (i + (1 if i % 2 else -1)) % count) for i in range(count)])
+    return pair, cross
+
+
+def apart_by(block, axis, stride):
+    return lax.ppermute(block, axis, [(i, i ^ stride) for i in range(lax.axis_size(axis))])
 
 
 def per_device_gathered(
@@ -362,28 +386,23 @@
     capacity = 2 * obs_count // device_count
     wide = error_inverse.shape[-1]
     cells = rows * lon_cols
-    order, numbers = gather_order(rows_y, cols_x)
-
+
+    at_y, at_x = lax.axis_index("gy"), lax.axis_index("gx")
+    flags = jnp.stack([at_y * cols_x + at_x, at_y % 2, at_y == 0, at_y == rows_y - 1]).astype(jnp.int32)
     direction_n = to_native(direction)
     residual_n = to_native(residual)
     solution_n = to_native(solution)
     lateral = jnp.stack([north_coef, east_coef, ocean.astype(jnp.float32)])[:, None]
     own = jnp.concatenate([direction_n, to_native(lateral)], axis=0)
-    low, high = from_neighbours(own)
-
-    blocks = error_inverse.reshape(1, wide, wide)
-    other = None
-    for axis, stride in order:
-        if other is not None:
-            blocks = jnp.concatenate([blocks, other], axis=0)
-        other = lax.ppermute(blocks, axis, [(i, i ^ stride) for i in range(lax.axis_size(axis))])
-
-    me = (lax.axis_index("gy") * cols_x + lax.axis_index("gx")).astype(jnp.int32).reshape(1)
+    pair, cross = from_neighbours(own)
+
+    matrix = error_inverse.reshape(1, wide, wide)
+    blocks = [matrix] + [apart_by(matrix, "gx", stride) for stride in range(2, cols_x, 2)]
     factors, interp = call(
-        functools.partial(prepare_kernel, tuple(numbers), capacity, lon_cols),
+        functools.partial(prepare_kernel, device_count, capacity, lon_cols),
         (f32(3, layers, 8, LANES), f32(cells, device_count * capacity)),
         (
-            me,
+            flags,
             vert_coef.reshape(layers, cells // LANES, LANES),
             obs_owner.reshape(1, obs_count),
             obs_row.reshape(1, obs_count),
@@ -392,32 +411,45 @@
         ),
         smem_first=True,
         flops=20_000_000,
+        mib=16,
     )
 
     extended = 3 * rows + (-3 * rows) % 8
-    packed, coef = call(
-        functools.partial(first_lateral_kernel, kv, rows, tiles),
-        (f32(cols_x, 2 * kv, LANES), f32(5, extended, lons)),
-        (own, low, high),
-        scratch=(pltpu.VMEM((3, extended, lons), jnp.float32),),
+    packed, coef, held_blocks = call(
+        functools.partial(first_lateral_kernel, kv, rows, tiles, len(blocks)),
+        (f32(cols_x, 2 * kv, LANES), f32(5, extended, lons), f32(len(blocks), wide, wide)),
+        (flags, own, pair, cross, *blocks),
+        scratch=(
+            pltpu.VMEM((3, extended, lons), jnp.float32),
+            pltpu.VMEM(own.shape, jnp.float32),
+            pltpu.VMEM(own.shape, jnp.float32),
+        ),
+        smem_first=True,
         flops=4_000_000,
     )
+    near = jnp.concatenate(
+        [held_blocks] + [apart_by(held_blocks, "gy", stride) for stride in range(1, rows_y)], axis=0
+    )
+    far = apart_by(near, "gx", 1)
     columns = lax.all_to_all(packed, "gx", split_axis=0, concat_axis=0, tiled=True)
     spread = call(
         functools.partial(observe_kernel, layers, held, capacity),
         f32(cols_x * 2 * kv, LANES),
-        (columns.reshape(cols_x * 2 * kv, LANES), factors, interp, blocks, other),
+        (columns.reshape(cols_x * 2 * kv, LANES), factors, interp, near, far),
         scratch=(pltpu.VMEM((2 * wide, LANES), jnp.float32),),
         flops=1_000_000_000,
+        mib=16,
     )
     tile = lax.all_to_all(
         spread.reshape(cols_x, 2 * kv, LANES), "gx", split_axis=0, concat_axis=0, tiled=True
     )
-    low, high = from_neighbours(tile)
+    pair, cross = from_neighbours(tile)
     image, sums = call(
         functools.partial(second_lateral_kernel, kv, rows, tiles),
         (f32(*direction_n.shape), f32(device_count, 1, LANES)),
-        (tile, low, high, coef, direction_n, residual_n),
+        (flags, tile, pair, cross, coef, direction_n, residual_n),
+        scratch=(pltpu.VMEM(tile.shape, jnp.float32), pltpu.VMEM(tile.shape, jnp.float32)),
+        smem_first=True,
         flops=4_000_000,
     )
     sums = lax.all_to_all(sums, ("gy", "gx"), split_axis=0, concat_axis=0, tiled=True)
@@ -432,15 +464,15 @@
 def gathers(mesh, shapes):
     rows_y, cols_x = mesh.shape["gy"], mesh.shape["gx"]
     devices = rows_y * cols_x
+    if any(size < 2 or size & (size - 1) for size in (rows_y, cols_x)):
+        return False
     direction, vert_coef, obs_row, error_inverse = shapes
     var_count, layers, lat_rows, lons = direction
     rows, held = lat_rows // rows_y, layers // cols_x
     obs_count, wide = obs_row[-1], error_inverse[-1]
     capacity = 2 * obs_count // devices
     return (
-        devices & (devices - 1) == 0
-        and devices > 1
-        and rows == NSTEP == 4
+        rows == NSTEP == 4
         and var_count == 4
         and (var_count * held) % 8 == 0
         and lons // cols_x * 2 == LANES

time: 96.4 us -> 77 us (0.80)
  starting transfers between devices: 27.8 us -> 17.9 us
  waiting for transfers between devices: 29.2 us -> 22.7 us
  blocking collectives: 23.3 us -> 19.3 us
  Pallas kernels: 9.73 us -> 11.4 us
  local copies, waits for them, and re-layouts: 4.05 us -> 2.65 us
    ppermute x9 -> x11, starting transfers between devices: 20.6 us -> 14.4 us  [the longest x7 7.95 us: apart_by(): lax.ppermute(block, axis, [(i, i ^ stride) for i in range(lax.axis_size(a...]
    ppermute x9 -> x11, waiting for transfers between devices: 26.4 us -> 20.5 us  [the longest x7 14.8 us: apart_by(): lax.ppermute(block, axis, [(i, i ^ stride) for i in range(lax.axis_size(a...]
    all_to_all x1, blocking collectives: 13.9 us -> 9.79 us  [per_device_gathered(): lax.all_to_all(sums, ('gy', 'gx'), split_axis=0, concat_axis=0, tiled=True)]
    all_to_all x1, starting transfers between devices: 7.19 us -> 3.52 us  [per_device_gathered(): lax.all_to_all(packed, 'gx', split_axis=0, concat_axis=0, tiled=True)]
    pallas_call x5, Pallas kernels: 9.73 us -> 11.4 us  [call(): pl.pallas_call(kernel, out_shape=out_shape, in_specs=specs, out_specs=tup...]
    unnamed x36 -> x29, local copies, waits for them, and re-layouts: 3.92 us -> 2.53 us
  transfers between devices with their start and end apart: 10 -> 12, of which waited for: 9 -> 7; matrix products, arithmetic and copies ran while one was open for 0% -> 0% of each run, Pallas kernels for 4% -> 4%
where the time goes in v2:
time: 77 us; the launch traced here: 76.6 us
  waiting for transfers between devices  22.7 us (29%)
  blocking collectives  19.3 us (25%)
  starting transfers between devices  17.9 us (23%)
  Pallas kernels  11.4 us (15%)
  local copies, waits for them, and re-layouts  2.65 us (3%)
  other arithmetic  1.74 us (2%)
  between operations  0.82 us (1%)
    ppermute x7, waiting for transfers between devices, apart_by(): lax.ppermute(block, axis, [(i, i ^ stride) for i in range(lax.axis_size(a...  14.8 us
    pallas_call x5, Pallas kernels, call(): pl.pallas_call(kernel, out_shape=out_shape, in_specs=specs, out_specs=tup...  11.4 us
    all_to_all x1, blocking collectives, per_device_gathered(): lax.all_to_all(sums, ('gy', 'gx'), split_axis=0, concat_axis=0, tiled=True)  9.79 us
    all_to_all x1, blocking collectives, per_device_gathered(): lax.all_to_all(spread.reshape(cols_x, 2 * kv, LANES), 'gx', split_axis=0,...  9.53 us
    ppermute x7, starting transfers between devices, apart_by(): lax.ppermute(block, axis, [(i, i ^ stride) for i in range(lax.axis_size(a...  7.95 us
    ppermute x2, waiting for transfers between devices, from_neighbours(): lax.ppermute(block, 'gy', [(i, (i + (1 if i % 2 else -1)) % count) for i...  5.27 us
    ppermute x2, starting transfers between devices, from_neighbours(): lax.ppermute(block, 'gy', [(i, (i + (1 if i % 2 else -1)) % count) for i...  5.09 us
    all_to_all x1, starting transfers between devices, per_device_gathered(): lax.all_to_all(packed, 'gx', split_axis=0, concat_axis=0, tiled=True)  3.52 us
  transfers between devices with their start and end apart: 12, of which 7 were waited for; matrix products, arithmetic and copies ran while one was open for 0% of the time, Pallas kernels for 4%

profile of v2, /device:TPU:0, one launch (start us, length us, event | category | flops | bytes accessed | tf_op | source)
XLA Modules:
  0.0 76.6 jit_solution(16359639358660185319)
XLA Ops:
  0.6 0.0 copy-start.11
  0.6 0.0 copy-start.12
  0.7 0.7 convert_bitcast_fusion
  1.4 0.0 copy-done.11
  1.4 0.0 copy-done.12
  1.4 0.0 copy-start.5
  1.4 0.9 %pad_maximum_fusion.own_ref = f32[304,128]{1,0:T(8,128)S(1)} fusion(f32[48,128]{1,0:T(8,128)S(1)} %bitcast.64, f32[256,128]{1,0:T(8,128)} %bitcast.48), kind=kLoop, calls=%fused_computation | loop fusion | flops 38912 | bytes 311296 | tf_op jit(solution)/shard_map/concatenate | solution.py:396
  2.3 4.0 %collective-permute-start.1 = (f32[304,128]{1,0:T(8,128)S(1)}, f32[304,128]{1,0:T(8,128)S(1)}, u32[]{:S(2)}, u32[]{:S(2)}) collective-permute-start(f32[304,128]{1,0:T(8,128)S(1)} %pad_maximum_fusion.own_ref), channel_id=1, source_target_pairs={{0,24},{8,16},{16,8},{24,0},{1,25},{9,17},{17,9},{25,1},{2,26},{10... | collective-permute-start | bytes 466952 | tf_op jit(solution)/shard_map/ppermute | solution.py:357
  6.3 0.5 collective-permute-start
  6.8 0.0 copy-done.5
  6.8 3.6 %collective-permute-start.4 = (f32[1,128,128]{2,1,0:T(8,128)S(1)}, f32[1,128,128]{2,1,0:T(8,128)S(1)}, u32[]{:S(2)}, u32[]{:S(2)}) collective-permute-start(f32[1,128,128]{2,1,0:T(8,128)S(1)} %bitcast.56), channel_id=1, source_target_pairs={{0,6},{1,7},{2,4},{3,5},{4,2},{5,3},{6,0},{7,1},{8,14},{9,15},{10,... | collective-permute-start | bytes 196616 | tf_op jit(solution)/shard_map/ppermute | solution.py:362
  10.4 0.0 collective-permute-start.3
  10.4 0.8 %collective-permute-start.2 = (f32[1,128,128]{2,1,0:T(8,128)S(1)}, f32[1,128,128]{2,1,0:T(8,128)S(1)}, u32[]{:S(2)}, u32[]{:S(2)}) collective-permute-start(f32[1,128,128]{2,1,0:T(8,128)S(1)} %bitcast.58), channel_id=1, source_target_pairs={{0,2},{1,3},{2,0},{3,1},{4,6},{5,7},{6,4},{7,5},{8,10},{9,11},{10,... | collective-permute-start | bytes 196616 | tf_op jit(solution)/shard_map/ppermute | solution.py:362
  11.2 0.1 pad_add_fusion.flags_ref
  11.3 2.1 %collective-permute-done.4.refs_3_ = f32[1,128,128]{2,1,0:T(8,128)S(1)} collective-permute-done((f32[1,128,128]{2,1,0:T(8,128)S(1)}, f32[1,128,128]{2,1,0:T(8,128)S(1)}, u32[]{:S(2)}, u32[]{:S(2)}) %collective-permute-start.4) | collective-permute-done | bytes 65568 | tf_op jit(solution)/shard_map/ppermute | solution.py:362
  13.4 2.3 %collective-permute-done.3.refs_2_ = f32[1,128,128]{2,1,0:T(8,128)S(1)} collective-permute-done((f32[1,128,128]{2,1,0:T(8,128)S(1)}, f32[1,128,128]{2,1,0:T(8,128)S(1)}, u32[]{:S(2)}, u32[]{:S(2)}) %collective-permute-start.3) | collective-permute-done | bytes 65568 | tf_op jit(solution)/shard_map/ppermute | solution.py:362
  15.7 0.0 collective-permute-done.2.refs_1_
  15.7 0.0 collective-permute-done.1.cross_ref
  15.7 0.0 collective-permute-done.pair_ref
  15.7 2.1 %shard_map.139 = (f32[8,32,128]{2,1,0:T(8,128)}, f32[5,16,512]{2,1,0:T(8,128)S(1)}, f32[4,128,128]{2,1,0:T(8,128)S(1)}) custom-call(s32[4]{0:T(128)S(1)} %pad_add_fusion.flags_ref, f32[304,128]{1,0:T(8,128)S(1)} %pad_maximum_fusion.own_ref, f32[304,128]{1,0:T(8,128)S(1)} %collective-permute-done.pair_ref, f32[304,128]{1,0:T(8,128)S(1)} %collective-permute-done.1.cross_ref, ...), custom_call_target="tpu_custom_call" | custom-call | flops 4000000 | bytes 729104 | tf_op jit(solution)/shard_map/pallas_call | solution.py:339
  17.8 1.5 %collective-permute-start.5 = (f32[4,128,128]{2,1,0:T(8,128)S(1)}, f32[4,128,128]{2,1,0:T(8,128)S(1)}, u32[]{:S(2)}, u32[]{:S(2)}) collective-permute-start(f32[4,128,128]{2,1,0:T(8,128)S(1)} %get-tuple-element.16), channel_id=1, source_target_pairs={{0,8},{8,0},{16,24},{24,16},{1,9},{9,1},{17,25},{25,17},{2,10},{10... | collective-permute-start | bytes 786440 | tf_op jit(solution)/shard_map/ppermute | solution.py:362
  19.3 0.5 collective-permute-start.6
  19.8 1.5 %collective-permute-start.7 = (f32[4,128,128]{2,1,0:T(8,128)S(1)}, f32[4,128,128]{2,1,0:T(8,128)S(1)}, u32[]{:S(2)}, u32[]{:S(2)}) collective-permute-start(f32[4,128,128]{2,1,0:T(8,128)S(1)} %get-tuple-element.16), channel_id=1, source_target_pairs={{0,24},{8,16},{16,8},{24,0},{1,25},{9,17},{17,9},{25,1},{2,26},{10... | collective-permute-start | bytes 786440 | tf_op jit(solution)/shard_map/ppermute | solution.py:362
  21.4 5.7 %collective-permute-done.5 = f32[4,128,128]{2,1,0:T(8,128)S(1)} collective-permute-done((f32[4,128,128]{2,1,0:T(8,128)S(1)}, f32[4,128,128]{2,1,0:T(8,128)S(1)}, u32[]{:S(2)}, u32[]{:S(2)}) %collective-permute-start.5) | collective-permute-done | bytes 262176 | tf_op jit(solution)/shard_map/ppermute | solution.py:362
  27.1 4.7 %collective-permute-done.6 = f32[4,128,128]{2,1,0:T(8,128)S(1)} collective-permute-done((f32[4,128,128]{2,1,0:T(8,128)S(1)}, f32[4,128,128]{2,1,0:T(8,128)S(1)}, u32[]{:S(2)}, u32[]{:S(2)}) %collective-permute-start.6) | collective-permute-done | bytes 262176 | tf_op jit(solution)/shard_map/ppermute | solution.py:362
  31.8 0.0 collective-permute-done.7
  31.8 0.1 collective-permute-start.8
  31.9 0.0 copy-start.10
  31.9 3.5 %all-to-all-start = ((f32[8,32,128]{2,1,0:T(8,128)}), f32[8,32,128]{2,1,0:T(8,128)S(1)}, u32[]{:S(2)}, u32[]{:S(2)}) async-start(f32[8,32,128]{2,1,0:T(8,128)} %get-tuple-element.13), calls=%async_computation | async-start | bytes 262144 | tf_op jit(solution)/shard_map/all_to_all | solution.py:434
  35.5 0.0 copy-done.10
  35.5 0.0 copy-start.8
  35.5 0.0 copy-start.9
  35.5 0.1 reshape.80.vert_ref
  35.6 0.0 copy-start.6
  35.6 0.0 copy-start.7
  35.6 0.5 copy-done.8
  36.2 0.0 copy-done.9
  36.2 0.1 copy-done.6
  36.3 0.0 copy-done.7
  36.3 2.9 %shard_map.140 = (f32[3,32,8,128]{3,2,1,0:T(8,128)S(1)}, f32[256,1024]{1,0:T(8,128)S(1)}) custom-call(s32[4]{0:T(128)S(1)} %pad_add_fusion.flags_ref, f32[32,2,128]{2,1,0:T(2,128)S(1)} %reshape.80.vert_ref, s32[1,512]{1,0:T(1,128)S(1)} %bitcast.61, s32[1,512]{1,0:T(1,128)S(1)} %bitcast.62, s32[1,512]{1,0:T(1,128)S(1)} %bitcast.63, f32[2,512]{1,0:T(2,128)S(1)} %bitcast.60), custom_call_target="tpu_custom_call" | custom-call | flops 20000000 | bytes 43024 | tf_op jit(solution)/shard_map/pallas_call | solution.py:339
  39.2 0.0 copy-start.2
  39.2 0.7 copy-done.2
  40.0 2.2 %all-to-all-done = f32[8,32,128]{2,1,0:T(8,128)S(1)} async-done(((f32[8,32,128]{2,1,0:T(8,128)}), f32[8,32,128]{2,1,0:T(8,128)S(1)}, u32[]{:S(2)}, u32[]{:S(2)}) %all-to-all-start) | async-done | bytes 131104 | tf_op jit(solution)/shard_map/all_to_all | solution.py:434
  42.2 0.0 collective-permute-done.8.far_ref
  42.2 0.0 copy-start.3
  42.2 1.0 %copy-done.3 = f32[3,32,8,128]{3,2,1,0:T(8,128)S(1)} copy-done((f32[3,32,8,128]{3,2,1,0:T(8,128)S(1)}, f32[3,32,8,128]{3,2,1,0:T(8,128)}, u32[]{:S(2)}) %copy-start.3) | copy-done | bytes 393240
  43.2 4.0 %shard_map.141 = f32[256,128]{1,0:T(8,128)S(1)} custom-call(f32[256,128]{1,0:T(8,128)S(1)} %bitcast.53, f32[3,32,8,128]{3,2,1,0:T(8,128)S(1)} %copy-done.3, f32[256,1024]{1,0:T(8,128)S(1)} %get-tuple-element.15.interp_ref, f32[16,128,128]{2,1,0:T(8,128)S(1)} %constant_dynamic-update-slice_fusion.near_ref, f32[16,128,128]{2,1,0:T(8,128)S(1)} %collective-permute-done.8.far_ref), custom_call_target="tpu_custom_call" | custom-call | flops 1000000000 | bytes 3670016 | tf_op jit(solution)/shard_map/pallas_call | solution.py:339
  47.1 0.0 copy-start
  47.1 0.0 copy-start.1
  47.1 9.5 %all_to_all.15.own_ref = f32[8,32,128]{2,1,0:T(8,128)S(1)} all-to-all(f32[8,32,128]{2,1,0:T(8,128)S(1)} %bitcast.54), channel_id=1, replica_groups=mesh['gy'=4,'gx'=8] {'gx'}, dimensions={0} | all-to-all | bytes 262144 | tf_op jit(solution)/shard_map/all_to_all | solution.py:443
  56.7 1.1 %collective-permute-start.10 = (f32[8,32,128]{2,1,0:T(8,128)S(1)}, f32[8,32,128]{2,1,0:T(8,128)S(1)}, u32[]{:S(2)}, u32[]{:S(2)}) collective-permute-start(f32[8,32,128]{2,1,0:T(8,128)S(1)} %all_to_all.15.own_ref), channel_id=1, source_target_pairs={{0,24},{8,16},{16,8},{24,0},{1,25},{9,17},{17,9},{25,1},{2,26},{10... | collective-permute-start | bytes 393224 | tf_op jit(solution)/shard_map/ppermute | solution.py:357
  57.8 0.8 %collective-permute-start.9 = (f32[8,32,128]{2,1,0:T(8,128)S(1)}, f32[8,32,128]{2,1,0:T(8,128)S(1)}, u32[]{:S(2)}, u32[]{:S(2)}) collective-permute-start(f32[8,32,128]{2,1,0:T(8,128)S(1)} %all_to_all.15.own_ref), channel_id=1, source_target_pairs={{0,8},{8,0},{16,24},{24,16},{1,9},{9,1},{17,25},{25,17},{2,10},{10... | collective-permute-start | bytes 393224 | tf_op jit(solution)/shard_map/ppermute | solution.py:356
  58.6 5.3 %collective-permute-done.10.cross_ref = f32[8,32,128]{2,1,0:T(8,128)S(1)} collective-permute-done((f32[8,32,128]{2,1,0:T(8,128)S(1)}, f32[8,32,128]{2,1,0:T(8,128)S(1)}, u32[]{:S(2)}, u32[]{:S(2)}) %collective-permute-start.10) | collective-permute-done | bytes 131104 | tf_op jit(solution)/shard_map/ppermute | solution.py:357
  63.9 0.4 collective-permute-done.9.pair_ref
  64.4 0.0 copy-done
  64.4 0.0 copy-done.1
  64.4 0.0 copy-start.4
  64.4 1.5 %shard_map.142 = (f32[256,128]{1,0:T(8,128)S(1)}, f32[32,1,128]{2,1,0:T(1,128)S(1)}) custom-call(s32[4]{0:T(128)S(1)} %pad_add_fusion.flags_ref, f32[8,32,128]{2,1,0:T(8,128)S(1)} %all_to_all.15.own_ref, f32[8,32,128]{2,1,0:T(8,128)S(1)} %collective-permute-done.9.pair_ref, f32[8,32,128]{2,1,0:T(8,128)S(1)} %collective-permute-done.10.cross_ref, ...), custom_call_target="tpu_custom_call" | custom-call | flops 4000000 | bytes 819216 | tf_op jit(solution)/shard_map/pallas_call | solution.py:339
  65.9 9.8 %all_to_all.16.sums_ref = f32[32,1,128]{2,1,0:T(1,128)S(1)} all-to-all(f32[32,1,128]{2,1,0:T(1,128)S(1)} %get-tuple-element.18), channel_id=1, replica_groups=mesh['gy'=4,'gx'=8] {'gy','gx'}, dimensions={0} | all-to-all | bytes 32768 | tf_op jit(solution)/shard_map/all_to_all | solution.py:455
  75.7 0.0 copy-done.4
  75.7 0.9 %shard_map.143 = (f32[256,128]{1,0:T(8,128)}, f32[256,128]{1,0:T(8,128)}, f32[256,128]{1,0:T(8,128)}) custom-call(f32[32,1,128]{2,1,0:T(1,128)S(1)} %all_to_all.16.sums_ref, f32[256,128]{1,0:T(8,128)S(1)} %bitcast.50, f32[256,128]{1,0:T(8,128)S(1)} %bitcast.55, f32[256,128]{1,0:T(8,128)S(1)} %bitcast.52, f32[256,128]{1,0:T(8,128)S(1)} %get-tuple-element.19.image_ref), custom_call_target="tpu_custom_call" | custom-call | flops 1000000 | bytes 540672 | tf_op jit(solution)/shard_map/pallas_call | solution.py:339
  (5 shorter events, 0.1 us)
Async XLA Ops:
  0.6 0.7 copy-start.11
  0.6 0.7 copy-start.12
  1.4 5.5 %copy-start.5 = (f32[1,1,128,128]{3,2,1,0:T(8,128)S(1)}, f32[1,1,128,128]{3,2,1,0:T(8,128)}, u32[]{:S(2)}) copy-start(f32[1,1,128,128]{3,2,1,0:T(8,128)} %param.23) | copy-start | bytes 196612
  2.3 13.4 %collective-permute-start.1 = (f32[304,128]{1,0:T(8,128)S(1)}, f32[304,128]{1,0:T(8,128)S(1)}, u32[]{:S(2)}, u32[]{:S(2)}) collective-permute-start(f32[304,128]{1,0:T(8,128)S(1)} %pad_maximum_fusion.own_ref), channel_id=1, source_target_pairs={{0,24},{8,16},{16,8},{24,0},{1,25},{9,17},{17,9},{25,1},{2,26},{10... | collective-permute-start | bytes 466952 | tf_op jit(solution)/shard_map/ppermute | solution.py:357
  6.3 9.4 %collective-permute-start = (f32[304,128]{1,0:T(8,128)S(1)}, f32[304,128]{1,0:T(8,128)S(1)}, u32[]{:S(2)}, u32[]{:S(2)}) collective-permute-start(f32[304,128]{1,0:T(8,128)S(1)} %pad_maximum_fusion.own_ref), channel_id=1, source_target_pairs={{0,8},{8,0},{16,24},{24,16},{1,9},{9,1},{17,25},{25,17},{2,10},{10... | collective-permute-start | bytes 466952 | tf_op jit(solution)/shard_map/ppermute | solution.py:356
  6.8 6.6 %collective-permute-start.4 = (f32[1,128,128]{2,1,0:T(8,128)S(1)}, f32[1,128,128]{2,1,0:T(8,128)S(1)}, u32[]{:S(2)}, u32[]{:S(2)}) collective-permute-start(f32[1,128,128]{2,1,0:T(8,128)S(1)} %bitcast.56), channel_id=1, source_target_pairs={{0,6},{1,7},{2,4},{3,5},{4,2},{5,3},{6,0},{7,1},{8,14},{9,15},{10,... | collective-permute-start | bytes 196616 | tf_op jit(solution)/shard_map/ppermute | solution.py:362
  10.4 5.2 %collective-permute-start.3 = (f32[1,128,128]{2,1,0:T(8,128)S(1)}, f32[1,128,128]{2,1,0:T(8,128)S(1)}, u32[]{:S(2)}, u32[]{:S(2)}) collective-permute-start(f32[1,128,128]{2,1,0:T(8,128)S(1)} %bitcast.57), channel_id=1, source_target_pairs={{0,4},{1,5},{2,6},{3,7},{4,0},{5,1},{6,2},{7,3},{8,12},{9,13},{10,... | collective-permute-start | bytes 196616 | tf_op jit(solution)/shard_map/ppermute | solution.py:362
  10.4 5.2 %collective-permute-start.2 = (f32[1,128,128]{2,1,0:T(8,128)S(1)}, f32[1,128,128]{2,1,0:T(8,128)S(1)}, u32[]{:S(2)}, u32[]{:S(2)}) collective-permute-start(f32[1,128,128]{2,1,0:T(8,128)S(1)} %bitcast.58), channel_id=1, source_target_pairs={{0,2},{1,3},{2,0},{3,1},{4,6},{5,7},{6,4},{7,5},{8,10},{9,11},{10,... | collective-permute-start | bytes 196616 | tf_op jit(solution)/shard_map/ppermute | solution.py:362
  17.8 9.2 %collective-permute-start.5 = (f32[4,128,128]{2,1,0:T(8,128)S(1)}, f32[4,128,128]{2,1,0:T(8,128)S(1)}, u32[]{:S(2)}, u32[]{:S(2)}) collective-permute-start(f32[4,128,128]{2,1,0:T(8,128)S(1)} %get-tuple-element.16), channel_id=1, source_target_pairs={{0,8},{8,0},{16,24},{24,16},{1,9},{9,1},{17,25},{25,17},{2,10},{10... | collective-permute-start | bytes 786440 | tf_op jit(solution)/shard_map/ppermute | solution.py:362
  19.3 12.5 %collective-permute-start.6 = (f32[4,128,128]{2,1,0:T(8,128)S(1)}, f32[4,128,128]{2,1,0:T(8,128)S(1)}, u32[]{:S(2)}, u32[]{:S(2)}) collective-permute-start(f32[4,128,128]{2,1,0:T(8,128)S(1)} %get-tuple-element.16), channel_id=1, source_target_pairs={{0,16},{8,24},{16,0},{24,8},{1,17},{9,25},{17,1},{25,9},{2,18},{10... | collective-permute-start | bytes 786440 | tf_op jit(solution)/shard_map/ppermute | solution.py:362
  19.8 12.0 %collective-permute-start.7 = (f32[4,128,128]{2,1,0:T(8,128)S(1)}, f32[4,128,128]{2,1,0:T(8,128)S(1)}, u32[]{:S(2)}, u32[]{:S(2)}) collective-permute-start(f32[4,128,128]{2,1,0:T(8,128)S(1)} %get-tuple-element.16), channel_id=1, source_target_pairs={{0,24},{8,16},{16,8},{24,0},{1,25},{9,17},{17,9},{25,1},{2,26},{10... | collective-permute-start | bytes 786440 | tf_op jit(solution)/shard_map/ppermute | solution.py:362
  31.8 10.3 %collective-permute-start.8 = (f32[16,128,128]{2,1,0:T(8,128)S(1)}, f32[16,128,128]{2,1,0:T(8,128)S(1)}, u32[]{:S(2)}, u32[]{:S(2)}) collective-permute-start(f32[16,128,128]{2,1,0:T(8,128)S(1)} %constant_dynamic-update-slice_fusion.near_ref), channel_id=1, source_target_pairs={{0,1},{1,0},{2,3},{3,2},{4,5},{5,4},{6,7},{7,6},{8,9},{9,8},{10,11... | collective-permute-start | bytes 3145736 | tf_op jit(solution)/shard_map/ppermute | solution.py:362
  31.9 3.5 %copy-start.10 = (f32[32,4,64]{2,1,0:T(4,128)S(1)}, f32[32,4,64]{2,1,0:T(4,128)}, u32[]{:S(2)}) copy-start(f32[32,4,64]{2,1,0:T(4,128)} %param.18) | copy-start | bytes 98308
  31.9 10.2 %all-to-all-start = ((f32[8,32,128]{2,1,0:T(8,128)}), f32[8,32,128]{2,1,0:T(8,128)S(1)}, u32[]{:S(2)}, u32[]{:S(2)}) async-start(f32[8,32,128]{2,1,0:T(8,128)} %get-tuple-element.13), calls=%async_computation | async-start | bytes 262144 | tf_op jit(solution)/shard_map/all_to_all | solution.py:434
  35.5 0.7 copy-start.8
  35.5 0.7 copy-start.9
  35.6 0.7 copy-start.6
  35.6 0.7 copy-start.7
  39.2 0.8 copy-start.2
  42.2 1.0 %copy-start.3 = (f32[3,32,8,128]{3,2,1,0:T(8,128)S(1)}, f32[3,32,8,128]{3,2,1,0:T(8,128)}, u32[]{:S(2)}) copy-start(f32[3,32,8,128]{3,2,1,0:T(8,128)} %copy-done.2) | copy-start | bytes 1179652
  47.1 17.2 %copy-start = (f32[4,4,4,512]{3,2,1,0:T(4,128)S(1)}, f32[4,4,4,512]{3,2,1,0:T(4,128)}, u32[]{:S(2)}) copy-start(f32[4,4,4,512]{3,2,1,0:T(4,128)} %param.12) | copy-start | bytes 393220
  47.1 17.2 %copy-start.1 = (f32[4,4,4,512]{3,2,1,0:T(4,128)S(1)}, f32[4,4,4,512]{3,2,1,0:T(4,128)}, u32[]{:S(2)}) copy-start(f32[4,4,4,512]{3,2,1,0:T(4,128)} %param.14) | copy-start | bytes 393220
  56.7 7.2 %collective-permute-start.10 = (f32[8,32,128]{2,1,0:T(8,128)S(1)}, f32[8,32,128]{2,1,0:T(8,128)S(1)}, u32[]{:S(2)}, u32[]{:S(2)}) collective-permute-start(f32[8,32,128]{2,1,0:T(8,128)S(1)} %all_to_all.15.own_ref), channel_id=1, source_target_pairs={{0,24},{8,16},{16,8},{24,0},{1,25},{9,17},{17,9},{25,1},{2,26},{10... | collective-permute-start | bytes 393224 | tf_op jit(solution)/shard_map/ppermute | solution.py:357
  57.8 6.6 %collective-permute-start.9 = (f32[8,32,128]{2,1,0:T(8,128)S(1)}, f32[8,32,128]{2,1,0:T(8,128)S(1)}, u32[]{:S(2)}, u32[]{:S(2)}) collective-permute-start(f32[8,32,128]{2,1,0:T(8,128)S(1)} %all_to_all.15.own_ref), channel_id=1, source_target_pairs={{0,8},{8,0},{16,24},{24,16},{1,9},{9,1},{17,25},{25,17},{2,10},{10... | collective-permute-start | bytes 393224 | tf_op jit(solution)/shard_map/ppermute | solution.py:356
  64.4 11.3 %copy-start.4 = (f32[4,4,4,512]{3,2,1,0:T(4,128)S(1)}, f32[4,4,4,512]{3,2,1,0:T(4,128)}, u32[]{:S(2)}) copy-start(f32[4,4,4,512]{3,2,1,0:T(4,128)} %param.13) | copy-start | bytes 393220

commit v3 on v2

--- a/solution.py
+++ b/solution.py
@@ -53,8 +53,9 @@
     return rows
 
 
-def sort_halo(flags_ref, pair_ref, cross_ref, low_ref, high_ref):
-    odd = flags_ref[1] == 1
+def sort_halo(pair_ref, cross_ref, low_ref, high_ref):
+    at_y, rows_y = lax.axis_index("gy"), lax.axis_size("gy")
+    odd = lax.rem(at_y, 2) == 1
 
     @pl.when(odd)
     def _():
@@ -66,22 +67,45 @@
         low_ref[...] = cross_ref[...]
         high_ref[...] = pair_ref[...]
 
-    @pl.when(flags_ref[2] == 1)
+    @pl.when(at_y == 0)
     def _():
         low_ref[...] = jnp.zeros_like(low_ref)
 
-    @pl.when(flags_ref[3] == 1)
+    @pl.when(at_y == rows_y - 1)
     def _():
         high_ref[...] = jnp.zeros_like(high_ref)
 
 
-def first_lateral_kernel(kv, rows, tiles, count, flags_ref, own_ref, pair_ref, cross_ref, *refs):
+def halo_kernel(direction_ref, north_ref, east_ref, ocean_ref, own_ref, mask_ref, sems):
+    cells, size = direction_ref.shape[0], north_ref.shape[0]
+    moves = (
+        (ocean_ref, mask_ref),
+        (direction_ref, own_ref.at[pl.ds(0, cells)]),
+        (north_ref, own_ref.at[pl.ds(cells, size)]),
+        (east_ref, own_ref.at[pl.ds(cells + size, size)]),
+    )
+    copies = [pltpu.make_async_copy(*move, sems.at[at]) for at, move in enumerate(moves)]
+    for copy in copies:
+        copy.start()
+    for copy in copies:
+        copy.wait()
+    own_ref[cells + 2 * size : cells + 3 * size, :] = mask_ref[...].astype(jnp.float32)
+
+
+def join_kernel(count, _, *refs):
+    blocks, (near_ref,) = refs[:count], refs[count:]
+    size = blocks[0].shape[0]
+    for at, block in enumerate(blocks):
+        near_ref[at * size : (at + 1) * size] = block[...]
+
+
+def first_lateral_kernel(kv, rows, tiles, count, _, own_ref, pair_ref, cross_ref, *refs):
     blocks, (packed_ref, coef_ref, held_ref, ext_ref, low_ref, high_ref) = refs[:count], refs[count:]
     lons = tiles * LANES
     cells = kv * tiles * rows
     for at, block in enumerate(blocks):
         held_ref[at] = block[0]
-    sort_halo(flags_ref, pair_ref, cross_ref, low_ref, high_ref)
+    sort_halo(pair_ref, cross_ref, low_ref, high_ref)
     ext_ref[...] = jnp.zeros_like(ext_ref)
     for kind in range(3):
         for block, ref in enumerate((low_ref, own_ref, high_ref)):
@@ -126,7 +150,6 @@
     kv,
     rows,
     tiles,
-    flags_ref,
     own_ref,
     pair_ref,
     cross_ref,
@@ -138,7 +161,7 @@
     low_ref,
     high_ref,
 ):
-    sort_halo(flags_ref, pair_ref, cross_ref, low_ref, high_ref)
+    sort_halo(pair_ref, cross_ref, low_ref, high_ref)
     low = lane_low((8, LANES))
     totals = [jnp.zeros((8, tiles * LANES), jnp.float32) for _ in range(4)]
     for half in range(kv // 8):
@@ -194,7 +217,7 @@
 
 
 def prepare_kernel(
-    devices, capacity, lon_cols, flags_ref, vert_ref, owner_ref, row_ref, col_ref, frac_ref, factor_ref, interp_ref
+    devices, capacity, lon_cols, vert_ref, owner_ref, row_ref, col_ref, frac_ref, factor_ref, interp_ref
 ):
     layers = vert_ref.shape[0]
     top = lax.broadcasted_iota(jnp.int32, (8, LANES), 0) < 4
@@ -213,7 +236,8 @@
         factor_ref[2, layer] = ratio
     count = owner_ref.shape[1]
     slots = devices * capacity
-    apart = jnp.bitwise_xor(owner_ref[...], flags_ref[0])
+    me = lax.axis_index("gy") * lax.axis_size("gx") + lax.axis_index("gx")
+    apart = jnp.bitwise_xor(owner_ref[...], me)
     place = jnp.bitwise_and(apart, 1) * (devices // 2) + jnp.right_shift(apart, 1)
     named = jnp.where(
         lax.broadcasted_iota(jnp.int32, (devices, count), 0) == place, 1.0, 0.0
@@ -275,34 +299,36 @@
         write(layer, value)
 
 
-def observe_kernel(
-    layers, held, capacity, packed_ref, factor_ref, interp_ref, near_ref, far_ref, out_ref, column_ref
+def packed_at(layer, held):
+    return pl.ds((layer // held) * 8 * held + layer % held, 8, stride=held)
+
+
+def profile_kernel(layers, held, packed_ref, factor_ref, interp_ref, profile_ref, column_ref):
+    kv = profile_ref.shape[0]
+
+    def read(layer):
+        return packed_ref[packed_at(layer, held), :]
+
+    def write(layer, value):
+        column_ref[pl.ds(layer, 8, stride=layers), :] = value
+
+    solve_columns(read, write, factor_ref, layers)
+    columns = jnp.concatenate([column_ref[0:kv, :], column_ref[kv : 2 * kv, :]], axis=1)
+    profile_ref[...] = jnp.dot(
+        columns, interp_ref[...], precision=HIGHEST, preferred_element_type=jnp.float32
+    )
+
+
+def spread_kernel(
+    layers, held, capacity, profile_ref, factor_ref, interp_ref, near_ref, far_ref, out_ref, column_ref
 ):
     kv = near_ref.shape[1]
-    block = 8 * held
-
-    def packed_at(layer):
-        return pl.ds((layer // held) * block + layer % held, 8, stride=held)
-
-    def column_at(layer):
-        return pl.ds(layer, 8, stride=layers)
-
-    def read_packed(layer):
-        return packed_ref[packed_at(layer), :]
-
-    def write_column(layer, value):
-        column_ref[column_at(layer), :] = value
-
-    solve_columns(read_packed, write_column, factor_ref, layers)
-    columns = jnp.concatenate([column_ref[0:kv, :], column_ref[kv : 2 * kv, :]], axis=1)
-    interp = interp_ref[...]
-    profile = jnp.dot(columns, interp, precision=HIGHEST, preferred_element_type=jnp.float32)
     owners = LANES // capacity
     mine = lax.broadcasted_iota(jnp.int32, (kv, LANES), 1) // capacity
     near = near_ref.shape[0]
     parts = []
-    for tile in range(profile.shape[1] // LANES):
-        values = profile[:, tile * LANES : (tile + 1) * LANES]
+    for tile in range(profile_ref.shape[1] // LANES):
+        values = profile_ref[:, tile * LANES : (tile + 1) * LANES]
         first = tile * owners
         ref, at = (near_ref, first) if first < near else (far_ref, first - near)
         matrices = ref[at : at + owners].reshape(owners * kv, kv)
@@ -311,30 +337,35 @@
         for owner in range(1, owners):
             kept = jnp.where(mine == owner, product[owner * kv : (owner + 1) * kv], kept)
         parts.append(kept)
-    weighted = jnp.concatenate(parts, axis=1)
     spread = lax.dot_general(
-        weighted, interp, (((1,), (1,)), ((), ())), precision=HIGHEST, preferred_element_type=jnp.float32
+        jnp.concatenate(parts, axis=1),
+        interp_ref[...],
+        (((1,), (1,)), ((), ())),
+        precision=HIGHEST,
+        preferred_element_type=jnp.float32,
     )
     column_ref[0:kv, :] = spread[:, :LANES]
     column_ref[kv : 2 * kv, :] = spread[:, LANES:]
 
-    def read_column(layer):
-        return column_ref[column_at(layer), :]
-
-    def write_packed(layer, value):
-        out_ref[packed_at(layer), :] = value
-
-    solve_columns(read_column, write_packed, factor_ref, layers)
+    def read(layer):
+        return column_ref[pl.ds(layer, 8, stride=layers), :]
+
+    def write(layer, value):
+        out_ref[packed_at(layer, held), :] = value
+
+    solve_columns(read, write, factor_ref, layers)
 
 
 def vmem(count):
     return [pl.BlockSpec(memory_space=pltpu.VMEM)] * count
 
 
-def call(kernel, out_shape, inputs, scratch=(), smem_first=False, flops=1_000_000, mib=8):
+def call(kernel, out_shape, inputs, scratch=(), after=False, hbm=False, flops=1_000_000, mib=8):
     specs = vmem(len(inputs))
-    if smem_first:
-        specs[0] = pl.BlockSpec(memory_space=pltpu.SMEM)
+    if after:
+        specs[0] = pl.BlockSpec(memory_space=pl.ANY)
+    if hbm:
+        specs = [pl.BlockSpec(memory_space=pltpu.HBM)] * len(inputs)
     moved = sum(math.prod(x.shape) * 4 for x in inputs)
     return pl.pallas_call(
         kernel,
@@ -387,13 +418,17 @@
     wide = error_inverse.shape[-1]
     cells = rows * lon_cols
 
-    at_y, at_x = lax.axis_index("gy"), lax.axis_index("gx")
-    flags = jnp.stack([at_y * cols_x + at_x, at_y % 2, at_y == 0, at_y == rows_y - 1]).astype(jnp.int32)
     direction_n = to_native(direction)
     residual_n = to_native(residual)
     solution_n = to_native(solution)
-    lateral = jnp.stack([north_coef, east_coef, ocean.astype(jnp.float32)])[:, None]
-    own = jnp.concatenate([direction_n, to_native(lateral)], axis=0)
+    faces = [to_native(x[None, None]) for x in (north_coef, east_coef, ocean)]
+    own = call(
+        halo_kernel,
+        f32(direction_n.shape[0] + 3 * faces[0].shape[0], LANES),
+        (direction_n, *faces),
+        scratch=(pltpu.VMEM(faces[0].shape, jnp.int32), pltpu.SemaphoreType.DMA((4,))),
+        hbm=True,
+    )
     pair, cross = from_neighbours(own)
 
     matrix = error_inverse.reshape(1, wide, wide)
@@ -402,14 +437,12 @@
         functools.partial(prepare_kernel, device_count, capacity, lon_cols),
         (f32(3, layers, 8, LANES), f32(cells, device_count * capacity)),
         (
-            flags,
             vert_coef.reshape(layers, cells // LANES, LANES),
             obs_owner.reshape(1, obs_count),
             obs_row.reshape(1, obs_count),
             obs_col.reshape(1, obs_count),
             obs_frac.reshape(2, obs_count),
         ),
-        smem_first=True,
         flops=20_000_000,
         mib=16,
     )
@@ -418,24 +451,37 @@
     packed, coef, held_blocks = call(
         functools.partial(first_lateral_kernel, kv, rows, tiles, len(blocks)),
         (f32(cols_x, 2 * kv, LANES), f32(5, extended, lons), f32(len(blocks), wide, wide)),
-        (flags, own, pair, cross, *blocks),
+        (factors, own, pair, cross, *blocks),
         scratch=(
             pltpu.VMEM((3, extended, lons), jnp.float32),
             pltpu.VMEM(own.shape, jnp.float32),
             pltpu.VMEM(own.shape, jnp.float32),
         ),
-        smem_first=True,
+        after=True,
         flops=4_000_000,
     )
-    near = jnp.concatenate(
-        [held_blocks] + [apart_by(held_blocks, "gy", stride) for stride in range(1, rows_y)], axis=0
+    fetched = [held_blocks] + [apart_by(held_blocks, "gy", stride) for stride in range(1, rows_y)]
+    columns = lax.all_to_all(packed, "gx", split_axis=0, concat_axis=0, tiled=True)
+    columns = columns.reshape(cols_x * 2 * kv, LANES)
+    near = call(
+        functools.partial(join_kernel, len(fetched)),
+        f32(device_count // 2, wide, wide),
+        (columns, *fetched),
+        after=True,
     )
     far = apart_by(near, "gx", 1)
-    columns = lax.all_to_all(packed, "gx", split_axis=0, concat_axis=0, tiled=True)
+    profile = call(
+        functools.partial(profile_kernel, layers, held),
+        f32(wide, device_count * capacity),
+        (columns, factors, interp),
+        scratch=(pltpu.VMEM((2 * wide, LANES), jnp.float32),),
+        flops=400_000_000,
+        mib=16,
+    )
     spread = call(
-        functools.partial(observe_kernel, layers, held, capacity),
+        functools.partial(spread_kernel, layers, held, capacity),
         f32(cols_x * 2 * kv, LANES),
-        (columns.reshape(cols_x * 2 * kv, LANES), factors, interp, near, far),
+        (profile, factors, interp, near, far),
         scratch=(pltpu.VMEM((2 * wide, LANES), jnp.float32),),
         flops=1_000_000_000,
         mib=16,
@@ -447,9 +493,8 @@
     image, sums = call(
         functools.partial(second_lateral_kernel, kv, rows, tiles),
         (f32(*direction_n.shape), f32(device_count, 1, LANES)),
-        (flags, tile, pair, cross, coef, direction_n, residual_n),
+        (tile, pair, cross, coef, direction_n, residual_n),
         scratch=(pltpu.VMEM(tile.shape, jnp.float32), pltpu.VMEM(tile.shape, jnp.float32)),
-        smem_first=True,
         flops=4_000_000,
     )
     sums = lax.all_to_all(sums, ("gy", "gx"), split_axis=0, concat_axis=0, tiled=True)

time: 77 us -> 68.2 us (0.89)
  waiting for transfers between devices: 22.7 us -> 8.82 us
  blocking collectives: 19.3 us -> 30.3 us
  starting transfers between devices: 17.9 us -> 14.6 us
  Pallas kernels: 11.4 us -> 9.48 us
  other arithmetic: 1.74 us -> 0 us
  local copies, waits for them, and re-layouts: 2.65 us -> 3.8 us
    ppermute x7, waiting for transfers between devices: 14.8 us -> 3.1 us  [apart_by(): lax.ppermute(block, axis, [(i, i ^ stride) for i in range(lax.axis_size(a...]
    all_to_all x0 -> x1, blocking collectives: none -> 10.3 us  [per_device_gathered(): lax.all_to_all(packed, 'gx', split_axis=0, concat_axis=0, tiled=True)]
    all_to_all x1 -> x0, starting transfers between devices: 3.52 us -> none  [per_device_gathered(): lax.all_to_all(packed, 'gx', split_axis=0, concat_axis=0, tiled=True)]
    all_to_all x1 -> x0, waiting for transfers between devices: 2.2 us -> none  [per_device_gathered(): lax.all_to_all(packed, 'gx', split_axis=0, concat_axis=0, tiled=True)]
    pallas_call x5 -> x8, Pallas kernels: 11.4 us -> 9.48 us  [call(): pl.pallas_call(kernel, out_shape=out_shape, in_specs=specs, out_specs=tup...]
    unnamed x29 -> x26, local copies, waits for them, and re-layouts: 2.53 us -> 3.7 us
    concatenate x1 -> x0, other arithmetic: 0.95 us -> none  [per_device_gathered(): own = jnp.concatenate([direction_n, to_native(lateral)], axis=0)]
    another operation x3 -> x0, other arithmetic: 0.79 us -> none  [the longest x2 0.72 us: per_device_gathered(): jnp.stack([north_coef, east_coef, ocean.astype(jnp.float32)])[:, None]]
  transfers between devices with their start and end apart: 12 -> 11, of which waited for: 7 -> 4; matrix products, arithmetic and copies ran while one was open for 0% -> 0% of each run, Pallas kernels for 4% -> 5%
where the time goes in v3:
time: 68.2 us; the launch traced here: 67.7 us
  blocking collectives  30.3 us (44%)
  starting transfers between devices  14.6 us (21%)
  Pallas kernels  9.48 us (14%)
  waiting for transfers between devices  8.82 us (13%)
  local copies, waits for them, and re-layouts  3.8 us (6%)
  between operations  0.77 us (1%)
    all_to_all x1, blocking collectives, per_device_gathered(): lax.all_to_all(sums, ('gy', 'gx'), split_axis=0, concat_axis=0, tiled=True)  10.3 us
    all_to_all x1, blocking collectives, per_device_gathered(): lax.all_to_all(packed, 'gx', split_axis=0, concat_axis=0, tiled=True)  10.3 us
    all_to_all x1, blocking collectives, per_device_gathered(): lax.all_to_all(spread.reshape(cols_x, 2 * kv, LANES), 'gx', split_axis=0,...  9.74 us
    pallas_call x8, Pallas kernels, call(): pl.pallas_call(kernel, out_shape=out_shape, in_specs=specs, out_specs=tup...  9.48 us
    ppermute x7, starting transfers between devices, apart_by(): lax.ppermute(block, axis, [(i, i ^ stride) for i in range(lax.axis_size(a...  8.01 us
    ppermute x2, starting transfers between devices, from_neighbours(): lax.ppermute(block, 'gy', [(i, (i + (1 if i % 2 else -1)) % count) for i...  5.49 us
    ppermute x2, waiting for transfers between devices, from_neighbours(): lax.ppermute(block, 'gy', [(i, (i + (1 if i % 2 else -1)) % count) for i...  5.17 us
    unnamed x26, local copies, waits for them, and re-layouts  3.7 us
  transfers between devices with their start and end apart: 11, of which 4 were waited for; matrix products, arithmetic and copies ran while one was open for 0% of the time, Pallas kernels for 5%

profile of v3, /device:TPU:0, one launch (start us, length us, event | category | flops | bytes accessed | tf_op | source)
XLA Modules:
  0.0 67.7 jit_solution(9661369981275078233)
XLA Ops:
  0.6 0.0 copy-start
  0.6 0.9 %copy-done = f32[4,4,4,512]{3,2,1,0:T(4,128)S(1)} copy-done((f32[4,4,4,512]{3,2,1,0:T(4,128)S(1)}, f32[4,4,4,512]{3,2,1,0:T(4,128)}, u32[]{:S(2)}) %copy-start) | copy-done | bytes 131096
  1.5 0.0 copy-start.5
  1.5 0.7 %copy-done.5 = f32[4,512]{1,0:T(4,128)S(1)} copy-done((f32[4,512]{1,0:T(4,128)S(1)}, f32[4,512]{1,0:T(4,128)}, u32[]{:S(2)}) %copy-start.5) | copy-done | bytes 8216
  2.2 0.0 copy-start.6
  2.2 0.7 %copy-done.6 = f32[4,512]{1,0:T(4,128)S(1)} copy-done((f32[4,512]{1,0:T(4,128)S(1)}, f32[4,512]{1,0:T(4,128)}, u32[]{:S(2)}) %copy-start.6) | copy-done | bytes 8216
  2.9 0.0 copy-start.7
  2.9 0.7 %copy-done.7 = s32[4,512]{1,0:T(4,128)S(1)} copy-done((s32[4,512]{1,0:T(4,128)S(1)}, s32[4,512]{1,0:T(4,128)}, u32[]{:S(2)}) %copy-start.7) | copy-done | bytes 8216
  3.6 0.0 copy-start.4
  3.6 0.0 copy-start.12
  3.6 0.2 shard_map.140.own_ref
  3.9 4.0 %collective-permute-start.1 = (f32[304,128]{1,0:T(8,128)S(1)}, f32[304,128]{1,0:T(8,128)S(1)}, u32[]{:S(2)}, u32[]{:S(2)}) collective-permute-start(f32[304,128]{1,0:T(8,128)S(1)} %shard_map.140.own_ref), channel_id=1, source_target_pairs={{0,24},{8,16},{16,8},{24,0},{1,25},{9,17},{17,9},{25,1},{2,26},{10... | collective-permute-start | bytes 466952 | tf_op jit(solution)/shard_map/ppermute | solution.py:388
  7.8 0.5 collective-permute-start
  8.4 0.0 copy-done.4
  8.4 3.6 %collective-permute-start.4 = (f32[1,128,128]{2,1,0:T(8,128)S(1)}, f32[1,128,128]{2,1,0:T(8,128)S(1)}, u32[]{:S(2)}, u32[]{:S(2)}) collective-permute-start(f32[1,128,128]{2,1,0:T(8,128)S(1)} %bitcast.61), channel_id=1, source_target_pairs={{0,6},{1,7},{2,4},{3,5},{4,2},{5,3},{6,0},{7,1},{8,14},{9,15},{10,... | collective-permute-start | bytes 196616 | tf_op jit(solution)/shard_map/ppermute | solution.py:393
  12.0 0.0 collective-permute-start.3
  12.0 0.8 %collective-permute-start.2 = (f32[1,128,128]{2,1,0:T(8,128)S(1)}, f32[1,128,128]{2,1,0:T(8,128)S(1)}, u32[]{:S(2)}, u32[]{:S(2)}) collective-permute-start(f32[1,128,128]{2,1,0:T(8,128)S(1)} %bitcast.63), channel_id=1, source_target_pairs={{0,2},{1,3},{2,0},{3,1},{4,6},{5,7},{6,4},{7,5},{8,10},{9,11},{10,... | collective-permute-start | bytes 196616 | tf_op jit(solution)/shard_map/ppermute | solution.py:393
  12.8 0.0 copy-done.12
  12.8 0.0 copy-start.10
  12.8 0.0 copy-start.11
  12.8 0.1 reshape.75.vert_ref
  12.9 0.0 copy-start.8
  12.9 0.0 copy-start.9
  12.9 0.6 copy-done.10
  13.4 0.0 copy-done.11
  13.5 0.1 copy-done.8
  13.6 0.0 copy-done.9
  13.6 2.4 %shard_map.139 = (f32[3,32,8,128]{3,2,1,0:T(8,128)S(1)}, f32[256,1024]{1,0:T(8,128)S(1)}) custom-call(f32[32,2,128]{2,1,0:T(2,128)S(1)} %reshape.75.vert_ref, s32[1,512]{1,0:T(1,128)S(1)} %bitcast.69, s32[1,512]{1,0:T(1,128)S(1)} %bitcast.70, s32[1,512]{1,0:T(1,128)S(1)} %bitcast.71, f32[2,512]{1,0:T(2,128)S(1)} %bitcast.68), custom_call_target="tpu_custom_call" | custom-call | flops 20000000 | bytes 43008 | tf_op jit(solution)/shard_map/pallas_call | solution.py:370
  16.0 0.0 collective-permute-done.4.refs_3_
  16.0 1.3 %collective-permute-done.3.refs_2_ = f32[1,128,128]{2,1,0:T(8,128)S(1)} collective-permute-done((f32[1,128,128]{2,1,0:T(8,128)S(1)}, f32[1,128,128]{2,1,0:T(8,128)S(1)}, u32[]{:S(2)}, u32[]{:S(2)}) %collective-permute-start.3) | collective-permute-done | bytes 65568 | tf_op jit(solution)/shard_map/ppermute | solution.py:393
  17.2 0.0 collective-permute-done.2.refs_1_
  17.2 0.0 collective-permute-done.1.cross_ref
  17.2 0.0 collective-permute-done.pair_ref
  17.2 0.9 %shard_map.141 = (f32[8,32,128]{2,1,0:T(8,128)S(1)}, f32[5,16,512]{2,1,0:T(8,128)S(1)}, f32[4,128,128]{2,1,0:T(8,128)S(1)}) custom-call(f32[3,32,8,128]{3,2,1,0:T(8,128)S(1)} %get-tuple-element.13._.factor_ref, f32[304,128]{1,0:T(8,128)S(1)} %shard_map.140.own_ref, f32[304,128]{1,0:T(8,128)S(1)} %collective-permute-done.pair_ref, ...), custom_call_target="tpu_custom_call" | custom-call | flops 4000000 | bytes 1122304 | tf_op jit(solution)/shard_map/pallas_call | solution.py:370
  18.2 1.5 %collective-permute-start.7 = (f32[4,128,128]{2,1,0:T(8,128)S(1)}, f32[4,128,128]{2,1,0:T(8,128)S(1)}, u32[]{:S(2)}, u32[]{:S(2)}) collective-permute-start(f32[4,128,128]{2,1,0:T(8,128)S(1)} %get-tuple-element.16.refs_0_), channel_id=1, source_target_pairs={{0,24},{8,16},{16,8},{24,0},{1,25},{9,17},{17,9},{25,1},{2,26},{10... | collective-permute-start | bytes 786440 | tf_op jit(solution)/shard_map/ppermute | solution.py:393
  19.7 1.5 %collective-permute-start.6 = (f32[4,128,128]{2,1,0:T(8,128)S(1)}, f32[4,128,128]{2,1,0:T(8,128)S(1)}, u32[]{:S(2)}, u32[]{:S(2)}) collective-permute-start(f32[4,128,128]{2,1,0:T(8,128)S(1)} %get-tuple-element.16.refs_0_), channel_id=1, source_target_pairs={{0,16},{8,24},{16,0},{24,8},{1,17},{9,25},{17,1},{25,9},{2,18},{10... | collective-permute-start | bytes 786440 | tf_op jit(solution)/shard_map/ppermute | solution.py:393
  21.2 0.5 collective-permute-start.5
  21.7 10.3 %all_to_all.15 = f32[8,32,128]{2,1,0:T(8,128)S(1)} all-to-all(f32[8,32,128]{2,1,0:T(8,128)S(1)} %get-tuple-element.14), channel_id=1, replica_groups=mesh['gy'=4,'gx'=8] {'gx'}, dimensions={0} | all-to-all | bytes 262144 | tf_op jit(solution)/shard_map/all_to_all | solution.py:464
  32.0 0.0 collective-permute-done.7.refs_3_
  32.0 0.0 collective-permute-done.6.refs_2_
  32.0 0.0 collective-permute-done.5.refs_1_
  32.0 0.1 shard_map.143.near_ref
  32.1 0.1 collective-permute-start.8
  32.2 0.8 %shard_map.142.profile_ref = f32[128,1024]{1,0:T(8,128)S(1)} custom-call(f32[256,128]{1,0:T(8,128)S(1)} %bitcast.53, f32[3,32,8,128]{3,2,1,0:T(8,128)S(1)} %get-tuple-element.13._.factor_ref, f32[256,1024]{1,0:T(8,128)S(1)} %get-tuple-element.15.interp_ref), custom_call_target="tpu_custom_call" | custom-call | flops 400000000 | bytes 1572864 | tf_op jit(solution)/shard_map/pallas_call | solution.py:370
  33.0 1.8 %collective-permute-done.8.far_ref = f32[16,128,128]{2,1,0:T(8,128)S(1)} collective-permute-done((f32[16,128,128]{2,1,0:T(8,128)S(1)}, f32[16,128,128]{2,1,0:T(8,128)S(1)}, u32[]{:S(2)}, u32[]{:S(2)}) %collective-permute-start.8) | collective-permute-done | bytes 1048608 | tf_op jit(solution)/shard_map/ppermute | solution.py:393
  34.8 3.2 %shard_map.144 = f32[256,128]{1,0:T(8,128)S(1)} custom-call(f32[128,1024]{1,0:T(8,128)S(1)} %shard_map.142.profile_ref, f32[3,32,8,128]{3,2,1,0:T(8,128)S(1)} %get-tuple-element.13._.factor_ref, f32[256,1024]{1,0:T(8,128)S(1)} %get-tuple-element.15.interp_ref, f32[16,128,128]{2,1,0:T(8,128)S(1)} %shard_map.143.near_ref, ...), custom_call_target="tpu_custom_call" | custom-call | flops 1000000000 | bytes 4063232 | tf_op jit(solution)/shard_map/pallas_call | solution.py:370
  38.0 0.0 copy-start.1
  38.0 0.0 copy-start.2
  38.0 9.7 %all_to_all.16.own_ref = f32[8,32,128]{2,1,0:T(8,128)S(1)} all-to-all(f32[8,32,128]{2,1,0:T(8,128)S(1)} %bitcast.57), channel_id=1, replica_groups=mesh['gy'=4,'gx'=8] {'gx'}, dimensions={0} | all-to-all | bytes 262144 | tf_op jit(solution)/shard_map/all_to_all | solution.py:489
  47.8 1.5 %collective-permute-start.10 = (f32[8,32,128]{2,1,0:T(8,128)S(1)}, f32[8,32,128]{2,1,0:T(8,128)S(1)}, u32[]{:S(2)}, u32[]{:S(2)}) collective-permute-start(f32[8,32,128]{2,1,0:T(8,128)S(1)} %all_to_all.16.own_ref), channel_id=1, source_target_pairs={{0,24},{8,16},{16,8},{24,0},{1,25},{9,17},{17,9},{25,1},{2,26},{10... | collective-permute-start | bytes 393224 | tf_op jit(solution)/shard_map/ppermute | solution.py:388
  49.3 0.5 collective-permute-start.9
  49.9 5.2 %collective-permute-done.10.cross_ref = f32[8,32,128]{2,1,0:T(8,128)S(1)} collective-permute-done((f32[8,32,128]{2,1,0:T(8,128)S(1)}, f32[8,32,128]{2,1,0:T(8,128)S(1)}, u32[]{:S(2)}, u32[]{:S(2)}) %collective-permute-start.10) | collective-permute-done | bytes 131104 | tf_op jit(solution)/shard_map/ppermute | solution.py:388
  55.0 0.5 collective-permute-done.9.pair_ref
  55.6 0.0 copy-done.1
  55.6 0.0 copy-done.2
  55.6 0.0 copy-start.3
  55.6 1.0 %shard_map.145 = (f32[256,128]{1,0:T(8,128)S(1)}, f32[32,1,128]{2,1,0:T(1,128)S(1)}) custom-call(f32[8,32,128]{2,1,0:T(8,128)S(1)} %all_to_all.16.own_ref, f32[8,32,128]{2,1,0:T(8,128)S(1)} %collective-permute-done.9.pair_ref, f32[8,32,128]{2,1,0:T(8,128)S(1)} %collective-permute-done.10.cross_ref, f32[5,16,512]{2,1,0:T(8,128)S(1)} %get-tuple-element.17.coef_ref, ...), custom_call_target="tpu_custom_call" | custom-call | flops 4000000 | bytes 819200 | tf_op jit(solution)/shard_map/pallas_call | solution.py:370
  56.6 10.3 %all_to_all.17.sums_ref = f32[32,1,128]{2,1,0:T(1,128)S(1)} all-to-all(f32[32,1,128]{2,1,0:T(1,128)S(1)} %get-tuple-element.18), channel_id=1, replica_groups=mesh['gy'=4,'gx'=8] {'gy','gx'}, dimensions={0} | all-to-all | bytes 32768 | tf_op jit(solution)/shard_map/all_to_all | solution.py:500
  66.8 0.0 copy-done.3
  66.8 0.9 %shard_map.146 = (f32[256,128]{1,0:T(8,128)}, f32[256,128]{1,0:T(8,128)}, f32[256,128]{1,0:T(8,128)}) custom-call(f32[32,1,128]{2,1,0:T(1,128)S(1)} %all_to_all.17.sums_ref, f32[256,128]{1,0:T(8,128)S(1)} %bitcast.56, f32[256,128]{1,0:T(8,128)S(1)} %bitcast.60, f32[256,128]{1,0:T(8,128)S(1)} %bitcast.59, f32[256,128]{1,0:T(8,128)S(1)} %get-tuple-element.19.image_ref), custom_call_target="tpu_custom_call" | custom-call | flops 1000000 | bytes 540672 | tf_op jit(solution)/shard_map/pallas_call | solution.py:370
Async XLA Ops:
  0.6 0.9 %copy-start = (f32[4,4,4,512]{3,2,1,0:T(4,128)S(1)}, f32[4,4,4,512]{3,2,1,0:T(4,128)}, u32[]{:S(2)}) copy-start(f32[4,4,4,512]{3,2,1,0:T(4,128)} %param.12) | copy-start | bytes 393220
  1.5 0.7 %copy-start.5 = (f32[4,512]{1,0:T(4,128)S(1)}, f32[4,512]{1,0:T(4,128)}, u32[]{:S(2)}) copy-start(f32[4,512]{1,0:T(4,128)} %param.15) | copy-start | bytes 24580
  2.2 0.7 %copy-start.6 = (f32[4,512]{1,0:T(4,128)S(1)}, f32[4,512]{1,0:T(4,128)}, u32[]{:S(2)}) copy-start(f32[4,512]{1,0:T(4,128)} %param.16) | copy-start | bytes 24580
  2.9 0.7 %copy-start.7 = (s32[4,512]{1,0:T(4,128)S(1)}, s32[4,512]{1,0:T(4,128)}, u32[]{:S(2)}) copy-start(s32[4,512]{1,0:T(4,128)} %param.17) | copy-start | bytes 24580
  3.6 4.7 %copy-start.4 = (f32[1,1,128,128]{3,2,1,0:T(8,128)S(1)}, f32[1,1,128,128]{3,2,1,0:T(8,128)}, u32[]{:S(2)}) copy-start(f32[1,1,128,128]{3,2,1,0:T(8,128)} %param.23) | copy-start | bytes 196612
  3.6 9.1 %copy-start.12 = (f32[32,4,64]{2,1,0:T(4,128)S(1)}, f32[32,4,64]{2,1,0:T(4,128)}, u32[]{:S(2)}) copy-start(f32[32,4,64]{2,1,0:T(4,128)} %param.18) | copy-start | bytes 98308
  3.9 13.4 %collective-permute-start.1 = (f32[304,128]{1,0:T(8,128)S(1)}, f32[304,128]{1,0:T(8,128)S(1)}, u32[]{:S(2)}, u32[]{:S(2)}) collective-permute-start(f32[304,128]{1,0:T(8,128)S(1)} %shard_map.140.own_ref), channel_id=1, source_target_pairs={{0,24},{8,16},{16,8},{24,0},{1,25},{9,17},{17,9},{25,1},{2,26},{10... | collective-permute-start | bytes 466952 | tf_op jit(solution)/shard_map/ppermute | solution.py:388
  7.8 9.4 %collective-permute-start = (f32[304,128]{1,0:T(8,128)S(1)}, f32[304,128]{1,0:T(8,128)S(1)}, u32[]{:S(2)}, u32[]{:S(2)}) collective-permute-start(f32[304,128]{1,0:T(8,128)S(1)} %shard_map.140.own_ref), channel_id=1, source_target_pairs={{0,8},{8,0},{16,24},{24,16},{1,9},{9,1},{17,25},{25,17},{2,10},{10... | collective-permute-start | bytes 466952 | tf_op jit(solution)/shard_map/ppermute | solution.py:387
  8.4 7.6 %collective-permute-start.4 = (f32[1,128,128]{2,1,0:T(8,128)S(1)}, f32[1,128,128]{2,1,0:T(8,128)S(1)}, u32[]{:S(2)}, u32[]{:S(2)}) collective-permute-start(f32[1,128,128]{2,1,0:T(8,128)S(1)} %bitcast.61), channel_id=1, source_target_pairs={{0,6},{1,7},{2,4},{3,5},{4,2},{5,3},{6,0},{7,1},{8,14},{9,15},{10,... | collective-permute-start | bytes 196616 | tf_op jit(solution)/shard_map/ppermute | solution.py:393
  12.0 5.2 %collective-permute-start.3 = (f32[1,128,128]{2,1,0:T(8,128)S(1)}, f32[1,128,128]{2,1,0:T(8,128)S(1)}, u32[]{:S(2)}, u32[]{:S(2)}) collective-permute-start(f32[1,128,128]{2,1,0:T(8,128)S(1)} %bitcast.62), channel_id=1, source_target_pairs={{0,4},{1,5},{2,6},{3,7},{4,0},{5,1},{6,2},{7,3},{8,12},{9,13},{10,... | collective-permute-start | bytes 196616 | tf_op jit(solution)/shard_map/ppermute | solution.py:393
  12.0 5.2 %collective-permute-start.2 = (f32[1,128,128]{2,1,0:T(8,128)S(1)}, f32[1,128,128]{2,1,0:T(8,128)S(1)}, u32[]{:S(2)}, u32[]{:S(2)}) collective-permute-start(f32[1,128,128]{2,1,0:T(8,128)S(1)} %bitcast.63), channel_id=1, source_target_pairs={{0,2},{1,3},{2,0},{3,1},{4,6},{5,7},{6,4},{7,5},{8,10},{9,11},{10,... | collective-permute-start | bytes 196616 | tf_op jit(solution)/shard_map/ppermute | solution.py:393
  12.8 0.7 %copy-start.10 = (s32[1,1,512]{2,1,0:T(1,128)S(1)}, s32[1,1,512]{2,1,0:T(1,128)}, u32[]{:S(2)}) copy-start(s32[1,1,512]{2,1,0:T(1,128)} %param.20) | copy-start | bytes 6148
  12.8 0.7 %copy-start.11 = (s32[1,1,512]{2,1,0:T(1,128)S(1)}, s32[1,1,512]{2,1,0:T(1,128)}, u32[]{:S(2)}) copy-start(s32[1,1,512]{2,1,0:T(1,128)} %param.21) | copy-start | bytes 6148
  12.9 0.7 %copy-start.8 = (f32[1,1,2,512]{3,2,1,0:T(2,128)S(1)}, f32[1,1,2,512]{3,2,1,0:T(2,128)}, u32[]{:S(2)}) copy-start(f32[1,1,2,512]{3,2,1,0:T(2,128)} %param.22) | copy-start | bytes 12292
  12.9 0.7 %copy-start.9 = (s32[1,1,512,1]{2,3,1,0:T(1,128)S(1)}, s32[1,1,512,1]{2,3,1,0:T(1,128)}, u32[]{:S(2)}) copy-start(s32[1,1,512,1]{2,3,1,0:T(1,128)} %param.19) | copy-start | bytes 6148
  18.2 13.8 %collective-permute-start.7 = (f32[4,128,128]{2,1,0:T(8,128)S(1)}, f32[4,128,128]{2,1,0:T(8,128)S(1)}, u32[]{:S(2)}, u32[]{:S(2)}) collective-permute-start(f32[4,128,128]{2,1,0:T(8,128)S(1)} %get-tuple-element.16.refs_0_), channel_id=1, source_target_pairs={{0,24},{8,16},{16,8},{24,0},{1,25},{9,17},{17,9},{25,1},{2,26},{10... | collective-permute-start | bytes 786440 | tf_op jit(solution)/shard_map/ppermute | solution.py:393
  19.7 12.3 %collective-permute-start.6 = (f32[4,128,128]{2,1,0:T(8,128)S(1)}, f32[4,128,128]{2,1,0:T(8,128)S(1)}, u32[]{:S(2)}, u32[]{:S(2)}) collective-permute-start(f32[4,128,128]{2,1,0:T(8,128)S(1)} %get-tuple-element.16.refs_0_), channel_id=1, source_target_pairs={{0,16},{8,24},{16,0},{24,8},{1,17},{9,25},{17,1},{25,9},{2,18},{10... | collective-permute-start | bytes 786440 | tf_op jit(solution)/shard_map/ppermute | solution.py:393
  21.2 10.8 %collective-permute-start.5 = (f32[4,128,128]{2,1,0:T(8,128)S(1)}, f32[4,128,128]{2,1,0:T(8,128)S(1)}, u32[]{:S(2)}, u32[]{:S(2)}) collective-permute-start(f32[4,128,128]{2,1,0:T(8,128)S(1)} %get-tuple-element.16.refs_0_), channel_id=1, source_target_pairs={{0,8},{8,0},{16,24},{24,16},{1,9},{9,1},{17,25},{25,17},{2,10},{10... | collective-permute-start | bytes 786440 | tf_op jit(solution)/shard_map/ppermute | solution.py:393
  32.1 2.7 %collective-permute-start.8 = (f32[16,128,128]{2,1,0:T(8,128)S(1)}, f32[16,128,128]{2,1,0:T(8,128)S(1)}, u32[]{:S(2)}, u32[]{:S(2)}) collective-permute-start(f32[16,128,128]{2,1,0:T(8,128)S(1)} %shard_map.143.near_ref), channel_id=1, source_target_pairs={{0,1},{1,0},{2,3},{3,2},{4,5},{5,4},{6,7},{7,6},{8,9},{9,8},{10,11... | collective-permute-start | bytes 3145736 | tf_op jit(solution)/shard_map/ppermute | solution.py:393
  38.0 17.5 %copy-start.1 = (f32[4,4,4,512]{3,2,1,0:T(4,128)S(1)}, f32[4,4,4,512]{3,2,1,0:T(4,128)}, u32[]{:S(2)}) copy-start(f32[4,4,4,512]{3,2,1,0:T(4,128)} %param.12) | copy-start | bytes 393220
  38.0 17.5 %copy-start.2 = (f32[4,4,4,512]{3,2,1,0:T(4,128)S(1)}, f32[4,4,4,512]{3,2,1,0:T(4,128)}, u32[]{:S(2)}) copy-start(f32[4,4,4,512]{3,2,1,0:T(4,128)} %param.14) | copy-start | bytes 393220
  47.8 7.2 %collective-permute-start.10 = (f32[8,32,128]{2,1,0:T(8,128)S(1)}, f32[8,32,128]{2,1,0:T(8,128)S(1)}, u32[]{:S(2)}, u32[]{:S(2)}) collective-permute-start(f32[8,32,128]{2,1,0:T(8,128)S(1)} %all_to_all.16.own_ref), channel_id=1, source_target_pairs={{0,24},{8,16},{16,8},{24,0},{1,25},{9,17},{17,9},{25,1},{2,26},{10... | collective-permute-start | bytes 393224 | tf_op jit(solution)/shard_map/ppermute | solution.py:388
  49.3 6.3 %collective-permute-start.9 = (f32[8,32,128]{2,1,0:T(8,128)S(1)}, f32[8,32,128]{2,1,0:T(8,128)S(1)}, u32[]{:S(2)}, u32[]{:S(2)}) collective-permute-start(f32[8,32,128]{2,1,0:T(8,128)S(1)} %all_to_all.16.own_ref), channel_id=1, source_target_pairs={{0,8},{8,0},{16,24},{24,16},{1,9},{9,1},{17,25},{25,17},{2,10},{10... | collective-permute-start | bytes 393224 | tf_op jit(solution)/shard_map/ppermute | solution.py:387
  55.6 11.3 %copy-start.3 = (f32[4,4,4,512]{3,2,1,0:T(4,128)S(1)}, f32[4,4,4,512]{3,2,1,0:T(4,128)}, u32[]{:S(2)}) copy-start(f32[4,4,4,512]{3,2,1,0:T(4,128)} %param.13) | copy-start | bytes 393220

commit v4 on v3

--- a/solution.py
+++ b/solution.py
@@ -10,7 +10,6 @@
 
 NSTEP = 4
 LANES = 128
-HIGHEST = lax.Precision.HIGHEST
 
 
 def to_native(tile):
@@ -92,14 +91,16 @@
     own_ref[cells + 2 * size : cells + 3 * size, :] = mask_ref[...].astype(jnp.float32)
 
 
-def join_kernel(count, _, *refs):
+def join_kernel(count, _, __, *refs):
     blocks, (near_ref,) = refs[:count], refs[count:]
     size = blocks[0].shape[0]
     for at, block in enumerate(blocks):
         near_ref[at * size : (at + 1) * size] = block[...]
 
 
-def first_lateral_kernel(kv, rows, tiles, count, _, own_ref, pair_ref, cross_ref, *refs):
+def first_lateral_kernel(
+    kv, rows, tiles, count, own_ref, north_ref, east_ref, ocean_ref, pair_ref, cross_ref, *refs
+):
     blocks, (packed_ref, coef_ref, held_ref, ext_ref, low_ref, high_ref) = refs[:count], refs[count:]
     lons = tiles * LANES
     cells = kv * tiles * rows
@@ -107,13 +108,13 @@
         held_ref[at] = block[0]
     sort_halo(pair_ref, cross_ref, low_ref, high_ref)
     ext_ref[...] = jnp.zeros_like(ext_ref)
-    for kind in range(3):
-        for block, ref in enumerate((low_ref, own_ref, high_ref)):
-            for tile in range(tiles):
-                start = cells + (kind * tiles + tile) * rows
-                ext_ref[kind, block * rows : (block + 1) * rows, tile * LANES : (tile + 1) * LANES] = ref[
-                    start : start + rows, :
-                ]
+    for kind, kept in enumerate((north_ref, east_ref, ocean_ref)):
+        for tile in range(tiles):
+            lanes = slice(tile * LANES, (tile + 1) * LANES)
+            start = cells + (kind * tiles + tile) * rows
+            ext_ref[kind, 0:rows, lanes] = low_ref[start : start + rows, :]
+            ext_ref[kind, rows : 2 * rows, lanes] = kept[tile * rows : (tile + 1) * rows, :].astype(jnp.float32)
+            ext_ref[kind, 2 * rows : 3 * rows, lanes] = high_ref[start : start + rows, :]
     total = ext_ref.shape[1]
     north, east, ocean = ext_ref[0], ext_ref[1], ext_ref[2]
     north_face = north * ocean * pltpu.roll(ocean, total - 1, 0)
@@ -216,44 +217,40 @@
     dir_ref[...] = residual_next + beta * direction
 
 
+def split(value):
+    high = value.astype(jnp.bfloat16)
+    return high, (value - high.astype(jnp.float32)).astype(jnp.bfloat16)
+
+
+def dot_parts(left, right, contract):
+    dims = (contract, ((), ()))
+    total = lax.dot_general(left[0], right[0], dims, preferred_element_type=jnp.float32)
+    total = total + lax.dot_general(left[0], right[1], dims, preferred_element_type=jnp.float32)
+    return total + lax.dot_general(left[1], right[0], dims, preferred_element_type=jnp.float32)
+
+
 def prepare_kernel(
-    devices, capacity, lon_cols, vert_ref, owner_ref, row_ref, col_ref, frac_ref, factor_ref, interp_ref
+    devices, capacity, lon_cols, _, owner_ref, row_ref, col_ref, frac_ref, high_ref, low_ref
 ):
-    layers = vert_ref.shape[0]
-    top = lax.broadcasted_iota(jnp.int32, (8, LANES), 0) < 4
-    coef = [
-        jnp.where(top, vert_ref[layer, 0:1, :], vert_ref[layer, 1:2, :]) for layer in range(layers)
-    ]
-    ratio = None
-    for layer in range(layers):
-        diagonal = 1.0 + coef[layer]
-        if layer > 0:
-            diagonal = diagonal + coef[layer - 1] - coef[layer - 1] * ratio
-        inverse = 1.0 / diagonal
-        ratio = coef[layer] * inverse
-        factor_ref[0, layer] = inverse
-        factor_ref[1, layer] = coef[layer - 1] * inverse if layer > 0 else jnp.zeros_like(inverse)
-        factor_ref[2, layer] = ratio
     count = owner_ref.shape[1]
     slots = devices * capacity
     me = lax.axis_index("gy") * lax.axis_size("gx") + lax.axis_index("gx")
     apart = jnp.bitwise_xor(owner_ref[...], me)
     place = jnp.bitwise_and(apart, 1) * (devices // 2) + jnp.right_shift(apart, 1)
-    named = jnp.where(
-        lax.broadcasted_iota(jnp.int32, (devices, count), 0) == place, 1.0, 0.0
-    )
-    before = jnp.where(
-        lax.broadcasted_iota(jnp.int32, (count, count), 0)
-        <= lax.broadcasted_iota(jnp.int32, (count, count), 1),
-        1.0,
-        0.0,
-    )
-    running = jnp.dot(named, before, preferred_element_type=jnp.float32)
-    rank = jnp.sum(named * running, axis=0, keepdims=True) - 1.0
+    named = lax.broadcasted_iota(jnp.int32, (devices, count), 0) == place
+    before = lax.broadcasted_iota(jnp.int32, (count, count), 0) <= lax.broadcasted_iota(
+        jnp.int32, (count, count), 1
+    )
+    running = jnp.dot(
+        jnp.where(named, 1.0, 0.0).astype(jnp.bfloat16),
+        jnp.where(before, 1.0, 0.0).astype(jnp.bfloat16),
+        preferred_element_type=jnp.float32,
+    )
+    rank = jnp.sum(jnp.where(named, running, 0.0), axis=0, keepdims=True) - 1.0
     slot = place * capacity + rank.astype(jnp.int32)
     chosen = jnp.where(
         lax.broadcasted_iota(jnp.int32, (slots, count), 0) == slot, 1.0, 0.0
-    )
+    ).astype(jnp.bfloat16)
     lat_frac = frac_ref[0:1, :]
     lon_frac = frac_ref[1:2, :]
     cell = (row_ref[...] * lon_cols + col_ref[...]).astype(jnp.float32)
@@ -268,13 +265,16 @@
         ],
         axis=0,
     )
+    high, rest = split(values)
+    low, rest = split(values - high.astype(jnp.float32))
+    parts = jnp.concatenate([high.astype(jnp.float32), low.astype(jnp.float32), rest.astype(jnp.float32)], axis=0)
     placed = lax.dot_general(
-        values, chosen, (((1,), (1,)), ((), ())), precision=HIGHEST, preferred_element_type=jnp.float32
-    )
+        parts.astype(jnp.bfloat16), chosen, (((1,), (1,)), ((), ())), preferred_element_type=jnp.float32
+    )
+    placed = placed[0:8] + placed[8:16] + placed[16:24]
     first = jnp.round(placed[4:5, :]).astype(jnp.int32)
-    index = lax.broadcasted_iota(jnp.int32, interp_ref.shape, 0)
-    away = index - first
-    interp_ref[...] = jnp.where(
+    away = lax.broadcasted_iota(jnp.int32, high_ref.shape, 0) - first
+    interp = jnp.where(
         away == 0,
         placed[0:1, :],
         jnp.where(
@@ -283,6 +283,23 @@
             jnp.where(away == lon_cols, placed[2:3, :], jnp.where(away == lon_cols + 1, placed[3:4, :], 0.0)),
         ),
     )
+    high_ref[...], low_ref[...] = split(interp)
+
+
+def vertical_factors_kernel(vert_ref, factor_ref):
+    layers = vert_ref.shape[0]
+    top = lax.broadcasted_iota(jnp.int32, (8, LANES), 0) < 4
+    coef = [jnp.where(top, vert_ref[layer, 0:1, :], vert_ref[layer, 1:2, :]) for layer in range(layers)]
+    ratio = None
+    for layer in range(layers):
+        diagonal = 1.0 + coef[layer]
+        if layer > 0:
+            diagonal = diagonal + coef[layer - 1] - coef[layer - 1] * ratio
+        inverse = 1.0 / diagonal
+        ratio = coef[layer] * inverse
+        factor_ref[0, layer] = inverse
+        factor_ref[1, layer] = coef[layer - 1] * inverse if layer > 0 else jnp.zeros_like(inverse)
+        factor_ref[2, layer] = ratio
 
 
 def solve_columns(read, write, factor_ref, layers):
@@ -303,8 +320,36 @@
     return pl.ds((layer // held) * 8 * held + layer % held, 8, stride=held)
 
 
-def profile_kernel(layers, held, packed_ref, factor_ref, interp_ref, profile_ref, column_ref):
+def weigh(profile, matrix_ref, capacity):
+    kv = matrix_ref.shape[1]
+    owners = LANES // capacity
+    mine = lax.broadcasted_iota(jnp.int32, (kv, LANES), 1) // capacity
+    tiles = []
+    for tile in range(matrix_ref.shape[0] // owners):
+        values = profile[:, tile * LANES : (tile + 1) * LANES]
+        masked = jnp.concatenate([jnp.where(mine == owner, values, 0.0) for owner in range(owners)], axis=0)
+        matrices = jnp.concatenate([matrix_ref[tile * owners + owner] for owner in range(owners)], axis=1)
+        tiles.append(dot_parts(split(matrices), split(masked), ((1,), (0,))))
+    return jnp.concatenate(tiles, axis=1)
+
+
+def profile_kernel(
+    layers,
+    held,
+    capacity,
+    packed_ref,
+    vert_ref,
+    high_ref,
+    low_ref,
+    near_ref,
+    weighted_ref,
+    profile_ref,
+    factor_ref,
+    column_ref,
+):
     kv = profile_ref.shape[0]
+    half = profile_ref.shape[1]
+    vertical_factors_kernel(vert_ref, factor_ref)
 
     def read(layer):
         return packed_ref[packed_at(layer, held), :]
@@ -314,36 +359,17 @@
 
     solve_columns(read, write, factor_ref, layers)
     columns = jnp.concatenate([column_ref[0:kv, :], column_ref[kv : 2 * kv, :]], axis=1)
-    profile_ref[...] = jnp.dot(
-        columns, interp_ref[...], precision=HIGHEST, preferred_element_type=jnp.float32
-    )
+    profile = dot_parts(split(columns), (high_ref[...], low_ref[...]), ((1,), (0,)))
+    profile_ref[...] = profile[:, half:]
+    weighted_ref[...] = weigh(profile[:, :half], near_ref, capacity)
 
 
 def spread_kernel(
-    layers, held, capacity, profile_ref, factor_ref, interp_ref, near_ref, far_ref, out_ref, column_ref
+    layers, held, capacity, near_ref, profile_ref, factor_ref, high_ref, low_ref, far_ref, out_ref, column_ref
 ):
-    kv = near_ref.shape[1]
-    owners = LANES // capacity
-    mine = lax.broadcasted_iota(jnp.int32, (kv, LANES), 1) // capacity
-    near = near_ref.shape[0]
-    parts = []
-    for tile in range(profile_ref.shape[1] // LANES):
-        values = profile_ref[:, tile * LANES : (tile + 1) * LANES]
-        first = tile * owners
-        ref, at = (near_ref, first) if first < near else (far_ref, first - near)
-        matrices = ref[at : at + owners].reshape(owners * kv, kv)
-        product = jnp.dot(matrices, values, precision=HIGHEST, preferred_element_type=jnp.float32)
-        kept = product[0:kv]
-        for owner in range(1, owners):
-            kept = jnp.where(mine == owner, product[owner * kv : (owner + 1) * kv], kept)
-        parts.append(kept)
-    spread = lax.dot_general(
-        jnp.concatenate(parts, axis=1),
-        interp_ref[...],
-        (((1,), (1,)), ((), ())),
-        precision=HIGHEST,
-        preferred_element_type=jnp.float32,
-    )
+    kv = near_ref.shape[0]
+    weighted = jnp.concatenate([near_ref[...], weigh(profile_ref[...], far_ref, capacity)], axis=1)
+    spread = dot_parts(split(weighted), (high_ref[...], low_ref[...]), ((1,), (1,)))
     column_ref[0:kv, :] = spread[:, :LANES]
     column_ref[kv : 2 * kv, :] = spread[:, LANES:]
 
@@ -360,10 +386,8 @@
     return [pl.BlockSpec(memory_space=pltpu.VMEM)] * count
 
 
-def call(kernel, out_shape, inputs, scratch=(), after=False, hbm=False, flops=1_000_000, mib=8):
-    specs = vmem(len(inputs))
-    if after:
-        specs[0] = pl.BlockSpec(memory_space=pl.ANY)
+def call(kernel, out_shape, inputs, scratch=(), after=0, hbm=False, flops=1_000_000, mib=8):
+    specs = [pl.BlockSpec(memory_space=pl.ANY)] * after + vmem(len(inputs) - after)
     if hbm:
         specs = [pl.BlockSpec(memory_space=pltpu.HBM)] * len(inputs)
     moved = sum(math.prod(x.shape) * 4 for x in inputs)
@@ -428,37 +452,38 @@
         (direction_n, *faces),
         scratch=(pltpu.VMEM(faces[0].shape, jnp.int32), pltpu.SemaphoreType.DMA((4,))),
         hbm=True,
+        mib=56,
     )
     pair, cross = from_neighbours(own)
 
     matrix = error_inverse.reshape(1, wide, wide)
     blocks = [matrix] + [apart_by(matrix, "gx", stride) for stride in range(2, cols_x, 2)]
-    factors, interp = call(
+    extended = 3 * rows + (-3 * rows) % 8
+    packed, coef, held_blocks = call(
+        functools.partial(first_lateral_kernel, kv, rows, tiles, len(blocks)),
+        (f32(cols_x, 2 * kv, LANES), f32(5, extended, lons), f32(len(blocks), wide, wide)),
+        (direction_n, *faces, pair, cross, *blocks),
+        scratch=(
+            pltpu.VMEM((3, extended, lons), jnp.float32),
+            pltpu.VMEM(own.shape, jnp.float32),
+            pltpu.VMEM(own.shape, jnp.float32),
+        ),
+        flops=4_000_000,
+    )
+    halves = jax.ShapeDtypeStruct((cells, device_count * capacity), jnp.bfloat16)
+    interp = call(
         functools.partial(prepare_kernel, device_count, capacity, lon_cols),
-        (f32(3, layers, 8, LANES), f32(cells, device_count * capacity)),
+        (halves, halves),
         (
-            vert_coef.reshape(layers, cells // LANES, LANES),
+            packed,
             obs_owner.reshape(1, obs_count),
             obs_row.reshape(1, obs_count),
             obs_col.reshape(1, obs_count),
             obs_frac.reshape(2, obs_count),
         ),
+        after=1,
         flops=20_000_000,
         mib=16,
-    )
-
-    extended = 3 * rows + (-3 * rows) % 8
-    packed, coef, held_blocks = call(
-        functools.partial(first_lateral_kernel, kv, rows, tiles, len(blocks)),
-        (f32(cols_x, 2 * kv, LANES), f32(5, extended, lons), f32(len(blocks), wide, wide)),
-        (factors, own, pair, cross, *blocks),
-        scratch=(
-            pltpu.VMEM((3, extended, lons), jnp.float32),
-            pltpu.VMEM(own.shape, jnp.float32),
-            pltpu.VMEM(own.shape, jnp.float32),
-        ),
-        after=True,
-        flops=4_000_000,
     )
     fetched = [held_blocks] + [apart_by(held_blocks, "gy", stride) for stride in range(1, rows_y)]
     columns = lax.all_to_all(packed, "gx", split_axis=0, concat_axis=0, tiled=True)
@@ -466,14 +491,15 @@
     near = call(
         functools.partial(join_kernel, len(fetched)),
         f32(device_count // 2, wide, wide),
-        (columns, *fetched),
-        after=True,
+        (columns, interp[0], *fetched),
+        after=2,
     )
     far = apart_by(near, "gx", 1)
-    profile = call(
-        functools.partial(profile_kernel, layers, held),
-        f32(wide, device_count * capacity),
-        (columns, factors, interp),
+    half = device_count // 2 * capacity
+    weighted, profile, factors = call(
+        functools.partial(profile_kernel, layers, held, capacity),
+        (f32(wide, half), f32(wide, half), f32(3, layers, 8, LANES)),
+        (columns, vert_coef.reshape(layers, cells // LANES, LANES), *interp, near),
         scratch=(pltpu.VMEM((2 * wide, LANES), jnp.float32),),
         flops=400_000_000,
         mib=16,
@@ -481,9 +507,9 @@
     spread = call(
         functools.partial(spread_kernel, layers, held, capacity),
         f32(cols_x * 2 * kv, LANES),
-        (profile, factors, interp, near, far),
+        (weighted, profile, factors, *interp, far),
         scratch=(pltpu.VMEM((2 * wide, LANES), jnp.float32),),
-        flops=1_000_000_000,
+        flops=400_000_000,
         mib=16,
     )
     tile = lax.all_to_all(

time: 68.2 us -> 66.4 us (0.974)
  blocking collectives: 30.3 us -> 20 us
  waiting for transfers between devices: 8.82 us -> 15.7 us
  starting transfers between devices: 14.6 us -> 18.3 us
  local copies, waits for them, and re-layouts: 3.8 us -> 2.15 us
    all_to_all x1 -> x0, blocking collectives: 10.3 us -> none  [per_device_gathered(): lax.all_to_all(packed, 'gx', split_axis=0, concat_axis=0, tiled=True)]
    all_to_all x0 -> x1, waiting for transfers between devices: none -> 4.94 us  [per_device_gathered(): lax.all_to_all(packed, 'gx', split_axis=0, concat_axis=0, tiled=True)]
    all_to_all x0 -> x1, starting transfers between devices: none -> 3.84 us  [per_device_gathered(): lax.all_to_all(packed, 'gx', split_axis=0, concat_axis=0, tiled=True)]
    ppermute x7, waiting for transfers between devices: 3.1 us -> 5.05 us  [apart_by(): lax.ppermute(block, axis, [(i, i ^ stride) for i in range(lax.axis_size(a...]
    unnamed x26 -> x28, local copies, waits for them, and re-layouts: 3.7 us -> 2.05 us
  transfers between devices with their start and end apart: 11 -> 12, of which waited for: 4 -> 6; matrix products, arithmetic and copies ran while one was open for 0% -> 0% of each run, Pallas kernels for 5% -> 4%
where the time goes in v4:
time: 66.4 us; the launch traced here: 66 us
  blocking collectives  20 us (30%)
  starting transfers between devices  18.3 us (28%)
  waiting for transfers between devices  15.7 us (24%)
  Pallas kernels  8.99 us (14%)
  local copies, waits for them, and re-layouts  2.15 us (3%)
  between operations  0.82 us (1%)
    all_to_all x1, blocking collectives, per_device_gathered(): lax.all_to_all(sums, ('gy', 'gx'), split_axis=0, concat_axis=0, tiled=True)  10.5 us
    all_to_all x1, blocking collectives, per_device_gathered(): lax.all_to_all(spread.reshape(cols_x, 2 * kv, LANES), 'gx', split_axis=0,...  9.53 us
    pallas_call x8, Pallas kernels, call(): pl.pallas_call(kernel, out_shape=out_shape, in_specs=specs, out_specs=tup...  8.99 us
    ppermute x7, starting transfers between devices, apart_by(): lax.ppermute(block, axis, [(i, i ^ stride) for i in range(lax.axis_size(a...  7.95 us
    ppermute x2, starting transfers between devices, from_neighbours(): lax.ppermute(block, 'gy', [(i, (i + (1 if i % 2 else -1)) % count) for i...  5.49 us
    ppermute x2, waiting for transfers between devices, from_neighbours(): lax.ppermute(block, 'gy', [(i, (i + (1 if i % 2 else -1)) % count) for i...  5.18 us
    ppermute x7, waiting for transfers between devices, apart_by(): lax.ppermute(block, axis, [(i, i ^ stride) for i in range(lax.axis_size(a...  5.05 us
    all_to_all x1, waiting for transfers between devices, per_device_gathered(): lax.all_to_all(packed, 'gx', split_axis=0, concat_axis=0, tiled=True)  4.94 us
  transfers between devices with their start and end apart: 12, of which 6 were waited for; matrix products, arithmetic and copies ran while one was open for 0% of the time, Pallas kernels for 4%

profile of v4, /device:TPU:0, one launch (start us, length us, event | category | flops | bytes accessed | tf_op | source)
XLA Modules:
  0.0 66.0 jit_solution(3541926568392045485)
XLA Ops:
  0.6 0.0 copy-start.5
  0.6 0.0 copy-start
  0.7 0.0 copy-start.6
  0.7 0.0 copy-start.7
  0.7 0.0 copy-start.8
  0.7 1.7 %shard_map.139 = f32[304,128]{1,0:T(8,128)} custom-call(f32[256,128]{1,0:T(8,128)} %bitcast.52, f32[16,128]{1,0:T(8,128)} %bitcast.66, f32[16,128]{1,0:T(8,128)} %bitcast.68, s32[16,128]{1,0:T(8,128)} %bitcast.70), custom_call_target="tpu_custom_call" | custom-call | flops 1000000 | bytes 155648 | tf_op jit(solution)/shard_map/pallas_call | solution.py:394
  2.4 4.0 %collective-permute-start.1 = (f32[304,128]{1,0:T(8,128)}, f32[304,128]{1,0:T(8,128)S(1)}, u32[]{:S(2)}, u32[]{:S(2)}) collective-permute-start(f32[304,128]{1,0:T(8,128)} %shard_map.139), channel_id=1, source_target_pairs={{0,24},{8,16},{16,8},{24,0},{1,25},{9,17},{17,9},{25,1},{2,26},{10... | collective-permute-start | bytes 466952 | tf_op jit(solution)/shard_map/ppermute | solution.py:412
  6.4 0.5 collective-permute-start
  6.9 0.0 copy-done.5
  6.9 3.6 %collective-permute-start.4 = (f32[1,128,128]{2,1,0:T(8,128)S(1)}, f32[1,128,128]{2,1,0:T(8,128)S(1)}, u32[]{:S(2)}, u32[]{:S(2)}) collective-permute-start(f32[1,128,128]{2,1,0:T(8,128)S(1)} %bitcast.62), channel_id=1, source_target_pairs={{0,6},{1,7},{2,4},{3,5},{4,2},{5,3},{6,0},{7,1},{8,14},{9,15},{10,... | collective-permute-start | bytes 196616 | tf_op jit(solution)/shard_map/ppermute | solution.py:417
  10.5 0.0 collective-permute-start.3
  10.5 0.8 %collective-permute-start.2 = (f32[1,128,128]{2,1,0:T(8,128)S(1)}, f32[1,128,128]{2,1,0:T(8,128)S(1)}, u32[]{:S(2)}, u32[]{:S(2)}) collective-permute-start(f32[1,128,128]{2,1,0:T(8,128)S(1)} %bitcast.64), channel_id=1, source_target_pairs={{0,2},{1,3},{2,0},{3,1},{4,6},{5,7},{6,4},{7,5},{8,10},{9,11},{10,... | collective-permute-start | bytes 196616 | tf_op jit(solution)/shard_map/ppermute | solution.py:417
  11.3 2.2 %collective-permute-done.4.refs_3_ = f32[1,128,128]{2,1,0:T(8,128)S(1)} collective-permute-done((f32[1,128,128]{2,1,0:T(8,128)S(1)}, f32[1,128,128]{2,1,0:T(8,128)S(1)}, u32[]{:S(2)}, u32[]{:S(2)}) %collective-permute-start.4) | collective-permute-done | bytes 65568 | tf_op jit(solution)/shard_map/ppermute | solution.py:417
  13.5 2.3 %collective-permute-done.3.refs_2_ = f32[1,128,128]{2,1,0:T(8,128)S(1)} collective-permute-done((f32[1,128,128]{2,1,0:T(8,128)S(1)}, f32[1,128,128]{2,1,0:T(8,128)S(1)}, u32[]{:S(2)}, u32[]{:S(2)}) %collective-permute-start.3) | collective-permute-done | bytes 65568 | tf_op jit(solution)/shard_map/ppermute | solution.py:417
  15.8 0.0 collective-permute-done.2.refs_1_
  15.8 0.0 collective-permute-done.1.cross_ref
  15.8 0.0 collective-permute-done.pair_ref
  15.8 0.0 copy-done
  15.8 0.0 copy-done.6
  15.8 0.0 copy-done.7
  15.8 0.0 copy-done.8
  15.8 1.7 %shard_map.140 = (f32[8,32,128]{2,1,0:T(8,128)}, f32[5,16,512]{2,1,0:T(8,128)S(1)}, f32[4,128,128]{2,1,0:T(8,128)S(1)}) custom-call(f32[256,128]{1,0:T(8,128)S(1)} %bitcast.53, f32[16,128]{1,0:T(8,128)S(1)} %bitcast.67, f32[16,128]{1,0:T(8,128)S(1)} %bitcast.69, s32[16,128]{1,0:T(8,128)S(1)} %bitcast.71, f32[304,128]{1,0:T(8,128)S(1)} %collective-permute-done.pair_ref, ...), custom_call_target="tpu_custom_call" | custom-call | flops 4000000 | bytes 729088 | tf_op jit(solution)/shard_map/pallas_call | solution.py:394
  17.5 0.0 copy-start.2
  17.5 0.7 %copy-done.2 = f32[5,16,512]{2,1,0:T(8,128)} copy-done((f32[5,16,512]{2,1,0:T(8,128)}, f32[5,16,512]{2,1,0:T(8,128)S(1)}, u32[]{:S(2)}) %copy-start.2) | copy-done | bytes 163864
  18.1 1.4 %collective-permute-start.7 = (f32[4,128,128]{2,1,0:T(8,128)S(1)}, f32[4,128,128]{2,1,0:T(8,128)S(1)}, u32[]{:S(2)}, u32[]{:S(2)}) collective-permute-start(f32[4,128,128]{2,1,0:T(8,128)S(1)} %get-tuple-element.19.refs_0_), channel_id=1, source_target_pairs={{0,24},{8,16},{16,8},{24,0},{1,25},{9,17},{17,9},{25,1},{2,26},{10... | collective-permute-start | bytes 786440 | tf_op jit(solution)/shard_map/ppermute | solution.py:417
  19.6 1.5 %collective-permute-start.6 = (f32[4,128,128]{2,1,0:T(8,128)S(1)}, f32[4,128,128]{2,1,0:T(8,128)S(1)}, u32[]{:S(2)}, u32[]{:S(2)}) collective-permute-start(f32[4,128,128]{2,1,0:T(8,128)S(1)} %get-tuple-element.19.refs_0_), channel_id=1, source_target_pairs={{0,16},{8,24},{16,0},{24,8},{1,17},{9,25},{17,1},{25,9},{2,18},{10... | collective-permute-start | bytes 786440 | tf_op jit(solution)/shard_map/ppermute | solution.py:417
  21.1 0.5 collective-permute-start.5
  21.6 0.0 copy-start.11
  21.6 0.0 copy-start.12
  21.6 3.8 %all-to-all-start = ((f32[8,32,128]{2,1,0:T(8,128)}), f32[8,32,128]{2,1,0:T(8,128)S(1)}, u32[]{:S(2)}, u32[]{:S(2)}) async-start(f32[8,32,128]{2,1,0:T(8,128)} %get-tuple-element.16._), calls=%async_computation | async-start | bytes 262144 | tf_op jit(solution)/shard_map/all_to_all | solution.py:489
  25.5 0.0 copy-start.9
  25.5 0.0 copy-start.10
  25.5 0.0 copy-done.11
  25.5 0.0 copy-done.12
  25.5 0.7 copy-done.9
  26.2 0.0 copy-done.10
  26.2 1.1 %shard_map.141 = (bf16[256,1024]{1,0:T(8,128)(2,1)S(1)}, bf16[256,1024]{1,0:T(8,128)(2,1)S(1)}) custom-call(f32[8,32,128]{2,1,0:T(8,128)} %get-tuple-element.16._, s32[1,512]{1,0:T(1,128)S(1)} %bitcast.73, s32[1,512]{1,0:T(1,128)S(1)} %bitcast.74, s32[1,512]{1,0:T(1,128)S(1)} %bitcast.75, f32[2,512]{1,0:T(2,128)S(1)} %bitcast.72), custom_call_target="tpu_custom_call" | custom-call | flops 20000000 | bytes 141312 | tf_op jit(solution)/shard_map/pallas_call | solution.py:394
  27.3 4.9 %all-to-all-done = f32[8,32,128]{2,1,0:T(8,128)S(1)} async-done(((f32[8,32,128]{2,1,0:T(8,128)}), f32[8,32,128]{2,1,0:T(8,128)S(1)}, u32[]{:S(2)}, u32[]{:S(2)}) %all-to-all-start) | async-done | bytes 131104 | tf_op jit(solution)/shard_map/all_to_all | solution.py:489
  32.3 0.0 collective-permute-done.7.refs_3_
  32.3 0.0 collective-permute-done.6.refs_2_
  32.3 0.0 collective-permute-done.5.refs_1_
  32.3 0.0 copy-start.13
  32.3 0.1 shard_map.142.near_ref
  32.4 0.1 collective-permute-start.8
  32.4 0.7 %copy-done.13 = f32[32,4,64]{2,1,0:T(4,128)S(1)} copy-done((f32[32,4,64]{2,1,0:T(4,128)S(1)}, f32[32,4,64]{2,1,0:T(4,128)}, u32[]{:S(2)}) %copy-start.13) | copy-done | bytes 32792
  33.1 0.1 reshape.82.vert_ref
  33.2 1.3 %shard_map.143 = (f32[128,512]{1,0:T(8,128)S(1)}, f32[128,512]{1,0:T(8,128)S(1)}, f32[3,32,8,128]{3,2,1,0:T(8,128)S(1)}) custom-call(f32[256,128]{1,0:T(8,128)S(1)} %bitcast.57, f32[32,2,128]{2,1,0:T(2,128)S(1)} %reshape.82.vert_ref, bf16[256,1024]{1,0:T(8,128)(2,1)S(1)} %get-tuple-element.17.__.high_ref, bf16[256,1024]{1,0:T(8,128)(2,1)S(1)} %get-tuple-element.18.low_ref, ...), custom_call_target="tpu_custom_call" | custom-call | flops 400000000 | bytes 3309568 | tf_op jit(solution)/shard_map/pallas_call | solution.py:394
  34.5 0.6 collective-permute-done.8.far_ref
  35.1 0.0 copy-start.3
  35.1 1.2 %shard_map.144 = f32[256,128]{1,0:T(8,128)S(1)} custom-call(f32[128,512]{1,0:T(8,128)S(1)} %get-tuple-element.20.near_ref, f32[128,512]{1,0:T(8,128)S(1)} %get-tuple-element.21.profile_ref, f32[3,32,8,128]{3,2,1,0:T(8,128)S(1)} %get-tuple-element.22.factor_ref, bf16[256,1024]{1,0:T(8,128)(2,1)S(1)} %get-tuple-element.17.__.high_ref, ...), custom_call_target="tpu_custom_call" | custom-call | flops 400000000 | bytes 4063232 | tf_op jit(solution)/shard_map/pallas_call | solution.py:394
  36.3 0.0 copy-start.1
  36.3 9.5 %all_to_all.15.own_ref = f32[8,32,128]{2,1,0:T(8,128)S(1)} all-to-all(f32[8,32,128]{2,1,0:T(8,128)S(1)} %bitcast.58), channel_id=1, replica_groups=mesh['gy'=4,'gx'=8] {'gx'}, dimensions={0} | all-to-all | bytes 262144 | tf_op jit(solution)/shard_map/all_to_all | solution.py:515
  45.9 1.5 %collective-permute-start.10 = (f32[8,32,128]{2,1,0:T(8,128)S(1)}, f32[8,32,128]{2,1,0:T(8,128)S(1)}, u32[]{:S(2)}, u32[]{:S(2)}) collective-permute-start(f32[8,32,128]{2,1,0:T(8,128)S(1)} %all_to_all.15.own_ref), channel_id=1, source_target_pairs={{0,24},{8,16},{16,8},{24,0},{1,25},{9,17},{17,9},{25,1},{2,26},{10... | collective-permute-start | bytes 393224 | tf_op jit(solution)/shard_map/ppermute | solution.py:412
  47.4 0.5 collective-permute-start.9
  47.9 5.2 %collective-permute-done.10.cross_ref = f32[8,32,128]{2,1,0:T(8,128)S(1)} collective-permute-done((f32[8,32,128]{2,1,0:T(8,128)S(1)}, f32[8,32,128]{2,1,0:T(8,128)S(1)}, u32[]{:S(2)}, u32[]{:S(2)}) %collective-permute-start.10) | collective-permute-done | bytes 131104 | tf_op jit(solution)/shard_map/ppermute | solution.py:412
  53.1 0.5 collective-permute-done.9.pair_ref
  53.7 0.0 copy-done.3
  53.7 0.0 copy-done.1
  53.7 0.0 copy-start.4
  53.7 1.0 %shard_map.145 = (f32[256,128]{1,0:T(8,128)S(1)}, f32[32,1,128]{2,1,0:T(1,128)S(1)}) custom-call(f32[8,32,128]{2,1,0:T(8,128)S(1)} %all_to_all.15.own_ref, f32[8,32,128]{2,1,0:T(8,128)S(1)} %collective-permute-done.9.pair_ref, f32[8,32,128]{2,1,0:T(8,128)S(1)} %collective-permute-done.10.cross_ref, f32[5,16,512]{2,1,0:T(8,128)S(1)} %copy-done.3, ...), custom_call_target="tpu_custom_call" | custom-call | flops 4000000 | bytes 819200 | tf_op jit(solution)/shard_map/pallas_call | solution.py:394
  54.7 10.5 %all_to_all.16.sums_ref = f32[32,1,128]{2,1,0:T(1,128)S(1)} all-to-all(f32[32,1,128]{2,1,0:T(1,128)S(1)} %get-tuple-element.24), channel_id=1, replica_groups=mesh['gy'=4,'gx'=8] {'gy','gx'}, dimensions={0} | all-to-all | bytes 32768 | tf_op jit(solution)/shard_map/all_to_all | solution.py:526
  65.1 0.0 copy-done.4
  65.1 0.9 %shard_map.146 = (f32[256,128]{1,0:T(8,128)}, f32[256,128]{1,0:T(8,128)}, f32[256,128]{1,0:T(8,128)}) custom-call(f32[32,1,128]{2,1,0:T(1,128)S(1)} %all_to_all.16.sums_ref, f32[256,128]{1,0:T(8,128)S(1)} %bitcast.55, f32[256,128]{1,0:T(8,128)S(1)} %bitcast.61, f32[256,128]{1,0:T(8,128)S(1)} %bitcast.60, f32[256,128]{1,0:T(8,128)S(1)} %get-tuple-element.25.image_ref), custom_call_target="tpu_custom_call" | custom-call | flops 1000000 | bytes 540672 | tf_op jit(solution)/shard_map/pallas_call | solution.py:394
Async XLA Ops:
  0.6 6.3 %copy-start.5 = (f32[1,1,128,128]{3,2,1,0:T(8,128)S(1)}, f32[1,1,128,128]{3,2,1,0:T(8,128)}, u32[]{:S(2)}) copy-start(f32[1,1,128,128]{3,2,1,0:T(8,128)} %param.23) | copy-start | bytes 196612
  0.6 15.1 %copy-start = (f32[4,4,4,512]{3,2,1,0:T(4,128)S(1)}, f32[4,4,4,512]{3,2,1,0:T(4,128)}, u32[]{:S(2)}) copy-start(f32[4,4,4,512]{3,2,1,0:T(4,128)} %param.12) | copy-start | bytes 393220
  0.7 15.1 %copy-start.6 = (f32[4,512]{1,0:T(4,128)S(1)}, f32[4,512]{1,0:T(4,128)}, u32[]{:S(2)}) copy-start(f32[4,512]{1,0:T(4,128)} %param.15) | copy-start | bytes 24580
  0.7 15.1 %copy-start.7 = (f32[4,512]{1,0:T(4,128)S(1)}, f32[4,512]{1,0:T(4,128)}, u32[]{:S(2)}) copy-start(f32[4,512]{1,0:T(4,128)} %param.16) | copy-start | bytes 24580
  0.7 15.1 %copy-start.8 = (s32[4,512]{1,0:T(4,128)S(1)}, s32[4,512]{1,0:T(4,128)}, u32[]{:S(2)}) copy-start(s32[4,512]{1,0:T(4,128)} %param.17) | copy-start | bytes 24580
  2.4 13.4 %collective-permute-start.1 = (f32[304,128]{1,0:T(8,128)}, f32[304,128]{1,0:T(8,128)S(1)}, u32[]{:S(2)}, u32[]{:S(2)}) collective-permute-start(f32[304,128]{1,0:T(8,128)} %shard_map.139), channel_id=1, source_target_pairs={{0,24},{8,16},{16,8},{24,0},{1,25},{9,17},{17,9},{25,1},{2,26},{10... | collective-permute-start | bytes 466952 | tf_op jit(solution)/shard_map/ppermute | solution.py:412
  6.4 9.4 %collective-permute-start = (f32[304,128]{1,0:T(8,128)}, f32[304,128]{1,0:T(8,128)S(1)}, u32[]{:S(2)}, u32[]{:S(2)}) collective-permute-start(f32[304,128]{1,0:T(8,128)} %shard_map.139), channel_id=1, source_target_pairs={{0,8},{8,0},{16,24},{24,16},{1,9},{9,1},{17,25},{25,17},{2,10},{10... | collective-permute-start | bytes 466952 | tf_op jit(solution)/shard_map/ppermute | solution.py:411
  6.9 6.6 %collective-permute-start.4 = (f32[1,128,128]{2,1,0:T(8,128)S(1)}, f32[1,128,128]{2,1,0:T(8,128)S(1)}, u32[]{:S(2)}, u32[]{:S(2)}) collective-permute-start(f32[1,128,128]{2,1,0:T(8,128)S(1)} %bitcast.62), channel_id=1, source_target_pairs={{0,6},{1,7},{2,4},{3,5},{4,2},{5,3},{6,0},{7,1},{8,14},{9,15},{10,... | collective-permute-start | bytes 196616 | tf_op jit(solution)/shard_map/ppermute | solution.py:417
  10.5 5.2 %collective-permute-start.3 = (f32[1,128,128]{2,1,0:T(8,128)S(1)}, f32[1,128,128]{2,1,0:T(8,128)S(1)}, u32[]{:S(2)}, u32[]{:S(2)}) collective-permute-start(f32[1,128,128]{2,1,0:T(8,128)S(1)} %bitcast.63), channel_id=1, source_target_pairs={{0,4},{1,5},{2,6},{3,7},{4,0},{5,1},{6,2},{7,3},{8,12},{9,13},{10,... | collective-permute-start | bytes 196616 | tf_op jit(solution)/shard_map/ppermute | solution.py:417
  10.5 5.2 %collective-permute-start.2 = (f32[1,128,128]{2,1,0:T(8,128)S(1)}, f32[1,128,128]{2,1,0:T(8,128)S(1)}, u32[]{:S(2)}, u32[]{:S(2)}) collective-permute-start(f32[1,128,128]{2,1,0:T(8,128)S(1)} %bitcast.64), channel_id=1, source_target_pairs={{0,2},{1,3},{2,0},{3,1},{4,6},{5,7},{6,4},{7,5},{8,10},{9,11},{10,... | collective-permute-start | bytes 196616 | tf_op jit(solution)/shard_map/ppermute | solution.py:417
  17.5 0.7 %copy-start.2 = (f32[5,16,512]{2,1,0:T(8,128)}, f32[5,16,512]{2,1,0:T(8,128)S(1)}, u32[]{:S(2)}) copy-start(f32[5,16,512]{2,1,0:T(8,128)S(1)} %get-tuple-element.23.coef_ref) | copy-start | bytes 491524
  18.1 14.1 %collective-permute-start.7 = (f32[4,128,128]{2,1,0:T(8,128)S(1)}, f32[4,128,128]{2,1,0:T(8,128)S(1)}, u32[]{:S(2)}, u32[]{:S(2)}) collective-permute-start(f32[4,128,128]{2,1,0:T(8,128)S(1)} %get-tuple-element.19.refs_0_), channel_id=1, source_target_pairs={{0,24},{8,16},{16,8},{24,0},{1,25},{9,17},{17,9},{25,1},{2,26},{10... | collective-permute-start | bytes 786440 | tf_op jit(solution)/shard_map/ppermute | solution.py:417
  19.6 12.7 %collective-permute-start.6 = (f32[4,128,128]{2,1,0:T(8,128)S(1)}, f32[4,128,128]{2,1,0:T(8,128)S(1)}, u32[]{:S(2)}, u32[]{:S(2)}) collective-permute-start(f32[4,128,128]{2,1,0:T(8,128)S(1)} %get-tuple-element.19.refs_0_), channel_id=1, source_target_pairs={{0,16},{8,24},{16,0},{24,8},{1,17},{9,25},{17,1},{25,9},{2,18},{10... | collective-permute-start | bytes 786440 | tf_op jit(solution)/shard_map/ppermute | solution.py:417
  21.1 11.2 %collective-permute-start.5 = (f32[4,128,128]{2,1,0:T(8,128)S(1)}, f32[4,128,128]{2,1,0:T(8,128)S(1)}, u32[]{:S(2)}, u32[]{:S(2)}) collective-permute-start(f32[4,128,128]{2,1,0:T(8,128)S(1)} %get-tuple-element.19.refs_0_), channel_id=1, source_target_pairs={{0,8},{8,0},{16,24},{24,16},{1,9},{9,1},{17,25},{25,17},{2,10},{10... | collective-permute-start | bytes 786440 | tf_op jit(solution)/shard_map/ppermute | solution.py:417
  21.6 3.9 %copy-start.11 = (s32[1,1,512]{2,1,0:T(1,128)S(1)}, s32[1,1,512]{2,1,0:T(1,128)}, u32[]{:S(2)}) copy-start(s32[1,1,512]{2,1,0:T(1,128)} %param.20) | copy-start | bytes 6148
  21.6 3.9 %copy-start.12 = (s32[1,1,512]{2,1,0:T(1,128)S(1)}, s32[1,1,512]{2,1,0:T(1,128)}, u32[]{:S(2)}) copy-start(s32[1,1,512]{2,1,0:T(1,128)} %param.21) | copy-start | bytes 6148
  21.6 10.6 %all-to-all-start = ((f32[8,32,128]{2,1,0:T(8,128)}), f32[8,32,128]{2,1,0:T(8,128)S(1)}, u32[]{:S(2)}, u32[]{:S(2)}) async-start(f32[8,32,128]{2,1,0:T(8,128)} %get-tuple-element.16._), calls=%async_computation | async-start | bytes 262144 | tf_op jit(solution)/shard_map/all_to_all | solution.py:489
  25.5 0.7 %copy-start.9 = (f32[1,1,2,512]{3,2,1,0:T(2,128)S(1)}, f32[1,1,2,512]{3,2,1,0:T(2,128)}, u32[]{:S(2)}) copy-start(f32[1,1,2,512]{3,2,1,0:T(2,128)} %param.22) | copy-start | bytes 12292
  25.5 0.7 %copy-start.10 = (s32[1,1,512,1]{2,3,1,0:T(1,128)S(1)}, s32[1,1,512,1]{2,3,1,0:T(1,128)}, u32[]{:S(2)}) copy-start(s32[1,1,512,1]{2,3,1,0:T(1,128)} %param.19) | copy-start | bytes 6148
  32.3 0.8 %copy-start.13 = (f32[32,4,64]{2,1,0:T(4,128)S(1)}, f32[32,4,64]{2,1,0:T(4,128)}, u32[]{:S(2)}) copy-start(f32[32,4,64]{2,1,0:T(4,128)} %param.18) | copy-start | bytes 98308
  32.4 2.7 %collective-permute-start.8 = (f32[16,128,128]{2,1,0:T(8,128)S(1)}, f32[16,128,128]{2,1,0:T(8,128)S(1)}, u32[]{:S(2)}, u32[]{:S(2)}) collective-permute-start(f32[16,128,128]{2,1,0:T(8,128)S(1)} %shard_map.142.near_ref), channel_id=1, source_target_pairs={{0,1},{1,0},{2,3},{3,2},{4,5},{5,4},{6,7},{7,6},{8,9},{9,8},{10,11... | collective-permute-start | bytes 3145736 | tf_op jit(solution)/shard_map/ppermute | solution.py:417
  35.1 18.6 %copy-start.3 = (f32[5,16,512]{2,1,0:T(8,128)S(1)}, f32[5,16,512]{2,1,0:T(8,128)}, u32[]{:S(2)}) copy-start(f32[5,16,512]{2,1,0:T(8,128)} %copy-done.2) | copy-start | bytes 491524
  36.3 17.3 %copy-start.1 = (f32[4,4,4,512]{3,2,1,0:T(4,128)S(1)}, f32[4,4,4,512]{3,2,1,0:T(4,128)}, u32[]{:S(2)}) copy-start(f32[4,4,4,512]{3,2,1,0:T(4,128)} %param.14) | copy-start | bytes 393220
  45.9 7.2 %collective-permute-start.10 = (f32[8,32,128]{2,1,0:T(8,128)S(1)}, f32[8,32,128]{2,1,0:T(8,128)S(1)}, u32[]{:S(2)}, u32[]{:S(2)}) collective-permute-start(f32[8,32,128]{2,1,0:T(8,128)S(1)} %all_to_all.15.own_ref), channel_id=1, source_target_pairs={{0,24},{8,16},{16,8},{24,0},{1,25},{9,17},{17,9},{25,1},{2,26},{10... | collective-permute-start | bytes 393224 | tf_op jit(solution)/shard_map/ppermute | solution.py:412
  47.4 6.3 %collective-permute-start.9 = (f32[8,32,128]{2,1,0:T(8,128)S(1)}, f32[8,32,128]{2,1,0:T(8,128)S(1)}, u32[]{:S(2)}, u32[]{:S(2)}) collective-permute-start(f32[8,32,128]{2,1,0:T(8,128)S(1)} %all_to_all.15.own_ref), channel_id=1, source_target_pairs={{0,8},{8,0},{16,24},{24,16},{1,9},{9,1},{17,25},{25,17},{2,10},{10... | collective-permute-start | bytes 393224 | tf_op jit(solution)/shard_map/ppermute | solution.py:411
  53.7 11.5 %copy-start.4 = (f32[4,4,4,512]{3,2,1,0:T(4,128)S(1)}, f32[4,4,4,512]{3,2,1,0:T(4,128)}, u32[]{:S(2)}) copy-start(f32[4,4,4,512]{3,2,1,0:T(4,128)} %param.13) | copy-start | bytes 393220

commit v5 on v4

--- a/solution.py
+++ b/solution.py
@@ -75,37 +75,53 @@
         high_ref[...] = jnp.zeros_like(high_ref)
 
 
-def halo_kernel(direction_ref, north_ref, east_ref, ocean_ref, own_ref, mask_ref, sems):
+def halo_kernel(direction_ref, north_ref, east_ref, ocean_ref, own_ref, mask_ref, ocean_mask_ref, sems):
     cells, size = direction_ref.shape[0], north_ref.shape[0]
+    mask = pltpu.make_async_copy(ocean_ref, mask_ref, sems.at[0])
     moves = (
-        (ocean_ref, mask_ref),
         (direction_ref, own_ref.at[pl.ds(0, cells)]),
         (north_ref, own_ref.at[pl.ds(cells, size)]),
         (east_ref, own_ref.at[pl.ds(cells + size, size)]),
     )
-    copies = [pltpu.make_async_copy(*move, sems.at[at]) for at, move in enumerate(moves)]
+    copies = [pltpu.make_async_copy(*move, sems.at[1 + at]) for at, move in enumerate(moves)]
+    mask.start()
     for copy in copies:
         copy.start()
+    mask.wait()
+    ocean_mask_ref[...] = mask_ref[...].astype(jnp.float32)
+    last = pltpu.make_async_copy(ocean_mask_ref, own_ref.at[pl.ds(cells + 2 * size, size)], sems.at[4])
+    last.start()
     for copy in copies:
         copy.wait()
-    own_ref[cells + 2 * size : cells + 3 * size, :] = mask_ref[...].astype(jnp.float32)
-
-
-def join_kernel(count, _, __, *refs):
-    blocks, (near_ref,) = refs[:count], refs[count:]
+    last.wait()
+
+
+def join_kernel(after, count, *refs):
+    blocks, (near_ref,) = refs[after : after + count], refs[after + count :]
     size = blocks[0].shape[0]
     for at, block in enumerate(blocks):
         near_ref[at * size : (at + 1) * size] = block[...]
 
 
 def first_lateral_kernel(
-    kv, rows, tiles, count, own_ref, north_ref, east_ref, ocean_ref, pair_ref, cross_ref, *refs
+    kv,
+    rows,
+    tiles,
+    _,
+    own_ref,
+    north_ref,
+    east_ref,
+    ocean_ref,
+    pair_ref,
+    cross_ref,
+    packed_ref,
+    coef_ref,
+    ext_ref,
+    low_ref,
+    high_ref,
 ):
-    blocks, (packed_ref, coef_ref, held_ref, ext_ref, low_ref, high_ref) = refs[:count], refs[count:]
     lons = tiles * LANES
     cells = kv * tiles * rows
-    for at, block in enumerate(blocks):
-        held_ref[at] = block[0]
     sort_halo(pair_ref, cross_ref, low_ref, high_ref)
     ext_ref[...] = jnp.zeros_like(ext_ref)
     for kind, kept in enumerate((north_ref, east_ref, ocean_ref)):
@@ -230,8 +246,19 @@
 
 
 def prepare_kernel(
-    devices, capacity, lon_cols, _, owner_ref, row_ref, col_ref, frac_ref, high_ref, low_ref
+    devices,
+    capacity,
+    lon_cols,
+    vert_ref,
+    owner_ref,
+    row_ref,
+    col_ref,
+    frac_ref,
+    factor_ref,
+    high_ref,
+    low_ref,
 ):
+    vertical_factors_of(vert_ref, factor_ref)
     count = owner_ref.shape[1]
     slots = devices * capacity
     me = lax.axis_index("gy") * lax.axis_size("gx") + lax.axis_index("gx")
@@ -286,7 +313,7 @@
     high_ref[...], low_ref[...] = split(interp)
 
 
-def vertical_factors_kernel(vert_ref, factor_ref):
+def vertical_factors_of(vert_ref, factor_ref):
     layers = vert_ref.shape[0]
     top = lax.broadcasted_iota(jnp.int32, (8, LANES), 0) < 4
     coef = [jnp.where(top, vert_ref[layer, 0:1, :], vert_ref[layer, 1:2, :]) for layer in range(layers)]
@@ -338,19 +365,16 @@
     held,
     capacity,
     packed_ref,
-    vert_ref,
+    factor_ref,
     high_ref,
     low_ref,
     near_ref,
     weighted_ref,
     profile_ref,
-    factor_ref,
     column_ref,
 ):
     kv = profile_ref.shape[0]
     half = profile_ref.shape[1]
-    vertical_factors_kernel(vert_ref, factor_ref)
-
     def read(layer):
         return packed_ref[packed_at(layer, held), :]
 
@@ -388,14 +412,15 @@
 
 def call(kernel, out_shape, inputs, scratch=(), after=0, hbm=False, flops=1_000_000, mib=8):
     specs = [pl.BlockSpec(memory_space=pl.ANY)] * after + vmem(len(inputs) - after)
+    outs = vmem(len(out_shape) if isinstance(out_shape, tuple) else 1)
     if hbm:
-        specs = [pl.BlockSpec(memory_space=pltpu.HBM)] * len(inputs)
+        specs, outs = ([pl.BlockSpec(memory_space=pltpu.HBM)] * len(x) for x in (specs, outs))
     moved = sum(math.prod(x.shape) * 4 for x in inputs)
     return pl.pallas_call(
         kernel,
         out_shape=out_shape,
         in_specs=specs,
-        out_specs=tuple(vmem(len(out_shape))) if isinstance(out_shape, tuple) else vmem(1)[0],
+        out_specs=tuple(outs) if isinstance(out_shape, tuple) else outs[0],
         scratch_shapes=list(scratch),
         compiler_params=pltpu.CompilerParams(vmem_limit_bytes=mib * 1024 * 1024),
         cost_estimate=pl.CostEstimate(flops=flops, bytes_accessed=moved, transcendentals=0),
@@ -450,7 +475,11 @@
         halo_kernel,
         f32(direction_n.shape[0] + 3 * faces[0].shape[0], LANES),
         (direction_n, *faces),
-        scratch=(pltpu.VMEM(faces[0].shape, jnp.int32), pltpu.SemaphoreType.DMA((4,))),
+        scratch=(
+            pltpu.VMEM(faces[0].shape, jnp.int32),
+            pltpu.VMEM(faces[0].shape, jnp.float32),
+            pltpu.SemaphoreType.DMA((5,)),
+        ),
         hbm=True,
         mib=56,
     )
@@ -458,11 +487,33 @@
 
     matrix = error_inverse.reshape(1, wide, wide)
     blocks = [matrix] + [apart_by(matrix, "gx", stride) for stride in range(2, cols_x, 2)]
+    halves = jax.ShapeDtypeStruct((cells, device_count * capacity), jnp.bfloat16)
+    factors, *interp = call(
+        functools.partial(prepare_kernel, device_count, capacity, lon_cols),
+        (f32(3, layers, 8, LANES), halves, halves),
+        (
+            vert_coef.reshape(layers, cells // LANES, LANES),
+            obs_owner.reshape(1, obs_count),
+            obs_row.reshape(1, obs_count),
+            obs_col.reshape(1, obs_count),
+            obs_frac.reshape(2, obs_count),
+        ),
+        flops=20_000_000,
+        mib=16,
+    )
+    held_blocks = call(
+        functools.partial(join_kernel, 1, len(blocks)),
+        f32(len(blocks), wide, wide),
+        (interp[0], *blocks),
+        after=1,
+    )
+
     extended = 3 * rows + (-3 * rows) % 8
-    packed, coef, held_blocks = call(
-        functools.partial(first_lateral_kernel, kv, rows, tiles, len(blocks)),
-        (f32(cols_x, 2 * kv, LANES), f32(5, extended, lons), f32(len(blocks), wide, wide)),
-        (direction_n, *faces, pair, cross, *blocks),
+    packed, coef = call(
+        functools.partial(first_lateral_kernel, kv, rows, tiles),
+        (f32(cols_x, 2 * kv, LANES), f32(5, extended, lons)),
+        (held_blocks, direction_n, *faces, pair, cross),
+        after=1,
         scratch=(
             pltpu.VMEM((3, extended, lons), jnp.float32),
             pltpu.VMEM(own.shape, jnp.float32),
@@ -470,36 +521,21 @@
         ),
         flops=4_000_000,
     )
-    halves = jax.ShapeDtypeStruct((cells, device_count * capacity), jnp.bfloat16)
-    interp = call(
-        functools.partial(prepare_kernel, device_count, capacity, lon_cols),
-        (halves, halves),
-        (
-            packed,
-            obs_owner.reshape(1, obs_count),
-            obs_row.reshape(1, obs_count),
-            obs_col.reshape(1, obs_count),
-            obs_frac.reshape(2, obs_count),
-        ),
-        after=1,
-        flops=20_000_000,
-        mib=16,
-    )
     fetched = [held_blocks] + [apart_by(held_blocks, "gy", stride) for stride in range(1, rows_y)]
     columns = lax.all_to_all(packed, "gx", split_axis=0, concat_axis=0, tiled=True)
     columns = columns.reshape(cols_x * 2 * kv, LANES)
     near = call(
-        functools.partial(join_kernel, len(fetched)),
+        functools.partial(join_kernel, 1, len(fetched)),
         f32(device_count // 2, wide, wide),
-        (columns, interp[0], *fetched),
-        after=2,
+        (columns, *fetched),
+        after=1,
     )
     far = apart_by(near, "gx", 1)
     half = device_count // 2 * capacity
-    weighted, profile, factors = call(
+    weighted, profile = call(
         functools.partial(profile_kernel, layers, held, capacity),
-        (f32(wide, half), f32(wide, half), f32(3, layers, 8, LANES)),
-        (columns, vert_coef.reshape(layers, cells // LANES, LANES), *interp, near),
+        (f32(wide, half), f32(wide, half)),
+        (columns, factors, *interp, near),
         scratch=(pltpu.VMEM((2 * wide, LANES), jnp.float32),),
         flops=400_000_000,
         mib=16,

time: 66.4 us -> 69.5 us (1.047)
  Pallas kernels: 8.99 us -> 12.6 us
  local copies, waits for them, and re-layouts: 2.15 us -> 0.82 us
  waiting for transfers between devices: 15.7 us -> 16.6 us
    ppermute x7, waiting for transfers between devices: 5.05 us -> 8.91 us  [apart_by(): lax.ppermute(block, axis, [(i, i ^ stride) for i in range(lax.axis_size(a...]
    pallas_call x8 -> x9, Pallas kernels: 8.99 us -> 12.6 us  [call(): pl.pallas_call(kernel, out_shape=out_shape, in_specs=specs, out_specs=tup...]
    all_to_all x1, waiting for transfers between devices: 4.94 us -> 1.98 us  [per_device_gathered(): lax.all_to_all(packed, 'gx', split_axis=0, concat_axis=0, tiled=True)]
    unnamed x28 -> x24, local copies, waits for them, and re-layouts: 2.05 us -> 0.72 us
  transfers between devices with their start and end apart: 12 -> 12, of which waited for: 6 -> 8; matrix products, arithmetic and copies ran while one was open for 0% -> 0% of each run, Pallas kernels for 4% -> 5%
where the time goes in v5:
time: 69.5 us; the launch traced here: 69.1 us
  blocking collectives  20.1 us (29%)
  starting transfers between devices  18.2 us (26%)
  waiting for transfers between devices  16.6 us (24%)
  Pallas kernels  12.6 us (18%)
  local copies, waits for them, and re-layouts  0.82 us (1%)
  between operations  0.78 us (1%)
    pallas_call x9, Pallas kernels, call(): pl.pallas_call(kernel, out_shape=out_shape, in_specs=specs, out_specs=tup...  12.6 us
    all_to_all x1, blocking collectives, per_device_gathered(): lax.all_to_all(sums, ('gy', 'gx'), split_axis=0, concat_axis=0, tiled=True)  10.7 us
    all_to_all x1, blocking collectives, per_device_gathered(): lax.all_to_all(spread.reshape(cols_x, 2 * kv, LANES), 'gx', split_axis=0,...  9.4 us
    ppermute x7, waiting for transfers between devices, apart_by(): lax.ppermute(block, axis, [(i, i ^ stride) for i in range(lax.axis_size(a...  8.91 us
    ppermute x7, starting transfers between devices, apart_by(): lax.ppermute(block, axis, [(i, i ^ stride) for i in range(lax.axis_size(a...  8.01 us
    ppermute x2, starting transfers between devices, from_neighbours(): lax.ppermute(block, 'gy', [(i, (i + (1 if i % 2 else -1)) % count) for i...  5.39 us
    ppermute x2, waiting for transfers between devices, from_neighbours(): lax.ppermute(block, 'gy', [(i, (i + (1 if i % 2 else -1)) % count) for i...  5.28 us
    all_to_all x1, starting transfers between devices, per_device_gathered(): lax.all_to_all(packed, 'gx', split_axis=0, concat_axis=0, tiled=True)  3.71 us
  transfers between devices with their start and end apart: 12, of which 8 were waited for; matrix products, arithmetic and copies ran while one was open for 0% of the time, Pallas kernels for 5%

profile of v5, /device:TPU:0, one launch (start us, length us, event | category | flops | bytes accessed | tf_op | source)
XLA Modules:
  0.0 69.1 jit_solution(13085923552517790873)
XLA Ops:
  0.6 0.0 copy-start.3
  0.6 0.0 copy-start.11
  0.7 5.6 %shard_map.141 = f32[304,128]{1,0:T(8,128)} custom-call(f32[256,128]{1,0:T(8,128)} %bitcast.52, f32[16,128]{1,0:T(8,128)} %bitcast.66, f32[16,128]{1,0:T(8,128)} %bitcast.68, s32[16,128]{1,0:T(8,128)} %bitcast.70), custom_call_target="tpu_custom_call" | custom-call | flops 1000000 | bytes 155648 | tf_op jit(solution)/shard_map/pallas_call | solution.py:419
  6.3 4.0 %collective-permute-start.4 = (f32[304,128]{1,0:T(8,128)}, f32[304,128]{1,0:T(8,128)S(1)}, u32[]{:S(2)}, u32[]{:S(2)}) collective-permute-start(f32[304,128]{1,0:T(8,128)} %shard_map.141), channel_id=1, source_target_pairs={{0,24},{8,16},{16,8},{24,0},{1,25},{9,17},{17,9},{25,1},{2,26},{10... | collective-permute-start | bytes 466952 | tf_op jit(solution)/shard_map/ppermute | solution.py:437
  10.2 0.5 collective-permute-start.3
  10.8 0.0 copy-done.3
  10.8 3.6 %collective-permute-start.2 = (f32[1,128,128]{2,1,0:T(8,128)S(1)}, f32[1,128,128]{2,1,0:T(8,128)S(1)}, u32[]{:S(2)}, u32[]{:S(2)}) collective-permute-start(f32[1,128,128]{2,1,0:T(8,128)S(1)} %bitcast.62), channel_id=1, source_target_pairs={{0,6},{1,7},{2,4},{3,5},{4,2},{5,3},{6,0},{7,1},{8,14},{9,15},{10,... | collective-permute-start | bytes 196616 | tf_op jit(solution)/shard_map/ppermute | solution.py:442
  14.4 0.0 collective-permute-start.1
  14.4 0.8 %collective-permute-start = (f32[1,128,128]{2,1,0:T(8,128)S(1)}, f32[1,128,128]{2,1,0:T(8,128)S(1)}, u32[]{:S(2)}, u32[]{:S(2)}) collective-permute-start(f32[1,128,128]{2,1,0:T(8,128)S(1)} %bitcast.64), channel_id=1, source_target_pairs={{0,2},{1,3},{2,0},{3,1},{4,6},{5,7},{6,4},{7,5},{8,10},{9,11},{10,... | collective-permute-start | bytes 196616 | tf_op jit(solution)/shard_map/ppermute | solution.py:442
  15.2 0.0 copy-done.11
  15.2 0.0 copy-start.9
  15.2 0.0 copy-start.10
  15.2 0.1 reshape.75.vert_ref
  15.3 0.0 copy-start.7
  15.3 0.0 copy-start.8
  15.3 0.6 copy-done.9
  15.8 0.0 copy-done.10
  15.9 0.1 copy-done.7
  16.0 0.0 copy-done.8
  16.0 1.1 %shard_map.139 = (f32[3,32,8,128]{3,2,1,0:T(8,128)S(1)}, bf16[256,1024]{1,0:T(8,128)(2,1)S(1)}, bf16[256,1024]{1,0:T(8,128)(2,1)S(1)}) custom-call(f32[32,2,128]{2,1,0:T(2,128)S(1)} %reshape.75.vert_ref, s32[1,512]{1,0:T(1,128)S(1)} %bitcast.73, s32[1,512]{1,0:T(1,128)S(1)} %bitcast.74, s32[1,512]{1,0:T(1,128)S(1)} %bitcast.75, f32[2,512]{1,0:T(2,128)S(1)} %bitcast.72), custom_call_target="tpu_custom_call" | custom-call | flops 20000000 | bytes 43008 | tf_op jit(solution)/shard_map/pallas_call | solution.py:419
  17.1 0.3 collective-permute-done.2.refs_4_
  17.4 2.3 %collective-permute-done.1.refs_3_ = f32[1,128,128]{2,1,0:T(8,128)S(1)} collective-permute-done((f32[1,128,128]{2,1,0:T(8,128)S(1)}, f32[1,128,128]{2,1,0:T(8,128)S(1)}, u32[]{:S(2)}, u32[]{:S(2)}) %collective-permute-start.1) | collective-permute-done | bytes 65568 | tf_op jit(solution)/shard_map/ppermute | solution.py:442
  19.6 0.0 collective-permute-done.refs_2_
  19.6 0.0 copy-start
  19.6 0.0 copy-start.4
  19.6 0.0 copy-start.5
  19.6 0.0 copy-start.6
  19.7 1.5 %collective-permute-start.7 = (f32[4,128,128]{2,1,0:T(8,128)S(1)}, f32[4,128,128]{2,1,0:T(8,128)S(1)}, u32[]{:S(2)}, u32[]{:S(2)}) collective-permute-start(f32[4,128,128]{2,1,0:T(8,128)S(1)} %shard_map.140._.refs_1_), channel_id=1, source_target_pairs={{0,24},{8,16},{16,8},{24,0},{1,25},{9,17},{17,9},{25,1},{2,26},{10... | collective-permute-start | bytes 786440 | tf_op jit(solution)/shard_map/ppermute | solution.py:442
  21.2 1.5 %collective-permute-start.6 = (f32[4,128,128]{2,1,0:T(8,128)S(1)}, f32[4,128,128]{2,1,0:T(8,128)S(1)}, u32[]{:S(2)}, u32[]{:S(2)}) collective-permute-start(f32[4,128,128]{2,1,0:T(8,128)S(1)} %shard_map.140._.refs_1_), channel_id=1, source_target_pairs={{0,16},{8,24},{16,0},{24,8},{1,17},{9,25},{17,1},{25,9},{2,18},{10... | collective-permute-start | bytes 786440 | tf_op jit(solution)/shard_map/ppermute | solution.py:442
  22.7 0.5 collective-permute-start.5
  23.2 0.0 collective-permute-done.4.cross_ref
  23.2 0.0 collective-permute-done.3.pair_ref
  23.2 0.0 copy-done
  23.2 0.0 copy-done.4
  23.3 0.0 copy-done.5
  23.3 0.0 copy-done.6
  23.3 1.6 %shard_map.142 = (f32[8,32,128]{2,1,0:T(8,128)}, f32[5,16,512]{2,1,0:T(8,128)S(1)}) custom-call(f32[4,128,128]{2,1,0:T(8,128)S(1)} %shard_map.140._.refs_1_, f32[256,128]{1,0:T(8,128)S(1)} %bitcast.53, f32[16,128]{1,0:T(8,128)S(1)} %bitcast.67, f32[16,128]{1,0:T(8,128)S(1)} %bitcast.69, s32[16,128]{1,0:T(8,128)S(1)} %bitcast.71, ...), custom_call_target="tpu_custom_call" | custom-call | flops 4000000 | bytes 729088 | tf_op jit(solution)/shard_map/pallas_call | solution.py:419
  24.9 3.7 %all-to-all-start = ((f32[8,32,128]{2,1,0:T(8,128)}), f32[8,32,128]{2,1,0:T(8,128)S(1)}, u32[]{:S(2)}, u32[]{:S(2)}) async-start(f32[8,32,128]{2,1,0:T(8,128)} %get-tuple-element.16), calls=%async_computation | async-start | bytes 262144 | tf_op jit(solution)/shard_map/all_to_all | solution.py:525
  28.6 1.3 %collective-permute-done.7.refs_4_ = f32[4,128,128]{2,1,0:T(8,128)S(1)} collective-permute-done((f32[4,128,128]{2,1,0:T(8,128)S(1)}, f32[4,128,128]{2,1,0:T(8,128)S(1)}, u32[]{:S(2)}, u32[]{:S(2)}) %collective-permute-start.7) | collective-permute-done | bytes 262176 | tf_op jit(solution)/shard_map/ppermute | solution.py:442
  29.9 3.5 %collective-permute-done.6.refs_3_ = f32[4,128,128]{2,1,0:T(8,128)S(1)} collective-permute-done((f32[4,128,128]{2,1,0:T(8,128)S(1)}, f32[4,128,128]{2,1,0:T(8,128)S(1)}, u32[]{:S(2)}, u32[]{:S(2)}) %collective-permute-start.6) | collective-permute-done | bytes 262176 | tf_op jit(solution)/shard_map/ppermute | solution.py:442
  33.4 0.0 collective-permute-done.5.refs_2_
  33.4 2.0 %all-to-all-done = f32[8,32,128]{2,1,0:T(8,128)S(1)} async-done(((f32[8,32,128]{2,1,0:T(8,128)}), f32[8,32,128]{2,1,0:T(8,128)S(1)}, u32[]{:S(2)}, u32[]{:S(2)}) %all-to-all-start) | async-done | bytes 131104 | tf_op jit(solution)/shard_map/all_to_all | solution.py:525
  35.4 0.1 shard_map.143.near_ref
  35.4 0.1 collective-permute-start.8
  35.5 1.0 %shard_map.144 = (f32[128,512]{1,0:T(8,128)S(1)}, f32[128,512]{1,0:T(8,128)S(1)}) custom-call(f32[256,128]{1,0:T(8,128)S(1)} %bitcast.57, f32[3,32,8,128]{3,2,1,0:T(8,128)S(1)} %get-tuple-element.17.factor_ref, bf16[256,1024]{1,0:T(8,128)(2,1)S(1)} %get-tuple-element.15.refs_0_.high_ref, bf16[256,1024]{1,0:T(8,128)(2,1)S(1)} %get-tuple-element.18.low_ref, ...), custom_call_target="tpu_custom_call" | custom-call | flops 400000000 | bytes 3670016 | tf_op jit(solution)/shard_map/pallas_call | solution.py:419
  36.6 1.6 %collective-permute-done.8.far_ref = f32[16,128,128]{2,1,0:T(8,128)S(1)} collective-permute-done((f32[16,128,128]{2,1,0:T(8,128)S(1)}, f32[16,128,128]{2,1,0:T(8,128)S(1)}, u32[]{:S(2)}, u32[]{:S(2)}) %collective-permute-start.8) | collective-permute-done | bytes 1048608 | tf_op jit(solution)/shard_map/ppermute | solution.py:442
  38.2 1.2 %shard_map.145 = f32[256,128]{1,0:T(8,128)S(1)} custom-call(f32[128,512]{1,0:T(8,128)S(1)} %get-tuple-element.19.near_ref, f32[128,512]{1,0:T(8,128)S(1)} %get-tuple-element.20.profile_ref, f32[3,32,8,128]{3,2,1,0:T(8,128)S(1)} %get-tuple-element.17.factor_ref, bf16[256,1024]{1,0:T(8,128)(2,1)S(1)} %get-tuple-element.15.refs_0_.high_ref, ...), custom_call_target="tpu_custom_call" | custom-call | flops 400000000 | bytes 4063232 | tf_op jit(solution)/shard_map/pallas_call | solution.py:419
  39.4 0.0 copy-start.1
  39.4 9.4 %all_to_all.15.own_ref = f32[8,32,128]{2,1,0:T(8,128)S(1)} all-to-all(f32[8,32,128]{2,1,0:T(8,128)S(1)} %bitcast.58), channel_id=1, replica_groups=mesh['gy'=4,'gx'=8] {'gx'}, dimensions={0} | all-to-all | bytes 262144 | tf_op jit(solution)/shard_map/all_to_all | solution.py:551
  48.8 1.4 %collective-permute-start.10 = (f32[8,32,128]{2,1,0:T(8,128)S(1)}, f32[8,32,128]{2,1,0:T(8,128)S(1)}, u32[]{:S(2)}, u32[]{:S(2)}) collective-permute-start(f32[8,32,128]{2,1,0:T(8,128)S(1)} %all_to_all.15.own_ref), channel_id=1, source_target_pairs={{0,24},{8,16},{16,8},{24,0},{1,25},{9,17},{17,9},{25,1},{2,26},{10... | collective-permute-start | bytes 393224 | tf_op jit(solution)/shard_map/ppermute | solution.py:437
  50.3 0.5 collective-permute-start.9
  50.8 5.3 %collective-permute-done.10.cross_ref = f32[8,32,128]{2,1,0:T(8,128)S(1)} collective-permute-done((f32[8,32,128]{2,1,0:T(8,128)S(1)}, f32[8,32,128]{2,1,0:T(8,128)S(1)}, u32[]{:S(2)}, u32[]{:S(2)}) %collective-permute-start.10) | collective-permute-done | bytes 131104 | tf_op jit(solution)/shard_map/ppermute | solution.py:437
  56.1 0.4 collective-permute-done.9.pair_ref
  56.5 0.0 copy-done.1
  56.5 0.0 copy-start.2
  56.5 1.0 %shard_map.146 = (f32[256,128]{1,0:T(8,128)S(1)}, f32[32,1,128]{2,1,0:T(1,128)S(1)}) custom-call(f32[8,32,128]{2,1,0:T(8,128)S(1)} %all_to_all.15.own_ref, f32[8,32,128]{2,1,0:T(8,128)S(1)} %collective-permute-done.9.pair_ref, f32[8,32,128]{2,1,0:T(8,128)S(1)} %collective-permute-done.10.cross_ref, f32[5,16,512]{2,1,0:T(8,128)S(1)} %get-tuple-element.21.coef_ref, ...), custom_call_target="tpu_custom_call" | custom-call | flops 4000000 | bytes 819200 | tf_op jit(solution)/shard_map/pallas_call | solution.py:419
  57.5 10.7 %all_to_all.16.sums_ref = f32[32,1,128]{2,1,0:T(1,128)S(1)} all-to-all(f32[32,1,128]{2,1,0:T(1,128)S(1)} %get-tuple-element.22), channel_id=1, replica_groups=mesh['gy'=4,'gx'=8] {'gy','gx'}, dimensions={0} | all-to-all | bytes 32768 | tf_op jit(solution)/shard_map/all_to_all | solution.py:562
  68.2 0.0 copy-done.2
  68.2 0.9 %shard_map.147 = (f32[256,128]{1,0:T(8,128)}, f32[256,128]{1,0:T(8,128)}, f32[256,128]{1,0:T(8,128)}) custom-call(f32[32,1,128]{2,1,0:T(1,128)S(1)} %all_to_all.16.sums_ref, f32[256,128]{1,0:T(8,128)S(1)} %bitcast.55, f32[256,128]{1,0:T(8,128)S(1)} %bitcast.61, f32[256,128]{1,0:T(8,128)S(1)} %bitcast.60, f32[256,128]{1,0:T(8,128)S(1)} %get-tuple-element.23.image_ref), custom_call_target="tpu_custom_call" | custom-call | flops 1000000 | bytes 540672 | tf_op jit(solution)/shard_map/pallas_call | solution.py:419
  (1 shorter events, 0.0 us)
Async XLA Ops:
  0.6 10.1 %copy-start.3 = (f32[1,1,128,128]{3,2,1,0:T(8,128)S(1)}, f32[1,1,128,128]{3,2,1,0:T(8,128)}, u32[]{:S(2)}) copy-start(f32[1,1,128,128]{3,2,1,0:T(8,128)} %param.23) | copy-start | bytes 196612
  0.6 14.5 %copy-start.11 = (f32[32,4,64]{2,1,0:T(4,128)S(1)}, f32[32,4,64]{2,1,0:T(4,128)}, u32[]{:S(2)}) copy-start(f32[32,4,64]{2,1,0:T(4,128)} %param.18) | copy-start | bytes 98308
  6.3 17.0 %collective-permute-start.4 = (f32[304,128]{1,0:T(8,128)}, f32[304,128]{1,0:T(8,128)S(1)}, u32[]{:S(2)}, u32[]{:S(2)}) collective-permute-start(f32[304,128]{1,0:T(8,128)} %shard_map.141), channel_id=1, source_target_pairs={{0,24},{8,16},{16,8},{24,0},{1,25},{9,17},{17,9},{25,1},{2,26},{10... | collective-permute-start | bytes 466952 | tf_op jit(solution)/shard_map/ppermute | solution.py:437
  10.2 13.0 %collective-permute-start.3 = (f32[304,128]{1,0:T(8,128)}, f32[304,128]{1,0:T(8,128)S(1)}, u32[]{:S(2)}, u32[]{:S(2)}) collective-permute-start(f32[304,128]{1,0:T(8,128)} %shard_map.141), channel_id=1, source_target_pairs={{0,8},{8,0},{16,24},{24,16},{1,9},{9,1},{17,25},{25,17},{2,10},{10... | collective-permute-start | bytes 466952 | tf_op jit(solution)/shard_map/ppermute | solution.py:436
  10.8 6.6 %collective-permute-start.2 = (f32[1,128,128]{2,1,0:T(8,128)S(1)}, f32[1,128,128]{2,1,0:T(8,128)S(1)}, u32[]{:S(2)}, u32[]{:S(2)}) collective-permute-start(f32[1,128,128]{2,1,0:T(8,128)S(1)} %bitcast.62), channel_id=1, source_target_pairs={{0,6},{1,7},{2,4},{3,5},{4,2},{5,3},{6,0},{7,1},{8,14},{9,15},{10,... | collective-permute-start | bytes 196616 | tf_op jit(solution)/shard_map/ppermute | solution.py:442
  14.4 5.2 %collective-permute-start.1 = (f32[1,128,128]{2,1,0:T(8,128)S(1)}, f32[1,128,128]{2,1,0:T(8,128)S(1)}, u32[]{:S(2)}, u32[]{:S(2)}) collective-permute-start(f32[1,128,128]{2,1,0:T(8,128)S(1)} %bitcast.63), channel_id=1, source_target_pairs={{0,4},{1,5},{2,6},{3,7},{4,0},{5,1},{6,2},{7,3},{8,12},{9,13},{10,... | collective-permute-start | bytes 196616 | tf_op jit(solution)/shard_map/ppermute | solution.py:442
  14.4 5.2 %collective-permute-start = (f32[1,128,128]{2,1,0:T(8,128)S(1)}, f32[1,128,128]{2,1,0:T(8,128)S(1)}, u32[]{:S(2)}, u32[]{:S(2)}) collective-permute-start(f32[1,128,128]{2,1,0:T(8,128)S(1)} %bitcast.64), channel_id=1, source_target_pairs={{0,2},{1,3},{2,0},{3,1},{4,6},{5,7},{6,4},{7,5},{8,10},{9,11},{10,... | collective-permute-start | bytes 196616 | tf_op jit(solution)/shard_map/ppermute | solution.py:442
  15.2 0.7 copy-start.9
  15.2 0.7 %copy-start.10 = (s32[1,1,512]{2,1,0:T(1,128)S(1)}, s32[1,1,512]{2,1,0:T(1,128)}, u32[]{:S(2)}) copy-start(s32[1,1,512]{2,1,0:T(1,128)} %param.21) | copy-start | bytes 6148
  15.3 0.7 copy-start.7
  15.3 0.7 copy-start.8
  19.6 3.6 %copy-start = (f32[4,4,4,512]{3,2,1,0:T(4,128)S(1)}, f32[4,4,4,512]{3,2,1,0:T(4,128)}, u32[]{:S(2)}) copy-start(f32[4,4,4,512]{3,2,1,0:T(4,128)} %param.12) | copy-start | bytes 393220
  19.6 3.6 %copy-start.4 = (f32[4,512]{1,0:T(4,128)S(1)}, f32[4,512]{1,0:T(4,128)}, u32[]{:S(2)}) copy-start(f32[4,512]{1,0:T(4,128)} %param.15) | copy-start | bytes 24580
  19.6 3.6 %copy-start.5 = (f32[4,512]{1,0:T(4,128)S(1)}, f32[4,512]{1,0:T(4,128)}, u32[]{:S(2)}) copy-start(f32[4,512]{1,0:T(4,128)} %param.16) | copy-start | bytes 24580
  19.6 3.6 %copy-start.6 = (s32[4,512]{1,0:T(4,128)S(1)}, s32[4,512]{1,0:T(4,128)}, u32[]{:S(2)}) copy-start(s32[4,512]{1,0:T(4,128)} %param.17) | copy-start | bytes 24580
  19.7 10.2 %collective-permute-start.7 = (f32[4,128,128]{2,1,0:T(8,128)S(1)}, f32[4,128,128]{2,1,0:T(8,128)S(1)}, u32[]{:S(2)}, u32[]{:S(2)}) collective-permute-start(f32[4,128,128]{2,1,0:T(8,128)S(1)} %shard_map.140._.refs_1_), channel_id=1, source_target_pairs={{0,24},{8,16},{16,8},{24,0},{1,25},{9,17},{17,9},{25,1},{2,26},{10... | collective-permute-start | bytes 786440 | tf_op jit(solution)/shard_map/ppermute | solution.py:442
  21.2 12.2 %collective-permute-start.6 = (f32[4,128,128]{2,1,0:T(8,128)S(1)}, f32[4,128,128]{2,1,0:T(8,128)S(1)}, u32[]{:S(2)}, u32[]{:S(2)}) collective-permute-start(f32[4,128,128]{2,1,0:T(8,128)S(1)} %shard_map.140._.refs_1_), channel_id=1, source_target_pairs={{0,16},{8,24},{16,0},{24,8},{1,17},{9,25},{17,1},{25,9},{2,18},{10... | collective-permute-start | bytes 786440 | tf_op jit(solution)/shard_map/ppermute | solution.py:442
  22.7 10.7 %collective-permute-start.5 = (f32[4,128,128]{2,1,0:T(8,128)S(1)}, f32[4,128,128]{2,1,0:T(8,128)S(1)}, u32[]{:S(2)}, u32[]{:S(2)}) collective-permute-start(f32[4,128,128]{2,1,0:T(8,128)S(1)} %shard_map.140._.refs_1_), channel_id=1, source_target_pairs={{0,8},{8,0},{16,24},{24,16},{1,9},{9,1},{17,25},{25,17},{2,10},{10... | collective-permute-start | bytes 786440 | tf_op jit(solution)/shard_map/ppermute | solution.py:442
  24.9 10.5 %all-to-all-start = ((f32[8,32,128]{2,1,0:T(8,128)}), f32[8,32,128]{2,1,0:T(8,128)S(1)}, u32[]{:S(2)}, u32[]{:S(2)}) async-start(f32[8,32,128]{2,1,0:T(8,128)} %get-tuple-element.16), calls=%async_computation | async-start | bytes 262144 | tf_op jit(solution)/shard_map/all_to_all | solution.py:525
  35.4 2.7 %collective-permute-start.8 = (f32[16,128,128]{2,1,0:T(8,128)S(1)}, f32[16,128,128]{2,1,0:T(8,128)S(1)}, u32[]{:S(2)}, u32[]{:S(2)}) collective-permute-start(f32[16,128,128]{2,1,0:T(8,128)S(1)} %shard_map.143.near_ref), channel_id=1, source_target_pairs={{0,1},{1,0},{2,3},{3,2},{4,5},{5,4},{6,7},{7,6},{8,9},{9,8},{10,11... | collective-permute-start | bytes 3145736 | tf_op jit(solution)/shard_map/ppermute | solution.py:442
  39.4 17.1 %copy-start.1 = (f32[4,4,4,512]{3,2,1,0:T(4,128)S(1)}, f32[4,4,4,512]{3,2,1,0:T(4,128)}, u32[]{:S(2)}) copy-start(f32[4,4,4,512]{3,2,1,0:T(4,128)} %param.14) | copy-start | bytes 393220
  48.8 7.2 %collective-permute-start.10 = (f32[8,32,128]{2,1,0:T(8,128)S(1)}, f32[8,32,128]{2,1,0:T(8,128)S(1)}, u32[]{:S(2)}, u32[]{:S(2)}) collective-permute-start(f32[8,32,128]{2,1,0:T(8,128)S(1)} %all_to_all.15.own_ref), channel_id=1, source_target_pairs={{0,24},{8,16},{16,8},{24,0},{1,25},{9,17},{17,9},{25,1},{2,26},{10... | collective-permute-start | bytes 393224 | tf_op jit(solution)/shard_map/ppermute | solution.py:437
  50.3 6.2 %collective-permute-start.9 = (f32[8,32,128]{2,1,0:T(8,128)S(1)}, f32[8,32,128]{2,1,0:T(8,128)S(1)}, u32[]{:S(2)}, u32[]{:S(2)}) collective-permute-start(f32[8,32,128]{2,1,0:T(8,128)S(1)} %all_to_all.15.own_ref), channel_id=1, source_target_pairs={{0,8},{8,0},{16,24},{24,16},{1,9},{9,1},{17,25},{25,17},{2,10},{10... | collective-permute-start | bytes 393224 | tf_op jit(solution)/shard_map/ppermute | solution.py:436
  56.5 11.7 %copy-start.2 = (f32[4,4,4,512]{3,2,1,0:T(4,128)S(1)}, f32[4,4,4,512]{3,2,1,0:T(4,128)}, u32[]{:S(2)}) copy-start(f32[4,4,4,512]{3,2,1,0:T(4,128)} %param.13) | copy-start | bytes 393220

commit v6 on v5

--- a/solution.py
+++ b/solution.py
@@ -75,25 +75,32 @@
         high_ref[...] = jnp.zeros_like(high_ref)
 
 
-def halo_kernel(direction_ref, north_ref, east_ref, ocean_ref, own_ref, mask_ref, ocean_mask_ref, sems):
+def halo_kernel(chunks, direction_ref, north_ref, east_ref, ocean_ref, own_ref, stage_ref, mask_ref, sems):
     cells, size = direction_ref.shape[0], north_ref.shape[0]
-    mask = pltpu.make_async_copy(ocean_ref, mask_ref, sems.at[0])
-    moves = (
-        (direction_ref, own_ref.at[pl.ds(0, cells)]),
-        (north_ref, own_ref.at[pl.ds(cells, size)]),
-        (east_ref, own_ref.at[pl.ds(cells + size, size)]),
-    )
-    copies = [pltpu.make_async_copy(*move, sems.at[1 + at]) for at, move in enumerate(moves)]
-    mask.start()
-    for copy in copies:
+    rows = cells // chunks
+    spans = [(direction_ref.at[pl.ds(at * rows, rows)], at * rows, rows) for at in range(chunks)]
+    spans += [(north_ref, cells, size), (east_ref, cells + size, size)]
+    arrive = [
+        pltpu.make_async_copy(source, stage_ref.at[pl.ds(start, count)], sems.at[0, at])
+        for at, (source, start, count) in enumerate(spans)
+    ]
+    arrive.append(pltpu.make_async_copy(ocean_ref, mask_ref, sems.at[0, len(spans)]))
+    spans.append((ocean_ref, cells + 2 * size, size))
+    leave = [
+        pltpu.make_async_copy(
+            stage_ref.at[pl.ds(start, count)], own_ref.at[pl.ds(start, count)], sems.at[1, at]
+        )
+        for at, (_, start, count) in enumerate(spans)
+    ]
+    for copy in arrive:
         copy.start()
-    mask.wait()
-    ocean_mask_ref[...] = mask_ref[...].astype(jnp.float32)
-    last = pltpu.make_async_copy(ocean_mask_ref, own_ref.at[pl.ds(cells + 2 * size, size)], sems.at[4])
-    last.start()
-    for copy in copies:
+    for at, copy in enumerate(arrive):
         copy.wait()
-    last.wait()
+        if at == len(arrive) - 1:
+            stage_ref[cells + 2 * size : cells + 3 * size, :] = mask_ref[...].astype(jnp.float32)
+        leave[at].start()
+    for copy in leave:
+        copy.wait()
 
 
 def join_kernel(after, count, *refs):
@@ -360,28 +367,19 @@
     return jnp.concatenate(tiles, axis=1)
 
 
-def profile_kernel(
-    layers,
-    held,
-    capacity,
-    packed_ref,
-    factor_ref,
-    high_ref,
-    low_ref,
-    near_ref,
-    weighted_ref,
-    profile_ref,
-    column_ref,
-):
+def smooth_kernel(layers, held, packed_ref, factor_ref, column_ref):
+    def read(layer):
+        return packed_ref[packed_at(layer, held), :]
+
+    def write(layer, value):
+        column_ref[pl.ds(layer, 8, stride=layers), :] = value
+
+    solve_columns(read, write, factor_ref, layers)
+
+
+def profile_kernel(capacity, column_ref, high_ref, low_ref, near_ref, weighted_ref, profile_ref):
     kv = profile_ref.shape[0]
     half = profile_ref.shape[1]
-    def read(layer):
-        return packed_ref[packed_at(layer, held), :]
-
-    def write(layer, value):
-        column_ref[pl.ds(layer, 8, stride=layers), :] = value
-
-    solve_columns(read, write, factor_ref, layers)
     columns = jnp.concatenate([column_ref[0:kv, :], column_ref[kv : 2 * kv, :]], axis=1)
     profile = dot_parts(split(columns), (high_ref[...], low_ref[...]), ((1,), (0,)))
     profile_ref[...] = profile[:, half:]
@@ -472,13 +470,13 @@
     solution_n = to_native(solution)
     faces = [to_native(x[None, None]) for x in (north_coef, east_coef, ocean)]
     own = call(
-        halo_kernel,
+        functools.partial(halo_kernel, 4),
         f32(direction_n.shape[0] + 3 * faces[0].shape[0], LANES),
         (direction_n, *faces),
         scratch=(
+            pltpu.VMEM((direction_n.shape[0] + 3 * faces[0].shape[0], LANES), jnp.float32),
             pltpu.VMEM(faces[0].shape, jnp.int32),
-            pltpu.VMEM(faces[0].shape, jnp.float32),
-            pltpu.SemaphoreType.DMA((5,)),
+            pltpu.SemaphoreType.DMA((2, 7)),
         ),
         hbm=True,
         mib=56,
@@ -523,20 +521,24 @@
     )
     fetched = [held_blocks] + [apart_by(held_blocks, "gy", stride) for stride in range(1, rows_y)]
     columns = lax.all_to_all(packed, "gx", split_axis=0, concat_axis=0, tiled=True)
-    columns = columns.reshape(cols_x * 2 * kv, LANES)
+    smoothed = call(
+        functools.partial(smooth_kernel, layers, held),
+        f32(2 * wide, LANES),
+        (columns.reshape(cols_x * 2 * kv, LANES), factors),
+        flops=400_000_000,
+    )
     near = call(
         functools.partial(join_kernel, 1, len(fetched)),
         f32(device_count // 2, wide, wide),
-        (columns, *fetched),
+        (smoothed, *fetched),
         after=1,
     )
     far = apart_by(near, "gx", 1)
     half = device_count // 2 * capacity
     weighted, profile = call(
-        functools.partial(profile_kernel, layers, held, capacity),
+        functools.partial(profile_kernel, capacity),
         (f32(wide, half), f32(wide, half)),
-        (columns, factors, *interp, near),
-        scratch=(pltpu.VMEM((2 * wide, LANES), jnp.float32),),
+        (smoothed, *interp, near),
         flops=400_000_000,
         mib=16,
     )

time: 69.5 us -> 72.5 us (1.043)
  waiting for transfers between devices: 16.6 us -> 21.5 us
  Pallas kernels: 12.6 us -> 8.55 us
  blocking collectives: 20.1 us -> 21.4 us
  local copies, waits for them, and re-layouts: 0.82 us -> 1.65 us
    pallas_call x9 -> x10, Pallas kernels: 12.6 us -> 8.55 us  [call(): pl.pallas_call(kernel, out_shape=out_shape, in_specs=specs, out_specs=tup...]
    ppermute x7, waiting for transfers between devices: 8.91 us -> 12.5 us  [apart_by(): lax.ppermute(block, axis, [(i, i ^ stride) for i in range(lax.axis_size(a...]
    all_to_all x1, blocking collectives: 9.4 us -> 11.4 us  [per_device_gathered(): lax.all_to_all(spread.reshape(cols_x, 2 * kv, LANES), 'gx', split_axis=0,...]
    all_to_all x1, waiting for transfers between devices: 1.98 us -> 3.29 us  [per_device_gathered(): lax.all_to_all(packed, 'gx', split_axis=0, concat_axis=0, tiled=True)]
    unnamed x24, local copies, waits for them, and re-layouts: 0.72 us -> 1.55 us
    all_to_all x1, blocking collectives: 10.7 us -> 9.92 us  [per_device_gathered(): lax.all_to_all(sums, ('gy', 'gx'), split_axis=0, concat_axis=0, tiled=True)]
  transfers between devices with their start and end apart: 12 -> 12, of which waited for: 8 -> 8; matrix products, arithmetic and copies ran while one was open for 0% -> 0% of each run, Pallas kernels for 5% -> 3%
where the time goes in v6:
time: 72.5 us; the launch traced here: 72.1 us
  waiting for transfers between devices  21.5 us (30%)
  blocking collectives  21.4 us (30%)
  starting transfers between devices  18.3 us (25%)
  Pallas kernels  8.55 us (12%)
  local copies, waits for them, and re-layouts  1.65 us (2%)
  between operations  0.77 us (1%)
    ppermute x7, waiting for transfers between devices, apart_by(): lax.ppermute(block, axis, [(i, i ^ stride) for i in range(lax.axis_size(a...  12.5 us
    all_to_all x1, blocking collectives, per_device_gathered(): lax.all_to_all(spread.reshape(cols_x, 2 * kv, LANES), 'gx', split_axis=0,...  11.4 us
    all_to_all x1, blocking collectives, per_device_gathered(): lax.all_to_all(sums, ('gy', 'gx'), split_axis=0, concat_axis=0, tiled=True)  9.92 us
    pallas_call x10, Pallas kernels, call(): pl.pallas_call(kernel, out_shape=out_shape, in_specs=specs, out_specs=tup...  8.55 us
    ppermute x7, starting transfers between devices, apart_by(): lax.ppermute(block, axis, [(i, i ^ stride) for i in range(lax.axis_size(a...  7.98 us
    ppermute x2, starting transfers between devices, from_neighbours(): lax.ppermute(block, 'gy', [(i, (i + (1 if i % 2 else -1)) % count) for i...  5.48 us
    ppermute x2, waiting for transfers between devices, from_neighbours(): lax.ppermute(block, 'gy', [(i, (i + (1 if i % 2 else -1)) % count) for i...  5.17 us
    all_to_all x1, starting transfers between devices, per_device_gathered(): lax.all_to_all(packed, 'gx', split_axis=0, concat_axis=0, tiled=True)  3.71 us
  transfers between devices with their start and end apart: 12, of which 8 were waited for; matrix products, arithmetic and copies ran while one was open for 0% of the time, Pallas kernels for 3%

profile of v6, /device:TPU:0, one launch (start us, length us, event | category | flops | bytes accessed | tf_op | source)
XLA Modules:
  0.0 72.1 jit_solution(1678814734077178217)
XLA Ops:
  0.6 0.0 copy-start.3
  0.6 0.0 copy-start.11
  0.7 1.6 %shard_map.141 = f32[304,128]{1,0:T(8,128)} custom-call(f32[256,128]{1,0:T(8,128)} %bitcast.52, f32[16,128]{1,0:T(8,128)} %bitcast.65, f32[16,128]{1,0:T(8,128)} %bitcast.67, s32[16,128]{1,0:T(8,128)} %bitcast.69), custom_call_target="tpu_custom_call" | custom-call | flops 1000000 | bytes 155648 | tf_op jit(solution)/shard_map/pallas_call | solution.py:417
  2.2 4.0 %collective-permute-start.4 = (f32[304,128]{1,0:T(8,128)}, f32[304,128]{1,0:T(8,128)S(1)}, u32[]{:S(2)}, u32[]{:S(2)}) collective-permute-start(f32[304,128]{1,0:T(8,128)} %shard_map.141), channel_id=1, source_target_pairs={{0,24},{8,16},{16,8},{24,0},{1,25},{9,17},{17,9},{25,1},{2,26},{10... | collective-permute-start | bytes 466952 | tf_op jit(solution)/shard_map/ppermute | solution.py:435
  6.2 0.5 collective-permute-start.3
  6.7 0.0 copy-done.3
  6.7 3.6 %collective-permute-start.2 = (f32[1,128,128]{2,1,0:T(8,128)S(1)}, f32[1,128,128]{2,1,0:T(8,128)S(1)}, u32[]{:S(2)}, u32[]{:S(2)}) collective-permute-start(f32[1,128,128]{2,1,0:T(8,128)S(1)} %bitcast.61), channel_id=1, source_target_pairs={{0,6},{1,7},{2,4},{3,5},{4,2},{5,3},{6,0},{7,1},{8,14},{9,15},{10,... | collective-permute-start | bytes 196616 | tf_op jit(solution)/shard_map/ppermute | solution.py:440
  10.3 0.0 collective-permute-start.1
  10.4 0.8 %collective-permute-start = (f32[1,128,128]{2,1,0:T(8,128)S(1)}, f32[1,128,128]{2,1,0:T(8,128)S(1)}, u32[]{:S(2)}, u32[]{:S(2)}) collective-permute-start(f32[1,128,128]{2,1,0:T(8,128)S(1)} %bitcast.63), channel_id=1, source_target_pairs={{0,2},{1,3},{2,0},{3,1},{4,6},{5,7},{6,4},{7,5},{8,10},{9,11},{10,... | collective-permute-start | bytes 196616 | tf_op jit(solution)/shard_map/ppermute | solution.py:440
  11.1 0.0 copy-done.11
  11.1 0.0 copy-start.9
  11.1 0.0 copy-start.10
  11.1 0.1 reshape.75.vert_ref
  11.2 0.0 copy-start.7
  11.3 0.0 copy-start.8
  11.3 0.6 copy-done.9
  11.8 0.0 copy-done.10
  11.8 0.1 copy-done.7
  11.9 0.0 copy-done.8
  11.9 1.1 %shard_map.139 = (f32[3,32,8,128]{3,2,1,0:T(8,128)S(1)}, bf16[256,1024]{1,0:T(8,128)(2,1)S(1)}, bf16[256,1024]{1,0:T(8,128)(2,1)S(1)}) custom-call(f32[32,2,128]{2,1,0:T(2,128)S(1)} %reshape.75.vert_ref, s32[1,512]{1,0:T(1,128)S(1)} %bitcast.72, s32[1,512]{1,0:T(1,128)S(1)} %bitcast.73, s32[1,512]{1,0:T(1,128)S(1)} %bitcast.74, f32[2,512]{1,0:T(2,128)S(1)} %bitcast.71), custom_call_target="tpu_custom_call" | custom-call | flops 20000000 | bytes 43008 | tf_op jit(solution)/shard_map/pallas_call | solution.py:417
  13.1 0.3 collective-permute-done.2.refs_4_
  13.3 2.3 %collective-permute-done.1.refs_3_ = f32[1,128,128]{2,1,0:T(8,128)S(1)} collective-permute-done((f32[1,128,128]{2,1,0:T(8,128)S(1)}, f32[1,128,128]{2,1,0:T(8,128)S(1)}, u32[]{:S(2)}, u32[]{:S(2)}) %collective-permute-start.1) | collective-permute-done | bytes 65568 | tf_op jit(solution)/shard_map/ppermute | solution.py:440
  15.6 0.0 collective-permute-done.refs_2_
  15.6 0.0 copy-start
  15.6 0.0 copy-start.4
  15.6 0.0 copy-start.5
  15.6 0.0 copy-start.6
  15.7 0.0 collective-permute-done.4.cross_ref
  15.7 0.0 collective-permute-done.3.pair_ref
  15.7 0.8 %copy-done = f32[4,4,4,512]{3,2,1,0:T(4,128)S(1)} copy-done((f32[4,4,4,512]{3,2,1,0:T(4,128)S(1)}, f32[4,4,4,512]{3,2,1,0:T(4,128)}, u32[]{:S(2)}) %copy-start) | copy-done | bytes 131096
  16.5 0.0 copy-done.4
  16.5 0.0 copy-done.5
  16.5 0.0 copy-done.6
  16.5 1.6 %shard_map.142 = (f32[8,32,128]{2,1,0:T(8,128)}, f32[5,16,512]{2,1,0:T(8,128)S(1)}) custom-call(f32[4,128,128]{2,1,0:T(8,128)S(1)} %shard_map.140._.refs_1_, f32[256,128]{1,0:T(8,128)S(1)} %bitcast.53, f32[16,128]{1,0:T(8,128)S(1)} %bitcast.66, f32[16,128]{1,0:T(8,128)S(1)} %bitcast.68, s32[16,128]{1,0:T(8,128)S(1)} %bitcast.70, ...), custom_call_target="tpu_custom_call" | custom-call | flops 4000000 | bytes 729088 | tf_op jit(solution)/shard_map/pallas_call | solution.py:417
  18.1 3.7 %all-to-all-start = ((f32[8,32,128]{2,1,0:T(8,128)}), f32[8,32,128]{2,1,0:T(8,128)S(1)}, u32[]{:S(2)}, u32[]{:S(2)}) async-start(f32[8,32,128]{2,1,0:T(8,128)} %get-tuple-element.16), calls=%async_computation | async-start | bytes 262144 | tf_op jit(solution)/shard_map/all_to_all | solution.py:523
  21.8 1.4 %collective-permute-start.7 = (f32[4,128,128]{2,1,0:T(8,128)S(1)}, f32[4,128,128]{2,1,0:T(8,128)S(1)}, u32[]{:S(2)}, u32[]{:S(2)}) collective-permute-start(f32[4,128,128]{2,1,0:T(8,128)S(1)} %shard_map.140._.refs_1_), channel_id=1, source_target_pairs={{0,24},{8,16},{16,8},{24,0},{1,25},{9,17},{17,9},{25,1},{2,26},{10... | collective-permute-start | bytes 786440 | tf_op jit(solution)/shard_map/ppermute | solution.py:440
  23.2 1.5 %collective-permute-start.6 = (f32[4,128,128]{2,1,0:T(8,128)S(1)}, f32[4,128,128]{2,1,0:T(8,128)S(1)}, u32[]{:S(2)}, u32[]{:S(2)}) collective-permute-start(f32[4,128,128]{2,1,0:T(8,128)S(1)} %shard_map.140._.refs_1_), channel_id=1, source_target_pairs={{0,16},{8,24},{16,0},{24,8},{1,17},{9,25},{17,1},{25,9},{2,18},{10... | collective-permute-start | bytes 786440 | tf_op jit(solution)/shard_map/ppermute | solution.py:440
  24.8 0.5 collective-permute-start.5
  25.3 3.3 %all-to-all-done = f32[8,32,128]{2,1,0:T(8,128)S(1)} async-done(((f32[8,32,128]{2,1,0:T(8,128)}), f32[8,32,128]{2,1,0:T(8,128)S(1)}, u32[]{:S(2)}, u32[]{:S(2)}) %all-to-all-start) | async-done | bytes 131104 | tf_op jit(solution)/shard_map/all_to_all | solution.py:523
  28.6 0.1 shard_map.143.refs_0_.column_ref
  28.7 3.1 %collective-permute-done.7.refs_4_ = f32[4,128,128]{2,1,0:T(8,128)S(1)} collective-permute-done((f32[4,128,128]{2,1,0:T(8,128)S(1)}, f32[4,128,128]{2,1,0:T(8,128)S(1)}, u32[]{:S(2)}, u32[]{:S(2)}) %collective-permute-start.7) | collective-permute-done | bytes 262176 | tf_op jit(solution)/shard_map/ppermute | solution.py:440
  31.9 5.2 %collective-permute-done.6.refs_3_ = f32[4,128,128]{2,1,0:T(8,128)S(1)} collective-permute-done((f32[4,128,128]{2,1,0:T(8,128)S(1)}, f32[4,128,128]{2,1,0:T(8,128)S(1)}, u32[]{:S(2)}, u32[]{:S(2)}) %collective-permute-start.6) | collective-permute-done | bytes 262176 | tf_op jit(solution)/shard_map/ppermute | solution.py:440
  37.0 0.0 collective-permute-done.5.refs_2_
  37.1 0.1 shard_map.144.near_ref
  37.1 0.1 collective-permute-start.8
  37.2 0.9 %shard_map.145 = (f32[128,512]{1,0:T(8,128)S(1)}, f32[128,512]{1,0:T(8,128)S(1)}) custom-call(f32[256,128]{1,0:T(8,128)S(1)} %shard_map.143.refs_0_.column_ref, bf16[256,1024]{1,0:T(8,128)(2,1)S(1)} %get-tuple-element.15.refs_0_.high_ref, bf16[256,1024]{1,0:T(8,128)(2,1)S(1)} %get-tuple-element.18.low_ref, f32[16,128,128]{2,1,0:T(8,128)S(1)} %shard_map.144.near_ref), custom_call_target="tpu_custom_call" | custom-call | flops 400000000 | bytes 3276800 | tf_op jit(solution)/shard_map/pallas_call | solution.py:417
  38.2 1.7 %collective-permute-done.8.far_ref = f32[16,128,128]{2,1,0:T(8,128)S(1)} collective-permute-done((f32[16,128,128]{2,1,0:T(8,128)S(1)}, f32[16,128,128]{2,1,0:T(8,128)S(1)}, u32[]{:S(2)}, u32[]{:S(2)}) %collective-permute-start.8) | collective-permute-done | bytes 1048608 | tf_op jit(solution)/shard_map/ppermute | solution.py:440
  39.9 1.2 %shard_map.146 = f32[256,128]{1,0:T(8,128)S(1)} custom-call(f32[128,512]{1,0:T(8,128)S(1)} %get-tuple-element.19.near_ref, f32[128,512]{1,0:T(8,128)S(1)} %get-tuple-element.20.profile_ref, f32[3,32,8,128]{3,2,1,0:T(8,128)S(1)} %get-tuple-element.17.factor_ref, bf16[256,1024]{1,0:T(8,128)(2,1)S(1)} %get-tuple-element.15.refs_0_.high_ref, ...), custom_call_target="tpu_custom_call" | custom-call | flops 400000000 | bytes 4063232 | tf_op jit(solution)/shard_map/pallas_call | solution.py:417
  41.1 0.0 copy-start.1
  41.1 11.4 %all_to_all.15.own_ref = f32[8,32,128]{2,1,0:T(8,128)S(1)} all-to-all(f32[8,32,128]{2,1,0:T(8,128)S(1)} %bitcast.56), channel_id=1, replica_groups=mesh['gy'=4,'gx'=8] {'gx'}, dimensions={0} | all-to-all | bytes 262144 | tf_op jit(solution)/shard_map/all_to_all | solution.py:553
  52.6 1.5 %collective-permute-start.10 = (f32[8,32,128]{2,1,0:T(8,128)S(1)}, f32[8,32,128]{2,1,0:T(8,128)S(1)}, u32[]{:S(2)}, u32[]{:S(2)}) collective-permute-start(f32[8,32,128]{2,1,0:T(8,128)S(1)} %all_to_all.15.own_ref), channel_id=1, source_target_pairs={{0,24},{8,16},{16,8},{24,0},{1,25},{9,17},{17,9},{25,1},{2,26},{10... | collective-permute-start | bytes 393224 | tf_op jit(solution)/shard_map/ppermute | solution.py:435
  54.1 0.5 collective-permute-start.9
  54.6 5.2 %collective-permute-done.10.cross_ref = f32[8,32,128]{2,1,0:T(8,128)S(1)} collective-permute-done((f32[8,32,128]{2,1,0:T(8,128)S(1)}, f32[8,32,128]{2,1,0:T(8,128)S(1)}, u32[]{:S(2)}, u32[]{:S(2)}) %collective-permute-start.10) | collective-permute-done | bytes 131104 | tf_op jit(solution)/shard_map/ppermute | solution.py:435
  59.8 0.5 collective-permute-done.9.pair_ref
  60.3 0.0 copy-done.1
  60.3 0.0 copy-start.2
  60.4 1.0 %shard_map.147 = (f32[256,128]{1,0:T(8,128)S(1)}, f32[32,1,128]{2,1,0:T(1,128)S(1)}) custom-call(f32[8,32,128]{2,1,0:T(8,128)S(1)} %all_to_all.15.own_ref, f32[8,32,128]{2,1,0:T(8,128)S(1)} %collective-permute-done.9.pair_ref, f32[8,32,128]{2,1,0:T(8,128)S(1)} %collective-permute-done.10.cross_ref, f32[5,16,512]{2,1,0:T(8,128)S(1)} %get-tuple-element.21.coef_ref, ...), custom_call_target="tpu_custom_call" | custom-call | flops 4000000 | bytes 819200 | tf_op jit(solution)/shard_map/pallas_call | solution.py:417
  61.3 9.9 %all_to_all.16.sums_ref = f32[32,1,128]{2,1,0:T(1,128)S(1)} all-to-all(f32[32,1,128]{2,1,0:T(1,128)S(1)} %get-tuple-element.22), channel_id=1, replica_groups=mesh['gy'=4,'gx'=8] {'gy','gx'}, dimensions={0} | all-to-all | bytes 32768 | tf_op jit(solution)/shard_map/all_to_all | solution.py:564
  71.2 0.0 copy-done.2
  71.2 0.9 %shard_map.148 = (f32[256,128]{1,0:T(8,128)}, f32[256,128]{1,0:T(8,128)}, f32[256,128]{1,0:T(8,128)}) custom-call(f32[32,1,128]{2,1,0:T(1,128)S(1)} %all_to_all.16.sums_ref, f32[256,128]{1,0:T(8,128)S(1)} %bitcast.55, f32[256,128]{1,0:T(8,128)S(1)} %bitcast.60, f32[256,128]{1,0:T(8,128)S(1)} %bitcast.58, f32[256,128]{1,0:T(8,128)S(1)} %get-tuple-element.23.image_ref), custom_call_target="tpu_custom_call" | custom-call | flops 1000000 | bytes 540672 | tf_op jit(solution)/shard_map/pallas_call | solution.py:417
  (1 shorter events, 0.0 us)
Async XLA Ops:
  0.6 6.1 %copy-start.3 = (f32[1,1,128,128]{3,2,1,0:T(8,128)S(1)}, f32[1,1,128,128]{3,2,1,0:T(8,128)}, u32[]{:S(2)}) copy-start(f32[1,1,128,128]{3,2,1,0:T(8,128)} %param.23) | copy-start | bytes 196612
  0.6 10.5 %copy-start.11 = (f32[32,4,64]{2,1,0:T(4,128)S(1)}, f32[32,4,64]{2,1,0:T(4,128)}, u32[]{:S(2)}) copy-start(f32[32,4,64]{2,1,0:T(4,128)} %param.18) | copy-start | bytes 98308
  2.2 13.4 %collective-permute-start.4 = (f32[304,128]{1,0:T(8,128)}, f32[304,128]{1,0:T(8,128)S(1)}, u32[]{:S(2)}, u32[]{:S(2)}) collective-permute-start(f32[304,128]{1,0:T(8,128)} %shard_map.141), channel_id=1, source_target_pairs={{0,24},{8,16},{16,8},{24,0},{1,25},{9,17},{17,9},{25,1},{2,26},{10... | collective-permute-start | bytes 466952 | tf_op jit(solution)/shard_map/ppermute | solution.py:435
  6.2 9.5 %collective-permute-start.3 = (f32[304,128]{1,0:T(8,128)}, f32[304,128]{1,0:T(8,128)S(1)}, u32[]{:S(2)}, u32[]{:S(2)}) collective-permute-start(f32[304,128]{1,0:T(8,128)} %shard_map.141), channel_id=1, source_target_pairs={{0,8},{8,0},{16,24},{24,16},{1,9},{9,1},{17,25},{25,17},{2,10},{10... | collective-permute-start | bytes 466952 | tf_op jit(solution)/shard_map/ppermute | solution.py:434
  6.7 6.6 %collective-permute-start.2 = (f32[1,128,128]{2,1,0:T(8,128)S(1)}, f32[1,128,128]{2,1,0:T(8,128)S(1)}, u32[]{:S(2)}, u32[]{:S(2)}) collective-permute-start(f32[1,128,128]{2,1,0:T(8,128)S(1)} %bitcast.61), channel_id=1, source_target_pairs={{0,6},{1,7},{2,4},{3,5},{4,2},{5,3},{6,0},{7,1},{8,14},{9,15},{10,... | collective-permute-start | bytes 196616 | tf_op jit(solution)/shard_map/ppermute | solution.py:440
  10.3 5.2 %collective-permute-start.1 = (f32[1,128,128]{2,1,0:T(8,128)S(1)}, f32[1,128,128]{2,1,0:T(8,128)S(1)}, u32[]{:S(2)}, u32[]{:S(2)}) collective-permute-start(f32[1,128,128]{2,1,0:T(8,128)S(1)} %bitcast.62), channel_id=1, source_target_pairs={{0,4},{1,5},{2,6},{3,7},{4,0},{5,1},{6,2},{7,3},{8,12},{9,13},{10,... | collective-permute-start | bytes 196616 | tf_op jit(solution)/shard_map/ppermute | solution.py:440
  10.4 5.2 %collective-permute-start = (f32[1,128,128]{2,1,0:T(8,128)S(1)}, f32[1,128,128]{2,1,0:T(8,128)S(1)}, u32[]{:S(2)}, u32[]{:S(2)}) collective-permute-start(f32[1,128,128]{2,1,0:T(8,128)S(1)} %bitcast.63), channel_id=1, source_target_pairs={{0,2},{1,3},{2,0},{3,1},{4,6},{5,7},{6,4},{7,5},{8,10},{9,11},{10,... | collective-permute-start | bytes 196616 | tf_op jit(solution)/shard_map/ppermute | solution.py:440
  11.1 0.7 copy-start.9
  11.1 0.7 copy-start.10
  11.2 0.7 copy-start.7
  11.3 0.7 copy-start.8
  15.6 0.9 %copy-start = (f32[4,4,4,512]{3,2,1,0:T(4,128)S(1)}, f32[4,4,4,512]{3,2,1,0:T(4,128)}, u32[]{:S(2)}) copy-start(f32[4,4,4,512]{3,2,1,0:T(4,128)} %param.12) | copy-start | bytes 393220
  15.6 0.9 %copy-start.4 = (f32[4,512]{1,0:T(4,128)S(1)}, f32[4,512]{1,0:T(4,128)}, u32[]{:S(2)}) copy-start(f32[4,512]{1,0:T(4,128)} %param.15) | copy-start | bytes 24580
  15.6 0.9 %copy-start.5 = (f32[4,512]{1,0:T(4,128)S(1)}, f32[4,512]{1,0:T(4,128)}, u32[]{:S(2)}) copy-start(f32[4,512]{1,0:T(4,128)} %param.16) | copy-start | bytes 24580
  15.6 0.9 %copy-start.6 = (s32[4,512]{1,0:T(4,128)S(1)}, s32[4,512]{1,0:T(4,128)}, u32[]{:S(2)}) copy-start(s32[4,512]{1,0:T(4,128)} %param.17) | copy-start | bytes 24580
  18.1 10.5 %all-to-all-start = ((f32[8,32,128]{2,1,0:T(8,128)}), f32[8,32,128]{2,1,0:T(8,128)S(1)}, u32[]{:S(2)}, u32[]{:S(2)}) async-start(f32[8,32,128]{2,1,0:T(8,128)} %get-tuple-element.16), calls=%async_computation | async-start | bytes 262144 | tf_op jit(solution)/shard_map/all_to_all | solution.py:523
  21.8 10.0 %collective-permute-start.7 = (f32[4,128,128]{2,1,0:T(8,128)S(1)}, f32[4,128,128]{2,1,0:T(8,128)S(1)}, u32[]{:S(2)}, u32[]{:S(2)}) collective-permute-start(f32[4,128,128]{2,1,0:T(8,128)S(1)} %shard_map.140._.refs_1_), channel_id=1, source_target_pairs={{0,24},{8,16},{16,8},{24,0},{1,25},{9,17},{17,9},{25,1},{2,26},{10... | collective-permute-start | bytes 786440 | tf_op jit(solution)/shard_map/ppermute | solution.py:440
  23.2 13.8 %collective-permute-start.6 = (f32[4,128,128]{2,1,0:T(8,128)S(1)}, f32[4,128,128]{2,1,0:T(8,128)S(1)}, u32[]{:S(2)}, u32[]{:S(2)}) collective-permute-start(f32[4,128,128]{2,1,0:T(8,128)S(1)} %shard_map.140._.refs_1_), channel_id=1, source_target_pairs={{0,16},{8,24},{16,0},{24,8},{1,17},{9,25},{17,1},{25,9},{2,18},{10... | collective-permute-start | bytes 786440 | tf_op jit(solution)/shard_map/ppermute | solution.py:440
  24.8 12.3 %collective-permute-start.5 = (f32[4,128,128]{2,1,0:T(8,128)S(1)}, f32[4,128,128]{2,1,0:T(8,128)S(1)}, u32[]{:S(2)}, u32[]{:S(2)}) collective-permute-start(f32[4,128,128]{2,1,0:T(8,128)S(1)} %shard_map.140._.refs_1_), channel_id=1, source_target_pairs={{0,8},{8,0},{16,24},{24,16},{1,9},{9,1},{17,25},{25,17},{2,10},{10... | collective-permute-start | bytes 786440 | tf_op jit(solution)/shard_map/ppermute | solution.py:440
  37.1 2.7 %collective-permute-start.8 = (f32[16,128,128]{2,1,0:T(8,128)S(1)}, f32[16,128,128]{2,1,0:T(8,128)S(1)}, u32[]{:S(2)}, u32[]{:S(2)}) collective-permute-start(f32[16,128,128]{2,1,0:T(8,128)S(1)} %shard_map.144.near_ref), channel_id=1, source_target_pairs={{0,1},{1,0},{2,3},{3,2},{4,5},{5,4},{6,7},{7,6},{8,9},{9,8},{10,11... | collective-permute-start | bytes 3145736 | tf_op jit(solution)/shard_map/ppermute | solution.py:440
  41.1 19.3 %copy-start.1 = (f32[4,4,4,512]{3,2,1,0:T(4,128)S(1)}, f32[4,4,4,512]{3,2,1,0:T(4,128)}, u32[]{:S(2)}) copy-start(f32[4,4,4,512]{3,2,1,0:T(4,128)} %param.14) | copy-start | bytes 393220
  52.6 7.2 %collective-permute-start.10 = (f32[8,32,128]{2,1,0:T(8,128)S(1)}, f32[8,32,128]{2,1,0:T(8,128)S(1)}, u32[]{:S(2)}, u32[]{:S(2)}) collective-permute-start(f32[8,32,128]{2,1,0:T(8,128)S(1)} %all_to_all.15.own_ref), channel_id=1, source_target_pairs={{0,24},{8,16},{16,8},{24,0},{1,25},{9,17},{17,9},{25,1},{2,26},{10... | collective-permute-start | bytes 393224 | tf_op jit(solution)/shard_map/ppermute | solution.py:435
  54.1 6.3 %collective-permute-start.9 = (f32[8,32,128]{2,1,0:T(8,128)S(1)}, f32[8,32,128]{2,1,0:T(8,128)S(1)}, u32[]{:S(2)}, u32[]{:S(2)}) collective-permute-start(f32[8,32,128]{2,1,0:T(8,128)S(1)} %all_to_all.15.own_ref), channel_id=1, source_target_pairs={{0,8},{8,0},{16,24},{24,16},{1,9},{9,1},{17,25},{25,17},{2,10},{10... | collective-permute-start | bytes 393224 | tf_op jit(solution)/shard_map/ppermute | solution.py:434
  60.3 10.9 %copy-start.2 = (f32[4,4,4,512]{3,2,1,0:T(4,128)S(1)}, f32[4,4,4,512]{3,2,1,0:T(4,128)}, u32[]{:S(2)}) copy-start(f32[4,4,4,512]{3,2,1,0:T(4,128)} %param.13) | copy-start | bytes 393220

commit v7 on v6

--- a/solution.py
+++ b/solution.py
@@ -525,7 +525,7 @@
         functools.partial(smooth_kernel, layers, held),
         f32(2 * wide, LANES),
         (columns.reshape(cols_x * 2 * kv, LANES), factors),
-        flops=400_000_000,
+        flops=1000,
     )
     near = call(
         functools.partial(join_kernel, 1, len(fetched)),

time: 72.5 us -> 64.7 us (0.89)
  waiting for transfers between devices: 21.5 us -> 9.96 us
  blocking collectives: 21.4 us -> 30.4 us
  starting transfers between devices: 18.3 us -> 14.5 us
  local copies, waits for them, and re-layouts: 1.65 us -> 0.82 us
    all_to_all x0 -> x1, blocking collectives: none -> 10.3 us  [per_device_gathered(): lax.all_to_all(packed, 'gx', split_axis=0, concat_axis=0, tiled=True)]
    ppermute x7, waiting for transfers between devices: 12.5 us -> 4.24 us  [apart_by(): lax.ppermute(block, axis, [(i, i ^ stride) for i in range(lax.axis_size(a...]
    all_to_all x1 -> x0, starting transfers between devices: 3.71 us -> none  [per_device_gathered(): lax.all_to_all(packed, 'gx', split_axis=0, concat_axis=0, tiled=True)]
    all_to_all x1 -> x0, waiting for transfers between devices: 3.29 us -> none  [per_device_gathered(): lax.all_to_all(packed, 'gx', split_axis=0, concat_axis=0, tiled=True)]
    all_to_all x1, blocking collectives: 11.4 us -> 9.4 us  [per_device_gathered(): lax.all_to_all(spread.reshape(cols_x, 2 * kv, LANES), 'gx', split_axis=0,...]
    unnamed x24, local copies, waits for them, and re-layouts: 1.55 us -> 0.72 us
    all_to_all x1, blocking collectives: 9.92 us -> 10.7 us  [per_device_gathered(): lax.all_to_all(sums, ('gy', 'gx'), split_axis=0, concat_axis=0, tiled=True)]
  transfers between devices with their start and end apart: 12 -> 11, of which waited for: 8 -> 5; matrix products, arithmetic and copies ran while one was open for 0% -> 0% of each run, Pallas kernels for 3% -> 5%
where the time goes in v7:
time: 64.7 us; the launch traced here: 64.4 us
  blocking collectives  30.4 us (47%)
  starting transfers between devices  14.5 us (22%)
  waiting for transfers between devices  9.96 us (15%)
  Pallas kernels  7.9 us (12%)
  local copies, waits for them, and re-layouts  0.82 us (1%)
  between operations  0.82 us (1%)
    all_to_all x1, blocking collectives, per_device_gathered(): lax.all_to_all(sums, ('gy', 'gx'), split_axis=0, concat_axis=0, tiled=True)  10.7 us
    all_to_all x1, blocking collectives, per_device_gathered(): lax.all_to_all(packed, 'gx', split_axis=0, concat_axis=0, tiled=True)  10.3 us
    all_to_all x1, blocking collectives, per_device_gathered(): lax.all_to_all(spread.reshape(cols_x, 2 * kv, LANES), 'gx', split_axis=0,...  9.4 us
    ppermute x7, starting transfers between devices, apart_by(): lax.ppermute(block, axis, [(i, i ^ stride) for i in range(lax.axis_size(a...  8.01 us
    pallas_call x10, Pallas kernels, call(): pl.pallas_call(kernel, out_shape=out_shape, in_specs=specs, out_specs=tup...  7.9 us
    ppermute x2, starting transfers between devices, from_neighbours(): lax.ppermute(block, 'gy', [(i, (i + (1 if i % 2 else -1)) % count) for i...  5.39 us
    ppermute x2, waiting for transfers between devices, from_neighbours(): lax.ppermute(block, 'gy', [(i, (i + (1 if i % 2 else -1)) % count) for i...  5.28 us
    ppermute x7, waiting for transfers between devices, apart_by(): lax.ppermute(block, axis, [(i, i ^ stride) for i in range(lax.axis_size(a...  4.24 us
  transfers between devices with their start and end apart: 11, of which 5 were waited for; matrix products, arithmetic and copies ran while one was open for 0% of the time, Pallas kernels for 5%

profile of v7, /device:TPU:0, one launch (start us, length us, event | category | flops | bytes accessed | tf_op | source)
XLA Modules:
  0.0 64.4 jit_solution(1320905240909418494)
XLA Ops:
  0.6 0.0 copy-start.3
  0.6 0.0 copy-start.11
  0.7 1.6 %shard_map.141 = f32[304,128]{1,0:T(8,128)} custom-call(f32[256,128]{1,0:T(8,128)} %bitcast.52, f32[16,128]{1,0:T(8,128)} %bitcast.65, f32[16,128]{1,0:T(8,128)} %bitcast.67, s32[16,128]{1,0:T(8,128)} %bitcast.69), custom_call_target="tpu_custom_call" | custom-call | flops 1000000 | bytes 155648 | tf_op jit(solution)/shard_map/pallas_call | solution.py:417
  2.3 4.0 %collective-permute-start.4 = (f32[304,128]{1,0:T(8,128)}, f32[304,128]{1,0:T(8,128)S(1)}, u32[]{:S(2)}, u32[]{:S(2)}) collective-permute-start(f32[304,128]{1,0:T(8,128)} %shard_map.141), channel_id=1, source_target_pairs={{0,24},{8,16},{16,8},{24,0},{1,25},{9,17},{17,9},{25,1},{2,26},{10... | collective-permute-start | bytes 466952 | tf_op jit(solution)/shard_map/ppermute | solution.py:435
  6.2 0.5 collective-permute-start.3
  6.8 0.0 copy-done.3
  6.8 3.6 %collective-permute-start.2 = (f32[1,128,128]{2,1,0:T(8,128)S(1)}, f32[1,128,128]{2,1,0:T(8,128)S(1)}, u32[]{:S(2)}, u32[]{:S(2)}) collective-permute-start(f32[1,128,128]{2,1,0:T(8,128)S(1)} %bitcast.61), channel_id=1, source_target_pairs={{0,6},{1,7},{2,4},{3,5},{4,2},{5,3},{6,0},{7,1},{8,14},{9,15},{10,... | collective-permute-start | bytes 196616 | tf_op jit(solution)/shard_map/ppermute | solution.py:440
  10.4 0.0 collective-permute-start.1
  10.4 0.8 %collective-permute-start = (f32[1,128,128]{2,1,0:T(8,128)S(1)}, f32[1,128,128]{2,1,0:T(8,128)S(1)}, u32[]{:S(2)}, u32[]{:S(2)}) collective-permute-start(f32[1,128,128]{2,1,0:T(8,128)S(1)} %bitcast.63), channel_id=1, source_target_pairs={{0,2},{1,3},{2,0},{3,1},{4,6},{5,7},{6,4},{7,5},{8,10},{9,11},{10,... | collective-permute-start | bytes 196616 | tf_op jit(solution)/shard_map/ppermute | solution.py:440
  11.1 0.0 copy-done.11
  11.1 0.0 copy-start.9
  11.1 0.0 copy-start.10
  11.1 0.1 reshape.75.vert_ref
  11.3 0.0 copy-start.7
  11.3 0.0 copy-start.8
  11.3 0.6 copy-done.9
  11.8 0.0 copy-done.10
  11.8 0.1 copy-done.7
  11.9 0.0 copy-done.8
  12.0 1.1 %shard_map.139 = (f32[3,32,8,128]{3,2,1,0:T(8,128)S(1)}, bf16[256,1024]{1,0:T(8,128)(2,1)S(1)}, bf16[256,1024]{1,0:T(8,128)(2,1)S(1)}) custom-call(f32[32,2,128]{2,1,0:T(2,128)S(1)} %reshape.75.vert_ref, s32[1,512]{1,0:T(1,128)S(1)} %bitcast.72, s32[1,512]{1,0:T(1,128)S(1)} %bitcast.73, s32[1,512]{1,0:T(1,128)S(1)} %bitcast.74, f32[2,512]{1,0:T(2,128)S(1)} %bitcast.71), custom_call_target="tpu_custom_call" | custom-call | flops 20000000 | bytes 43008 | tf_op jit(solution)/shard_map/pallas_call | solution.py:417
  13.1 0.3 collective-permute-done.2.refs_4_
  13.4 2.3 %collective-permute-done.1.refs_3_ = f32[1,128,128]{2,1,0:T(8,128)S(1)} collective-permute-done((f32[1,128,128]{2,1,0:T(8,128)S(1)}, f32[1,128,128]{2,1,0:T(8,128)S(1)}, u32[]{:S(2)}, u32[]{:S(2)}) %collective-permute-start.1) | collective-permute-done | bytes 65568 | tf_op jit(solution)/shard_map/ppermute | solution.py:440
  15.6 0.0 collective-permute-done.refs_2_
  15.6 0.0 copy-start
  15.6 0.0 copy-start.4
  15.6 0.0 copy-start.5
  15.6 0.0 copy-start.6
  15.7 1.5 %collective-permute-start.7 = (f32[4,128,128]{2,1,0:T(8,128)S(1)}, f32[4,128,128]{2,1,0:T(8,128)S(1)}, u32[]{:S(2)}, u32[]{:S(2)}) collective-permute-start(f32[4,128,128]{2,1,0:T(8,128)S(1)} %shard_map.140._.refs_1_), channel_id=1, source_target_pairs={{0,24},{8,16},{16,8},{24,0},{1,25},{9,17},{17,9},{25,1},{2,26},{10... | collective-permute-start | bytes 786440 | tf_op jit(solution)/shard_map/ppermute | solution.py:440
  17.2 1.5 %collective-permute-start.6 = (f32[4,128,128]{2,1,0:T(8,128)S(1)}, f32[4,128,128]{2,1,0:T(8,128)S(1)}, u32[]{:S(2)}, u32[]{:S(2)}) collective-permute-start(f32[4,128,128]{2,1,0:T(8,128)S(1)} %shard_map.140._.refs_1_), channel_id=1, source_target_pairs={{0,16},{8,24},{16,0},{24,8},{1,17},{9,25},{17,1},{25,9},{2,18},{10... | collective-permute-start | bytes 786440 | tf_op jit(solution)/shard_map/ppermute | solution.py:440
  18.7 0.5 collective-permute-start.5
  19.2 0.0 collective-permute-done.4.cross_ref
  19.2 0.0 collective-permute-done.3.pair_ref
  19.2 0.0 copy-done
  19.2 0.0 copy-done.4
  19.2 0.0 copy-done.5
  19.2 0.0 copy-done.6
  19.3 0.9 %shard_map.142 = (f32[8,32,128]{2,1,0:T(8,128)S(1)}, f32[5,16,512]{2,1,0:T(8,128)S(1)}) custom-call(f32[4,128,128]{2,1,0:T(8,128)S(1)} %shard_map.140._.refs_1_, f32[256,128]{1,0:T(8,128)S(1)} %bitcast.53, f32[16,128]{1,0:T(8,128)S(1)} %bitcast.66, f32[16,128]{1,0:T(8,128)S(1)} %bitcast.68, s32[16,128]{1,0:T(8,128)S(1)} %bitcast.70, ...), custom_call_target="tpu_custom_call" | custom-call | flops 4000000 | bytes 729088 | tf_op jit(solution)/shard_map/pallas_call | solution.py:417
  20.2 10.3 %all_to_all.15 = f32[8,32,128]{2,1,0:T(8,128)S(1)} all-to-all(f32[8,32,128]{2,1,0:T(8,128)S(1)} %get-tuple-element.16), channel_id=1, replica_groups=mesh['gy'=4,'gx'=8] {'gx'}, dimensions={0} | all-to-all | bytes 262144 | tf_op jit(solution)/shard_map/all_to_all | solution.py:523
  30.5 0.1 shard_map.143.refs_0_.column_ref
  30.6 0.0 collective-permute-done.7.refs_4_
  30.6 0.0 collective-permute-done.6.refs_3_
  30.6 0.0 collective-permute-done.5.refs_2_
  30.7 0.1 shard_map.144.near_ref
  30.7 0.1 collective-permute-start.8
  30.8 0.9 %shard_map.145 = (f32[128,512]{1,0:T(8,128)S(1)}, f32[128,512]{1,0:T(8,128)S(1)}) custom-call(f32[256,128]{1,0:T(8,128)S(1)} %shard_map.143.refs_0_.column_ref, bf16[256,1024]{1,0:T(8,128)(2,1)S(1)} %get-tuple-element.15.refs_0_.high_ref, bf16[256,1024]{1,0:T(8,128)(2,1)S(1)} %get-tuple-element.18.low_ref, f32[16,128,128]{2,1,0:T(8,128)S(1)} %shard_map.144.near_ref), custom_call_target="tpu_custom_call" | custom-call | flops 400000000 | bytes 3276800 | tf_op jit(solution)/shard_map/pallas_call | solution.py:417
  31.7 1.7 %collective-permute-done.8.far_ref = f32[16,128,128]{2,1,0:T(8,128)S(1)} collective-permute-done((f32[16,128,128]{2,1,0:T(8,128)S(1)}, f32[16,128,128]{2,1,0:T(8,128)S(1)}, u32[]{:S(2)}, u32[]{:S(2)}) %collective-permute-start.8) | collective-permute-done | bytes 1048608 | tf_op jit(solution)/shard_map/ppermute | solution.py:440
  33.5 1.2 %shard_map.146 = f32[256,128]{1,0:T(8,128)S(1)} custom-call(f32[128,512]{1,0:T(8,128)S(1)} %get-tuple-element.19.near_ref, f32[128,512]{1,0:T(8,128)S(1)} %get-tuple-element.20.profile_ref, f32[3,32,8,128]{3,2,1,0:T(8,128)S(1)} %get-tuple-element.17.factor_ref, bf16[256,1024]{1,0:T(8,128)(2,1)S(1)} %get-tuple-element.15.refs_0_.high_ref, ...), custom_call_target="tpu_custom_call" | custom-call | flops 400000000 | bytes 4063232 | tf_op jit(solution)/shard_map/pallas_call | solution.py:417
  34.7 0.0 copy-start.1
  34.7 9.4 %all_to_all.16.own_ref = f32[8,32,128]{2,1,0:T(8,128)S(1)} all-to-all(f32[8,32,128]{2,1,0:T(8,128)S(1)} %bitcast.56), channel_id=1, replica_groups=mesh['gy'=4,'gx'=8] {'gx'}, dimensions={0} | all-to-all | bytes 262144 | tf_op jit(solution)/shard_map/all_to_all | solution.py:553
  44.1 1.4 %collective-permute-start.10 = (f32[8,32,128]{2,1,0:T(8,128)S(1)}, f32[8,32,128]{2,1,0:T(8,128)S(1)}, u32[]{:S(2)}, u32[]{:S(2)}) collective-permute-start(f32[8,32,128]{2,1,0:T(8,128)S(1)} %all_to_all.16.own_ref), channel_id=1, source_target_pairs={{0,24},{8,16},{16,8},{24,0},{1,25},{9,17},{17,9},{25,1},{2,26},{10... | collective-permute-start | bytes 393224 | tf_op jit(solution)/shard_map/ppermute | solution.py:435
  45.6 0.5 collective-permute-start.9
  46.1 5.3 %collective-permute-done.10.cross_ref = f32[8,32,128]{2,1,0:T(8,128)S(1)} collective-permute-done((f32[8,32,128]{2,1,0:T(8,128)S(1)}, f32[8,32,128]{2,1,0:T(8,128)S(1)}, u32[]{:S(2)}, u32[]{:S(2)}) %collective-permute-start.10) | collective-permute-done | bytes 131104 | tf_op jit(solution)/shard_map/ppermute | solution.py:435
  51.4 0.4 collective-permute-done.9.pair_ref
  51.8 0.0 copy-done.1
  51.8 0.0 copy-start.2
  51.8 1.0 %shard_map.147 = (f32[256,128]{1,0:T(8,128)S(1)}, f32[32,1,128]{2,1,0:T(1,128)S(1)}) custom-call(f32[8,32,128]{2,1,0:T(8,128)S(1)} %all_to_all.16.own_ref, f32[8,32,128]{2,1,0:T(8,128)S(1)} %collective-permute-done.9.pair_ref, f32[8,32,128]{2,1,0:T(8,128)S(1)} %collective-permute-done.10.cross_ref, f32[5,16,512]{2,1,0:T(8,128)S(1)} %get-tuple-element.21.coef_ref, ...), custom_call_target="tpu_custom_call" | custom-call | flops 4000000 | bytes 819200 | tf_op jit(solution)/shard_map/pallas_call | solution.py:417
  52.8 10.7 %all_to_all.17.sums_ref = f32[32,1,128]{2,1,0:T(1,128)S(1)} all-to-all(f32[32,1,128]{2,1,0:T(1,128)S(1)} %get-tuple-element.22), channel_id=1, replica_groups=mesh['gy'=4,'gx'=8] {'gy','gx'}, dimensions={0} | all-to-all | bytes 32768 | tf_op jit(solution)/shard_map/all_to_all | solution.py:564
  63.5 0.0 copy-done.2
  63.5 0.9 %shard_map.148 = (f32[256,128]{1,0:T(8,128)}, f32[256,128]{1,0:T(8,128)}, f32[256,128]{1,0:T(8,128)}) custom-call(f32[32,1,128]{2,1,0:T(1,128)S(1)} %all_to_all.17.sums_ref, f32[256,128]{1,0:T(8,128)S(1)} %bitcast.55, f32[256,128]{1,0:T(8,128)S(1)} %bitcast.60, f32[256,128]{1,0:T(8,128)S(1)} %bitcast.59, f32[256,128]{1,0:T(8,128)S(1)} %get-tuple-element.23.image_ref), custom_call_target="tpu_custom_call" | custom-call | flops 1000000 | bytes 540672 | tf_op jit(solution)/shard_map/pallas_call | solution.py:417
  (1 shorter events, 0.0 us)
Async XLA Ops:
  0.6 6.1 %copy-start.3 = (f32[1,1,128,128]{3,2,1,0:T(8,128)S(1)}, f32[1,1,128,128]{3,2,1,0:T(8,128)}, u32[]{:S(2)}) copy-start(f32[1,1,128,128]{3,2,1,0:T(8,128)} %param.23) | copy-start | bytes 196612
  0.6 10.5 %copy-start.11 = (f32[32,4,64]{2,1,0:T(4,128)S(1)}, f32[32,4,64]{2,1,0:T(4,128)}, u32[]{:S(2)}) copy-start(f32[32,4,64]{2,1,0:T(4,128)} %param.18) | copy-start | bytes 98308
  2.3 17.0 %collective-permute-start.4 = (f32[304,128]{1,0:T(8,128)}, f32[304,128]{1,0:T(8,128)S(1)}, u32[]{:S(2)}, u32[]{:S(2)}) collective-permute-start(f32[304,128]{1,0:T(8,128)} %shard_map.141), channel_id=1, source_target_pairs={{0,24},{8,16},{16,8},{24,0},{1,25},{9,17},{17,9},{25,1},{2,26},{10... | collective-permute-start | bytes 466952 | tf_op jit(solution)/shard_map/ppermute | solution.py:435
  6.2 13.0 %collective-permute-start.3 = (f32[304,128]{1,0:T(8,128)}, f32[304,128]{1,0:T(8,128)S(1)}, u32[]{:S(2)}, u32[]{:S(2)}) collective-permute-start(f32[304,128]{1,0:T(8,128)} %shard_map.141), channel_id=1, source_target_pairs={{0,8},{8,0},{16,24},{24,16},{1,9},{9,1},{17,25},{25,17},{2,10},{10... | collective-permute-start | bytes 466952 | tf_op jit(solution)/shard_map/ppermute | solution.py:434
  6.8 6.6 %collective-permute-start.2 = (f32[1,128,128]{2,1,0:T(8,128)S(1)}, f32[1,128,128]{2,1,0:T(8,128)S(1)}, u32[]{:S(2)}, u32[]{:S(2)}) collective-permute-start(f32[1,128,128]{2,1,0:T(8,128)S(1)} %bitcast.61), channel_id=1, source_target_pairs={{0,6},{1,7},{2,4},{3,5},{4,2},{5,3},{6,0},{7,1},{8,14},{9,15},{10,... | collective-permute-start | bytes 196616 | tf_op jit(solution)/shard_map/ppermute | solution.py:440
  10.4 5.2 %collective-permute-start.1 = (f32[1,128,128]{2,1,0:T(8,128)S(1)}, f32[1,128,128]{2,1,0:T(8,128)S(1)}, u32[]{:S(2)}, u32[]{:S(2)}) collective-permute-start(f32[1,128,128]{2,1,0:T(8,128)S(1)} %bitcast.62), channel_id=1, source_target_pairs={{0,4},{1,5},{2,6},{3,7},{4,0},{5,1},{6,2},{7,3},{8,12},{9,13},{10,... | collective-permute-start | bytes 196616 | tf_op jit(solution)/shard_map/ppermute | solution.py:440
  10.4 5.2 %collective-permute-start = (f32[1,128,128]{2,1,0:T(8,128)S(1)}, f32[1,128,128]{2,1,0:T(8,128)S(1)}, u32[]{:S(2)}, u32[]{:S(2)}) collective-permute-start(f32[1,128,128]{2,1,0:T(8,128)S(1)} %bitcast.63), channel_id=1, source_target_pairs={{0,2},{1,3},{2,0},{3,1},{4,6},{5,7},{6,4},{7,5},{8,10},{9,11},{10,... | collective-permute-start | bytes 196616 | tf_op jit(solution)/shard_map/ppermute | solution.py:440
  11.1 0.7 %copy-start.9 = (s32[1,1,512]{2,1,0:T(1,128)S(1)}, s32[1,1,512]{2,1,0:T(1,128)}, u32[]{:S(2)}) copy-start(s32[1,1,512]{2,1,0:T(1,128)} %param.20) | copy-start | bytes 6148
  11.1 0.7 %copy-start.10 = (s32[1,1,512]{2,1,0:T(1,128)S(1)}, s32[1,1,512]{2,1,0:T(1,128)}, u32[]{:S(2)}) copy-start(s32[1,1,512]{2,1,0:T(1,128)} %param.21) | copy-start | bytes 6148
  11.3 0.7 %copy-start.7 = (f32[1,1,2,512]{3,2,1,0:T(2,128)S(1)}, f32[1,1,2,512]{3,2,1,0:T(2,128)}, u32[]{:S(2)}) copy-start(f32[1,1,2,512]{3,2,1,0:T(2,128)} %param.22) | copy-start | bytes 12292
  11.3 0.7 %copy-start.8 = (s32[1,1,512,1]{2,3,1,0:T(1,128)S(1)}, s32[1,1,512,1]{2,3,1,0:T(1,128)}, u32[]{:S(2)}) copy-start(s32[1,1,512,1]{2,3,1,0:T(1,128)} %param.19) | copy-start | bytes 6148
  15.6 3.6 %copy-start = (f32[4,4,4,512]{3,2,1,0:T(4,128)S(1)}, f32[4,4,4,512]{3,2,1,0:T(4,128)}, u32[]{:S(2)}) copy-start(f32[4,4,4,512]{3,2,1,0:T(4,128)} %param.12) | copy-start | bytes 393220
  15.6 3.6 %copy-start.4 = (f32[4,512]{1,0:T(4,128)S(1)}, f32[4,512]{1,0:T(4,128)}, u32[]{:S(2)}) copy-start(f32[4,512]{1,0:T(4,128)} %param.15) | copy-start | bytes 24580
  15.6 3.6 %copy-start.5 = (f32[4,512]{1,0:T(4,128)S(1)}, f32[4,512]{1,0:T(4,128)}, u32[]{:S(2)}) copy-start(f32[4,512]{1,0:T(4,128)} %param.16) | copy-start | bytes 24580
  15.6 3.6 %copy-start.6 = (s32[4,512]{1,0:T(4,128)S(1)}, s32[4,512]{1,0:T(4,128)}, u32[]{:S(2)}) copy-start(s32[4,512]{1,0:T(4,128)} %param.17) | copy-start | bytes 24580
  15.7 15.0 %collective-permute-start.7 = (f32[4,128,128]{2,1,0:T(8,128)S(1)}, f32[4,128,128]{2,1,0:T(8,128)S(1)}, u32[]{:S(2)}, u32[]{:S(2)}) collective-permute-start(f32[4,128,128]{2,1,0:T(8,128)S(1)} %shard_map.140._.refs_1_), channel_id=1, source_target_pairs={{0,24},{8,16},{16,8},{24,0},{1,25},{9,17},{17,9},{25,1},{2,26},{10... | collective-permute-start | bytes 786440 | tf_op jit(solution)/shard_map/ppermute | solution.py:440
  17.2 13.5 %collective-permute-start.6 = (f32[4,128,128]{2,1,0:T(8,128)S(1)}, f32[4,128,128]{2,1,0:T(8,128)S(1)}, u32[]{:S(2)}, u32[]{:S(2)}) collective-permute-start(f32[4,128,128]{2,1,0:T(8,128)S(1)} %shard_map.140._.refs_1_), channel_id=1, source_target_pairs={{0,16},{8,24},{16,0},{24,8},{1,17},{9,25},{17,1},{25,9},{2,18},{10... | collective-permute-start | bytes 786440 | tf_op jit(solution)/shard_map/ppermute | solution.py:440
  18.7 12.0 %collective-permute-start.5 = (f32[4,128,128]{2,1,0:T(8,128)S(1)}, f32[4,128,128]{2,1,0:T(8,128)S(1)}, u32[]{:S(2)}, u32[]{:S(2)}) collective-permute-start(f32[4,128,128]{2,1,0:T(8,128)S(1)} %shard_map.140._.refs_1_), channel_id=1, source_target_pairs={{0,8},{8,0},{16,24},{24,16},{1,9},{9,1},{17,25},{25,17},{2,10},{10... | collective-permute-start | bytes 786440 | tf_op jit(solution)/shard_map/ppermute | solution.py:440
  30.7 2.7 %collective-permute-start.8 = (f32[16,128,128]{2,1,0:T(8,128)S(1)}, f32[16,128,128]{2,1,0:T(8,128)S(1)}, u32[]{:S(2)}, u32[]{:S(2)}) collective-permute-start(f32[16,128,128]{2,1,0:T(8,128)S(1)} %shard_map.144.near_ref), channel_id=1, source_target_pairs={{0,1},{1,0},{2,3},{3,2},{4,5},{5,4},{6,7},{7,6},{8,9},{9,8},{10,11... | collective-permute-start | bytes 3145736 | tf_op jit(solution)/shard_map/ppermute | solution.py:440
  34.7 17.1 %copy-start.1 = (f32[4,4,4,512]{3,2,1,0:T(4,128)S(1)}, f32[4,4,4,512]{3,2,1,0:T(4,128)}, u32[]{:S(2)}) copy-start(f32[4,4,4,512]{3,2,1,0:T(4,128)} %param.14) | copy-start | bytes 393220
  44.1 7.2 %collective-permute-start.10 = (f32[8,32,128]{2,1,0:T(8,128)S(1)}, f32[8,32,128]{2,1,0:T(8,128)S(1)}, u32[]{:S(2)}, u32[]{:S(2)}) collective-permute-start(f32[8,32,128]{2,1,0:T(8,128)S(1)} %all_to_all.16.own_ref), channel_id=1, source_target_pairs={{0,24},{8,16},{16,8},{24,0},{1,25},{9,17},{17,9},{25,1},{2,26},{10... | collective-permute-start | bytes 393224 | tf_op jit(solution)/shard_map/ppermute | solution.py:435
  45.6 6.2 %collective-permute-start.9 = (f32[8,32,128]{2,1,0:T(8,128)S(1)}, f32[8,32,128]{2,1,0:T(8,128)S(1)}, u32[]{:S(2)}, u32[]{:S(2)}) collective-permute-start(f32[8,32,128]{2,1,0:T(8,128)S(1)} %all_to_all.16.own_ref), channel_id=1, source_target_pairs={{0,8},{8,0},{16,24},{24,16},{1,9},{9,1},{17,25},{25,17},{2,10},{10... | collective-permute-start | bytes 393224 | tf_op jit(solution)/shard_map/ppermute | solution.py:434
  51.8 11.7 %copy-start.2 = (f32[4,4,4,512]{3,2,1,0:T(4,128)S(1)}, f32[4,4,4,512]{3,2,1,0:T(4,128)}, u32[]{:S(2)}) copy-start(f32[4,4,4,512]{3,2,1,0:T(4,128)} %param.13) | copy-start | bytes 393220

commit v8 on v7

--- a/solution.py
+++ b/solution.py
@@ -73,6 +73,34 @@
     @pl.when(at_y == rows_y - 1)
     def _():
         high_ref[...] = jnp.zeros_like(high_ref)
+
+
+def triangle_masks():
+    shape = (LANES // 2, LANES)
+    lane = lax.broadcasted_iota(jnp.int32, shape, 1)
+    return lane, lane - lax.broadcasted_iota(jnp.int32, shape, 0)
+
+
+def pack_symmetric(matrix, packed_ref):
+    half = LANES // 2
+    lane, away = triangle_masks()
+    top, bottom = matrix[:half], matrix[half:]
+    corner = jnp.where(away <= 0, top, pltpu.roll(bottom, half, 1))
+    packed_ref[0:half, :] = jnp.where(lane < half, corner, top)
+    diagonal = jnp.sum(jnp.where(away == half, bottom, 0.0), axis=0, keepdims=True)
+    packed_ref[half:, :] = jnp.broadcast_to(diagonal, (packed_ref.shape[0] - half, LANES))
+
+
+def unpack_symmetric(packed):
+    half = LANES // 2
+    lane, away = triangle_masks()
+    rows, diagonal = packed[:half], packed[half : half + 1]
+    turned = jnp.concatenate([rows, rows], axis=0).T
+    top = jnp.where((lane < half) & (away > 0), turned[:half], rows)
+    corner = jnp.where(
+        away > half, pltpu.roll(rows, half, 1), jnp.where(away == half, diagonal, turned[:half])
+    )
+    return jnp.concatenate([top, jnp.where(lane < half, turned[half:], corner)], axis=0)
 
 
 def halo_kernel(chunks, direction_ref, north_ref, east_ref, ocean_ref, own_ref, stage_ref, mask_ref, sems):
@@ -108,6 +136,14 @@
     size = blocks[0].shape[0]
     for at, block in enumerate(blocks):
         near_ref[at * size : (at + 1) * size] = block[...]
+
+
+def pack_kernel(_, *refs):
+    blocks, (packed_ref,) = refs[:-1], refs[-1:]
+    size = blocks[0].shape[0]
+    for at, block in enumerate(blocks):
+        for inner in range(size):
+            pack_symmetric(block[inner], packed_ref.at[at * size + inner])
 
 
 def first_lateral_kernel(
@@ -354,16 +390,16 @@
     return pl.ds((layer // held) * 8 * held + layer % held, 8, stride=held)
 
 
-def weigh(profile, matrix_ref, capacity):
-    kv = matrix_ref.shape[1]
+def weigh(profile, matrices, capacity):
+    kv = profile.shape[0]
     owners = LANES // capacity
     mine = lax.broadcasted_iota(jnp.int32, (kv, LANES), 1) // capacity
     tiles = []
-    for tile in range(matrix_ref.shape[0] // owners):
+    for tile in range(profile.shape[1] // LANES):
         values = profile[:, tile * LANES : (tile + 1) * LANES]
         masked = jnp.concatenate([jnp.where(mine == owner, values, 0.0) for owner in range(owners)], axis=0)
-        matrices = jnp.concatenate([matrix_ref[tile * owners + owner] for owner in range(owners)], axis=1)
-        tiles.append(dot_parts(split(matrices), split(masked), ((1,), (0,))))
+        beside = jnp.concatenate([matrices(tile * owners + owner) for owner in range(owners)], axis=1)
+        tiles.append(dot_parts(split(beside), split(masked), ((1,), (0,))))
     return jnp.concatenate(tiles, axis=1)
 
 
@@ -377,20 +413,21 @@
     solve_columns(read, write, factor_ref, layers)
 
 
-def profile_kernel(capacity, column_ref, high_ref, low_ref, near_ref, weighted_ref, profile_ref):
-    kv = profile_ref.shape[0]
-    half = profile_ref.shape[1]
+def profile_kernel(capacity, column_ref, high_ref, low_ref, *refs):
+    near_refs, (weighted_ref, profile_ref) = refs[:-2], refs[-2:]
+    kv, half = profile_ref.shape
+    size = near_refs[0].shape[0]
     columns = jnp.concatenate([column_ref[0:kv, :], column_ref[kv : 2 * kv, :]], axis=1)
     profile = dot_parts(split(columns), (high_ref[...], low_ref[...]), ((1,), (0,)))
     profile_ref[...] = profile[:, half:]
-    weighted_ref[...] = weigh(profile[:, :half], near_ref, capacity)
+    weighted_ref[...] = weigh(profile[:, :half], lambda at: near_refs[at // size][at % size], capacity)
 
 
 def spread_kernel(
     layers, held, capacity, near_ref, profile_ref, factor_ref, high_ref, low_ref, far_ref, out_ref, column_ref
 ):
     kv = near_ref.shape[0]
-    weighted = jnp.concatenate([near_ref[...], weigh(profile_ref[...], far_ref, capacity)], axis=1)
+    weighted = jnp.concatenate([near_ref[...], weigh(profile_ref[...], lambda at: unpack_symmetric(far_ref[at]), capacity)], axis=1)
     spread = dot_parts(split(weighted), (high_ref[...], low_ref[...]), ((1,), (1,)))
     column_ref[0:kv, :] = spread[:, :LANES]
     column_ref[kv : 2 * kv, :] = spread[:, LANES:]
@@ -499,18 +536,11 @@
         flops=20_000_000,
         mib=16,
     )
-    held_blocks = call(
-        functools.partial(join_kernel, 1, len(blocks)),
-        f32(len(blocks), wide, wide),
-        (interp[0], *blocks),
-        after=1,
-    )
-
     extended = 3 * rows + (-3 * rows) % 8
     packed, coef = call(
         functools.partial(first_lateral_kernel, kv, rows, tiles),
         (f32(cols_x, 2 * kv, LANES), f32(5, extended, lons)),
-        (held_blocks, direction_n, *faces, pair, cross),
+        (interp[0], direction_n, *faces, pair, cross),
         after=1,
         scratch=(
             pltpu.VMEM((3, extended, lons), jnp.float32),
@@ -519,6 +549,13 @@
         ),
         flops=4_000_000,
     )
+    held_blocks = call(
+        functools.partial(join_kernel, 1, len(blocks)),
+        f32(len(blocks), wide, wide),
+        (packed, *blocks),
+        after=1,
+    )
+
     fetched = [held_blocks] + [apart_by(held_blocks, "gy", stride) for stride in range(1, rows_y)]
     columns = lax.all_to_all(packed, "gx", split_axis=0, concat_axis=0, tiled=True)
     smoothed = call(
@@ -527,18 +564,18 @@
         (columns.reshape(cols_x * 2 * kv, LANES), factors),
         flops=1000,
     )
-    near = call(
-        functools.partial(join_kernel, 1, len(fetched)),
-        f32(device_count // 2, wide, wide),
-        (smoothed, *fetched),
-        after=1,
-    )
-    far = apart_by(near, "gx", 1)
+    far = apart_by(
+        call(
+            pack_kernel, f32(device_count // 2, wide // 2 + 8, wide), (smoothed, *fetched), after=1
+        ),
+        "gx",
+        1,
+    )
     half = device_count // 2 * capacity
     weighted, profile = call(
         functools.partial(profile_kernel, capacity),
         (f32(wide, half), f32(wide, half)),
-        (smoothed, *interp, near),
+        (smoothed, *interp, *fetched),
         flops=400_000_000,
         mib=16,
     )

time: 64.7 us -> 64 us (0.989)
  waiting for transfers between devices: 9.96 us -> 8.95 us
  local copies, waits for them, and re-layouts: 0.82 us -> 0.16 us
    ppermute x7, waiting for transfers between devices: 4.24 us -> 1.68 us  [apart_by(): lax.ppermute(block, axis, [(i, i ^ stride) for i in range(lax.axis_size(a...]
    ppermute x2, waiting for transfers between devices: 0.44 us -> 2.09 us  [from_neighbours(): pair = lax.ppermute(block, 'gy', [(i, i ^ 1) for i in range(count)])]
    all_to_all x1, blocking collectives: 10.7 us -> 9.92 us  [per_device_gathered(): lax.all_to_all(sums, ('gy', 'gx'), split_axis=0, concat_axis=0, tiled=True)]
    all_to_all x1, blocking collectives: 9.4 us -> 10.2 us  [per_device_gathered(): lax.all_to_all(spread.reshape(cols_x, 2 * kv, LANES), 'gx', split_axis=0,...]
    unnamed x24, local copies, waits for them, and re-layouts: 0.72 us -> 0.06 us
where the time goes in v8:
time: 64 us; the launch traced here: 63.8 us
  blocking collectives  31 us (48%)
  starting transfers between devices  14.6 us (23%)
  waiting for transfers between devices  8.95 us (14%)
  Pallas kernels  8.26 us (13%)
  between operations  0.88 us (1%)
    all_to_all x1, blocking collectives, per_device_gathered(): lax.all_to_all(packed, 'gx', split_axis=0, concat_axis=0, tiled=True)  10.9 us
    all_to_all x1, blocking collectives, per_device_gathered(): lax.all_to_all(spread.reshape(cols_x, 2 * kv, LANES), 'gx', split_axis=0,...  10.2 us
    all_to_all x1, blocking collectives, per_device_gathered(): lax.all_to_all(sums, ('gy', 'gx'), split_axis=0, concat_axis=0, tiled=True)  9.92 us
    pallas_call x10, Pallas kernels, call(): pl.pallas_call(kernel, out_shape=out_shape, in_specs=specs, out_specs=tup...  8.26 us
    ppermute x7, starting transfers between devices, apart_by(): lax.ppermute(block, axis, [(i, i ^ stride) for i in range(lax.axis_size(a...  8.01 us
    ppermute x2, starting transfers between devices, from_neighbours(): lax.ppermute(block, 'gy', [(i, (i + (1 if i % 2 else -1)) % count) for i...  5.48 us
    ppermute x2, waiting for transfers between devices, from_neighbours(): lax.ppermute(block, 'gy', [(i, (i + (1 if i % 2 else -1)) % count) for i...  5.18 us
    ppermute x2, waiting for transfers between devices, from_neighbours(): pair = lax.ppermute(block, 'gy', [(i, i ^ 1) for i in range(count)])  2.09 us
  transfers between devices with their start and end apart: 11, of which 5 were waited for; matrix products, arithmetic and copies ran while one was open for 0% of the time, Pallas kernels for 5%

profile of v8, /device:TPU:0, one launch (start us, length us, event | category | flops | bytes accessed | tf_op | source)
XLA Modules:
  0.0 63.8 jit_solution(8848817476059776753)
XLA Ops:
  0.6 0.0 copy-start.3
  0.6 0.0 copy-start.11
  0.7 0.0 copy-start.7
  0.7 0.0 copy-start.8
  0.7 0.0 copy-start.9
  0.7 0.0 copy-start.10
  0.7 1.6 %shard_map.140 = f32[304,128]{1,0:T(8,128)} custom-call(f32[256,128]{1,0:T(8,128)} %bitcast.52, f32[16,128]{1,0:T(8,128)} %bitcast.65, f32[16,128]{1,0:T(8,128)} %bitcast.67, s32[16,128]{1,0:T(8,128)} %bitcast.69), custom_call_target="tpu_custom_call" | custom-call | flops 1000000 | bytes 155648 | tf_op jit(solution)/shard_map/pallas_call | solution.py:454
  2.3 0.0 copy-start
  2.3 4.0 %collective-permute-start.1 = (f32[304,128]{1,0:T(8,128)}, f32[304,128]{1,0:T(8,128)S(1)}, u32[]{:S(2)}, u32[]{:S(2)}) collective-permute-start(f32[304,128]{1,0:T(8,128)} %shard_map.140), channel_id=1, source_target_pairs={{0,24},{8,16},{16,8},{24,0},{1,25},{9,17},{17,9},{25,1},{2,26},{10... | collective-permute-start | bytes 466952 | tf_op jit(solution)/shard_map/ppermute | solution.py:472
  6.3 0.5 collective-permute-start
  6.8 0.0 copy-done.3
  6.8 3.6 %collective-permute-start.4 = (f32[1,128,128]{2,1,0:T(8,128)S(1)}, f32[1,128,128]{2,1,0:T(8,128)S(1)}, u32[]{:S(2)}, u32[]{:S(2)}) collective-permute-start(f32[1,128,128]{2,1,0:T(8,128)S(1)} %bitcast.61), channel_id=1, source_target_pairs={{0,6},{1,7},{2,4},{3,5},{4,2},{5,3},{6,0},{7,1},{8,14},{9,15},{10,... | collective-permute-start | bytes 196616 | tf_op jit(solution)/shard_map/ppermute | solution.py:477
  10.4 0.0 collective-permute-start.3
  10.4 0.8 %collective-permute-start.2 = (f32[1,128,128]{2,1,0:T(8,128)S(1)}, f32[1,128,128]{2,1,0:T(8,128)S(1)}, u32[]{:S(2)}, u32[]{:S(2)}) collective-permute-start(f32[1,128,128]{2,1,0:T(8,128)S(1)} %bitcast.63), channel_id=1, source_target_pairs={{0,2},{1,3},{2,0},{3,1},{4,6},{5,7},{6,4},{7,5},{8,10},{9,11},{10,... | collective-permute-start | bytes 196616 | tf_op jit(solution)/shard_map/ppermute | solution.py:477
  11.2 0.0 copy-done.11
  11.2 0.1 reshape.75.vert_ref
  11.3 0.0 copy-done.7
  11.3 0.0 copy-done.8
  11.3 0.0 copy-done.9
  11.4 0.0 copy-done.10
  11.4 0.0 copy-start.4
  11.4 0.0 copy-start.5
  11.4 0.0 copy-start.6
  11.4 1.1 %shard_map.139 = (f32[3,32,8,128]{3,2,1,0:T(8,128)S(1)}, bf16[256,1024]{1,0:T(8,128)(2,1)S(1)}, bf16[256,1024]{1,0:T(8,128)(2,1)S(1)}) custom-call(f32[32,2,128]{2,1,0:T(2,128)S(1)} %reshape.75.vert_ref, s32[1,512]{1,0:T(1,128)S(1)} %bitcast.72, s32[1,512]{1,0:T(1,128)S(1)} %bitcast.73, s32[1,512]{1,0:T(1,128)S(1)} %bitcast.74, f32[2,512]{1,0:T(2,128)S(1)} %bitcast.71), custom_call_target="tpu_custom_call" | custom-call | flops 20000000 | bytes 43008 | tf_op jit(solution)/shard_map/pallas_call | solution.py:454
  12.5 0.0 collective-permute-done.1.cross_ref
  12.6 1.6 %collective-permute-done.pair_ref = f32[304,128]{1,0:T(8,128)S(1)} collective-permute-done((f32[304,128]{1,0:T(8,128)}, f32[304,128]{1,0:T(8,128)S(1)}, u32[]{:S(2)}, u32[]{:S(2)}) %collective-permute-start) | collective-permute-done | bytes 155680 | tf_op jit(solution)/shard_map/ppermute | solution.py:471
  14.1 0.0 copy-done
  14.1 0.0 copy-done.4
  14.1 0.0 copy-done.5
  14.1 0.0 copy-done.6
  14.1 0.9 %shard_map.141 = (f32[8,32,128]{2,1,0:T(8,128)S(1)}, f32[5,16,512]{2,1,0:T(8,128)S(1)}) custom-call(bf16[256,1024]{1,0:T(8,128)(2,1)S(1)} %get-tuple-element.15._.high_ref, f32[256,128]{1,0:T(8,128)S(1)} %bitcast.53, f32[16,128]{1,0:T(8,128)S(1)} %bitcast.66, f32[16,128]{1,0:T(8,128)S(1)} %bitcast.68, s32[16,128]{1,0:T(8,128)S(1)} %bitcast.70, ...), custom_call_target="tpu_custom_call" | custom-call | flops 4000000 | bytes 1515520 | tf_op jit(solution)/shard_map/pallas_call | solution.py:454
  15.1 0.0 collective-permute-done.4.refs_4_
  15.1 0.6 collective-permute-done.3.refs_3_
  15.7 0.0 collective-permute-done.2.refs_2_
  15.7 1.5 %collective-permute-start.7 = (f32[4,128,128]{2,1,0:T(8,128)S(1)}, f32[4,128,128]{2,1,0:T(8,128)S(1)}, u32[]{:S(2)}, u32[]{:S(2)}) collective-permute-start(f32[4,128,128]{2,1,0:T(8,128)S(1)} %shard_map.143.refs_0_), channel_id=1, source_target_pairs={{0,24},{8,16},{16,8},{24,0},{1,25},{9,17},{17,9},{25,1},{2,26},{10... | collective-permute-start | bytes 786440 | tf_op jit(solution)/shard_map/ppermute | solution.py:477
  17.2 1.5 %collective-permute-start.6 = (f32[4,128,128]{2,1,0:T(8,128)S(1)}, f32[4,128,128]{2,1,0:T(8,128)S(1)}, u32[]{:S(2)}, u32[]{:S(2)}) collective-permute-start(f32[4,128,128]{2,1,0:T(8,128)S(1)} %shard_map.143.refs_0_), channel_id=1, source_target_pairs={{0,16},{8,24},{16,0},{24,8},{1,17},{9,25},{17,1},{25,9},{2,18},{10... | collective-permute-start | bytes 786440 | tf_op jit(solution)/shard_map/ppermute | solution.py:477
  18.7 0.5 collective-permute-start.5
  19.3 10.9 %all_to_all.15 = f32[8,32,128]{2,1,0:T(8,128)S(1)} all-to-all(f32[8,32,128]{2,1,0:T(8,128)S(1)} %get-tuple-element.16.refs_0_), channel_id=1, replica_groups=mesh['gy'=4,'gx'=8] {'gx'}, dimensions={0} | all-to-all | bytes 262144 | tf_op jit(solution)/shard_map/all_to_all | solution.py:560
  30.1 0.1 shard_map.142.column_ref._
  30.3 0.0 collective-permute-done.7.refs_3_
  30.3 0.0 collective-permute-done.6.refs_2_
  30.3 0.0 collective-permute-done.5.refs_1_
  30.3 0.2 shard_map.145
  30.5 0.1 collective-permute-start.8
  30.6 0.9 %shard_map.144 = (f32[128,512]{1,0:T(8,128)S(1)}, f32[128,512]{1,0:T(8,128)S(1)}) custom-call(f32[256,128]{1,0:T(8,128)S(1)} %shard_map.142.column_ref._, bf16[256,1024]{1,0:T(8,128)(2,1)S(1)} %get-tuple-element.15._.high_ref, bf16[256,1024]{1,0:T(8,128)(2,1)S(1)} %get-tuple-element.18.low_ref, f32[4,128,128]{2,1,0:T(8,128)S(1)} %shard_map.143.refs_0_, ...), custom_call_target="tpu_custom_call" | custom-call | flops 400000000 | bytes 3276800 | tf_op jit(solution)/shard_map/pallas_call | solution.py:454
  31.5 1.1 %collective-permute-done.8.far_ref = f32[16,72,128]{2,1,0:T(8,128)S(1)} collective-permute-done((f32[16,72,128]{2,1,0:T(8,128)S(1)}, f32[16,72,128]{2,1,0:T(8,128)S(1)}, u32[]{:S(2)}, u32[]{:S(2)}) %collective-permute-start.8) | collective-permute-done | bytes 589856 | tf_op jit(solution)/shard_map/ppermute | solution.py:477
  32.6 1.4 %shard_map.146 = f32[256,128]{1,0:T(8,128)S(1)} custom-call(f32[128,512]{1,0:T(8,128)S(1)} %get-tuple-element.19.near_ref, f32[128,512]{1,0:T(8,128)S(1)} %get-tuple-element.20.profile_ref, f32[3,32,8,128]{3,2,1,0:T(8,128)S(1)} %get-tuple-element.17.factor_ref, bf16[256,1024]{1,0:T(8,128)(2,1)S(1)} %get-tuple-element.15._.high_ref, ...), custom_call_target="tpu_custom_call" | custom-call | flops 400000000 | bytes 3604480 | tf_op jit(solution)/shard_map/pallas_call | solution.py:454
  34.0 0.0 copy-start.1
  34.0 10.2 %all_to_all.16.own_ref = f32[8,32,128]{2,1,0:T(8,128)S(1)} all-to-all(f32[8,32,128]{2,1,0:T(8,128)S(1)} %bitcast.59), channel_id=1, replica_groups=mesh['gy'=4,'gx'=8] {'gx'}, dimensions={0} | all-to-all | bytes 262144 | tf_op jit(solution)/shard_map/all_to_all | solution.py:590
  44.2 1.5 %collective-permute-start.10 = (f32[8,32,128]{2,1,0:T(8,128)S(1)}, f32[8,32,128]{2,1,0:T(8,128)S(1)}, u32[]{:S(2)}, u32[]{:S(2)}) collective-permute-start(f32[8,32,128]{2,1,0:T(8,128)S(1)} %all_to_all.16.own_ref), channel_id=1, source_target_pairs={{0,24},{8,16},{16,8},{24,0},{1,25},{9,17},{17,9},{25,1},{2,26},{10... | collective-permute-start | bytes 393224 | tf_op jit(solution)/shard_map/ppermute | solution.py:472
  45.7 0.5 collective-permute-start.9
  46.3 5.2 %collective-permute-done.10.cross_ref = f32[8,32,128]{2,1,0:T(8,128)S(1)} collective-permute-done((f32[8,32,128]{2,1,0:T(8,128)S(1)}, f32[8,32,128]{2,1,0:T(8,128)S(1)}, u32[]{:S(2)}, u32[]{:S(2)}) %collective-permute-start.10) | collective-permute-done | bytes 131104 | tf_op jit(solution)/shard_map/ppermute | solution.py:472
  51.5 0.5 collective-permute-done.9.pair_ref
  52.0 0.0 copy-done.1
  52.0 0.0 copy-start.2
  52.0 1.0 %shard_map.147 = (f32[256,128]{1,0:T(8,128)S(1)}, f32[32,1,128]{2,1,0:T(1,128)S(1)}) custom-call(f32[8,32,128]{2,1,0:T(8,128)S(1)} %all_to_all.16.own_ref, f32[8,32,128]{2,1,0:T(8,128)S(1)} %collective-permute-done.9.pair_ref, f32[8,32,128]{2,1,0:T(8,128)S(1)} %collective-permute-done.10.cross_ref, f32[5,16,512]{2,1,0:T(8,128)S(1)} %get-tuple-element.21.coef_ref, ...), custom_call_target="tpu_custom_call" | custom-call | flops 4000000 | bytes 819200 | tf_op jit(solution)/shard_map/pallas_call | solution.py:454
  53.0 9.9 %all_to_all.17.sums_ref = f32[32,1,128]{2,1,0:T(1,128)S(1)} all-to-all(f32[32,1,128]{2,1,0:T(1,128)S(1)} %get-tuple-element.22), channel_id=1, replica_groups=mesh['gy'=4,'gx'=8] {'gy','gx'}, dimensions={0} | all-to-all | bytes 32768 | tf_op jit(solution)/shard_map/all_to_all | solution.py:601
  62.9 0.0 copy-done.2
  62.9 0.9 %shard_map.148 = (f32[256,128]{1,0:T(8,128)}, f32[256,128]{1,0:T(8,128)}, f32[256,128]{1,0:T(8,128)}) custom-call(f32[32,1,128]{2,1,0:T(1,128)S(1)} %all_to_all.17.sums_ref, f32[256,128]{1,0:T(8,128)S(1)} %bitcast.55, f32[256,128]{1,0:T(8,128)S(1)} %bitcast.60, f32[256,128]{1,0:T(8,128)S(1)} %bitcast.58, f32[256,128]{1,0:T(8,128)S(1)} %get-tuple-element.23.image_ref), custom_call_target="tpu_custom_call" | custom-call | flops 1000000 | bytes 540672 | tf_op jit(solution)/shard_map/pallas_call | solution.py:454
  (1 shorter events, 0.0 us)
Async XLA Ops:
  0.6 6.2 %copy-start.3 = (f32[1,1,128,128]{3,2,1,0:T(8,128)S(1)}, f32[1,1,128,128]{3,2,1,0:T(8,128)}, u32[]{:S(2)}) copy-start(f32[1,1,128,128]{3,2,1,0:T(8,128)} %param.23) | copy-start | bytes 196612
  0.6 10.6 %copy-start.11 = (f32[32,4,64]{2,1,0:T(4,128)S(1)}, f32[32,4,64]{2,1,0:T(4,128)}, u32[]{:S(2)}) copy-start(f32[32,4,64]{2,1,0:T(4,128)} %param.18) | copy-start | bytes 98308
  0.7 10.7 %copy-start.7 = (f32[1,1,2,512]{3,2,1,0:T(2,128)S(1)}, f32[1,1,2,512]{3,2,1,0:T(2,128)}, u32[]{:S(2)}) copy-start(f32[1,1,2,512]{3,2,1,0:T(2,128)} %param.22) | copy-start | bytes 12292
  0.7 10.7 %copy-start.8 = (s32[1,1,512,1]{2,3,1,0:T(1,128)S(1)}, s32[1,1,512,1]{2,3,1,0:T(1,128)}, u32[]{:S(2)}) copy-start(s32[1,1,512,1]{2,3,1,0:T(1,128)} %param.19) | copy-start | bytes 6148
  0.7 10.7 %copy-start.9 = (s32[1,1,512]{2,1,0:T(1,128)S(1)}, s32[1,1,512]{2,1,0:T(1,128)}, u32[]{:S(2)}) copy-start(s32[1,1,512]{2,1,0:T(1,128)} %param.20) | copy-start | bytes 6148
  0.7 10.7 %copy-start.10 = (s32[1,1,512]{2,1,0:T(1,128)S(1)}, s32[1,1,512]{2,1,0:T(1,128)}, u32[]{:S(2)}) copy-start(s32[1,1,512]{2,1,0:T(1,128)} %param.21) | copy-start | bytes 6148
  2.3 11.8 %copy-start = (f32[4,4,4,512]{3,2,1,0:T(4,128)S(1)}, f32[4,4,4,512]{3,2,1,0:T(4,128)}, u32[]{:S(2)}) copy-start(f32[4,4,4,512]{3,2,1,0:T(4,128)} %param.12) | copy-start | bytes 393220
  2.3 10.2 %collective-permute-start.1 = (f32[304,128]{1,0:T(8,128)}, f32[304,128]{1,0:T(8,128)S(1)}, u32[]{:S(2)}, u32[]{:S(2)}) collective-permute-start(f32[304,128]{1,0:T(8,128)} %shard_map.140), channel_id=1, source_target_pairs={{0,24},{8,16},{16,8},{24,0},{1,25},{9,17},{17,9},{25,1},{2,26},{10... | collective-permute-start | bytes 466952 | tf_op jit(solution)/shard_map/ppermute | solution.py:472
  6.3 7.8 %collective-permute-start = (f32[304,128]{1,0:T(8,128)}, f32[304,128]{1,0:T(8,128)S(1)}, u32[]{:S(2)}, u32[]{:S(2)}) collective-permute-start(f32[304,128]{1,0:T(8,128)} %shard_map.140), channel_id=1, source_target_pairs={{0,8},{8,0},{16,24},{24,16},{1,9},{9,1},{17,25},{25,17},{2,10},{10... | collective-permute-start | bytes 466952 | tf_op jit(solution)/shard_map/ppermute | solution.py:471
  6.8 8.2 %collective-permute-start.4 = (f32[1,128,128]{2,1,0:T(8,128)S(1)}, f32[1,128,128]{2,1,0:T(8,128)S(1)}, u32[]{:S(2)}, u32[]{:S(2)}) collective-permute-start(f32[1,128,128]{2,1,0:T(8,128)S(1)} %bitcast.61), channel_id=1, source_target_pairs={{0,6},{1,7},{2,4},{3,5},{4,2},{5,3},{6,0},{7,1},{8,14},{9,15},{10,... | collective-permute-start | bytes 196616 | tf_op jit(solution)/shard_map/ppermute | solution.py:477
  10.4 5.2 %collective-permute-start.3 = (f32[1,128,128]{2,1,0:T(8,128)S(1)}, f32[1,128,128]{2,1,0:T(8,128)S(1)}, u32[]{:S(2)}, u32[]{:S(2)}) collective-permute-start(f32[1,128,128]{2,1,0:T(8,128)S(1)} %bitcast.62), channel_id=1, source_target_pairs={{0,4},{1,5},{2,6},{3,7},{4,0},{5,1},{6,2},{7,3},{8,12},{9,13},{10,... | collective-permute-start | bytes 196616 | tf_op jit(solution)/shard_map/ppermute | solution.py:477
  10.4 5.2 %collective-permute-start.2 = (f32[1,128,128]{2,1,0:T(8,128)S(1)}, f32[1,128,128]{2,1,0:T(8,128)S(1)}, u32[]{:S(2)}, u32[]{:S(2)}) collective-permute-start(f32[1,128,128]{2,1,0:T(8,128)S(1)} %bitcast.63), channel_id=1, source_target_pairs={{0,2},{1,3},{2,0},{3,1},{4,6},{5,7},{6,4},{7,5},{8,10},{9,11},{10,... | collective-permute-start | bytes 196616 | tf_op jit(solution)/shard_map/ppermute | solution.py:477
  11.4 2.8 %copy-start.4 = (f32[4,512]{1,0:T(4,128)S(1)}, f32[4,512]{1,0:T(4,128)}, u32[]{:S(2)}) copy-start(f32[4,512]{1,0:T(4,128)} %param.15) | copy-start | bytes 24580
  11.4 2.7 %copy-start.5 = (f32[4,512]{1,0:T(4,128)S(1)}, f32[4,512]{1,0:T(4,128)}, u32[]{:S(2)}) copy-start(f32[4,512]{1,0:T(4,128)} %param.16) | copy-start | bytes 24580
  11.4 2.7 %copy-start.6 = (s32[4,512]{1,0:T(4,128)S(1)}, s32[4,512]{1,0:T(4,128)}, u32[]{:S(2)}) copy-start(s32[4,512]{1,0:T(4,128)} %param.17) | copy-start | bytes 24580
  15.7 14.6 %collective-permute-start.7 = (f32[4,128,128]{2,1,0:T(8,128)S(1)}, f32[4,128,128]{2,1,0:T(8,128)S(1)}, u32[]{:S(2)}, u32[]{:S(2)}) collective-permute-start(f32[4,128,128]{2,1,0:T(8,128)S(1)} %shard_map.143.refs_0_), channel_id=1, source_target_pairs={{0,24},{8,16},{16,8},{24,0},{1,25},{9,17},{17,9},{25,1},{2,26},{10... | collective-permute-start | bytes 786440 | tf_op jit(solution)/shard_map/ppermute | solution.py:477
  17.2 13.1 %collective-permute-start.6 = (f32[4,128,128]{2,1,0:T(8,128)S(1)}, f32[4,128,128]{2,1,0:T(8,128)S(1)}, u32[]{:S(2)}, u32[]{:S(2)}) collective-permute-start(f32[4,128,128]{2,1,0:T(8,128)S(1)} %shard_map.143.refs_0_), channel_id=1, source_target_pairs={{0,16},{8,24},{16,0},{24,8},{1,17},{9,25},{17,1},{25,9},{2,18},{10... | collective-permute-start | bytes 786440 | tf_op jit(solution)/shard_map/ppermute | solution.py:477
  18.7 11.6 %collective-permute-start.5 = (f32[4,128,128]{2,1,0:T(8,128)S(1)}, f32[4,128,128]{2,1,0:T(8,128)S(1)}, u32[]{:S(2)}, u32[]{:S(2)}) collective-permute-start(f32[4,128,128]{2,1,0:T(8,128)S(1)} %shard_map.143.refs_0_), channel_id=1, source_target_pairs={{0,8},{8,0},{16,24},{24,16},{1,9},{9,1},{17,25},{25,17},{2,10},{10... | collective-permute-start | bytes 786440 | tf_op jit(solution)/shard_map/ppermute | solution.py:477
  30.5 2.1 %collective-permute-start.8 = (f32[16,72,128]{2,1,0:T(8,128)S(1)}, f32[16,72,128]{2,1,0:T(8,128)S(1)}, u32[]{:S(2)}, u32[]{:S(2)}) collective-permute-start(f32[16,72,128]{2,1,0:T(8,128)S(1)} %shard_map.145), channel_id=1, source_target_pairs={{0,1},{1,0},{2,3},{3,2},{4,5},{5,4},{6,7},{7,6},{8,9},{9,8},{10,11... | collective-permute-start | bytes 1769480 | tf_op jit(solution)/shard_map/ppermute | solution.py:477
  34.0 18.0 %copy-start.1 = (f32[4,4,4,512]{3,2,1,0:T(4,128)S(1)}, f32[4,4,4,512]{3,2,1,0:T(4,128)}, u32[]{:S(2)}) copy-start(f32[4,4,4,512]{3,2,1,0:T(4,128)} %param.14) | copy-start | bytes 393220
  44.2 7.2 %collective-permute-start.10 = (f32[8,32,128]{2,1,0:T(8,128)S(1)}, f32[8,32,128]{2,1,0:T(8,128)S(1)}, u32[]{:S(2)}, u32[]{:S(2)}) collective-permute-start(f32[8,32,128]{2,1,0:T(8,128)S(1)} %all_to_all.16.own_ref), channel_id=1, source_target_pairs={{0,24},{8,16},{16,8},{24,0},{1,25},{9,17},{17,9},{25,1},{2,26},{10... | collective-permute-start | bytes 393224 | tf_op jit(solution)/shard_map/ppermute | solution.py:472
  45.7 6.3 %collective-permute-start.9 = (f32[8,32,128]{2,1,0:T(8,128)S(1)}, f32[8,32,128]{2,1,0:T(8,128)S(1)}, u32[]{:S(2)}, u32[]{:S(2)}) collective-permute-start(f32[8,32,128]{2,1,0:T(8,128)S(1)} %all_to_all.16.own_ref), channel_id=1, source_target_pairs={{0,8},{8,0},{16,24},{24,16},{1,9},{9,1},{17,25},{25,17},{2,10},{10... | collective-permute-start | bytes 393224 | tf_op jit(solution)/shard_map/ppermute | solution.py:471
  52.0 10.9 %copy-start.2 = (f32[4,4,4,512]{3,2,1,0:T(4,128)S(1)}, f32[4,4,4,512]{3,2,1,0:T(4,128)}, u32[]{:S(2)}) copy-start(f32[4,4,4,512]{3,2,1,0:T(4,128)} %param.13) | copy-start | bytes 393220

commit v9 on v8

--- a/solution.py
+++ b/solution.py
@@ -22,9 +22,9 @@
     return flat.reshape(kv, lons // LANES, rows, LANES).swapaxes(1, 2).reshape(shape)
 
 
-def native_rows(ref, base, row, rows, tiles, half):
+def native_rows(ref, row, rows, tiles, half):
     parts = [
-        ref[pl.ds(base + (half * 8 * tiles + tile) * rows + row, 8, stride=tiles * rows), :]
+        ref[pl.ds((half * 8 * tiles + tile) * rows + row, 8, stride=tiles * rows), :]
         for tile in range(tiles)
     ]
     return jnp.concatenate(parts, axis=1)
@@ -53,8 +53,7 @@
 
 
 def sort_halo(pair_ref, cross_ref, low_ref, high_ref):
-    at_y, rows_y = lax.axis_index("gy"), lax.axis_size("gy")
-    odd = lax.rem(at_y, 2) == 1
+    odd = lax.rem(lax.axis_index("gy"), 2) == 1
 
     @pl.when(odd)
     def _():
@@ -65,14 +64,6 @@
     def _():
         low_ref[...] = cross_ref[...]
         high_ref[...] = pair_ref[...]
-
-    @pl.when(at_y == 0)
-    def _():
-        low_ref[...] = jnp.zeros_like(low_ref)
-
-    @pl.when(at_y == rows_y - 1)
-    def _():
-        high_ref[...] = jnp.zeros_like(high_ref)
 
 
 def triangle_masks():
@@ -103,30 +94,46 @@
     return jnp.concatenate([top, jnp.where(lane < half, turned[half:], corner)], axis=0)
 
 
-def halo_kernel(chunks, direction_ref, north_ref, east_ref, ocean_ref, own_ref, stage_ref, mask_ref, sems):
+def halo_kernel(
+    chunks, direction_ref, north_ref, east_ref, ocean_ref, own_ref, stage_ref, mask_ref, sems
+):
     cells, size = direction_ref.shape[0], north_ref.shape[0]
     rows = cells // chunks
-    spans = [(direction_ref.at[pl.ds(at * rows, rows)], at * rows, rows) for at in range(chunks)]
-    spans += [(north_ref, cells, size), (east_ref, cells + size, size)]
+    spans = [(at * rows, rows) for at in range(chunks)] + [(cells, 2 * size)]
+    faces = [
+        pltpu.make_async_copy(ref, to, sems.at[0, at])
+        for at, (ref, to) in enumerate(
+            (
+                (ocean_ref, mask_ref),
+                (north_ref, stage_ref.at[pl.ds(cells, size)]),
+                (east_ref, stage_ref.at[pl.ds(cells + size, size)]),
+            )
+        )
+    ]
     arrive = [
-        pltpu.make_async_copy(source, stage_ref.at[pl.ds(start, count)], sems.at[0, at])
-        for at, (source, start, count) in enumerate(spans)
+        pltpu.make_async_copy(
+            direction_ref.at[pl.ds(start, count)], stage_ref.at[pl.ds(start, count)], sems.at[0, 3 + at]
+        )
+        for at, (start, count) in enumerate(spans[:-1])
     ]
-    arrive.append(pltpu.make_async_copy(ocean_ref, mask_ref, sems.at[0, len(spans)]))
-    spans.append((ocean_ref, cells + 2 * size, size))
     leave = [
         pltpu.make_async_copy(
             stage_ref.at[pl.ds(start, count)], own_ref.at[pl.ds(start, count)], sems.at[1, at]
         )
-        for at, (_, start, count) in enumerate(spans)
+        for at, (start, count) in enumerate(spans)
     ]
-    for copy in arrive:
+    for copy in arrive + faces:
         copy.start()
     for at, copy in enumerate(arrive):
         copy.wait()
-        if at == len(arrive) - 1:
-            stage_ref[cells + 2 * size : cells + 3 * size, :] = mask_ref[...].astype(jnp.float32)
         leave[at].start()
+    for copy in faces:
+        copy.wait()
+    mask = mask_ref[...].astype(jnp.float32)
+    for kind in range(2):
+        here = slice(cells + kind * size, cells + (kind + 1) * size)
+        stage_ref[here, :] = stage_ref[here, :] * mask
+    leave[-1].start()
     for copy in leave:
         copy.wait()
 
@@ -166,18 +173,29 @@
     lons = tiles * LANES
     cells = kv * tiles * rows
     sort_halo(pair_ref, cross_ref, low_ref, high_ref)
+    at_y, rows_y = lax.axis_index("gy"), lax.axis_size("gy")
+    inside = (
+        jnp.where(at_y > 0, 1.0, 0.0).astype(jnp.float32),
+        jnp.where(at_y < rows_y - 1, 1.0, 0.0).astype(jnp.float32),
+    )
     ext_ref[...] = jnp.zeros_like(ext_ref)
-    for kind, kept in enumerate((north_ref, east_ref, ocean_ref)):
-        for tile in range(tiles):
-            lanes = slice(tile * LANES, (tile + 1) * LANES)
-            start = cells + (kind * tiles + tile) * rows
-            ext_ref[kind, 0:rows, lanes] = low_ref[start : start + rows, :]
-            ext_ref[kind, rows : 2 * rows, lanes] = kept[tile * rows : (tile + 1) * rows, :].astype(jnp.float32)
-            ext_ref[kind, 2 * rows : 3 * rows, lanes] = high_ref[start : start + rows, :]
+    for tile in range(tiles):
+        lanes = slice(tile * LANES, (tile + 1) * LANES)
+        here = slice(tile * rows, (tile + 1) * rows)
+        mask = ocean_ref[here, :].astype(jnp.float32)
+        ext_ref[0, rows : 2 * rows, lanes] = north_ref[here, :] * mask
+        ext_ref[1, rows : 2 * rows, lanes] = east_ref[here, :] * mask
+        ext_ref[2, rows : 2 * rows, lanes] = mask
+        for block, ref in ((0, low_ref), (2, high_ref)):
+            across = slice(block * rows, (block + 1) * rows)
+            for kind in range(2):
+                start = cells + (kind * tiles + tile) * rows
+                ext_ref[kind, across, lanes] = ref[start : start + rows, :] * inside[block // 2]
+            ext_ref[2, across, lanes] = jnp.where(ext_ref[0, across, lanes] > 0.0, 1.0, 0.0)
     total = ext_ref.shape[1]
-    north, east, ocean = ext_ref[0], ext_ref[1], ext_ref[2]
-    north_face = north * ocean * pltpu.roll(ocean, total - 1, 0)
-    east_face = east * ocean * pltpu.roll(ocean, lons - 1, 1)
+    ocean = ext_ref[2]
+    north_face = ext_ref[0] * pltpu.roll(ocean, total - 1, 0)
+    east_face = ext_ref[1] * pltpu.roll(ocean, lons - 1, 1)
     south_face = pltpu.roll(north_face, 1, 0)
     west_face = pltpu.roll(east_face, 1, 1)
     coef_ref[0] = ocean - north_face - south_face - east_face - west_face
@@ -188,16 +206,16 @@
     low = lane_low((8, LANES))
     for half in range(kv // 8):
         grown = [
-            native_rows(ref, 0, row, rows, tiles, half)
+            native_rows(ref, row, rows, tiles, half)
             for ref in (low_ref, own_ref, high_ref)
             for row in range(rows)
         ]
         done = lateral_rows(grown, coef_ref, rows)
         for pair in range(rows // 2):
+            at = pair * kv + half * 8
             for tile in range(tiles):
                 first = done[2 * pair][:, tile * LANES : (tile + 1) * LANES]
                 second = done[2 * pair + 1][:, tile * LANES : (tile + 1) * LANES]
-                at = pair * kv + half * 8
                 packed_ref[2 * tile, at : at + 8, :] = jnp.where(
                     low, first, pltpu.roll(second, LANES // 2, 1)
                 )
@@ -239,8 +257,8 @@
                 grown.append(jnp.concatenate(seconds, axis=1))
         done = lateral_rows(grown, coef_ref, rows)
         for row in range(rows):
-            direction = native_rows(direction_ref, 0, row, rows, tiles, half)
-            residual = native_rows(residual_ref, 0, row, rows, tiles, half)
+            direction = native_rows(direction_ref, row, rows, tiles, half)
+            residual = native_rows(residual_ref, row, rows, tiles, half)
             image = direction + done[row]
             for tile in range(tiles):
                 image_ref[pl.ds((half * 8 * tiles + tile) * rows + row, 8, stride=tiles * rows), :] = image[
@@ -508,10 +526,10 @@
     faces = [to_native(x[None, None]) for x in (north_coef, east_coef, ocean)]
     own = call(
         functools.partial(halo_kernel, 4),
-        f32(direction_n.shape[0] + 3 * faces[0].shape[0], LANES),
+        f32(direction_n.shape[0] + 2 * faces[0].shape[0], LANES),
         (direction_n, *faces),
         scratch=(
-            pltpu.VMEM((direction_n.shape[0] + 3 * faces[0].shape[0], LANES), jnp.float32),
+            pltpu.VMEM((direction_n.shape[0] + 2 * faces[0].shape[0], LANES), jnp.float32),
             pltpu.VMEM(faces[0].shape, jnp.int32),
             pltpu.SemaphoreType.DMA((2, 7)),
         ),

time: 64 us -> 63.6 us (level)
  no operation moved by 1% of the time
where the time goes in v9:
time: 63.6 us; the launch traced here: 63.4 us
  blocking collectives  30.5 us (48%)
  starting transfers between devices  14.6 us (23%)
  waiting for transfers between devices  9.02 us (14%)
  Pallas kernels  8.18 us (13%)
  between operations  0.88 us (1%)
    all_to_all x1, blocking collectives, per_device_gathered(): lax.all_to_all(packed, 'gx', split_axis=0, concat_axis=0, tiled=True)  10.4 us
    all_to_all x1, blocking collectives, per_device_gathered(): lax.all_to_all(spread.reshape(cols_x, 2 * kv, LANES), 'gx', split_axis=0,...  10.2 us
    all_to_all x1, blocking collectives, per_device_gathered(): lax.all_to_all(sums, ('gy', 'gx'), split_axis=0, concat_axis=0, tiled=True)  9.93 us
    pallas_call x10, Pallas kernels, call(): pl.pallas_call(kernel, out_shape=out_shape, in_specs=specs, out_specs=tup...  8.18 us
    ppermute x7, starting transfers between devices, apart_by(): lax.ppermute(block, axis, [(i, i ^ stride) for i in range(lax.axis_size(a...  8.01 us
    ppermute x2, starting transfers between devices, from_neighbours(): lax.ppermute(block, 'gy', [(i, (i + (1 if i % 2 else -1)) % count) for i...  5.49 us
    ppermute x2, waiting for transfers between devices, from_neighbours(): lax.ppermute(block, 'gy', [(i, (i + (1 if i % 2 else -1)) % count) for i...  5.18 us
    ppermute x7, waiting for transfers between devices, apart_by(): lax.ppermute(block, axis, [(i, i ^ stride) for i in range(lax.axis_size(a...  2.1 us
  transfers between devices with their start and end apart: 11, of which 5 were waited for; matrix products, arithmetic and copies ran while one was open for 0% of the time, Pallas kernels for 5%

profile of v9, /device:TPU:0, one launch (start us, length us, event | category | flops | bytes accessed | tf_op | source)
XLA Modules:
  0.0 63.4 jit_solution(10919044839949783446)
XLA Ops:
  0.6 0.0 copy-start.3
  0.6 0.0 copy-start.11
  0.7 0.0 copy-start.7
  0.7 0.0 copy-start.8
  0.7 0.0 copy-start.9
  0.7 0.0 copy-start.10
  0.7 1.6 %shard_map.140 = f32[288,128]{1,0:T(8,128)} custom-call(f32[256,128]{1,0:T(8,128)} %bitcast.52, f32[16,128]{1,0:T(8,128)} %bitcast.65, f32[16,128]{1,0:T(8,128)} %bitcast.67, s32[16,128]{1,0:T(8,128)} %bitcast.69), custom_call_target="tpu_custom_call" | custom-call | flops 1000000 | bytes 155648 | tf_op jit(solution)/shard_map/pallas_call | solution.py:472
  2.3 0.0 copy-start
  2.3 4.0 %collective-permute-start.1 = (f32[288,128]{1,0:T(8,128)}, f32[288,128]{1,0:T(8,128)S(1)}, u32[]{:S(2)}, u32[]{:S(2)}) collective-permute-start(f32[288,128]{1,0:T(8,128)} %shard_map.140), channel_id=1, source_target_pairs={{0,24},{8,16},{16,8},{24,0},{1,25},{9,17},{17,9},{25,1},{2,26},{10... | collective-permute-start | bytes 442376 | tf_op jit(solution)/shard_map/ppermute | solution.py:490
  6.3 0.5 collective-permute-start
  6.8 0.0 copy-done.3
  6.8 3.6 %collective-permute-start.4 = (f32[1,128,128]{2,1,0:T(8,128)S(1)}, f32[1,128,128]{2,1,0:T(8,128)S(1)}, u32[]{:S(2)}, u32[]{:S(2)}) collective-permute-start(f32[1,128,128]{2,1,0:T(8,128)S(1)} %bitcast.61), channel_id=1, source_target_pairs={{0,6},{1,7},{2,4},{3,5},{4,2},{5,3},{6,0},{7,1},{8,14},{9,15},{10,... | collective-permute-start | bytes 196616 | tf_op jit(solution)/shard_map/ppermute | solution.py:495
  10.4 0.0 collective-permute-start.3
  10.4 0.8 %collective-permute-start.2 = (f32[1,128,128]{2,1,0:T(8,128)S(1)}, f32[1,128,128]{2,1,0:T(8,128)S(1)}, u32[]{:S(2)}, u32[]{:S(2)}) collective-permute-start(f32[1,128,128]{2,1,0:T(8,128)S(1)} %bitcast.63), channel_id=1, source_target_pairs={{0,2},{1,3},{2,0},{3,1},{4,6},{5,7},{6,4},{7,5},{8,10},{9,11},{10,... | collective-permute-start | bytes 196616 | tf_op jit(solution)/shard_map/ppermute | solution.py:495
  11.2 0.0 copy-done.11
  11.2 0.1 reshape.75.vert_ref
  11.3 0.0 copy-done.7
  11.3 0.0 copy-done.8
  11.3 0.0 copy-done.9
  11.4 0.0 copy-done.10
  11.4 0.0 copy-start.4
  11.4 0.0 copy-start.5
  11.4 0.0 copy-start.6
  11.4 1.1 %shard_map.139 = (f32[3,32,8,128]{3,2,1,0:T(8,128)S(1)}, bf16[256,1024]{1,0:T(8,128)(2,1)S(1)}, bf16[256,1024]{1,0:T(8,128)(2,1)S(1)}) custom-call(f32[32,2,128]{2,1,0:T(2,128)S(1)} %reshape.75.vert_ref, s32[1,512]{1,0:T(1,128)S(1)} %bitcast.72, s32[1,512]{1,0:T(1,128)S(1)} %bitcast.73, s32[1,512]{1,0:T(1,128)S(1)} %bitcast.74, f32[2,512]{1,0:T(2,128)S(1)} %bitcast.71), custom_call_target="tpu_custom_call" | custom-call | flops 20000000 | bytes 43008 | tf_op jit(solution)/shard_map/pallas_call | solution.py:472
  12.5 0.0 collective-permute-done.1.cross_ref
  12.6 1.2 %collective-permute-done.pair_ref = f32[288,128]{1,0:T(8,128)S(1)} collective-permute-done((f32[288,128]{1,0:T(8,128)}, f32[288,128]{1,0:T(8,128)S(1)}, u32[]{:S(2)}, u32[]{:S(2)}) %collective-permute-start) | collective-permute-done | bytes 147488 | tf_op jit(solution)/shard_map/ppermute | solution.py:489
  13.8 0.0 copy-done
  13.8 0.0 copy-done.4
  13.8 0.0 copy-done.5
  13.8 0.0 copy-done.6
  13.8 0.9 %shard_map.141 = (f32[8,32,128]{2,1,0:T(8,128)S(1)}, f32[5,16,512]{2,1,0:T(8,128)S(1)}) custom-call(bf16[256,1024]{1,0:T(8,128)(2,1)S(1)} %get-tuple-element.15._.high_ref, f32[256,128]{1,0:T(8,128)S(1)} %bitcast.53, f32[16,128]{1,0:T(8,128)S(1)} %bitcast.66, f32[16,128]{1,0:T(8,128)S(1)} %bitcast.68, s32[16,128]{1,0:T(8,128)S(1)} %bitcast.70, ...), custom_call_target="tpu_custom_call" | custom-call | flops 4000000 | bytes 1499136 | tf_op jit(solution)/shard_map/pallas_call | solution.py:472
  14.6 0.0 collective-permute-done.4.refs_4_
  14.7 1.0 %collective-permute-done.3.refs_3_ = f32[1,128,128]{2,1,0:T(8,128)S(1)} collective-permute-done((f32[1,128,128]{2,1,0:T(8,128)S(1)}, f32[1,128,128]{2,1,0:T(8,128)S(1)}, u32[]{:S(2)}, u32[]{:S(2)}) %collective-permute-start.3) | collective-permute-done | bytes 65568 | tf_op jit(solution)/shard_map/ppermute | solution.py:495
  15.7 0.0 collective-permute-done.2.refs_2_
  15.7 1.5 %collective-permute-start.7 = (f32[4,128,128]{2,1,0:T(8,128)S(1)}, f32[4,128,128]{2,1,0:T(8,128)S(1)}, u32[]{:S(2)}, u32[]{:S(2)}) collective-permute-start(f32[4,128,128]{2,1,0:T(8,128)S(1)} %shard_map.143.refs_0_), channel_id=1, source_target_pairs={{0,24},{8,16},{16,8},{24,0},{1,25},{9,17},{17,9},{25,1},{2,26},{10... | collective-permute-start | bytes 786440 | tf_op jit(solution)/shard_map/ppermute | solution.py:495
  17.2 1.5 %collective-permute-start.6 = (f32[4,128,128]{2,1,0:T(8,128)S(1)}, f32[4,128,128]{2,1,0:T(8,128)S(1)}, u32[]{:S(2)}, u32[]{:S(2)}) collective-permute-start(f32[4,128,128]{2,1,0:T(8,128)S(1)} %shard_map.143.refs_0_), channel_id=1, source_target_pairs={{0,16},{8,24},{16,0},{24,8},{1,17},{9,25},{17,1},{25,9},{2,18},{10... | collective-permute-start | bytes 786440 | tf_op jit(solution)/shard_map/ppermute | solution.py:495
  18.7 0.5 collective-permute-start.5
  19.3 10.4 %all_to_all.15 = f32[8,32,128]{2,1,0:T(8,128)S(1)} all-to-all(f32[8,32,128]{2,1,0:T(8,128)S(1)} %get-tuple-element.16.refs_0_), channel_id=1, replica_groups=mesh['gy'=4,'gx'=8] {'gx'}, dimensions={0} | all-to-all | bytes 262144 | tf_op jit(solution)/shard_map/all_to_all | solution.py:578
  29.7 0.1 shard_map.142.column_ref._
  29.8 0.0 collective-permute-done.7.refs_3_
  29.9 0.0 collective-permute-done.6.refs_2_
  29.9 0.0 collective-permute-done.5.refs_1_
  29.9 0.2 shard_map.145
  30.1 0.1 collective-permute-start.8
  30.2 0.9 %shard_map.144 = (f32[128,512]{1,0:T(8,128)S(1)}, f32[128,512]{1,0:T(8,128)S(1)}) custom-call(f32[256,128]{1,0:T(8,128)S(1)} %shard_map.142.column_ref._, bf16[256,1024]{1,0:T(8,128)(2,1)S(1)} %get-tuple-element.15._.high_ref, bf16[256,1024]{1,0:T(8,128)(2,1)S(1)} %get-tuple-element.18.low_ref, f32[4,128,128]{2,1,0:T(8,128)S(1)} %shard_map.143.refs_0_, ...), custom_call_target="tpu_custom_call" | custom-call | flops 400000000 | bytes 3276800 | tf_op jit(solution)/shard_map/pallas_call | solution.py:472
  31.1 1.1 %collective-permute-done.8.far_ref = f32[16,72,128]{2,1,0:T(8,128)S(1)} collective-permute-done((f32[16,72,128]{2,1,0:T(8,128)S(1)}, f32[16,72,128]{2,1,0:T(8,128)S(1)}, u32[]{:S(2)}, u32[]{:S(2)}) %collective-permute-start.8) | collective-permute-done | bytes 589856 | tf_op jit(solution)/shard_map/ppermute | solution.py:495
  32.2 1.4 %shard_map.146 = f32[256,128]{1,0:T(8,128)S(1)} custom-call(f32[128,512]{1,0:T(8,128)S(1)} %get-tuple-element.19.near_ref, f32[128,512]{1,0:T(8,128)S(1)} %get-tuple-element.20.profile_ref, f32[3,32,8,128]{3,2,1,0:T(8,128)S(1)} %get-tuple-element.17.factor_ref, bf16[256,1024]{1,0:T(8,128)(2,1)S(1)} %get-tuple-element.15._.high_ref, ...), custom_call_target="tpu_custom_call" | custom-call | flops 400000000 | bytes 3604480 | tf_op jit(solution)/shard_map/pallas_call | solution.py:472
  33.6 0.0 copy-start.1
  33.6 10.2 %all_to_all.16.own_ref = f32[8,32,128]{2,1,0:T(8,128)S(1)} all-to-all(f32[8,32,128]{2,1,0:T(8,128)S(1)} %bitcast.59), channel_id=1, replica_groups=mesh['gy'=4,'gx'=8] {'gx'}, dimensions={0} | all-to-all | bytes 262144 | tf_op jit(solution)/shard_map/all_to_all | solution.py:608
  43.8 1.5 %collective-permute-start.10 = (f32[8,32,128]{2,1,0:T(8,128)S(1)}, f32[8,32,128]{2,1,0:T(8,128)S(1)}, u32[]{:S(2)}, u32[]{:S(2)}) collective-permute-start(f32[8,32,128]{2,1,0:T(8,128)S(1)} %all_to_all.16.own_ref), channel_id=1, source_target_pairs={{0,24},{8,16},{16,8},{24,0},{1,25},{9,17},{17,9},{25,1},{2,26},{10... | collective-permute-start | bytes 393224 | tf_op jit(solution)/shard_map/ppermute | solution.py:490
  45.3 0.5 collective-permute-start.9
  45.9 5.2 %collective-permute-done.10.cross_ref = f32[8,32,128]{2,1,0:T(8,128)S(1)} collective-permute-done((f32[8,32,128]{2,1,0:T(8,128)S(1)}, f32[8,32,128]{2,1,0:T(8,128)S(1)}, u32[]{:S(2)}, u32[]{:S(2)}) %collective-permute-start.10) | collective-permute-done | bytes 131104 | tf_op jit(solution)/shard_map/ppermute | solution.py:490
  51.0 0.5 collective-permute-done.9.pair_ref
  51.6 0.0 copy-done.1
  51.6 0.0 copy-start.2
  51.6 0.9 %shard_map.147 = (f32[256,128]{1,0:T(8,128)S(1)}, f32[32,1,128]{2,1,0:T(1,128)S(1)}) custom-call(f32[8,32,128]{2,1,0:T(8,128)S(1)} %all_to_all.16.own_ref, f32[8,32,128]{2,1,0:T(8,128)S(1)} %collective-permute-done.9.pair_ref, f32[8,32,128]{2,1,0:T(8,128)S(1)} %collective-permute-done.10.cross_ref, f32[5,16,512]{2,1,0:T(8,128)S(1)} %get-tuple-element.21.coef_ref, ...), custom_call_target="tpu_custom_call" | custom-call | flops 4000000 | bytes 819200 | tf_op jit(solution)/shard_map/pallas_call | solution.py:472
  52.5 9.9 %all_to_all.17.sums_ref = f32[32,1,128]{2,1,0:T(1,128)S(1)} all-to-all(f32[32,1,128]{2,1,0:T(1,128)S(1)} %get-tuple-element.22), channel_id=1, replica_groups=mesh['gy'=4,'gx'=8] {'gy','gx'}, dimensions={0} | all-to-all | bytes 32768 | tf_op jit(solution)/shard_map/all_to_all | solution.py:619
  62.5 0.0 copy-done.2
  62.5 0.9 %shard_map.148 = (f32[256,128]{1,0:T(8,128)}, f32[256,128]{1,0:T(8,128)}, f32[256,128]{1,0:T(8,128)}) custom-call(f32[32,1,128]{2,1,0:T(1,128)S(1)} %all_to_all.17.sums_ref, f32[256,128]{1,0:T(8,128)S(1)} %bitcast.55, f32[256,128]{1,0:T(8,128)S(1)} %bitcast.60, f32[256,128]{1,0:T(8,128)S(1)} %bitcast.58, f32[256,128]{1,0:T(8,128)S(1)} %get-tuple-element.23.image_ref), custom_call_target="tpu_custom_call" | custom-call | flops 1000000 | bytes 540672 | tf_op jit(solution)/shard_map/pallas_call | solution.py:472
  (1 shorter events, 0.0 us)
Async XLA Ops:
  0.6 6.2 %copy-start.3 = (f32[1,1,128,128]{3,2,1,0:T(8,128)S(1)}, f32[1,1,128,128]{3,2,1,0:T(8,128)}, u32[]{:S(2)}) copy-start(f32[1,1,128,128]{3,2,1,0:T(8,128)} %param.23) | copy-start | bytes 196612
  0.6 10.6 %copy-start.11 = (f32[32,4,64]{2,1,0:T(4,128)S(1)}, f32[32,4,64]{2,1,0:T(4,128)}, u32[]{:S(2)}) copy-start(f32[32,4,64]{2,1,0:T(4,128)} %param.18) | copy-start | bytes 98308
  0.7 10.7 %copy-start.7 = (f32[1,1,2,512]{3,2,1,0:T(2,128)S(1)}, f32[1,1,2,512]{3,2,1,0:T(2,128)}, u32[]{:S(2)}) copy-start(f32[1,1,2,512]{3,2,1,0:T(2,128)} %param.22) | copy-start | bytes 12292
  0.7 10.7 %copy-start.8 = (s32[1,1,512,1]{2,3,1,0:T(1,128)S(1)}, s32[1,1,512,1]{2,3,1,0:T(1,128)}, u32[]{:S(2)}) copy-start(s32[1,1,512,1]{2,3,1,0:T(1,128)} %param.19) | copy-start | bytes 6148
  0.7 10.7 %copy-start.9 = (s32[1,1,512]{2,1,0:T(1,128)S(1)}, s32[1,1,512]{2,1,0:T(1,128)}, u32[]{:S(2)}) copy-start(s32[1,1,512]{2,1,0:T(1,128)} %param.20) | copy-start | bytes 6148
  0.7 10.7 %copy-start.10 = (s32[1,1,512]{2,1,0:T(1,128)S(1)}, s32[1,1,512]{2,1,0:T(1,128)}, u32[]{:S(2)}) copy-start(s32[1,1,512]{2,1,0:T(1,128)} %param.21) | copy-start | bytes 6148
  2.3 11.4 %copy-start = (f32[4,4,4,512]{3,2,1,0:T(4,128)S(1)}, f32[4,4,4,512]{3,2,1,0:T(4,128)}, u32[]{:S(2)}) copy-start(f32[4,4,4,512]{3,2,1,0:T(4,128)} %param.12) | copy-start | bytes 393220
  2.3 10.2 %collective-permute-start.1 = (f32[288,128]{1,0:T(8,128)}, f32[288,128]{1,0:T(8,128)S(1)}, u32[]{:S(2)}, u32[]{:S(2)}) collective-permute-start(f32[288,128]{1,0:T(8,128)} %shard_map.140), channel_id=1, source_target_pairs={{0,24},{8,16},{16,8},{24,0},{1,25},{9,17},{17,9},{25,1},{2,26},{10... | collective-permute-start | bytes 442376 | tf_op jit(solution)/shard_map/ppermute | solution.py:490
  6.3 7.5 %collective-permute-start = (f32[288,128]{1,0:T(8,128)}, f32[288,128]{1,0:T(8,128)S(1)}, u32[]{:S(2)}, u32[]{:S(2)}) collective-permute-start(f32[288,128]{1,0:T(8,128)} %shard_map.140), channel_id=1, source_target_pairs={{0,8},{8,0},{16,24},{24,16},{1,9},{9,1},{17,25},{25,17},{2,10},{10... | collective-permute-start | bytes 442376 | tf_op jit(solution)/shard_map/ppermute | solution.py:489
  6.8 7.8 %collective-permute-start.4 = (f32[1,128,128]{2,1,0:T(8,128)S(1)}, f32[1,128,128]{2,1,0:T(8,128)S(1)}, u32[]{:S(2)}, u32[]{:S(2)}) collective-permute-start(f32[1,128,128]{2,1,0:T(8,128)S(1)} %bitcast.61), channel_id=1, source_target_pairs={{0,6},{1,7},{2,4},{3,5},{4,2},{5,3},{6,0},{7,1},{8,14},{9,15},{10,... | collective-permute-start | bytes 196616 | tf_op jit(solution)/shard_map/ppermute | solution.py:495
  10.4 5.2 %collective-permute-start.3 = (f32[1,128,128]{2,1,0:T(8,128)S(1)}, f32[1,128,128]{2,1,0:T(8,128)S(1)}, u32[]{:S(2)}, u32[]{:S(2)}) collective-permute-start(f32[1,128,128]{2,1,0:T(8,128)S(1)} %bitcast.62), channel_id=1, source_target_pairs={{0,4},{1,5},{2,6},{3,7},{4,0},{5,1},{6,2},{7,3},{8,12},{9,13},{10,... | collective-permute-start | bytes 196616 | tf_op jit(solution)/shard_map/ppermute | solution.py:495
  10.4 5.2 %collective-permute-start.2 = (f32[1,128,128]{2,1,0:T(8,128)S(1)}, f32[1,128,128]{2,1,0:T(8,128)S(1)}, u32[]{:S(2)}, u32[]{:S(2)}) collective-permute-start(f32[1,128,128]{2,1,0:T(8,128)S(1)} %bitcast.63), channel_id=1, source_target_pairs={{0,2},{1,3},{2,0},{3,1},{4,6},{5,7},{6,4},{7,5},{8,10},{9,11},{10,... | collective-permute-start | bytes 196616 | tf_op jit(solution)/shard_map/ppermute | solution.py:495
  11.4 2.4 %copy-start.4 = (f32[4,512]{1,0:T(4,128)S(1)}, f32[4,512]{1,0:T(4,128)}, u32[]{:S(2)}) copy-start(f32[4,512]{1,0:T(4,128)} %param.15) | copy-start | bytes 24580
  11.4 2.4 %copy-start.5 = (f32[4,512]{1,0:T(4,128)S(1)}, f32[4,512]{1,0:T(4,128)}, u32[]{:S(2)}) copy-start(f32[4,512]{1,0:T(4,128)} %param.16) | copy-start | bytes 24580
  11.4 2.4 %copy-start.6 = (s32[4,512]{1,0:T(4,128)S(1)}, s32[4,512]{1,0:T(4,128)}, u32[]{:S(2)}) copy-start(s32[4,512]{1,0:T(4,128)} %param.17) | copy-start | bytes 24580
  15.7 14.1 %collective-permute-start.7 = (f32[4,128,128]{2,1,0:T(8,128)S(1)}, f32[4,128,128]{2,1,0:T(8,128)S(1)}, u32[]{:S(2)}, u32[]{:S(2)}) collective-permute-start(f32[4,128,128]{2,1,0:T(8,128)S(1)} %shard_map.143.refs_0_), channel_id=1, source_target_pairs={{0,24},{8,16},{16,8},{24,0},{1,25},{9,17},{17,9},{25,1},{2,26},{10... | collective-permute-start | bytes 786440 | tf_op jit(solution)/shard_map/ppermute | solution.py:495
  17.2 12.7 %collective-permute-start.6 = (f32[4,128,128]{2,1,0:T(8,128)S(1)}, f32[4,128,128]{2,1,0:T(8,128)S(1)}, u32[]{:S(2)}, u32[]{:S(2)}) collective-permute-start(f32[4,128,128]{2,1,0:T(8,128)S(1)} %shard_map.143.refs_0_), channel_id=1, source_target_pairs={{0,16},{8,24},{16,0},{24,8},{1,17},{9,25},{17,1},{25,9},{2,18},{10... | collective-permute-start | bytes 786440 | tf_op jit(solution)/shard_map/ppermute | solution.py:495
  18.7 11.1 %collective-permute-start.5 = (f32[4,128,128]{2,1,0:T(8,128)S(1)}, f32[4,128,128]{2,1,0:T(8,128)S(1)}, u32[]{:S(2)}, u32[]{:S(2)}) collective-permute-start(f32[4,128,128]{2,1,0:T(8,128)S(1)} %shard_map.143.refs_0_), channel_id=1, source_target_pairs={{0,8},{8,0},{16,24},{24,16},{1,9},{9,1},{17,25},{25,17},{2,10},{10... | collective-permute-start | bytes 786440 | tf_op jit(solution)/shard_map/ppermute | solution.py:495
  30.1 2.1 %collective-permute-start.8 = (f32[16,72,128]{2,1,0:T(8,128)S(1)}, f32[16,72,128]{2,1,0:T(8,128)S(1)}, u32[]{:S(2)}, u32[]{:S(2)}) collective-permute-start(f32[16,72,128]{2,1,0:T(8,128)S(1)} %shard_map.145), channel_id=1, source_target_pairs={{0,1},{1,0},{2,3},{3,2},{4,5},{5,4},{6,7},{7,6},{8,9},{9,8},{10,11... | collective-permute-start | bytes 1769480 | tf_op jit(solution)/shard_map/ppermute | solution.py:495
  33.6 18.0 %copy-start.1 = (f32[4,4,4,512]{3,2,1,0:T(4,128)S(1)}, f32[4,4,4,512]{3,2,1,0:T(4,128)}, u32[]{:S(2)}) copy-start(f32[4,4,4,512]{3,2,1,0:T(4,128)} %param.14) | copy-start | bytes 393220
  43.8 7.2 %collective-permute-start.10 = (f32[8,32,128]{2,1,0:T(8,128)S(1)}, f32[8,32,128]{2,1,0:T(8,128)S(1)}, u32[]{:S(2)}, u32[]{:S(2)}) collective-permute-start(f32[8,32,128]{2,1,0:T(8,128)S(1)} %all_to_all.16.own_ref), channel_id=1, source_target_pairs={{0,24},{8,16},{16,8},{24,0},{1,25},{9,17},{17,9},{25,1},{2,26},{10... | collective-permute-start | bytes 393224 | tf_op jit(solution)/shard_map/ppermute | solution.py:490
  45.3 6.3 %collective-permute-start.9 = (f32[8,32,128]{2,1,0:T(8,128)S(1)}, f32[8,32,128]{2,1,0:T(8,128)S(1)}, u32[]{:S(2)}, u32[]{:S(2)}) collective-permute-start(f32[8,32,128]{2,1,0:T(8,128)S(1)} %all_to_all.16.own_ref), channel_id=1, source_target_pairs={{0,8},{8,0},{16,24},{24,16},{1,9},{9,1},{17,25},{25,17},{2,10},{10... | collective-permute-start | bytes 393224 | tf_op jit(solution)/shard_map/ppermute | solution.py:489
  51.6 10.9 %copy-start.2 = (f32[4,4,4,512]{3,2,1,0:T(4,128)S(1)}, f32[4,4,4,512]{3,2,1,0:T(4,128)}, u32[]{:S(2)}) copy-start(f32[4,4,4,512]{3,2,1,0:T(4,128)} %param.13) | copy-start | bytes 393220

commit v10 on v9

--- a/solution.py
+++ b/solution.py
@@ -138,19 +138,17 @@
         copy.wait()
 
 
-def join_kernel(after, count, *refs):
-    blocks, (near_ref,) = refs[after : after + count], refs[after + count :]
+def join_kernel(_, *refs):
+    blocks, (out_ref,) = refs[:-1], refs[-1:]
     size = blocks[0].shape[0]
     for at, block in enumerate(blocks):
-        near_ref[at * size : (at + 1) * size] = block[...]
-
-
-def pack_kernel(_, *refs):
+        out_ref[at * size : (at + 1) * size] = block[:, : out_ref.shape[1], :]
+
+
+def hold_kernel(_, *refs):
     blocks, (packed_ref,) = refs[:-1], refs[-1:]
-    size = blocks[0].shape[0]
     for at, block in enumerate(blocks):
-        for inner in range(size):
-            pack_symmetric(block[inner], packed_ref.at[at * size + inner])
+        pack_symmetric(block[0], packed_ref.at[at])
 
 
 def first_lateral_kernel(
@@ -438,7 +436,9 @@
     columns = jnp.concatenate([column_ref[0:kv, :], column_ref[kv : 2 * kv, :]], axis=1)
     profile = dot_parts(split(columns), (high_ref[...], low_ref[...]), ((1,), (0,)))
     profile_ref[...] = profile[:, half:]
-    weighted_ref[...] = weigh(profile[:, :half], lambda at: near_refs[at // size][at % size], capacity)
+    weighted_ref[...] = weigh(
+        profile[:, :half], lambda at: unpack_symmetric(near_refs[at // size][at % size]), capacity
+    )
 
 
 def spread_kernel(
@@ -568,12 +568,8 @@
         flops=4_000_000,
     )
     held_blocks = call(
-        functools.partial(join_kernel, 1, len(blocks)),
-        f32(len(blocks), wide, wide),
-        (packed, *blocks),
-        after=1,
-    )
-
+        hold_kernel, f32(len(blocks), wide - 8, wide), (packed, *blocks), after=1
+    )
     fetched = [held_blocks] + [apart_by(held_blocks, "gy", stride) for stride in range(1, rows_y)]
     columns = lax.all_to_all(packed, "gx", split_axis=0, concat_axis=0, tiled=True)
     smoothed = call(
@@ -584,7 +580,7 @@
     )
     far = apart_by(
         call(
-            pack_kernel, f32(device_count // 2, wide // 2 + 8, wide), (smoothed, *fetched), after=1
+            join_kernel, f32(device_count // 2, wide // 2 + 8, wide), (columns, *fetched), after=1
         ),
         "gx",
         1,

time: 63.6 us -> 63.3 us (level)
  no operation moved by 1% of the time
where the time goes in v10:
time: 63.3 us; the launch traced here: 63 us
  blocking collectives  30.5 us (48%)
  starting transfers between devices  14.6 us (23%)
  waiting for transfers between devices  8.84 us (14%)
  Pallas kernels  8.13 us (13%)
  between operations  0.86 us (1%)
    all_to_all x1, blocking collectives, per_device_gathered(): lax.all_to_all(packed, 'gx', split_axis=0, concat_axis=0, tiled=True)  10.4 us
    all_to_all x1, blocking collectives, per_device_gathered(): lax.all_to_all(sums, ('gy', 'gx'), split_axis=0, concat_axis=0, tiled=True)  10.4 us
    all_to_all x1, blocking collectives, per_device_gathered(): lax.all_to_all(spread.reshape(cols_x, 2 * kv, LANES), 'gx', split_axis=0,...  9.63 us
    pallas_call x10, Pallas kernels, call(): pl.pallas_call(kernel, out_shape=out_shape, in_specs=specs, out_specs=tup...  8.13 us
    ppermute x7, starting transfers between devices, apart_by(): lax.ppermute(block, axis, [(i, i ^ stride) for i in range(lax.axis_size(a...  8.01 us
    ppermute x2, starting transfers between devices, from_neighbours(): lax.ppermute(block, 'gy', [(i, (i + (1 if i % 2 else -1)) % count) for i...  5.49 us
    ppermute x2, waiting for transfers between devices, from_neighbours(): lax.ppermute(block, 'gy', [(i, (i + (1 if i % 2 else -1)) % count) for i...  5.17 us
    ppermute x7, waiting for transfers between devices, apart_by(): lax.ppermute(block, axis, [(i, i ^ stride) for i in range(lax.axis_size(a...  1.92 us
  transfers between devices with their start and end apart: 11, of which 5 were waited for; matrix products, arithmetic and copies ran while one was open for 0% of the time, Pallas kernels for 5%

profile of v10, /device:TPU:0, one launch (start us, length us, event | category | flops | bytes accessed | tf_op | source)
XLA Modules:
  0.0 63.0 jit_solution(3202988988865450838)
XLA Ops:
  0.6 0.0 copy-start.3
  0.6 0.0 copy-start.11
  0.7 0.0 copy-start.7
  0.7 0.0 copy-start.8
  0.7 0.0 copy-start.9
  0.7 0.0 copy-start.10
  0.7 1.6 %shard_map.140 = f32[288,128]{1,0:T(8,128)} custom-call(f32[256,128]{1,0:T(8,128)} %bitcast.52, f32[16,128]{1,0:T(8,128)} %bitcast.65, f32[16,128]{1,0:T(8,128)} %bitcast.67, s32[16,128]{1,0:T(8,128)} %bitcast.69), custom_call_target="tpu_custom_call" | custom-call | flops 1000000 | bytes 155648 | tf_op jit(solution)/shard_map/pallas_call | solution.py:472
  2.3 0.0 copy-start
  2.3 4.0 %collective-permute-start.1 = (f32[288,128]{1,0:T(8,128)}, f32[288,128]{1,0:T(8,128)S(1)}, u32[]{:S(2)}, u32[]{:S(2)}) collective-permute-start(f32[288,128]{1,0:T(8,128)} %shard_map.140), channel_id=1, source_target_pairs={{0,24},{8,16},{16,8},{24,0},{1,25},{9,17},{17,9},{25,1},{2,26},{10... | collective-permute-start | bytes 442376 | tf_op jit(solution)/shard_map/ppermute | solution.py:490
  6.3 0.5 collective-permute-start
  6.8 0.0 copy-done.3
  6.8 3.6 %collective-permute-start.4 = (f32[1,128,128]{2,1,0:T(8,128)S(1)}, f32[1,128,128]{2,1,0:T(8,128)S(1)}, u32[]{:S(2)}, u32[]{:S(2)}) collective-permute-start(f32[1,128,128]{2,1,0:T(8,128)S(1)} %bitcast.61), channel_id=1, source_target_pairs={{0,6},{1,7},{2,4},{3,5},{4,2},{5,3},{6,0},{7,1},{8,14},{9,15},{10,... | collective-permute-start | bytes 196616 | tf_op jit(solution)/shard_map/ppermute | solution.py:495
  10.4 0.0 collective-permute-start.3
  10.4 0.8 %collective-permute-start.2 = (f32[1,128,128]{2,1,0:T(8,128)S(1)}, f32[1,128,128]{2,1,0:T(8,128)S(1)}, u32[]{:S(2)}, u32[]{:S(2)}) collective-permute-start(f32[1,128,128]{2,1,0:T(8,128)S(1)} %bitcast.63), channel_id=1, source_target_pairs={{0,2},{1,3},{2,0},{3,1},{4,6},{5,7},{6,4},{7,5},{8,10},{9,11},{10,... | collective-permute-start | bytes 196616 | tf_op jit(solution)/shard_map/ppermute | solution.py:495
  11.2 0.0 copy-done.11
  11.2 0.1 reshape.75.vert_ref
  11.3 0.0 copy-done.7
  11.3 0.0 copy-done.8
  11.3 0.0 copy-done.9
  11.4 0.0 copy-done.10
  11.4 0.0 copy-start.4
  11.4 0.0 copy-start.5
  11.4 0.0 copy-start.6
  11.4 1.1 %shard_map.139 = (f32[3,32,8,128]{3,2,1,0:T(8,128)S(1)}, bf16[256,1024]{1,0:T(8,128)(2,1)S(1)}, bf16[256,1024]{1,0:T(8,128)(2,1)S(1)}) custom-call(f32[32,2,128]{2,1,0:T(2,128)S(1)} %reshape.75.vert_ref, s32[1,512]{1,0:T(1,128)S(1)} %bitcast.72, s32[1,512]{1,0:T(1,128)S(1)} %bitcast.73, s32[1,512]{1,0:T(1,128)S(1)} %bitcast.74, f32[2,512]{1,0:T(2,128)S(1)} %bitcast.71), custom_call_target="tpu_custom_call" | custom-call | flops 20000000 | bytes 43008 | tf_op jit(solution)/shard_map/pallas_call | solution.py:472
  12.5 0.0 collective-permute-done.1.cross_ref
  12.6 1.2 %collective-permute-done.pair_ref = f32[288,128]{1,0:T(8,128)S(1)} collective-permute-done((f32[288,128]{1,0:T(8,128)}, f32[288,128]{1,0:T(8,128)S(1)}, u32[]{:S(2)}, u32[]{:S(2)}) %collective-permute-start) | collective-permute-done | bytes 147488 | tf_op jit(solution)/shard_map/ppermute | solution.py:489
  13.8 0.0 copy-done
  13.8 0.0 copy-done.4
  13.8 0.0 copy-done.5
  13.8 0.0 copy-done.6
  13.8 0.9 %shard_map.141 = (f32[8,32,128]{2,1,0:T(8,128)S(1)}, f32[5,16,512]{2,1,0:T(8,128)S(1)}) custom-call(bf16[256,1024]{1,0:T(8,128)(2,1)S(1)} %get-tuple-element.15._.high_ref, f32[256,128]{1,0:T(8,128)S(1)} %bitcast.53, f32[16,128]{1,0:T(8,128)S(1)} %bitcast.66, f32[16,128]{1,0:T(8,128)S(1)} %bitcast.68, s32[16,128]{1,0:T(8,128)S(1)} %bitcast.70, ...), custom_call_target="tpu_custom_call" | custom-call | flops 4000000 | bytes 1499136 | tf_op jit(solution)/shard_map/pallas_call | solution.py:472
  14.6 0.0 collective-permute-done.4.refs_3_
  14.7 1.0 %collective-permute-done.3.refs_2_ = f32[1,128,128]{2,1,0:T(8,128)S(1)} collective-permute-done((f32[1,128,128]{2,1,0:T(8,128)S(1)}, f32[1,128,128]{2,1,0:T(8,128)S(1)}, u32[]{:S(2)}, u32[]{:S(2)}) %collective-permute-start.3) | collective-permute-done | bytes 65568 | tf_op jit(solution)/shard_map/ppermute | solution.py:495
  15.7 0.0 collective-permute-done.2.refs_1_
  15.7 0.1 shard_map.143.refs_0_
  15.8 1.5 %collective-permute-start.7 = (f32[4,120,128]{2,1,0:T(8,128)S(1)}, f32[4,120,128]{2,1,0:T(8,128)S(1)}, u32[]{:S(2)}, u32[]{:S(2)}) collective-permute-start(f32[4,120,128]{2,1,0:T(8,128)S(1)} %shard_map.143.refs_0_), channel_id=1, source_target_pairs={{0,24},{8,16},{16,8},{24,0},{1,25},{9,17},{17,9},{25,1},{2,26},{10... | collective-permute-start | bytes 737288 | tf_op jit(solution)/shard_map/ppermute | solution.py:495
  17.3 1.5 %collective-permute-start.6 = (f32[4,120,128]{2,1,0:T(8,128)S(1)}, f32[4,120,128]{2,1,0:T(8,128)S(1)}, u32[]{:S(2)}, u32[]{:S(2)}) collective-permute-start(f32[4,120,128]{2,1,0:T(8,128)S(1)} %shard_map.143.refs_0_), channel_id=1, source_target_pairs={{0,16},{8,24},{16,0},{24,8},{1,17},{9,25},{17,1},{25,9},{2,18},{10... | collective-permute-start | bytes 737288 | tf_op jit(solution)/shard_map/ppermute | solution.py:495
  18.8 0.5 collective-permute-start.5
  19.3 10.4 %all_to_all.15._ = f32[8,32,128]{2,1,0:T(8,128)S(1)} all-to-all(f32[8,32,128]{2,1,0:T(8,128)S(1)} %get-tuple-element.16._), channel_id=1, replica_groups=mesh['gy'=4,'gx'=8] {'gx'}, dimensions={0} | all-to-all | bytes 262144 | tf_op jit(solution)/shard_map/all_to_all | solution.py:574
  29.8 0.0 collective-permute-done.7.refs_3_
  29.8 0.0 collective-permute-done.6.refs_2_
  29.8 0.0 collective-permute-done.5.refs_1_
  29.8 0.1 collective-permute-start.8
  29.9 0.1 shard_map.142.column_ref
  30.1 1.0 %shard_map.144 = (f32[128,512]{1,0:T(8,128)S(1)}, f32[128,512]{1,0:T(8,128)S(1)}) custom-call(f32[256,128]{1,0:T(8,128)S(1)} %shard_map.142.column_ref, bf16[256,1024]{1,0:T(8,128)(2,1)S(1)} %get-tuple-element.15._.high_ref, bf16[256,1024]{1,0:T(8,128)(2,1)S(1)} %get-tuple-element.18.low_ref, f32[4,120,128]{2,1,0:T(8,128)S(1)} %shard_map.143.refs_0_, ...), custom_call_target="tpu_custom_call" | custom-call | flops 400000000 | bytes 3211264 | tf_op jit(solution)/shard_map/pallas_call | solution.py:472
  31.0 0.9 %collective-permute-done.8.far_ref = f32[16,72,128]{2,1,0:T(8,128)S(1)} collective-permute-done((f32[16,72,128]{2,1,0:T(8,128)S(1)}, f32[16,72,128]{2,1,0:T(8,128)S(1)}, u32[]{:S(2)}, u32[]{:S(2)}) %collective-permute-start.8) | collective-permute-done | bytes 589856 | tf_op jit(solution)/shard_map/ppermute | solution.py:495
  31.9 1.4 %shard_map.146 = f32[256,128]{1,0:T(8,128)S(1)} custom-call(f32[128,512]{1,0:T(8,128)S(1)} %get-tuple-element.19.near_ref, f32[128,512]{1,0:T(8,128)S(1)} %get-tuple-element.20.profile_ref, f32[3,32,8,128]{3,2,1,0:T(8,128)S(1)} %get-tuple-element.17.factor_ref, bf16[256,1024]{1,0:T(8,128)(2,1)S(1)} %get-tuple-element.15._.high_ref, ...), custom_call_target="tpu_custom_call" | custom-call | flops 400000000 | bytes 3604480 | tf_op jit(solution)/shard_map/pallas_call | solution.py:472
  33.4 0.0 copy-start.1
  33.4 9.6 %all_to_all.16.own_ref = f32[8,32,128]{2,1,0:T(8,128)S(1)} all-to-all(f32[8,32,128]{2,1,0:T(8,128)S(1)} %bitcast.59), channel_id=1, replica_groups=mesh['gy'=4,'gx'=8] {'gx'}, dimensions={0} | all-to-all | bytes 262144 | tf_op jit(solution)/shard_map/all_to_all | solution.py:604
  43.0 1.5 %collective-permute-start.10 = (f32[8,32,128]{2,1,0:T(8,128)S(1)}, f32[8,32,128]{2,1,0:T(8,128)S(1)}, u32[]{:S(2)}, u32[]{:S(2)}) collective-permute-start(f32[8,32,128]{2,1,0:T(8,128)S(1)} %all_to_all.16.own_ref), channel_id=1, source_target_pairs={{0,24},{8,16},{16,8},{24,0},{1,25},{9,17},{17,9},{25,1},{2,26},{10... | collective-permute-start | bytes 393224 | tf_op jit(solution)/shard_map/ppermute | solution.py:490
  44.5 0.5 collective-permute-start.9
  45.1 5.2 %collective-permute-done.10.cross_ref = f32[8,32,128]{2,1,0:T(8,128)S(1)} collective-permute-done((f32[8,32,128]{2,1,0:T(8,128)S(1)}, f32[8,32,128]{2,1,0:T(8,128)S(1)}, u32[]{:S(2)}, u32[]{:S(2)}) %collective-permute-start.10) | collective-permute-done | bytes 131104 | tf_op jit(solution)/shard_map/ppermute | solution.py:490
  50.2 0.5 collective-permute-done.9.pair_ref
  50.8 0.0 copy-done.1
  50.8 0.0 copy-start.2
  50.8 0.9 %shard_map.147 = (f32[256,128]{1,0:T(8,128)S(1)}, f32[32,1,128]{2,1,0:T(1,128)S(1)}) custom-call(f32[8,32,128]{2,1,0:T(8,128)S(1)} %all_to_all.16.own_ref, f32[8,32,128]{2,1,0:T(8,128)S(1)} %collective-permute-done.9.pair_ref, f32[8,32,128]{2,1,0:T(8,128)S(1)} %collective-permute-done.10.cross_ref, f32[5,16,512]{2,1,0:T(8,128)S(1)} %get-tuple-element.21.coef_ref, ...), custom_call_target="tpu_custom_call" | custom-call | flops 4000000 | bytes 819200 | tf_op jit(solution)/shard_map/pallas_call | solution.py:472
  51.7 10.4 %all_to_all.17.sums_ref = f32[32,1,128]{2,1,0:T(1,128)S(1)} all-to-all(f32[32,1,128]{2,1,0:T(1,128)S(1)} %get-tuple-element.22), channel_id=1, replica_groups=mesh['gy'=4,'gx'=8] {'gy','gx'}, dimensions={0} | all-to-all | bytes 32768 | tf_op jit(solution)/shard_map/all_to_all | solution.py:615
  62.1 0.0 copy-done.2
  62.1 0.9 %shard_map.148 = (f32[256,128]{1,0:T(8,128)}, f32[256,128]{1,0:T(8,128)}, f32[256,128]{1,0:T(8,128)}) custom-call(f32[32,1,128]{2,1,0:T(1,128)S(1)} %all_to_all.17.sums_ref, f32[256,128]{1,0:T(8,128)S(1)} %bitcast.55, f32[256,128]{1,0:T(8,128)S(1)} %bitcast.60, f32[256,128]{1,0:T(8,128)S(1)} %bitcast.58, f32[256,128]{1,0:T(8,128)S(1)} %get-tuple-element.23.image_ref), custom_call_target="tpu_custom_call" | custom-call | flops 1000000 | bytes 540672 | tf_op jit(solution)/shard_map/pallas_call | solution.py:472
  (1 shorter events, 0.0 us)
Async XLA Ops:
  0.6 6.2 %copy-start.3 = (f32[1,1,128,128]{3,2,1,0:T(8,128)S(1)}, f32[1,1,128,128]{3,2,1,0:T(8,128)}, u32[]{:S(2)}) copy-start(f32[1,1,128,128]{3,2,1,0:T(8,128)} %param.23) | copy-start | bytes 196612
  0.6 10.6 %copy-start.11 = (f32[32,4,64]{2,1,0:T(4,128)S(1)}, f32[32,4,64]{2,1,0:T(4,128)}, u32[]{:S(2)}) copy-start(f32[32,4,64]{2,1,0:T(4,128)} %param.18) | copy-start | bytes 98308
  0.7 10.7 %copy-start.7 = (f32[1,1,2,512]{3,2,1,0:T(2,128)S(1)}, f32[1,1,2,512]{3,2,1,0:T(2,128)}, u32[]{:S(2)}) copy-start(f32[1,1,2,512]{3,2,1,0:T(2,128)} %param.22) | copy-start | bytes 12292
  0.7 10.7 %copy-start.8 = (s32[1,1,512,1]{2,3,1,0:T(1,128)S(1)}, s32[1,1,512,1]{2,3,1,0:T(1,128)}, u32[]{:S(2)}) copy-start(s32[1,1,512,1]{2,3,1,0:T(1,128)} %param.19) | copy-start | bytes 6148
  0.7 10.7 %copy-start.9 = (s32[1,1,512]{2,1,0:T(1,128)S(1)}, s32[1,1,512]{2,1,0:T(1,128)}, u32[]{:S(2)}) copy-start(s32[1,1,512]{2,1,0:T(1,128)} %param.20) | copy-start | bytes 6148
  0.7 10.7 %copy-start.10 = (s32[1,1,512]{2,1,0:T(1,128)S(1)}, s32[1,1,512]{2,1,0:T(1,128)}, u32[]{:S(2)}) copy-start(s32[1,1,512]{2,1,0:T(1,128)} %param.21) | copy-start | bytes 6148
  2.3 11.4 %copy-start = (f32[4,4,4,512]{3,2,1,0:T(4,128)S(1)}, f32[4,4,4,512]{3,2,1,0:T(4,128)}, u32[]{:S(2)}) copy-start(f32[4,4,4,512]{3,2,1,0:T(4,128)} %param.12) | copy-start | bytes 393220
  2.3 10.2 %collective-permute-start.1 = (f32[288,128]{1,0:T(8,128)}, f32[288,128]{1,0:T(8,128)S(1)}, u32[]{:S(2)}, u32[]{:S(2)}) collective-permute-start(f32[288,128]{1,0:T(8,128)} %shard_map.140), channel_id=1, source_target_pairs={{0,24},{8,16},{16,8},{24,0},{1,25},{9,17},{17,9},{25,1},{2,26},{10... | collective-permute-start | bytes 442376 | tf_op jit(solution)/shard_map/ppermute | solution.py:490
  6.3 7.5 %collective-permute-start = (f32[288,128]{1,0:T(8,128)}, f32[288,128]{1,0:T(8,128)S(1)}, u32[]{:S(2)}, u32[]{:S(2)}) collective-permute-start(f32[288,128]{1,0:T(8,128)} %shard_map.140), channel_id=1, source_target_pairs={{0,8},{8,0},{16,24},{24,16},{1,9},{9,1},{17,25},{25,17},{2,10},{10... | collective-permute-start | bytes 442376 | tf_op jit(solution)/shard_map/ppermute | solution.py:489
  6.8 7.8 %collective-permute-start.4 = (f32[1,128,128]{2,1,0:T(8,128)S(1)}, f32[1,128,128]{2,1,0:T(8,128)S(1)}, u32[]{:S(2)}, u32[]{:S(2)}) collective-permute-start(f32[1,128,128]{2,1,0:T(8,128)S(1)} %bitcast.61), channel_id=1, source_target_pairs={{0,6},{1,7},{2,4},{3,5},{4,2},{5,3},{6,0},{7,1},{8,14},{9,15},{10,... | collective-permute-start | bytes 196616 | tf_op jit(solution)/shard_map/ppermute | solution.py:495
  10.4 5.2 %collective-permute-start.3 = (f32[1,128,128]{2,1,0:T(8,128)S(1)}, f32[1,128,128]{2,1,0:T(8,128)S(1)}, u32[]{:S(2)}, u32[]{:S(2)}) collective-permute-start(f32[1,128,128]{2,1,0:T(8,128)S(1)} %bitcast.62), channel_id=1, source_target_pairs={{0,4},{1,5},{2,6},{3,7},{4,0},{5,1},{6,2},{7,3},{8,12},{9,13},{10,... | collective-permute-start | bytes 196616 | tf_op jit(solution)/shard_map/ppermute | solution.py:495
  10.4 5.2 %collective-permute-start.2 = (f32[1,128,128]{2,1,0:T(8,128)S(1)}, f32[1,128,128]{2,1,0:T(8,128)S(1)}, u32[]{:S(2)}, u32[]{:S(2)}) collective-permute-start(f32[1,128,128]{2,1,0:T(8,128)S(1)} %bitcast.63), channel_id=1, source_target_pairs={{0,2},{1,3},{2,0},{3,1},{4,6},{5,7},{6,4},{7,5},{8,10},{9,11},{10,... | collective-permute-start | bytes 196616 | tf_op jit(solution)/shard_map/ppermute | solution.py:495
  11.4 2.4 %copy-start.4 = (f32[4,512]{1,0:T(4,128)S(1)}, f32[4,512]{1,0:T(4,128)}, u32[]{:S(2)}) copy-start(f32[4,512]{1,0:T(4,128)} %param.15) | copy-start | bytes 24580
  11.4 2.4 %copy-start.5 = (f32[4,512]{1,0:T(4,128)S(1)}, f32[4,512]{1,0:T(4,128)}, u32[]{:S(2)}) copy-start(f32[4,512]{1,0:T(4,128)} %param.16) | copy-start | bytes 24580
  11.4 2.4 %copy-start.6 = (s32[4,512]{1,0:T(4,128)S(1)}, s32[4,512]{1,0:T(4,128)}, u32[]{:S(2)}) copy-start(s32[4,512]{1,0:T(4,128)} %param.17) | copy-start | bytes 24580
  15.8 14.0 %collective-permute-start.7 = (f32[4,120,128]{2,1,0:T(8,128)S(1)}, f32[4,120,128]{2,1,0:T(8,128)S(1)}, u32[]{:S(2)}, u32[]{:S(2)}) collective-permute-start(f32[4,120,128]{2,1,0:T(8,128)S(1)} %shard_map.143.refs_0_), channel_id=1, source_target_pairs={{0,24},{8,16},{16,8},{24,0},{1,25},{9,17},{17,9},{25,1},{2,26},{10... | collective-permute-start | bytes 737288 | tf_op jit(solution)/shard_map/ppermute | solution.py:495
  17.3 12.5 %collective-permute-start.6 = (f32[4,120,128]{2,1,0:T(8,128)S(1)}, f32[4,120,128]{2,1,0:T(8,128)S(1)}, u32[]{:S(2)}, u32[]{:S(2)}) collective-permute-start(f32[4,120,128]{2,1,0:T(8,128)S(1)} %shard_map.143.refs_0_), channel_id=1, source_target_pairs={{0,16},{8,24},{16,0},{24,8},{1,17},{9,25},{17,1},{25,9},{2,18},{10... | collective-permute-start | bytes 737288 | tf_op jit(solution)/shard_map/ppermute | solution.py:495
  18.8 11.0 %collective-permute-start.5 = (f32[4,120,128]{2,1,0:T(8,128)S(1)}, f32[4,120,128]{2,1,0:T(8,128)S(1)}, u32[]{:S(2)}, u32[]{:S(2)}) collective-permute-start(f32[4,120,128]{2,1,0:T(8,128)S(1)} %shard_map.143.refs_0_), channel_id=1, source_target_pairs={{0,8},{8,0},{16,24},{24,16},{1,9},{9,1},{17,25},{25,17},{2,10},{10... | collective-permute-start | bytes 737288 | tf_op jit(solution)/shard_map/ppermute | solution.py:495
  29.8 2.1 %collective-permute-start.8 = (f32[16,72,128]{2,1,0:T(8,128)S(1)}, f32[16,72,128]{2,1,0:T(8,128)S(1)}, u32[]{:S(2)}, u32[]{:S(2)}) collective-permute-start(f32[16,72,128]{2,1,0:T(8,128)S(1)} %shard_map.145), channel_id=1, source_target_pairs={{0,1},{1,0},{2,3},{3,2},{4,5},{5,4},{6,7},{7,6},{8,9},{9,8},{10,11... | collective-permute-start | bytes 1769480 | tf_op jit(solution)/shard_map/ppermute | solution.py:495
  33.4 17.4 %copy-start.1 = (f32[4,4,4,512]{3,2,1,0:T(4,128)S(1)}, f32[4,4,4,512]{3,2,1,0:T(4,128)}, u32[]{:S(2)}) copy-start(f32[4,4,4,512]{3,2,1,0:T(4,128)} %param.14) | copy-start | bytes 393220
  43.0 7.2 %collective-permute-start.10 = (f32[8,32,128]{2,1,0:T(8,128)S(1)}, f32[8,32,128]{2,1,0:T(8,128)S(1)}, u32[]{:S(2)}, u32[]{:S(2)}) collective-permute-start(f32[8,32,128]{2,1,0:T(8,128)S(1)} %all_to_all.16.own_ref), channel_id=1, source_target_pairs={{0,24},{8,16},{16,8},{24,0},{1,25},{9,17},{17,9},{25,1},{2,26},{10... | collective-permute-start | bytes 393224 | tf_op jit(solution)/shard_map/ppermute | solution.py:490
  44.5 6.3 %collective-permute-start.9 = (f32[8,32,128]{2,1,0:T(8,128)S(1)}, f32[8,32,128]{2,1,0:T(8,128)S(1)}, u32[]{:S(2)}, u32[]{:S(2)}) collective-permute-start(f32[8,32,128]{2,1,0:T(8,128)S(1)} %all_to_all.16.own_ref), channel_id=1, source_target_pairs={{0,8},{8,0},{16,24},{24,16},{1,9},{9,1},{17,25},{25,17},{2,10},{10... | collective-permute-start | bytes 393224 | tf_op jit(solution)/shard_map/ppermute | solution.py:489
  50.8 11.4 %copy-start.2 = (f32[4,4,4,512]{3,2,1,0:T(4,128)S(1)}, f32[4,4,4,512]{3,2,1,0:T(4,128)}, u32[]{:S(2)}) copy-start(f32[4,4,4,512]{3,2,1,0:T(4,128)} %param.13) | copy-start | bytes 393220

commit v11 on v10

--- a/solution.py
+++ b/solution.py
@@ -52,18 +52,10 @@
     return rows
 
 
-def sort_halo(pair_ref, cross_ref, low_ref, high_ref):
+def by_parity(pair_ref, cross_ref, body):
     odd = lax.rem(lax.axis_index("gy"), 2) == 1
-
-    @pl.when(odd)
-    def _():
-        low_ref[...] = pair_ref[...]
-        high_ref[...] = cross_ref[...]
-
-    @pl.when(jnp.logical_not(odd))
-    def _():
-        low_ref[...] = cross_ref[...]
-        high_ref[...] = pair_ref[...]
+    pl.when(odd)(lambda: body(pair_ref, cross_ref))
+    pl.when(jnp.logical_not(odd))(lambda: body(cross_ref, pair_ref))
 
 
 def triangle_masks():
@@ -165,61 +157,62 @@
     packed_ref,
     coef_ref,
     ext_ref,
-    low_ref,
-    high_ref,
 ):
     lons = tiles * LANES
     cells = kv * tiles * rows
-    sort_halo(pair_ref, cross_ref, low_ref, high_ref)
-    at_y, rows_y = lax.axis_index("gy"), lax.axis_size("gy")
-    inside = (
-        jnp.where(at_y > 0, 1.0, 0.0).astype(jnp.float32),
-        jnp.where(at_y < rows_y - 1, 1.0, 0.0).astype(jnp.float32),
-    )
-    ext_ref[...] = jnp.zeros_like(ext_ref)
-    for tile in range(tiles):
-        lanes = slice(tile * LANES, (tile + 1) * LANES)
-        here = slice(tile * rows, (tile + 1) * rows)
-        mask = ocean_ref[here, :].astype(jnp.float32)
-        ext_ref[0, rows : 2 * rows, lanes] = north_ref[here, :] * mask
-        ext_ref[1, rows : 2 * rows, lanes] = east_ref[here, :] * mask
-        ext_ref[2, rows : 2 * rows, lanes] = mask
-        for block, ref in ((0, low_ref), (2, high_ref)):
-            across = slice(block * rows, (block + 1) * rows)
-            for kind in range(2):
-                start = cells + (kind * tiles + tile) * rows
-                ext_ref[kind, across, lanes] = ref[start : start + rows, :] * inside[block // 2]
-            ext_ref[2, across, lanes] = jnp.where(ext_ref[0, across, lanes] > 0.0, 1.0, 0.0)
-    total = ext_ref.shape[1]
-    ocean = ext_ref[2]
-    north_face = ext_ref[0] * pltpu.roll(ocean, total - 1, 0)
-    east_face = ext_ref[1] * pltpu.roll(ocean, lons - 1, 1)
-    south_face = pltpu.roll(north_face, 1, 0)
-    west_face = pltpu.roll(east_face, 1, 1)
-    coef_ref[0] = ocean - north_face - south_face - east_face - west_face
-    coef_ref[1] = north_face
-    coef_ref[2] = south_face
-    coef_ref[3] = east_face
-    coef_ref[4] = west_face
-    low = lane_low((8, LANES))
-    for half in range(kv // 8):
-        grown = [
-            native_rows(ref, row, rows, tiles, half)
-            for ref in (low_ref, own_ref, high_ref)
-            for row in range(rows)
-        ]
-        done = lateral_rows(grown, coef_ref, rows)
-        for pair in range(rows // 2):
-            at = pair * kv + half * 8
-            for tile in range(tiles):
-                first = done[2 * pair][:, tile * LANES : (tile + 1) * LANES]
-                second = done[2 * pair + 1][:, tile * LANES : (tile + 1) * LANES]
-                packed_ref[2 * tile, at : at + 8, :] = jnp.where(
-                    low, first, pltpu.roll(second, LANES // 2, 1)
-                )
-                packed_ref[2 * tile + 1, at : at + 8, :] = jnp.where(
-                    low, pltpu.roll(first, LANES // 2, 1), second
-                )
+
+    def body(low_ref, high_ref):
+        at_y, rows_y = lax.axis_index("gy"), lax.axis_size("gy")
+        inside = (
+            jnp.where(at_y > 0, 1.0, 0.0).astype(jnp.float32),
+            jnp.where(at_y < rows_y - 1, 1.0, 0.0).astype(jnp.float32),
+        )
+        ext_ref[...] = jnp.zeros_like(ext_ref)
+        for tile in range(tiles):
+            lanes = slice(tile * LANES, (tile + 1) * LANES)
+            here = slice(tile * rows, (tile + 1) * rows)
+            mask = ocean_ref[here, :].astype(jnp.float32)
+            ext_ref[0, rows : 2 * rows, lanes] = north_ref[here, :] * mask
+            ext_ref[1, rows : 2 * rows, lanes] = east_ref[here, :] * mask
+            ext_ref[2, rows : 2 * rows, lanes] = mask
+            for block, ref in ((0, low_ref), (2, high_ref)):
+                across = slice(block * rows, (block + 1) * rows)
+                for kind in range(2):
+                    start = cells + (kind * tiles + tile) * rows
+                    ext_ref[kind, across, lanes] = ref[start : start + rows, :] * inside[block // 2]
+                ext_ref[2, across, lanes] = jnp.where(ext_ref[0, across, lanes] > 0.0, 1.0, 0.0)
+        total = ext_ref.shape[1]
+        ocean = ext_ref[2]
+        north_face = ext_ref[0] * pltpu.roll(ocean, total - 1, 0)
+        east_face = ext_ref[1] * pltpu.roll(ocean, lons - 1, 1)
+        south_face = pltpu.roll(north_face, 1, 0)
+        west_face = pltpu.roll(east_face, 1, 1)
+        coef_ref[0] = ocean - north_face - south_face - east_face - west_face
+        coef_ref[1] = north_face
+        coef_ref[2] = south_face
+        coef_ref[3] = east_face
+        coef_ref[4] = west_face
+        low = lane_low((8, LANES))
+        for half in range(kv // 8):
+            grown = [
+                native_rows(ref, row, rows, tiles, half)
+                for ref in (low_ref, own_ref, high_ref)
+                for row in range(rows)
+            ]
+            done = lateral_rows(grown, coef_ref, rows)
+            for pair in range(rows // 2):
+                at = pair * kv + half * 8
+                for tile in range(tiles):
+                    first = done[2 * pair][:, tile * LANES : (tile + 1) * LANES]
+                    second = done[2 * pair + 1][:, tile * LANES : (tile + 1) * LANES]
+                    packed_ref[2 * tile, at : at + 8, :] = jnp.where(
+                        low, first, pltpu.roll(second, LANES // 2, 1)
+                    )
+                    packed_ref[2 * tile + 1, at : at + 8, :] = jnp.where(
+                        low, pltpu.roll(first, LANES // 2, 1), second
+                    )
+
+    by_parity(pair_ref, cross_ref, body)
 
 
 def second_lateral_kernel(
@@ -234,44 +227,45 @@
     residual_ref,
     image_ref,
     sums_ref,
-    low_ref,
-    high_ref,
 ):
-    sort_halo(pair_ref, cross_ref, low_ref, high_ref)
-    low = lane_low((8, LANES))
-    totals = [jnp.zeros((8, tiles * LANES), jnp.float32) for _ in range(4)]
-    for half in range(kv // 8):
-        grown = []
-        for ref in (low_ref, own_ref, high_ref):
-            for pair in range(rows // 2):
-                firsts, seconds = [], []
-                at = pair * kv + half * 8
+
+    def body(low_ref, high_ref):
+        low = lane_low((8, LANES))
+        totals = [jnp.zeros((8, tiles * LANES), jnp.float32) for _ in range(4)]
+        for half in range(kv // 8):
+            grown = []
+            for ref in (low_ref, own_ref, high_ref):
+                for pair in range(rows // 2):
+                    firsts, seconds = [], []
+                    at = pair * kv + half * 8
+                    for tile in range(tiles):
+                        even = ref[2 * tile, at : at + 8, :]
+                        odd = ref[2 * tile + 1, at : at + 8, :]
+                        firsts.append(jnp.where(low, even, pltpu.roll(odd, LANES // 2, 1)))
+                        seconds.append(jnp.where(low, pltpu.roll(even, LANES // 2, 1), odd))
+                    grown.append(jnp.concatenate(firsts, axis=1))
+                    grown.append(jnp.concatenate(seconds, axis=1))
+            done = lateral_rows(grown, coef_ref, rows)
+            for row in range(rows):
+                direction = native_rows(direction_ref, row, rows, tiles, half)
+                residual = native_rows(residual_ref, row, rows, tiles, half)
+                image = direction + done[row]
                 for tile in range(tiles):
-                    even = ref[2 * tile, at : at + 8, :]
-                    odd = ref[2 * tile + 1, at : at + 8, :]
-                    firsts.append(jnp.where(low, even, pltpu.roll(odd, LANES // 2, 1)))
-                    seconds.append(jnp.where(low, pltpu.roll(even, LANES // 2, 1), odd))
-                grown.append(jnp.concatenate(firsts, axis=1))
-                grown.append(jnp.concatenate(seconds, axis=1))
-        done = lateral_rows(grown, coef_ref, rows)
-        for row in range(rows):
-            direction = native_rows(direction_ref, row, rows, tiles, half)
-            residual = native_rows(residual_ref, row, rows, tiles, half)
-            image = direction + done[row]
-            for tile in range(tiles):
-                image_ref[pl.ds((half * 8 * tiles + tile) * rows + row, 8, stride=tiles * rows), :] = image[
-                    :, tile * LANES : (tile + 1) * LANES
-                ]
-            totals[0] = totals[0] + residual * residual
-            totals[1] = totals[1] + direction * image
-            totals[2] = totals[2] + residual * image
-            totals[3] = totals[3] + image * image
-    lane = lax.broadcasted_iota(jnp.int32, (1, LANES), 1)
-    line = jnp.zeros((1, LANES), jnp.float32)
-    for at, total in enumerate(totals):
-        line = jnp.where(lane == at, jnp.sum(total), line)
-    for device in range(sums_ref.shape[0]):
-        sums_ref[device] = line
+                    image_ref[pl.ds((half * 8 * tiles + tile) * rows + row, 8, stride=tiles * rows), :] = image[
+                        :, tile * LANES : (tile + 1) * LANES
+                    ]
+                totals[0] = totals[0] + residual * residual
+                totals[1] = totals[1] + direction * image
+                totals[2] = totals[2] + residual * image
+                totals[3] = totals[3] + image * image
+        lane = lax.broadcasted_iota(jnp.int32, (1, LANES), 1)
+        line = jnp.zeros((1, LANES), jnp.float32)
+        for at, total in enumerate(totals):
+            line = jnp.where(lane == at, jnp.sum(total), line)
+        for device in range(sums_ref.shape[0]):
+            sums_ref[device] = line
+
+    by_parity(pair_ref, cross_ref, body)
 
 
 def update_kernel(sums_ref, direction_ref, solution_ref, residual_ref, image_ref, sol_ref, res_ref, dir_ref):
@@ -562,8 +556,6 @@
         after=1,
         scratch=(
             pltpu.VMEM((3, extended, lons), jnp.float32),
-            pltpu.VMEM(own.shape, jnp.float32),
-            pltpu.VMEM(own.shape, jnp.float32),
         ),
         flops=4_000_000,
     )
@@ -609,7 +601,6 @@
         functools.partial(second_lateral_kernel, kv, rows, tiles),
         (f32(*direction_n.shape), f32(device_count, 1, LANES)),
         (tile, pair, cross, coef, direction_n, residual_n),
-        scratch=(pltpu.VMEM(tile.shape, jnp.float32), pltpu.VMEM(tile.shape, jnp.float32)),
         flops=4_000_000,
     )
     sums = lax.all_to_all(sums, ("gy", "gx"), split_axis=0, concat_axis=0, tiled=True)

time: 63.3 us -> 63.3 us (level)
  no operation moved by 1% of the time
where the time goes in v11:
time: 63.3 us; the launch traced here: 63 us
  blocking collectives  30.5 us (48%)
  starting transfers between devices  14.6 us (23%)
  waiting for transfers between devices  8.86 us (14%)
  Pallas kernels  8.09 us (13%)
  between operations  0.87 us (1%)
    all_to_all x1, blocking collectives, per_device_gathered(): lax.all_to_all(packed, 'gx', split_axis=0, concat_axis=0, tiled=True)  10.4 us
    all_to_all x1, blocking collectives, per_device_gathered(): lax.all_to_all(sums, ('gy', 'gx'), split_axis=0, concat_axis=0, tiled=True)  10.4 us
    all_to_all x1, blocking collectives, per_device_gathered(): lax.all_to_all(spread.reshape(cols_x, 2 * kv, LANES), 'gx', split_axis=0,...  9.63 us
    pallas_call x10, Pallas kernels, call(): pl.pallas_call(kernel, out_shape=out_shape, in_specs=specs, out_specs=tup...  8.09 us
    ppermute x7, starting transfers between devices, apart_by(): lax.ppermute(block, axis, [(i, i ^ stride) for i in range(lax.axis_size(a...  8.01 us
    ppermute x2, starting transfers between devices, from_neighbours(): lax.ppermute(block, 'gy', [(i, (i + (1 if i % 2 else -1)) % count) for i...  5.49 us
    ppermute x2, waiting for transfers between devices, from_neighbours(): lax.ppermute(block, 'gy', [(i, (i + (1 if i % 2 else -1)) % count) for i...  5.17 us
    ppermute x7, waiting for transfers between devices, apart_by(): lax.ppermute(block, axis, [(i, i ^ stride) for i in range(lax.axis_size(a...  1.94 us
  transfers between devices with their start and end apart: 11, of which 5 were waited for; matrix products, arithmetic and copies ran while one was open for 0% of the time, Pallas kernels for 5%

profile of v11, /device:TPU:0, one launch (start us, length us, event | category | flops | bytes accessed | tf_op | source)
XLA Modules:
  0.0 63.0 jit_solution(5671830946093624494)
XLA Ops:
  0.6 0.0 copy-start.3
  0.6 0.0 copy-start.11
  0.7 0.0 copy-start.7
  0.7 0.0 copy-start.8
  0.7 0.0 copy-start.9
  0.7 0.0 copy-start.10
  0.7 1.6 %shard_map.140 = f32[288,128]{1,0:T(8,128)} custom-call(f32[256,128]{1,0:T(8,128)} %bitcast.52, f32[16,128]{1,0:T(8,128)} %bitcast.65, f32[16,128]{1,0:T(8,128)} %bitcast.67, s32[16,128]{1,0:T(8,128)} %bitcast.69), custom_call_target="tpu_custom_call" | custom-call | flops 1000000 | bytes 155648 | tf_op jit(solution)/shard_map/pallas_call | solution.py:466
  2.3 0.0 copy-start
  2.3 4.0 %collective-permute-start.1 = (f32[288,128]{1,0:T(8,128)}, f32[288,128]{1,0:T(8,128)S(1)}, u32[]{:S(2)}, u32[]{:S(2)}) collective-permute-start(f32[288,128]{1,0:T(8,128)} %shard_map.140), channel_id=1, source_target_pairs={{0,24},{8,16},{16,8},{24,0},{1,25},{9,17},{17,9},{25,1},{2,26},{10... | collective-permute-start | bytes 442376 | tf_op jit(solution)/shard_map/ppermute | solution.py:484
  6.3 0.5 collective-permute-start
  6.8 0.0 copy-done.3
  6.8 3.6 %collective-permute-start.4 = (f32[1,128,128]{2,1,0:T(8,128)S(1)}, f32[1,128,128]{2,1,0:T(8,128)S(1)}, u32[]{:S(2)}, u32[]{:S(2)}) collective-permute-start(f32[1,128,128]{2,1,0:T(8,128)S(1)} %bitcast.61), channel_id=1, source_target_pairs={{0,6},{1,7},{2,4},{3,5},{4,2},{5,3},{6,0},{7,1},{8,14},{9,15},{10,... | collective-permute-start | bytes 196616 | tf_op jit(solution)/shard_map/ppermute | solution.py:489
  10.4 0.0 collective-permute-start.3
  10.4 0.8 %collective-permute-start.2 = (f32[1,128,128]{2,1,0:T(8,128)S(1)}, f32[1,128,128]{2,1,0:T(8,128)S(1)}, u32[]{:S(2)}, u32[]{:S(2)}) collective-permute-start(f32[1,128,128]{2,1,0:T(8,128)S(1)} %bitcast.63), channel_id=1, source_target_pairs={{0,2},{1,3},{2,0},{3,1},{4,6},{5,7},{6,4},{7,5},{8,10},{9,11},{10,... | collective-permute-start | bytes 196616 | tf_op jit(solution)/shard_map/ppermute | solution.py:489
  11.2 0.0 copy-done.11
  11.2 0.1 reshape.75.vert_ref
  11.3 0.0 copy-done.7
  11.3 0.0 copy-done.8
  11.3 0.0 copy-done.9
  11.4 0.0 copy-done.10
  11.4 0.0 copy-start.4
  11.4 0.0 copy-start.5
  11.4 0.0 copy-start.6
  11.4 1.1 %shard_map.139 = (f32[3,32,8,128]{3,2,1,0:T(8,128)S(1)}, bf16[256,1024]{1,0:T(8,128)(2,1)S(1)}, bf16[256,1024]{1,0:T(8,128)(2,1)S(1)}) custom-call(f32[32,2,128]{2,1,0:T(2,128)S(1)} %reshape.75.vert_ref, s32[1,512]{1,0:T(1,128)S(1)} %bitcast.72, s32[1,512]{1,0:T(1,128)S(1)} %bitcast.73, s32[1,512]{1,0:T(1,128)S(1)} %bitcast.74, f32[2,512]{1,0:T(2,128)S(1)} %bitcast.71), custom_call_target="tpu_custom_call" | custom-call | flops 20000000 | bytes 43008 | tf_op jit(solution)/shard_map/pallas_call | solution.py:466
  12.5 0.0 collective-permute-done.1.cross_ref
  12.6 1.2 %collective-permute-done.pair_ref = f32[288,128]{1,0:T(8,128)S(1)} collective-permute-done((f32[288,128]{1,0:T(8,128)}, f32[288,128]{1,0:T(8,128)S(1)}, u32[]{:S(2)}, u32[]{:S(2)}) %collective-permute-start) | collective-permute-done | bytes 147488 | tf_op jit(solution)/shard_map/ppermute | solution.py:483
  13.8 0.0 copy-done
  13.8 0.0 copy-done.4
  13.8 0.0 copy-done.5
  13.8 0.0 copy-done.6
  13.8 0.8 %shard_map.141 = (f32[8,32,128]{2,1,0:T(8,128)S(1)}, f32[5,16,512]{2,1,0:T(8,128)S(1)}) custom-call(bf16[256,1024]{1,0:T(8,128)(2,1)S(1)} %get-tuple-element.15._.high_ref, f32[256,128]{1,0:T(8,128)S(1)} %bitcast.53, f32[16,128]{1,0:T(8,128)S(1)} %bitcast.66, f32[16,128]{1,0:T(8,128)S(1)} %bitcast.68, s32[16,128]{1,0:T(8,128)S(1)} %bitcast.70, ...), custom_call_target="tpu_custom_call" | custom-call | flops 4000000 | bytes 1499136 | tf_op jit(solution)/shard_map/pallas_call | solution.py:466
  14.6 0.0 collective-permute-done.4.refs_3_
  14.6 1.0 %collective-permute-done.3.refs_2_ = f32[1,128,128]{2,1,0:T(8,128)S(1)} collective-permute-done((f32[1,128,128]{2,1,0:T(8,128)S(1)}, f32[1,128,128]{2,1,0:T(8,128)S(1)}, u32[]{:S(2)}, u32[]{:S(2)}) %collective-permute-start.3) | collective-permute-done | bytes 65568 | tf_op jit(solution)/shard_map/ppermute | solution.py:489
  15.7 0.0 collective-permute-done.2.refs_1_
  15.7 0.1 shard_map.143.refs_0_
  15.8 1.5 %collective-permute-start.7 = (f32[4,120,128]{2,1,0:T(8,128)S(1)}, f32[4,120,128]{2,1,0:T(8,128)S(1)}, u32[]{:S(2)}, u32[]{:S(2)}) collective-permute-start(f32[4,120,128]{2,1,0:T(8,128)S(1)} %shard_map.143.refs_0_), channel_id=1, source_target_pairs={{0,24},{8,16},{16,8},{24,0},{1,25},{9,17},{17,9},{25,1},{2,26},{10... | collective-permute-start | bytes 737288 | tf_op jit(solution)/shard_map/ppermute | solution.py:489
  17.3 1.5 %collective-permute-start.6 = (f32[4,120,128]{2,1,0:T(8,128)S(1)}, f32[4,120,128]{2,1,0:T(8,128)S(1)}, u32[]{:S(2)}, u32[]{:S(2)}) collective-permute-start(f32[4,120,128]{2,1,0:T(8,128)S(1)} %shard_map.143.refs_0_), channel_id=1, source_target_pairs={{0,16},{8,24},{16,0},{24,8},{1,17},{9,25},{17,1},{25,9},{2,18},{10... | collective-permute-start | bytes 737288 | tf_op jit(solution)/shard_map/ppermute | solution.py:489
  18.8 0.5 collective-permute-start.5
  19.3 10.4 %all_to_all.15._ = f32[8,32,128]{2,1,0:T(8,128)S(1)} all-to-all(f32[8,32,128]{2,1,0:T(8,128)S(1)} %get-tuple-element.16._), channel_id=1, replica_groups=mesh['gy'=4,'gx'=8] {'gx'}, dimensions={0} | all-to-all | bytes 262144 | tf_op jit(solution)/shard_map/all_to_all | solution.py:566
  29.8 0.0 collective-permute-done.7.refs_3_
  29.8 0.0 collective-permute-done.6.refs_2_
  29.8 0.0 collective-permute-done.5.refs_1_
  29.8 0.1 collective-permute-start.8
  29.9 0.1 shard_map.142.column_ref
  30.1 1.0 %shard_map.144 = (f32[128,512]{1,0:T(8,128)S(1)}, f32[128,512]{1,0:T(8,128)S(1)}) custom-call(f32[256,128]{1,0:T(8,128)S(1)} %shard_map.142.column_ref, bf16[256,1024]{1,0:T(8,128)(2,1)S(1)} %get-tuple-element.15._.high_ref, bf16[256,1024]{1,0:T(8,128)(2,1)S(1)} %get-tuple-element.18.low_ref, f32[4,120,128]{2,1,0:T(8,128)S(1)} %shard_map.143.refs_0_, ...), custom_call_target="tpu_custom_call" | custom-call | flops 400000000 | bytes 3211264 | tf_op jit(solution)/shard_map/pallas_call | solution.py:466
  31.0 0.9 %collective-permute-done.8.far_ref = f32[16,72,128]{2,1,0:T(8,128)S(1)} collective-permute-done((f32[16,72,128]{2,1,0:T(8,128)S(1)}, f32[16,72,128]{2,1,0:T(8,128)S(1)}, u32[]{:S(2)}, u32[]{:S(2)}) %collective-permute-start.8) | collective-permute-done | bytes 589856 | tf_op jit(solution)/shard_map/ppermute | solution.py:489
  31.9 1.4 %shard_map.146 = f32[256,128]{1,0:T(8,128)S(1)} custom-call(f32[128,512]{1,0:T(8,128)S(1)} %get-tuple-element.19.near_ref, f32[128,512]{1,0:T(8,128)S(1)} %get-tuple-element.20.profile_ref, f32[3,32,8,128]{3,2,1,0:T(8,128)S(1)} %get-tuple-element.17.factor_ref, bf16[256,1024]{1,0:T(8,128)(2,1)S(1)} %get-tuple-element.15._.high_ref, ...), custom_call_target="tpu_custom_call" | custom-call | flops 400000000 | bytes 3604480 | tf_op jit(solution)/shard_map/pallas_call | solution.py:466
  33.3 0.0 copy-start.1
  33.4 9.6 %all_to_all.16.own_ref = f32[8,32,128]{2,1,0:T(8,128)S(1)} all-to-all(f32[8,32,128]{2,1,0:T(8,128)S(1)} %bitcast.59), channel_id=1, replica_groups=mesh['gy'=4,'gx'=8] {'gx'}, dimensions={0} | all-to-all | bytes 262144 | tf_op jit(solution)/shard_map/all_to_all | solution.py:596
  43.0 1.5 %collective-permute-start.10 = (f32[8,32,128]{2,1,0:T(8,128)S(1)}, f32[8,32,128]{2,1,0:T(8,128)S(1)}, u32[]{:S(2)}, u32[]{:S(2)}) collective-permute-start(f32[8,32,128]{2,1,0:T(8,128)S(1)} %all_to_all.16.own_ref), channel_id=1, source_target_pairs={{0,24},{8,16},{16,8},{24,0},{1,25},{9,17},{17,9},{25,1},{2,26},{10... | collective-permute-start | bytes 393224 | tf_op jit(solution)/shard_map/ppermute | solution.py:484
  44.5 0.5 collective-permute-start.9
  45.1 5.2 %collective-permute-done.10.cross_ref = f32[8,32,128]{2,1,0:T(8,128)S(1)} collective-permute-done((f32[8,32,128]{2,1,0:T(8,128)S(1)}, f32[8,32,128]{2,1,0:T(8,128)S(1)}, u32[]{:S(2)}, u32[]{:S(2)}) %collective-permute-start.10) | collective-permute-done | bytes 131104 | tf_op jit(solution)/shard_map/ppermute | solution.py:484
  50.2 0.5 collective-permute-done.9.pair_ref
  50.8 0.0 copy-done.1
  50.8 0.0 copy-start.2
  50.8 0.9 %shard_map.147 = (f32[256,128]{1,0:T(8,128)S(1)}, f32[32,1,128]{2,1,0:T(1,128)S(1)}) custom-call(f32[8,32,128]{2,1,0:T(8,128)S(1)} %all_to_all.16.own_ref, f32[8,32,128]{2,1,0:T(8,128)S(1)} %collective-permute-done.9.pair_ref, f32[8,32,128]{2,1,0:T(8,128)S(1)} %collective-permute-done.10.cross_ref, f32[5,16,512]{2,1,0:T(8,128)S(1)} %get-tuple-element.21.coef_ref, ...), custom_call_target="tpu_custom_call" | custom-call | flops 4000000 | bytes 819200 | tf_op jit(solution)/shard_map/pallas_call | solution.py:466
  51.7 10.4 %all_to_all.17.sums_ref = f32[32,1,128]{2,1,0:T(1,128)S(1)} all-to-all(f32[32,1,128]{2,1,0:T(1,128)S(1)} %get-tuple-element.22), channel_id=1, replica_groups=mesh['gy'=4,'gx'=8] {'gy','gx'}, dimensions={0} | all-to-all | bytes 32768 | tf_op jit(solution)/shard_map/all_to_all | solution.py:606
  62.1 0.0 copy-done.2
  62.1 0.9 %shard_map.148 = (f32[256,128]{1,0:T(8,128)}, f32[256,128]{1,0:T(8,128)}, f32[256,128]{1,0:T(8,128)}) custom-call(f32[32,1,128]{2,1,0:T(1,128)S(1)} %all_to_all.17.sums_ref, f32[256,128]{1,0:T(8,128)S(1)} %bitcast.55, f32[256,128]{1,0:T(8,128)S(1)} %bitcast.60, f32[256,128]{1,0:T(8,128)S(1)} %bitcast.58, f32[256,128]{1,0:T(8,128)S(1)} %get-tuple-element.23.image_ref), custom_call_target="tpu_custom_call" | custom-call | flops 1000000 | bytes 540672 | tf_op jit(solution)/shard_map/pallas_call | solution.py:466
  (1 shorter events, 0.0 us)
Async XLA Ops:
  0.6 6.2 %copy-start.3 = (f32[1,1,128,128]{3,2,1,0:T(8,128)S(1)}, f32[1,1,128,128]{3,2,1,0:T(8,128)}, u32[]{:S(2)}) copy-start(f32[1,1,128,128]{3,2,1,0:T(8,128)} %param.23) | copy-start | bytes 196612
  0.6 10.6 %copy-start.11 = (f32[32,4,64]{2,1,0:T(4,128)S(1)}, f32[32,4,64]{2,1,0:T(4,128)}, u32[]{:S(2)}) copy-start(f32[32,4,64]{2,1,0:T(4,128)} %param.18) | copy-start | bytes 98308
  0.7 10.7 %copy-start.7 = (f32[1,1,2,512]{3,2,1,0:T(2,128)S(1)}, f32[1,1,2,512]{3,2,1,0:T(2,128)}, u32[]{:S(2)}) copy-start(f32[1,1,2,512]{3,2,1,0:T(2,128)} %param.22) | copy-start | bytes 12292
  0.7 10.7 %copy-start.8 = (s32[1,1,512,1]{2,3,1,0:T(1,128)S(1)}, s32[1,1,512,1]{2,3,1,0:T(1,128)}, u32[]{:S(2)}) copy-start(s32[1,1,512,1]{2,3,1,0:T(1,128)} %param.19) | copy-start | bytes 6148
  0.7 10.7 %copy-start.9 = (s32[1,1,512]{2,1,0:T(1,128)S(1)}, s32[1,1,512]{2,1,0:T(1,128)}, u32[]{:S(2)}) copy-start(s32[1,1,512]{2,1,0:T(1,128)} %param.20) | copy-start | bytes 6148
  0.7 10.7 %copy-start.10 = (s32[1,1,512]{2,1,0:T(1,128)S(1)}, s32[1,1,512]{2,1,0:T(1,128)}, u32[]{:S(2)}) copy-start(s32[1,1,512]{2,1,0:T(1,128)} %param.21) | copy-start | bytes 6148
  2.3 11.4 %copy-start = (f32[4,4,4,512]{3,2,1,0:T(4,128)S(1)}, f32[4,4,4,512]{3,2,1,0:T(4,128)}, u32[]{:S(2)}) copy-start(f32[4,4,4,512]{3,2,1,0:T(4,128)} %param.12) | copy-start | bytes 393220
  2.3 10.2 %collective-permute-start.1 = (f32[288,128]{1,0:T(8,128)}, f32[288,128]{1,0:T(8,128)S(1)}, u32[]{:S(2)}, u32[]{:S(2)}) collective-permute-start(f32[288,128]{1,0:T(8,128)} %shard_map.140), channel_id=1, source_target_pairs={{0,24},{8,16},{16,8},{24,0},{1,25},{9,17},{17,9},{25,1},{2,26},{10... | collective-permute-start | bytes 442376 | tf_op jit(solution)/shard_map/ppermute | solution.py:484
  6.3 7.5 %collective-permute-start = (f32[288,128]{1,0:T(8,128)}, f32[288,128]{1,0:T(8,128)S(1)}, u32[]{:S(2)}, u32[]{:S(2)}) collective-permute-start(f32[288,128]{1,0:T(8,128)} %shard_map.140), channel_id=1, source_target_pairs={{0,8},{8,0},{16,24},{24,16},{1,9},{9,1},{17,25},{25,17},{2,10},{10... | collective-permute-start | bytes 442376 | tf_op jit(solution)/shard_map/ppermute | solution.py:483
  6.8 7.8 %collective-permute-start.4 = (f32[1,128,128]{2,1,0:T(8,128)S(1)}, f32[1,128,128]{2,1,0:T(8,128)S(1)}, u32[]{:S(2)}, u32[]{:S(2)}) collective-permute-start(f32[1,128,128]{2,1,0:T(8,128)S(1)} %bitcast.61), channel_id=1, source_target_pairs={{0,6},{1,7},{2,4},{3,5},{4,2},{5,3},{6,0},{7,1},{8,14},{9,15},{10,... | collective-permute-start | bytes 196616 | tf_op jit(solution)/shard_map/ppermute | solution.py:489
  10.4 5.2 %collective-permute-start.3 = (f32[1,128,128]{2,1,0:T(8,128)S(1)}, f32[1,128,128]{2,1,0:T(8,128)S(1)}, u32[]{:S(2)}, u32[]{:S(2)}) collective-permute-start(f32[1,128,128]{2,1,0:T(8,128)S(1)} %bitcast.62), channel_id=1, source_target_pairs={{0,4},{1,5},{2,6},{3,7},{4,0},{5,1},{6,2},{7,3},{8,12},{9,13},{10,... | collective-permute-start | bytes 196616 | tf_op jit(solution)/shard_map/ppermute | solution.py:489
  10.4 5.2 %collective-permute-start.2 = (f32[1,128,128]{2,1,0:T(8,128)S(1)}, f32[1,128,128]{2,1,0:T(8,128)S(1)}, u32[]{:S(2)}, u32[]{:S(2)}) collective-permute-start(f32[1,128,128]{2,1,0:T(8,128)S(1)} %bitcast.63), channel_id=1, source_target_pairs={{0,2},{1,3},{2,0},{3,1},{4,6},{5,7},{6,4},{7,5},{8,10},{9,11},{10,... | collective-permute-start | bytes 196616 | tf_op jit(solution)/shard_map/ppermute | solution.py:489
  11.4 2.4 %copy-start.4 = (f32[4,512]{1,0:T(4,128)S(1)}, f32[4,512]{1,0:T(4,128)}, u32[]{:S(2)}) copy-start(f32[4,512]{1,0:T(4,128)} %param.15) | copy-start | bytes 24580
  11.4 2.4 %copy-start.5 = (f32[4,512]{1,0:T(4,128)S(1)}, f32[4,512]{1,0:T(4,128)}, u32[]{:S(2)}) copy-start(f32[4,512]{1,0:T(4,128)} %param.16) | copy-start | bytes 24580
  11.4 2.4 %copy-start.6 = (s32[4,512]{1,0:T(4,128)S(1)}, s32[4,512]{1,0:T(4,128)}, u32[]{:S(2)}) copy-start(s32[4,512]{1,0:T(4,128)} %param.17) | copy-start | bytes 24580
  15.8 14.0 %collective-permute-start.7 = (f32[4,120,128]{2,1,0:T(8,128)S(1)}, f32[4,120,128]{2,1,0:T(8,128)S(1)}, u32[]{:S(2)}, u32[]{:S(2)}) collective-permute-start(f32[4,120,128]{2,1,0:T(8,128)S(1)} %shard_map.143.refs_0_), channel_id=1, source_target_pairs={{0,24},{8,16},{16,8},{24,0},{1,25},{9,17},{17,9},{25,1},{2,26},{10... | collective-permute-start | bytes 737288 | tf_op jit(solution)/shard_map/ppermute | solution.py:489
  17.3 12.5 %collective-permute-start.6 = (f32[4,120,128]{2,1,0:T(8,128)S(1)}, f32[4,120,128]{2,1,0:T(8,128)S(1)}, u32[]{:S(2)}, u32[]{:S(2)}) collective-permute-start(f32[4,120,128]{2,1,0:T(8,128)S(1)} %shard_map.143.refs_0_), channel_id=1, source_target_pairs={{0,16},{8,24},{16,0},{24,8},{1,17},{9,25},{17,1},{25,9},{2,18},{10... | collective-permute-start | bytes 737288 | tf_op jit(solution)/shard_map/ppermute | solution.py:489
  18.8 11.0 %collective-permute-start.5 = (f32[4,120,128]{2,1,0:T(8,128)S(1)}, f32[4,120,128]{2,1,0:T(8,128)S(1)}, u32[]{:S(2)}, u32[]{:S(2)}) collective-permute-start(f32[4,120,128]{2,1,0:T(8,128)S(1)} %shard_map.143.refs_0_), channel_id=1, source_target_pairs={{0,8},{8,0},{16,24},{24,16},{1,9},{9,1},{17,25},{25,17},{2,10},{10... | collective-permute-start | bytes 737288 | tf_op jit(solution)/shard_map/ppermute | solution.py:489
  29.8 2.1 %collective-permute-start.8 = (f32[16,72,128]{2,1,0:T(8,128)S(1)}, f32[16,72,128]{2,1,0:T(8,128)S(1)}, u32[]{:S(2)}, u32[]{:S(2)}) collective-permute-start(f32[16,72,128]{2,1,0:T(8,128)S(1)} %shard_map.145), channel_id=1, source_target_pairs={{0,1},{1,0},{2,3},{3,2},{4,5},{5,4},{6,7},{7,6},{8,9},{9,8},{10,11... | collective-permute-start | bytes 1769480 | tf_op jit(solution)/shard_map/ppermute | solution.py:489
  33.3 17.4 %copy-start.1 = (f32[4,4,4,512]{3,2,1,0:T(4,128)S(1)}, f32[4,4,4,512]{3,2,1,0:T(4,128)}, u32[]{:S(2)}) copy-start(f32[4,4,4,512]{3,2,1,0:T(4,128)} %param.14) | copy-start | bytes 393220
  43.0 7.2 %collective-permute-start.10 = (f32[8,32,128]{2,1,0:T(8,128)S(1)}, f32[8,32,128]{2,1,0:T(8,128)S(1)}, u32[]{:S(2)}, u32[]{:S(2)}) collective-permute-start(f32[8,32,128]{2,1,0:T(8,128)S(1)} %all_to_all.16.own_ref), channel_id=1, source_target_pairs={{0,24},{8,16},{16,8},{24,0},{1,25},{9,17},{17,9},{25,1},{2,26},{10... | collective-permute-start | bytes 393224 | tf_op jit(solution)/shard_map/ppermute | solution.py:484
  44.5 6.3 %collective-permute-start.9 = (f32[8,32,128]{2,1,0:T(8,128)S(1)}, f32[8,32,128]{2,1,0:T(8,128)S(1)}, u32[]{:S(2)}, u32[]{:S(2)}) collective-permute-start(f32[8,32,128]{2,1,0:T(8,128)S(1)} %all_to_all.16.own_ref), channel_id=1, source_target_pairs={{0,8},{8,0},{16,24},{24,16},{1,9},{9,1},{17,25},{25,17},{2,10},{10... | collective-permute-start | bytes 393224 | tf_op jit(solution)/shard_map/ppermute | solution.py:483
  50.8 11.3 %copy-start.2 = (f32[4,4,4,512]{3,2,1,0:T(4,128)S(1)}, f32[4,4,4,512]{3,2,1,0:T(4,128)}, u32[]{:S(2)}) copy-start(f32[4,4,4,512]{3,2,1,0:T(4,128)} %param.13) | copy-start | bytes 393220

commit v12 on v10

--- a/solution.py
+++ b/solution.py
@@ -430,23 +430,27 @@
 
 
 def profile_kernel(capacity, column_ref, high_ref, low_ref, *refs):
-    near_refs, (weighted_ref, profile_ref) = refs[:-2], refs[-2:]
+    near_refs, (spread_ref, profile_ref) = refs[:-2], refs[-2:]
     kv, half = profile_ref.shape
     size = near_refs[0].shape[0]
     columns = jnp.concatenate([column_ref[0:kv, :], column_ref[kv : 2 * kv, :]], axis=1)
     profile = dot_parts(split(columns), (high_ref[...], low_ref[...]), ((1,), (0,)))
     profile_ref[...] = profile[:, half:]
-    weighted_ref[...] = weigh(
+    weighted = weigh(
         profile[:, :half], lambda at: unpack_symmetric(near_refs[at // size][at % size]), capacity
     )
+    spread_ref[...] = dot_parts(split(weighted), (high_ref[:, :half], low_ref[:, :half]), ((1,), (1,)))
 
 
 def spread_kernel(
     layers, held, capacity, near_ref, profile_ref, factor_ref, high_ref, low_ref, far_ref, out_ref, column_ref
 ):
     kv = near_ref.shape[0]
-    weighted = jnp.concatenate([near_ref[...], weigh(profile_ref[...], lambda at: unpack_symmetric(far_ref[at]), capacity)], axis=1)
-    spread = dot_parts(split(weighted), (high_ref[...], low_ref[...]), ((1,), (1,)))
+    half = profile_ref.shape[1]
+    weighted = weigh(profile_ref[...], lambda at: unpack_symmetric(far_ref[at]), capacity)
+    spread = near_ref[...] + dot_parts(
+        split(weighted), (high_ref[:, half:], low_ref[:, half:]), ((1,), (1,))
+    )
     column_ref[0:kv, :] = spread[:, :LANES]
     column_ref[kv : 2 * kv, :] = spread[:, LANES:]
 
@@ -588,7 +592,7 @@
     half = device_count // 2 * capacity
     weighted, profile = call(
         functools.partial(profile_kernel, capacity),
-        (f32(wide, half), f32(wide, half)),
+        (f32(wide, cells), f32(wide, half)),
         (smoothed, *interp, *fetched),
         flops=400_000_000,
         mib=16,

time: 63.3 us -> 63.1 us (level)
  no operation moved by 1% of the time
where the time goes in v12:
time: 63.1 us; the launch traced here: 62.8 us
  blocking collectives  30.5 us (48%)
  starting transfers between devices  14.6 us (23%)
  waiting for transfers between devices  8.56 us (14%)
  Pallas kernels  8.19 us (13%)
  between operations  0.87 us (1%)
    all_to_all x1, blocking collectives, per_device_gathered(): lax.all_to_all(packed, 'gx', split_axis=0, concat_axis=0, tiled=True)  10.4 us
    all_to_all x1, blocking collectives, per_device_gathered(): lax.all_to_all(sums, ('gy', 'gx'), split_axis=0, concat_axis=0, tiled=True)  10.4 us
    all_to_all x1, blocking collectives, per_device_gathered(): lax.all_to_all(spread.reshape(cols_x, 2 * kv, LANES), 'gx', split_axis=0,...  9.63 us
    pallas_call x10, Pallas kernels, call(): pl.pallas_call(kernel, out_shape=out_shape, in_specs=specs, out_specs=tup...  8.19 us
    ppermute x7, starting transfers between devices, apart_by(): lax.ppermute(block, axis, [(i, i ^ stride) for i in range(lax.axis_size(a...  8.01 us
    ppermute x2, starting transfers between devices, from_neighbours(): lax.ppermute(block, 'gy', [(i, (i + (1 if i % 2 else -1)) % count) for i...  5.49 us
    ppermute x2, waiting for transfers between devices, from_neighbours(): lax.ppermute(block, 'gy', [(i, (i + (1 if i % 2 else -1)) % count) for i...  5.18 us
    ppermute x2, waiting for transfers between devices, from_neighbours(): pair = lax.ppermute(block, 'gy', [(i, i ^ 1) for i in range(count)])  1.75 us
  transfers between devices with their start and end apart: 11, of which 5 were waited for; matrix products, arithmetic and copies ran while one was open for 0% of the time, Pallas kernels for 5%

profile of v12, /device:TPU:0, one launch (start us, length us, event | category | flops | bytes accessed | tf_op | source)
XLA Modules:
  0.0 62.8 jit_solution(4863166401895129896)
XLA Ops:
  0.6 0.0 copy-start.3
  0.6 0.0 copy-start.11
  0.7 0.0 copy-start.7
  0.7 0.0 copy-start.8
  0.7 0.0 copy-start.9
  0.7 0.0 copy-start.10
  0.7 1.6 %shard_map.140 = f32[288,128]{1,0:T(8,128)} custom-call(f32[256,128]{1,0:T(8,128)} %bitcast.52, f32[16,128]{1,0:T(8,128)} %bitcast.65, f32[16,128]{1,0:T(8,128)} %bitcast.67, s32[16,128]{1,0:T(8,128)} %bitcast.69), custom_call_target="tpu_custom_call" | custom-call | flops 1000000 | bytes 155648 | tf_op jit(solution)/shard_map/pallas_call | solution.py:476
  2.3 0.0 copy-start
  2.3 4.0 %collective-permute-start.1 = (f32[288,128]{1,0:T(8,128)}, f32[288,128]{1,0:T(8,128)S(1)}, u32[]{:S(2)}, u32[]{:S(2)}) collective-permute-start(f32[288,128]{1,0:T(8,128)} %shard_map.140), channel_id=1, source_target_pairs={{0,24},{8,16},{16,8},{24,0},{1,25},{9,17},{17,9},{25,1},{2,26},{10... | collective-permute-start | bytes 442376 | tf_op jit(solution)/shard_map/ppermute | solution.py:494
  6.3 0.5 collective-permute-start
  6.8 0.0 copy-done.3
  6.8 3.6 %collective-permute-start.4 = (f32[1,128,128]{2,1,0:T(8,128)S(1)}, f32[1,128,128]{2,1,0:T(8,128)S(1)}, u32[]{:S(2)}, u32[]{:S(2)}) collective-permute-start(f32[1,128,128]{2,1,0:T(8,128)S(1)} %bitcast.61), channel_id=1, source_target_pairs={{0,6},{1,7},{2,4},{3,5},{4,2},{5,3},{6,0},{7,1},{8,14},{9,15},{10,... | collective-permute-start | bytes 196616 | tf_op jit(solution)/shard_map/ppermute | solution.py:499
  10.4 0.0 collective-permute-start.3
  10.4 0.8 %collective-permute-start.2 = (f32[1,128,128]{2,1,0:T(8,128)S(1)}, f32[1,128,128]{2,1,0:T(8,128)S(1)}, u32[]{:S(2)}, u32[]{:S(2)}) collective-permute-start(f32[1,128,128]{2,1,0:T(8,128)S(1)} %bitcast.63), channel_id=1, source_target_pairs={{0,2},{1,3},{2,0},{3,1},{4,6},{5,7},{6,4},{7,5},{8,10},{9,11},{10,... | collective-permute-start | bytes 196616 | tf_op jit(solution)/shard_map/ppermute | solution.py:499
  11.2 0.0 copy-done.11
  11.2 0.1 reshape.75.vert_ref
  11.3 0.0 copy-done.7
  11.3 0.0 copy-done.8
  11.3 0.0 copy-done.9
  11.4 0.0 copy-done.10
  11.4 0.0 copy-start.4
  11.4 0.0 copy-start.5
  11.4 0.0 copy-start.6
  11.4 1.1 %shard_map.139 = (f32[3,32,8,128]{3,2,1,0:T(8,128)S(1)}, bf16[256,1024]{1,0:T(8,128)(2,1)S(1)}, bf16[256,1024]{1,0:T(8,128)(2,1)S(1)}) custom-call(f32[32,2,128]{2,1,0:T(2,128)S(1)} %reshape.75.vert_ref, s32[1,512]{1,0:T(1,128)S(1)} %bitcast.72, s32[1,512]{1,0:T(1,128)S(1)} %bitcast.73, s32[1,512]{1,0:T(1,128)S(1)} %bitcast.74, f32[2,512]{1,0:T(2,128)S(1)} %bitcast.71), custom_call_target="tpu_custom_call" | custom-call | flops 20000000 | bytes 43008 | tf_op jit(solution)/shard_map/pallas_call | solution.py:476
  12.5 0.0 collective-permute-done.1.cross_ref
  12.6 1.2 %collective-permute-done.pair_ref = f32[288,128]{1,0:T(8,128)S(1)} collective-permute-done((f32[288,128]{1,0:T(8,128)}, f32[288,128]{1,0:T(8,128)S(1)}, u32[]{:S(2)}, u32[]{:S(2)}) %collective-permute-start) | collective-permute-done | bytes 147488 | tf_op jit(solution)/shard_map/ppermute | solution.py:493
  13.8 0.0 copy-done
  13.8 0.0 copy-done.4
  13.8 0.0 copy-done.5
  13.8 0.0 copy-done.6
  13.8 0.9 %shard_map.141 = (f32[8,32,128]{2,1,0:T(8,128)S(1)}, f32[5,16,512]{2,1,0:T(8,128)S(1)}) custom-call(bf16[256,1024]{1,0:T(8,128)(2,1)S(1)} %get-tuple-element.15._.high_ref, f32[256,128]{1,0:T(8,128)S(1)} %bitcast.53, f32[16,128]{1,0:T(8,128)S(1)} %bitcast.66, f32[16,128]{1,0:T(8,128)S(1)} %bitcast.68, s32[16,128]{1,0:T(8,128)S(1)} %bitcast.70, ...), custom_call_target="tpu_custom_call" | custom-call | flops 4000000 | bytes 1499136 | tf_op jit(solution)/shard_map/pallas_call | solution.py:476
  14.6 0.0 collective-permute-done.4.refs_3_
  14.7 1.0 %collective-permute-done.3.refs_2_ = f32[1,128,128]{2,1,0:T(8,128)S(1)} collective-permute-done((f32[1,128,128]{2,1,0:T(8,128)S(1)}, f32[1,128,128]{2,1,0:T(8,128)S(1)}, u32[]{:S(2)}, u32[]{:S(2)}) %collective-permute-start.3) | collective-permute-done | bytes 65568 | tf_op jit(solution)/shard_map/ppermute | solution.py:499
  15.7 0.0 collective-permute-done.2.refs_1_
  15.7 0.1 shard_map.143.refs_0_
  15.8 1.5 %collective-permute-start.7 = (f32[4,120,128]{2,1,0:T(8,128)S(1)}, f32[4,120,128]{2,1,0:T(8,128)S(1)}, u32[]{:S(2)}, u32[]{:S(2)}) collective-permute-start(f32[4,120,128]{2,1,0:T(8,128)S(1)} %shard_map.143.refs_0_), channel_id=1, source_target_pairs={{0,24},{8,16},{16,8},{24,0},{1,25},{9,17},{17,9},{25,1},{2,26},{10... | collective-permute-start | bytes 737288 | tf_op jit(solution)/shard_map/ppermute | solution.py:499
  17.3 1.5 %collective-permute-start.6 = (f32[4,120,128]{2,1,0:T(8,128)S(1)}, f32[4,120,128]{2,1,0:T(8,128)S(1)}, u32[]{:S(2)}, u32[]{:S(2)}) collective-permute-start(f32[4,120,128]{2,1,0:T(8,128)S(1)} %shard_map.143.refs_0_), channel_id=1, source_target_pairs={{0,16},{8,24},{16,0},{24,8},{1,17},{9,25},{17,1},{25,9},{2,18},{10... | collective-permute-start | bytes 737288 | tf_op jit(solution)/shard_map/ppermute | solution.py:499
  18.8 0.5 collective-permute-start.5
  19.3 10.4 %all_to_all.15._ = f32[8,32,128]{2,1,0:T(8,128)S(1)} all-to-all(f32[8,32,128]{2,1,0:T(8,128)S(1)} %get-tuple-element.16._), channel_id=1, replica_groups=mesh['gy'=4,'gx'=8] {'gx'}, dimensions={0} | all-to-all | bytes 262144 | tf_op jit(solution)/shard_map/all_to_all | solution.py:578
  29.8 0.0 collective-permute-done.7.refs_3_
  29.8 0.0 collective-permute-done.6.refs_2_
  29.8 0.0 collective-permute-done.5.refs_1_
  29.8 0.1 collective-permute-start.8
  29.9 0.1 shard_map.142.column_ref
  30.1 1.2 %shard_map.144 = (f32[128,256]{1,0:T(8,128)S(1)}, f32[128,512]{1,0:T(8,128)S(1)}) custom-call(f32[256,128]{1,0:T(8,128)S(1)} %shard_map.142.column_ref, bf16[256,1024]{1,0:T(8,128)(2,1)S(1)} %get-tuple-element.15._.high_ref, bf16[256,1024]{1,0:T(8,128)(2,1)S(1)} %get-tuple-element.18.low_ref, f32[4,120,128]{2,1,0:T(8,128)S(1)} %shard_map.143.refs_0_, ...), custom_call_target="tpu_custom_call" | custom-call | flops 400000000 | bytes 3211264 | tf_op jit(solution)/shard_map/pallas_call | solution.py:476
  31.3 0.6 collective-permute-done.8.far_ref
  31.9 1.2 %shard_map.146 = f32[256,128]{1,0:T(8,128)S(1)} custom-call(f32[128,256]{1,0:T(8,128)S(1)} %get-tuple-element.19.near_ref, f32[128,512]{1,0:T(8,128)S(1)} %get-tuple-element.20.profile_ref, f32[3,32,8,128]{3,2,1,0:T(8,128)S(1)} %get-tuple-element.17.factor_ref, bf16[256,1024]{1,0:T(8,128)(2,1)S(1)} %get-tuple-element.15._.high_ref, ...), custom_call_target="tpu_custom_call" | custom-call | flops 400000000 | bytes 3473408 | tf_op jit(solution)/shard_map/pallas_call | solution.py:476
  33.1 0.0 copy-start.1
  33.1 9.6 %all_to_all.16.own_ref = f32[8,32,128]{2,1,0:T(8,128)S(1)} all-to-all(f32[8,32,128]{2,1,0:T(8,128)S(1)} %bitcast.57), channel_id=1, replica_groups=mesh['gy'=4,'gx'=8] {'gx'}, dimensions={0} | all-to-all | bytes 262144 | tf_op jit(solution)/shard_map/all_to_all | solution.py:608
  42.8 1.5 %collective-permute-start.10 = (f32[8,32,128]{2,1,0:T(8,128)S(1)}, f32[8,32,128]{2,1,0:T(8,128)S(1)}, u32[]{:S(2)}, u32[]{:S(2)}) collective-permute-start(f32[8,32,128]{2,1,0:T(8,128)S(1)} %all_to_all.16.own_ref), channel_id=1, source_target_pairs={{0,24},{8,16},{16,8},{24,0},{1,25},{9,17},{17,9},{25,1},{2,26},{10... | collective-permute-start | bytes 393224 | tf_op jit(solution)/shard_map/ppermute | solution.py:494
  44.3 0.5 collective-permute-start.9
  44.8 5.2 %collective-permute-done.10.cross_ref = f32[8,32,128]{2,1,0:T(8,128)S(1)} collective-permute-done((f32[8,32,128]{2,1,0:T(8,128)S(1)}, f32[8,32,128]{2,1,0:T(8,128)S(1)}, u32[]{:S(2)}, u32[]{:S(2)}) %collective-permute-start.10) | collective-permute-done | bytes 131104 | tf_op jit(solution)/shard_map/ppermute | solution.py:494
  50.0 0.5 collective-permute-done.9.pair_ref
  50.6 0.0 copy-done.1
  50.6 0.0 copy-start.2
  50.6 0.9 %shard_map.147 = (f32[256,128]{1,0:T(8,128)S(1)}, f32[32,1,128]{2,1,0:T(1,128)S(1)}) custom-call(f32[8,32,128]{2,1,0:T(8,128)S(1)} %all_to_all.16.own_ref, f32[8,32,128]{2,1,0:T(8,128)S(1)} %collective-permute-done.9.pair_ref, f32[8,32,128]{2,1,0:T(8,128)S(1)} %collective-permute-done.10.cross_ref, f32[5,16,512]{2,1,0:T(8,128)S(1)} %get-tuple-element.21.coef_ref, ...), custom_call_target="tpu_custom_call" | custom-call | flops 4000000 | bytes 819200 | tf_op jit(solution)/shard_map/pallas_call | solution.py:476
  51.5 10.4 %all_to_all.17.sums_ref = f32[32,1,128]{2,1,0:T(1,128)S(1)} all-to-all(f32[32,1,128]{2,1,0:T(1,128)S(1)} %get-tuple-element.22), channel_id=1, replica_groups=mesh['gy'=4,'gx'=8] {'gy','gx'}, dimensions={0} | all-to-all | bytes 32768 | tf_op jit(solution)/shard_map/all_to_all | solution.py:619
  61.9 0.0 copy-done.2
  61.9 0.9 %shard_map.148 = (f32[256,128]{1,0:T(8,128)}, f32[256,128]{1,0:T(8,128)}, f32[256,128]{1,0:T(8,128)}) custom-call(f32[32,1,128]{2,1,0:T(1,128)S(1)} %all_to_all.17.sums_ref, f32[256,128]{1,0:T(8,128)S(1)} %bitcast.55, f32[256,128]{1,0:T(8,128)S(1)} %bitcast.60, f32[256,128]{1,0:T(8,128)S(1)} %bitcast.59, f32[256,128]{1,0:T(8,128)S(1)} %get-tuple-element.23.image_ref), custom_call_target="tpu_custom_call" | custom-call | flops 1000000 | bytes 540672 | tf_op jit(solution)/shard_map/pallas_call | solution.py:476
  (1 shorter events, 0.0 us)
Async XLA Ops:
  0.6 6.2 %copy-start.3 = (f32[1,1,128,128]{3,2,1,0:T(8,128)S(1)}, f32[1,1,128,128]{3,2,1,0:T(8,128)}, u32[]{:S(2)}) copy-start(f32[1,1,128,128]{3,2,1,0:T(8,128)} %param.23) | copy-start | bytes 196612
  0.6 10.6 %copy-start.11 = (f32[32,4,64]{2,1,0:T(4,128)S(1)}, f32[32,4,64]{2,1,0:T(4,128)}, u32[]{:S(2)}) copy-start(f32[32,4,64]{2,1,0:T(4,128)} %param.18) | copy-start | bytes 98308
  0.7 10.7 %copy-start.7 = (f32[1,1,2,512]{3,2,1,0:T(2,128)S(1)}, f32[1,1,2,512]{3,2,1,0:T(2,128)}, u32[]{:S(2)}) copy-start(f32[1,1,2,512]{3,2,1,0:T(2,128)} %param.22) | copy-start | bytes 12292
  0.7 10.7 %copy-start.8 = (s32[1,1,512,1]{2,3,1,0:T(1,128)S(1)}, s32[1,1,512,1]{2,3,1,0:T(1,128)}, u32[]{:S(2)}) copy-start(s32[1,1,512,1]{2,3,1,0:T(1,128)} %param.19) | copy-start | bytes 6148
  0.7 10.7 %copy-start.9 = (s32[1,1,512]{2,1,0:T(1,128)S(1)}, s32[1,1,512]{2,1,0:T(1,128)}, u32[]{:S(2)}) copy-start(s32[1,1,512]{2,1,0:T(1,128)} %param.20) | copy-start | bytes 6148
  0.7 10.7 %copy-start.10 = (s32[1,1,512]{2,1,0:T(1,128)S(1)}, s32[1,1,512]{2,1,0:T(1,128)}, u32[]{:S(2)}) copy-start(s32[1,1,512]{2,1,0:T(1,128)} %param.21) | copy-start | bytes 6148
  2.3 11.4 %copy-start = (f32[4,4,4,512]{3,2,1,0:T(4,128)S(1)}, f32[4,4,4,512]{3,2,1,0:T(4,128)}, u32[]{:S(2)}) copy-start(f32[4,4,4,512]{3,2,1,0:T(4,128)} %param.12) | copy-start | bytes 393220
  2.3 10.2 %collective-permute-start.1 = (f32[288,128]{1,0:T(8,128)}, f32[288,128]{1,0:T(8,128)S(1)}, u32[]{:S(2)}, u32[]{:S(2)}) collective-permute-start(f32[288,128]{1,0:T(8,128)} %shard_map.140), channel_id=1, source_target_pairs={{0,24},{8,16},{16,8},{24,0},{1,25},{9,17},{17,9},{25,1},{2,26},{10... | collective-permute-start | bytes 442376 | tf_op jit(solution)/shard_map/ppermute | solution.py:494
  6.3 7.5 %collective-permute-start = (f32[288,128]{1,0:T(8,128)}, f32[288,128]{1,0:T(8,128)S(1)}, u32[]{:S(2)}, u32[]{:S(2)}) collective-permute-start(f32[288,128]{1,0:T(8,128)} %shard_map.140), channel_id=1, source_target_pairs={{0,8},{8,0},{16,24},{24,16},{1,9},{9,1},{17,25},{25,17},{2,10},{10... | collective-permute-start | bytes 442376 | tf_op jit(solution)/shard_map/ppermute | solution.py:493
  6.8 7.8 %collective-permute-start.4 = (f32[1,128,128]{2,1,0:T(8,128)S(1)}, f32[1,128,128]{2,1,0:T(8,128)S(1)}, u32[]{:S(2)}, u32[]{:S(2)}) collective-permute-start(f32[1,128,128]{2,1,0:T(8,128)S(1)} %bitcast.61), channel_id=1, source_target_pairs={{0,6},{1,7},{2,4},{3,5},{4,2},{5,3},{6,0},{7,1},{8,14},{9,15},{10,... | collective-permute-start | bytes 196616 | tf_op jit(solution)/shard_map/ppermute | solution.py:499
  10.4 5.2 %collective-permute-start.3 = (f32[1,128,128]{2,1,0:T(8,128)S(1)}, f32[1,128,128]{2,1,0:T(8,128)S(1)}, u32[]{:S(2)}, u32[]{:S(2)}) collective-permute-start(f32[1,128,128]{2,1,0:T(8,128)S(1)} %bitcast.62), channel_id=1, source_target_pairs={{0,4},{1,5},{2,6},{3,7},{4,0},{5,1},{6,2},{7,3},{8,12},{9,13},{10,... | collective-permute-start | bytes 196616 | tf_op jit(solution)/shard_map/ppermute | solution.py:499
  10.4 5.2 %collective-permute-start.2 = (f32[1,128,128]{2,1,0:T(8,128)S(1)}, f32[1,128,128]{2,1,0:T(8,128)S(1)}, u32[]{:S(2)}, u32[]{:S(2)}) collective-permute-start(f32[1,128,128]{2,1,0:T(8,128)S(1)} %bitcast.63), channel_id=1, source_target_pairs={{0,2},{1,3},{2,0},{3,1},{4,6},{5,7},{6,4},{7,5},{8,10},{9,11},{10,... | collective-permute-start | bytes 196616 | tf_op jit(solution)/shard_map/ppermute | solution.py:499
  11.4 2.4 %copy-start.4 = (f32[4,512]{1,0:T(4,128)S(1)}, f32[4,512]{1,0:T(4,128)}, u32[]{:S(2)}) copy-start(f32[4,512]{1,0:T(4,128)} %param.15) | copy-start | bytes 24580
  11.4 2.4 %copy-start.5 = (f32[4,512]{1,0:T(4,128)S(1)}, f32[4,512]{1,0:T(4,128)}, u32[]{:S(2)}) copy-start(f32[4,512]{1,0:T(4,128)} %param.16) | copy-start | bytes 24580
  11.4 2.4 %copy-start.6 = (s32[4,512]{1,0:T(4,128)S(1)}, s32[4,512]{1,0:T(4,128)}, u32[]{:S(2)}) copy-start(s32[4,512]{1,0:T(4,128)} %param.17) | copy-start | bytes 24580
  15.8 14.0 %collective-permute-start.7 = (f32[4,120,128]{2,1,0:T(8,128)S(1)}, f32[4,120,128]{2,1,0:T(8,128)S(1)}, u32[]{:S(2)}, u32[]{:S(2)}) collective-permute-start(f32[4,120,128]{2,1,0:T(8,128)S(1)} %shard_map.143.refs_0_), channel_id=1, source_target_pairs={{0,24},{8,16},{16,8},{24,0},{1,25},{9,17},{17,9},{25,1},{2,26},{10... | collective-permute-start | bytes 737288 | tf_op jit(solution)/shard_map/ppermute | solution.py:499
  17.3 12.5 %collective-permute-start.6 = (f32[4,120,128]{2,1,0:T(8,128)S(1)}, f32[4,120,128]{2,1,0:T(8,128)S(1)}, u32[]{:S(2)}, u32[]{:S(2)}) collective-permute-start(f32[4,120,128]{2,1,0:T(8,128)S(1)} %shard_map.143.refs_0_), channel_id=1, source_target_pairs={{0,16},{8,24},{16,0},{24,8},{1,17},{9,25},{17,1},{25,9},{2,18},{10... | collective-permute-start | bytes 737288 | tf_op jit(solution)/shard_map/ppermute | solution.py:499
  18.8 11.0 %collective-permute-start.5 = (f32[4,120,128]{2,1,0:T(8,128)S(1)}, f32[4,120,128]{2,1,0:T(8,128)S(1)}, u32[]{:S(2)}, u32[]{:S(2)}) collective-permute-start(f32[4,120,128]{2,1,0:T(8,128)S(1)} %shard_map.143.refs_0_), channel_id=1, source_target_pairs={{0,8},{8,0},{16,24},{24,16},{1,9},{9,1},{17,25},{25,17},{2,10},{10... | collective-permute-start | bytes 737288 | tf_op jit(solution)/shard_map/ppermute | solution.py:499
  29.8 2.1 %collective-permute-start.8 = (f32[16,72,128]{2,1,0:T(8,128)S(1)}, f32[16,72,128]{2,1,0:T(8,128)S(1)}, u32[]{:S(2)}, u32[]{:S(2)}) collective-permute-start(f32[16,72,128]{2,1,0:T(8,128)S(1)} %shard_map.145), channel_id=1, source_target_pairs={{0,1},{1,0},{2,3},{3,2},{4,5},{5,4},{6,7},{7,6},{8,9},{9,8},{10,11... | collective-permute-start | bytes 1769480 | tf_op jit(solution)/shard_map/ppermute | solution.py:499
  33.1 17.4 %copy-start.1 = (f32[4,4,4,512]{3,2,1,0:T(4,128)S(1)}, f32[4,4,4,512]{3,2,1,0:T(4,128)}, u32[]{:S(2)}) copy-start(f32[4,4,4,512]{3,2,1,0:T(4,128)} %param.14) | copy-start | bytes 393220
  42.8 7.2 %collective-permute-start.10 = (f32[8,32,128]{2,1,0:T(8,128)S(1)}, f32[8,32,128]{2,1,0:T(8,128)S(1)}, u32[]{:S(2)}, u32[]{:S(2)}) collective-permute-start(f32[8,32,128]{2,1,0:T(8,128)S(1)} %all_to_all.16.own_ref), channel_id=1, source_target_pairs={{0,24},{8,16},{16,8},{24,0},{1,25},{9,17},{17,9},{25,1},{2,26},{10... | collective-permute-start | bytes 393224 | tf_op jit(solution)/shard_map/ppermute | solution.py:494
  44.3 6.3 %collective-permute-start.9 = (f32[8,32,128]{2,1,0:T(8,128)S(1)}, f32[8,32,128]{2,1,0:T(8,128)S(1)}, u32[]{:S(2)}, u32[]{:S(2)}) collective-permute-start(f32[8,32,128]{2,1,0:T(8,128)S(1)} %all_to_all.16.own_ref), channel_id=1, source_target_pairs={{0,8},{8,0},{16,24},{24,16},{1,9},{9,1},{17,25},{25,17},{2,10},{10... | collective-permute-start | bytes 393224 | tf_op jit(solution)/shard_map/ppermute | solution.py:493
  50.6 11.4 %copy-start.2 = (f32[4,4,4,512]{3,2,1,0:T(4,128)S(1)}, f32[4,4,4,512]{3,2,1,0:T(4,128)}, u32[]{:S(2)}) copy-start(f32[4,4,4,512]{3,2,1,0:T(4,128)} %param.13) | copy-start | bytes 393220
